TPU v7x, 32 devices: a whole 2x2x4 slice. The times are simulated.
32 devices in a mesh: wide: 8 (over y, x, core), narrow: 4 (over z).
Axes of the slice: x: 2, y: 2, z: 4, core: 2. Of those that a mesh axis runs over, the one named last changes fastest.
Arguments:
- state: float32 [512, 512, 128], P('wide', 'narrow'), may hold values from -6 to 6
- volatility: float32 [512, 512, 128], P('wide', 'narrow'), may hold values from 0.2 to 1.2
- cotangent: float32 [512, 512, 128], P('wide', 'narrow'), may hold values from -6 to 6
- solve_first: float32 [512, 512], replicated, may hold values from -2 to 2
- solve_second: float32 [512, 512], replicated, may hold values from -2 to 2
- solve_third: float32 [128, 128], replicated, may hold values from -2 to 2
- patch_index: int32 [512, 512], P('wide', 'narrow'), may hold values from 0 to 3071
Outputs:
- adjoint: float32 [512, 512, 128], P('wide', 'narrow')
- vega: float32 [3072], P(('wide', 'narrow'))
All inputs are finite; a program needn't handle non-finite values.
Results may differ from a plain program's by a relative error of at most 0.000071.
Values sent between devices are 32-bit elements; how exact they have to be, the bound alone decides.
No kernel may reach another device: no remote copies, remote signals or barrier semaphores. Data moves between devices by JAX's collectives and lax.ppermute only.
A program may use at most 320 MiB of HBM per device.

v0:
```python
import jax
import jax.numpy as jnp
from jax import lax
from jax.sharding import PartitionSpec as P

PATCHES = 3072


time_step = 0.4
theta_weight = 0.5
frozen_coef = 0.2
correction = 0.5 * 0.4
vega_scale = 1.0 / 32.0
correlations = ((0, 1, 0.5), (0, 2, 0.3), (1, 2, -0.4))


def padded_2(cells, sides, width):
    for axis, dim in sides:
        count = lax.axis_size(axis)
        ends = count - 1
        head = lax.slice_in_dim(cells, 0, width, axis=dim)
        tail = lax.slice_in_dim(cells, cells.shape[dim] - width, cells.shape[dim], axis=dim)
        cells = jnp.concatenate(
            [
                lax.ppermute(tail, axis, [(i, (i + 1) % count) for i in range(ends)]),
                cells,
                lax.ppermute(head, axis, [((i + 1) % count, i) for i in range(ends)]),
            ],
            axis=dim,
        )
    return cells


def along_third(values, offset):
    if offset == 0:
        return values
    zero_layer = jnp.zeros_like(values[..., :1])
    if offset > 0:
        return jnp.concatenate([values[..., 1:], zero_layer], axis=-1)
    return jnp.concatenate([zero_layer, values[..., :-1]], axis=-1)


def shifted(padded, offsets):
    lead = padded.ndim - 3
    slices = [slice(None)] * lead
    for position in range(2):
        offset = offsets[position]
        length = padded.shape[lead + position]
        slices.append(slice(1 + offset, length - 1 + offset))
    slices.append(slice(None))
    return along_third(padded[tuple(slices)], offsets[2])


def second_parts(padded):
    centre = shifted(padded, [0, 0, 0])
    result = []
    for axis_number in range(3):
        upward = [0, 0, 0]
        upward[axis_number] = 1
        downward = [0, 0, 0]
        downward[axis_number] = -1
        result.append(shifted(padded, upward) + shifted(padded, downward) - 2.0 * centre)
    return tuple(result)


def cross_term(padded, first_axis, second_axis):

    def corner(sign_first, sign_second):
        offsets = [0, 0, 0]
        offsets[first_axis] = sign_first
        offsets[second_axis] = sign_second
        return shifted(padded, offsets)

    return 0.25 * (corner(1, 1) - corner(1, -1) - corner(-1, 1) + corner(-1, -1))


def mixed_of(padded):
    total = None
    for first_axis, second_axis, weight in correlations:
        term = weight * cross_term(padded, first_axis, second_axis)
        total = term if total is None else total + term
    return total


def contract(matrix, field, axis_number, transposed):
    letters = "xyz"
    source = letters[axis_number]
    matrix_form = source + "w" if transposed else "w" + source
    result_form = letters.replace(source, "w")
    return jnp.einsum(
        matrix_form + "," + letters + "->" + result_form,
        matrix,
        field,
        precision=lax.Precision.HIGHEST,
    )


def line_x(field, matrix, transposed):

    def solve_lines(pieces):
        solved = contract(matrix, pieces, 0, transposed)
        return lax.all_to_all(solved, "wide", split_axis=0, concat_axis=1, tiled=True)

    return solve_lines(lax.all_to_all(field, "wide", split_axis=1, concat_axis=0, tiled=True))


def line_y(field, matrix, transposed):

    def solve_lines(pieces):
        solved = contract(matrix, pieces, 1, transposed)
        return lax.all_to_all(solved, "narrow", split_axis=1, concat_axis=2, tiled=True)

    return solve_lines(lax.all_to_all(field, "narrow", split_axis=2, concat_axis=1, tiled=True))


def rimmed(stacked):
    return padded_2(stacked, (("wide", 1), ("narrow", 2)), 1)


def third_second(field):
    return along_third(field, 1) + along_third(field, -1) - 2.0 * field


def on_device(state, volatility, cotangent, solve_first, solve_second, solve_third, patch_index):
    coefficient = 0.5 * volatility * volatility
    padded = rimmed(state[None])
    parts = second_parts(padded)
    second_x, second_y, second_z = (parts[0][0], parts[1][0], parts[2][0])
    source = mixed_of(padded)[0] + second_x + second_y + second_z
    start = state + time_step * coefficient * source
    damping = theta_weight * time_step * frozen_coef
    level = line_x(start - damping * second_x, solve_first, False)
    level = line_y(level - damping * second_y, solve_second, False)
    level = contract(solve_third, level - damping * second_z, 2, False)
    drift = mixed_of(rimmed((level - state)[None]))[0]
    back_third = contract(solve_third, cotangent, 2, True)
    back_second = line_y(back_third, solve_second, True)
    carried = line_x(back_second, solve_first, True)
    reaction = mixed_of(rimmed((correction * coefficient * carried)[None]))[0]
    total = cotangent + reaction
    upper_third = contract(solve_third, total, 2, True)
    upper_second = line_y(upper_third, solve_second, True)
    adjoint_start = line_x(upper_second, solve_first, True)
    scaled = time_step * coefficient * adjoint_start
    padded = rimmed(jnp.stack([scaled, adjoint_start, upper_second]))
    parts = second_parts(padded)
    spread = mixed_of(padded[0:1])[0] + parts[0][0] + parts[1][0] + parts[2][0]
    lines = parts[0][1] + parts[1][2] + third_second(upper_third)
    adjoint = adjoint_start + spread - reaction - damping * lines
    sensitivity = volatility * (correction * carried * drift + time_step * adjoint_start * source)
    column = jnp.sum(sensitivity, axis=2)
    partial_sums = jax.ops.segment_sum(
        column.reshape(-1), patch_index.reshape(-1), num_segments=PATCHES
    )
    vega = lax.psum_scatter(partial_sums, ("wide", "narrow"), scatter_dimension=0, tiled=True)
    return (adjoint, vega * vega_scale)


def solution(mesh):
    placed = (
        P("wide", "narrow", None),
        P("wide", "narrow", None),
        P("wide", "narrow", None),
        P(),
        P(),
        P(),
        P("wide", "narrow"),
    )
    return jax.shard_map(
        on_device,
        mesh=mesh,
        in_specs=placed,
        out_specs=(P("wide", "narrow", None), P(("wide", "narrow"))),
        check_vma=False,
    )
```

profile of v0, /device:TPU:0, one launch (start us, length us, event | category | flops | bytes accessed | tf_op | source)
XLA Modules:
  0.0 1405.9 jit_solution(14329647489158471148)
XLA Ops:
  12.7 99.5 %all_to_all.216 = f32[64,128,128]{1,0,2:T(8,128)S(1)} all-to-all(f32[64,128,128]{1,0,2:T(8,128)} %copy.115), channel_id=1, replica_groups=mesh['wide'=8,'narrow'=4] {'narrow'}, dimensions={2} | all-to-all | bytes 8388608 | tf_op jit(solution)/shard_map/all_to_all | solution.py:113
  122.3 9.8 convolution_bitcast_fusion.2
  149.9 98.2 %all_to_all.217 = f32[4,1,262144]{2,1,0:T(1,128)} all-to-all(f32[4,1,262144]{2,1,0:T(1,128)} %reshape.38), channel_id=1, replica_groups=mesh['wide'=8,'narrow'=4] {'narrow'}, dimensions={0} | all-to-all | bytes 8388608 | tf_op jit(solution)/shard_map/all_to_all | solution.py:111
  248.6 15.3 %reduce = f32[4,262144]{1,0:T(4,128)} reduce(f32[4,1,262144]{2,1,0:T(1,128)} %all_to_all.217, f32[]{:T(128)} %broadcast.194), dimensions={1}, to_apply=%all_to_all.160.reduce_sub_computation | reduce | bytes 8388612 | tf_op jit(solution)/shard_map/all_to_all | solution.py:111
  263.9 9.3 reshape.39
  308.6 36.1 %all-to-all-done.2 = f32[64,128,128]{2,0,1:T(8,128)} async-done(((f32[64,128,128]{2,0,1:T(8,128)}), f32[64,128,128]{2,0,1:T(8,128)}, u32[]{:S(2)}, u32[]{:S(2)}) %all-to-all-start.2) | async-done | bytes 4194336 | tf_op jit(solution)/shard_map/all_to_all | solution.py:104
  349.3 9.5 fusion.66
  364.2 18.2 %all-to-all-start.3 = ((f32[512,16,128]{2,1,0:T(8,128)}), f32[512,16,128]{2,1,0:T(8,128)}, u32[]{:S(2)}, u32[]{:S(2)}) async-start(f32[512,16,128]{2,1,0:T(8,128)} %copy.125), calls=%async_computation.3 | async-start | bytes 8388608 | tf_op jit(solution)/shard_map/all_to_all | solution.py:102
  382.4 16.6 %fusion.10 = (f32[1,64,128,127]{3,2,1,0:T(8,128)}, f32[1,64,128,127]{3,2,1,0:T(8,128)}, f32[1,64,128,127]{3,2,1,0:T(8,128)}, f32[1,64,128,127]{3,2,1,0:T(8,128)}...) fusion(f32[1,1,128,128]{3,2,1,0:T(8,128)S(1)} %collective-permute-done.9, f32[1,64,128,128]{3,2,1,0:T(8,128)} %bitcast.170, ...), kind=kLoop, calls=%fused_computation.41 | loop fusion | flops 4161536 | bytes 37683200 | tf_op jit(solution)/shard_map/concatenate | solution.py:23
  409.6 27.7 %bitcast_subtract_fusion.3 = (f32[64,128,128]{2,1,0:T(8,128)}, f32[64,128,128]{2,1,0:T(8,128)}) fusion(f32[64,128,128]{2,1,0:T(8,128)S(1)} %copy-done.2, f32[64,128,128]{2,1,0:T(8,128)} %param.8, f32[1,64,128,128]{3,2,1,0:T(8,128)S(1)} %bitcast.172, f32[1,1,128,128]{3,2,1,0:T(8,128)S(1)} %collective-permute-done.8, ...), kind=kLoop, calls=%fused_computation.127 | loop fusion | flops 34603008 | bytes 87883776 | tf_op jit(solution)/shard_map/sub | solution.py:132
  482.1 21.2 %fusion.51 = f32[64,128,128]{2,1,0:T(8,128)} fusion(f32[1,64,128,128]{3,2,1,0:T(8,128)} %bitcast.187, f32[1,1,128,128]{3,2,1,0:T(8,128)S(1)} %collective-permute-done, f32[1,1,128,128]{3,2,1,0:T(8,128)S(1)} %collective-permute-done.1, f32[1,66,129,128]{3,2,1,0:T(8,128)} %copy-done.18, f32[1,66,129,128]{3,2,1,0:T(8,128)} %copy-done.17, ...), kind=kLoop, calls=%fused_computation.115 | loop fusion | flops 22020096 | bytes 50266112 | tf_op jit(solution)/shard_map/squeeze | solution.py:139
  525.8 16.1 %fusion.72 = f32[512,16,128]{0,2,1:T(8,128)} fusion(f32[512,16,128]{2,1,0:T(8,128)S(1)} %bitcast.202, f32[512,512]{1,0:T(8,128)S(1)} %copy-done.22), kind=kOutput, calls=%fused_computation.146 | convolution fusion | flops 6442450944 | bytes 9437184 | tf_op jit(solution)/shard_map/wx,xyz->wyz/dot_general | solution.py:90
  547.3 54.7 %all-to-all-done.4 = f32[64,128,128]{1,0,2:T(8,128)} async-done(((f32[64,128,128]{1,0,2:T(8,128)}), f32[64,128,128]{1,0,2:T(8,128)}, u32[]{:S(2)}, u32[]{:S(2)}) %all-to-all-start.4) | async-done | bytes 4194336 | tf_op jit(solution)/shard_map/all_to_all | solution.py:113
  602.0 52.5 %all-to-all-start.9 = ((f32[512,16,128]{2,1,0:T(8,128)}), f32[512,16,128]{2,1,0:T(8,128)}, u32[]{:S(2)}, u32[]{:S(2)}) async-start(f32[512,16,128]{2,1,0:T(8,128)} %copy.146), calls=%async_computation.9 | async-start | bytes 8388608 | tf_op jit(solution)/shard_map/all_to_all | solution.py:102
  666.9 9.9 convolution_bitcast_fusion.1
  724.6 74.6 %all-to-all-done.5 = f32[4,1,262144]{2,1,0:T(1,128)} async-done(((f32[4,1,262144]{2,1,0:T(1,128)}), f32[4,1,262144]{2,1,0:T(1,128)}, u32[]{:S(2)}, u32[]{:S(2)}) %all-to-all-start.5) | async-done | bytes 4194336 | tf_op jit(solution)/shard_map/all_to_all | solution.py:111
  804.2 15.3 %reduce.1 = f32[4,262144]{1,0:T(4,128)} reduce(f32[4,1,262144]{2,1,0:T(1,128)} %all-to-all-done.5, f32[]{:T(128)} %broadcast.194), dimensions={1}, to_apply=%all_to_all.176.reduce_sub_computation | reduce | bytes 8388612 | tf_op jit(solution)/shard_map/all_to_all | solution.py:111
  819.6 9.3 reshape.41
  846.8 50.1 %all-to-all-done.10 = f32[64,128,128]{1,0,2:T(8,128)} async-done(((f32[64,128,128]{1,0,2:T(8,128)}), f32[64,128,128]{1,0,2:T(8,128)}, u32[]{:S(2)}, u32[]{:S(2)}) %all-to-all-start.10) | async-done | bytes 4194336 | tf_op jit(solution)/shard_map/all_to_all | solution.py:113
  914.7 10.0 convolution_bitcast_fusion
  961.1 9.5 fusion.69
  976.1 71.0 %all-to-all-done.11 = f32[4,1,262144]{2,1,0:T(1,128)} async-done(((f32[4,1,262144]{2,1,0:T(1,128)}), f32[4,1,262144]{2,1,0:T(1,128)}, u32[]{:S(2)}, u32[]{:S(2)}) %all-to-all-start.11) | async-done | bytes 4194336 | tf_op jit(solution)/shard_map/all_to_all | solution.py:111
  1052.2 15.3 %reduce.2 = f32[4,262144]{1,0:T(4,128)} reduce(f32[4,1,262144]{2,1,0:T(1,128)} %all-to-all-done.11, f32[]{:T(128)} %broadcast.194), dimensions={1}, to_apply=%all_to_all.200.reduce_sub_computation | reduce | bytes 8388612 | tf_op jit(solution)/shard_map/all_to_all | solution.py:111
  1094.9 9.5 subtract_bitcast_fusion
  1149.5 21.3 %fusion.18 = (f32[64,128,128]{2,1,0:T(8,128)}, f32[64,128,128]{2,1,0:T(8,128)}) fusion(f32[64,128,128]{2,1,0:T(8,128)} %param.8, f32[1,64,128,128]{3,2,1,0:T(8,128)S(1)} %copy-done.12, f32[1,1,128,128]{3,2,1,0:T(8,128)S(1)} %collective-permute-done.12, f32[1,1,128,128]{3,2,1,0:T(8,128)S(1)} %collective-permute-done.13, f32[1,66,129,128]{3,2,1,0:T(8,128)} %copy-done.16, ...), kind=kLoop, calls=%fused_computation.50 | loop fusion | flops 32505856 | bytes 71237632 | tf_op jit(solution)/shard_map/mul | solution.py:150
  1170.9 9.9 pad_maximum_fusion.7
  1187.4 21.6 %fusion.94 = (f32[3,64,128,127]{3,2,1,0:T(8,128)}, f32[3,64,128,127]{3,2,1,0:T(8,128)}) fusion(f32[3,64,128,128]{3,2,1,0:T(8,128)} %pad_maximum_fusion.7), kind=kLoop, calls=%fused_computation.183 | loop fusion | bytes 49938432 | tf_op jit(solution)/shard_map/slice | solution.py:39
  1212.4 43.4 %scatter_custom_fusion = f32[3072]{0:T(1024)S(1)} fusion(s32[8192]{0:T(1024)} %bitcast.206, f32[8192]{0:T(1024)S(1)} %bitcast.205, f32[]{:T(128)} %constant.15.clone.1), kind=kCustom, calls=%fused_computation.175 | custom fusion | flops 8192 | bytes 12800 | tf_op jit(solution)/shard_map/scatter-add | solution.py:152
  1255.7 40.0 %all-reduce.38 = f32[3072]{0:T(1024)S(1)} all-reduce(f32[3072]{0:T(1024)S(1)} %scatter_custom_fusion), channel_id=2, replica_groups=mesh['wide'=8,'narrow'=4] {'wide','narrow'}, use_global_device_ids=true, to_apply=%region_2.0.clone | all-reduce | flops 3072 | bytes 24576
  1306.0 10.8 pad_maximum_fusion
  1332.1 33.9 %broadcast_multiply_fusion = (f32[3,64,128,128]{3,2,1,0:T(8,128)}, f32[3,64,128,128]{3,2,1,0:T(8,128)}, f32[3,64,128,128]{3,2,1,0:T(8,128)}) fusion(f32[1,64,128,128]{3,2,1,0:T(8,128)} %copy.141, f32[1,64,128,128]{3,2,1,0:T(8,128)} %bitcast.175, f32[1,64,128,128]{3,2,1,0:T(8,128)} %bitcast.180, f32[3,66,129,128]{3,2,1,0:T(8,128)} %get-tuple-element.9, ...), kind=kLoop, calls=%fused_computation.14 | loop fusion | flops 40894464 | bytes 75890688 | tf_op jit(solution)/shard_map/mul | solution.py:62
  1366.0 39.7 %fusion.35 = f32[64,128,128]{2,1,0:T(8,128)} fusion(f32[3,64,128,128]{3,2,1,0:T(8,128)} %get-tuple-element.15, f32[3,64,128,128]{3,2,1,0:T(8,128)} %get-tuple-element.16, f32[64,128,128]{2,1,0:T(8,128)} %fusion.51, f32[3,64,128,128]{3,2,1,0:T(8,128)} %get-tuple-element.14, f32[3,64,128,127]{3,2,1,0:T(8,128)} %get-tuple-element.13, ...), kind=kLoop, calls=%fused_computation.78 | loop fusion | flops 60817408 | bytes 117440512 | tf_op jit(solution)/shard_map/sub | solution.py:149
  (156 shorter events, 424.7 us)
Async XLA Ops:
  0.6 121.7 %copy-start = (f32[512,512]{1,0:T(8,128)S(1)}, f32[512,512]{1,0:T(8,128)}, u32[]{:S(2)}) copy-start(f32[512,512]{1,0:T(8,128)} %param.11) | copy-start | bytes 3145732
  290.9 53.7 %all-to-all-start.2 = ((f32[64,128,128]{2,0,1:T(8,128)}), f32[64,128,128]{2,0,1:T(8,128)}, u32[]{:S(2)}, u32[]{:S(2)}) async-start(f32[64,128,128]{2,0,1:T(8,128)} %copy.121), calls=%async_computation.2 | async-start | bytes 8388608 | tf_op jit(solution)/shard_map/all_to_all | solution.py:104
  296.4 4.3 collective-permute-start.9
  297.7 3.9 collective-permute-start.8
  302.7 96.3 %collective-permute-start.10 = (f32[1,66,1,128]{3,2,1,0:T(1,128)S(1)}, f32[1,66,1,128]{3,2,1,0:T(1,128)S(1)}, u32[]{:S(2)}, u32[]{:S(2)}) collective-permute-start(f32[1,66,1,128]{3,2,1,0:T(1,128)S(1)} %get-tuple-element.39), channel_id=1, source_target_pairs={{1,0},{2,1},{3,2},{5,4},{6,5},{7,6},{9,8},{10,9},{11,10},{13,12},{... | collective-permute-start | bytes 101384 | tf_op jit(solution)/shard_map/ppermute | solution.py:27
  304.0 95.0 %collective-permute-start.11 = (f32[1,66,1,128]{3,2,1,0:T(1,128)S(1)}, f32[1,66,1,128]{3,2,1,0:T(1,128)S(1)}, u32[]{:S(2)}, u32[]{:S(2)}) collective-permute-start(f32[1,66,1,128]{3,2,1,0:T(1,128)S(1)} %get-tuple-element.40), channel_id=1, source_target_pairs={{0,1},{1,2},{2,3},{4,5},{5,6},{6,7},{8,9},{9,10},{10,11},{12,13},{... | collective-permute-start | bytes 101384 | tf_op jit(solution)/shard_map/ppermute | solution.py:25
  364.2 79.7 %all-to-all-start.3 = ((f32[512,16,128]{2,1,0:T(8,128)}), f32[512,16,128]{2,1,0:T(8,128)}, u32[]{:S(2)}, u32[]{:S(2)}) async-start(f32[512,16,128]{2,1,0:T(8,128)} %copy.125), calls=%async_computation.3 | async-start | bytes 8388608 | tf_op jit(solution)/shard_map/all_to_all | solution.py:102
  443.9 72.0 %all-to-all-start.8 = ((f32[64,128,128]{2,0,1:T(8,128)}), f32[64,128,128]{2,0,1:T(8,128)}, u32[]{:S(2)}, u32[]{:S(2)}) async-start(f32[64,128,128]{2,0,1:T(8,128)} %copy.142), calls=%async_computation.8 | async-start | bytes 8388608 | tf_op jit(solution)/shard_map/all_to_all | solution.py:104
  454.4 17.2 %copy-start.13 = (f32[64,128,128]{2,1,0:T(8,128)}, f32[64,128,128]{2,1,0:T(8,128)S(1)}, u32[]{:S(2)}) copy-start(f32[64,128,128]{2,1,0:T(8,128)S(1)} %bitcast_multiply_fusion.3) | copy-start | bytes 12582916
  454.4 5.3 collective-permute-start.1
  455.7 4.9 collective-permute-start
  460.7 10.9 collective-permute-start.2
  462.0 9.6 collective-permute-start.3
  482.1 21.2 %copy-start.23 = (f32[128,128]{1,0:T(8,128)S(1)}, f32[128,128]{1,0:T(8,128)}, u32[]{:S(2)}) copy-start(f32[128,128]{1,0:T(8,128)} %param.12) | copy-start | bytes 196612
  515.9 86.1 %all-to-all-start.4 = ((f32[64,128,128]{1,0,2:T(8,128)}), f32[64,128,128]{1,0,2:T(8,128)}, u32[]{:S(2)}, u32[]{:S(2)}) async-start(f32[64,128,128]{1,0,2:T(8,128)} %copy.127), calls=%async_computation.4 | async-start | bytes 8388608 | tf_op jit(solution)/shard_map/all_to_all | solution.py:113
  602.0 101.7 %all-to-all-start.9 = ((f32[512,16,128]{2,1,0:T(8,128)}), f32[512,16,128]{2,1,0:T(8,128)}, u32[]{:S(2)}, u32[]{:S(2)}) async-start(f32[512,16,128]{2,1,0:T(8,128)} %copy.146), calls=%async_computation.9 | async-start | bytes 8388608 | tf_op jit(solution)/shard_map/all_to_all | solution.py:102
  703.7 95.5 %all-to-all-start.5 = ((f32[4,1,262144]{2,1,0:T(1,128)}), f32[4,1,262144]{2,1,0:T(1,128)}, u32[]{:S(2)}, u32[]{:S(2)}) async-start(f32[4,1,262144]{2,1,0:T(1,128)} %reshape.40), calls=%async_computation.5 | async-start | bytes 8388608 | tf_op jit(solution)/shard_map/all_to_all | solution.py:111
  799.2 97.7 %all-to-all-start.10 = ((f32[64,128,128]{1,0,2:T(8,128)}), f32[64,128,128]{1,0,2:T(8,128)}, u32[]{:S(2)}, u32[]{:S(2)}) async-start(f32[64,128,128]{1,0,2:T(8,128)} %copy.148), calls=%async_computation.10 | async-start | bytes 8388608 | tf_op jit(solution)/shard_map/all_to_all | solution.py:113
  896.9 54.6 %all-to-all-start.6 = ((f32[64,128,128]{2,0,1:T(8,128)}), f32[64,128,128]{2,0,1:T(8,128)}, u32[]{:S(2)}, u32[]{:S(2)}) async-start(f32[64,128,128]{2,0,1:T(8,128)} %copy.133), calls=%async_computation.6 | async-start | bytes 8388608 | tf_op jit(solution)/shard_map/all_to_all | solution.py:104
  951.5 95.7 %all-to-all-start.11 = ((f32[4,1,262144]{2,1,0:T(1,128)}), f32[4,1,262144]{2,1,0:T(1,128)}, u32[]{:S(2)}, u32[]{:S(2)}) async-start(f32[4,1,262144]{2,1,0:T(1,128)} %reshape.42), calls=%async_computation.11 | async-start | bytes 8388608 | tf_op jit(solution)/shard_map/all_to_all | solution.py:111
  1047.1 96.1 %all-to-all-start.7 = ((f32[512,16,128]{2,1,0:T(8,128)}), f32[512,16,128]{2,1,0:T(8,128)}, u32[]{:S(2)}, u32[]{:S(2)}) async-start(f32[512,16,128]{2,1,0:T(8,128)} %copy.137), calls=%async_computation.7 | async-start | bytes 8388608 | tf_op jit(solution)/shard_map/all_to_all | solution.py:102
  1104.4 20.4 %copy-start.11 = (f32[1,64,128,128]{3,2,1,0:T(8,128)}, f32[1,64,128,128]{3,2,1,0:T(8,128)S(1)}, u32[]{:S(2)}) copy-start(f32[1,64,128,128]{3,2,1,0:T(8,128)S(1)} %subtract_bitcast_fusion) | copy-start | bytes 12582916
  1104.4 9.2 collective-permute-start.13
  1105.7 7.9 collective-permute-start.12
  1113.7 11.1 collective-permute-start.14
  1115.0 9.8 collective-permute-start.15
  1146.2 24.6 %copy-start.4 = (f32[64,8,16,128]{3,2,1,0:T(8,128)}, f32[64,8,16,128]{3,2,1,0:T(8,128)S(1)}, u32[]{:S(2)}) copy-start(f32[64,8,16,128]{3,2,1,0:T(8,128)S(1)} %copy.138) | copy-start | bytes 12582916
  1181.8 113.9 %collective-permute-start.4 = (f32[3,1,128,128]{3,2,1,0:T(8,128)S(1)}, f32[3,1,128,128]{3,2,1,0:T(8,128)S(1)}, u32[]{:S(2)}, u32[]{:S(2)}) collective-permute-start(f32[3,1,128,128]{3,2,1,0:T(8,128)S(1)} %get-tuple-element.17), channel_id=1, source_target_pairs={{0,4},{4,8},{8,12},{12,16},{16,20},{20,24},{24,28},{1,5},{5,9},{9,... | collective-permute-start | bytes 589832 | tf_op jit(solution)/shard_map/ppermute | solution.py:25
  1185.9 109.8 %collective-permute-start.5 = (f32[3,1,128,128]{3,2,1,0:T(8,128)S(1)}, f32[3,1,128,128]{3,2,1,0:T(8,128)S(1)}, u32[]{:S(2)}, u32[]{:S(2)}) collective-permute-start(f32[3,1,128,128]{3,2,1,0:T(8,128)S(1)} %get-tuple-element.18), channel_id=1, source_target_pairs={{4,0},{8,4},{12,8},{16,12},{20,16},{24,20},{28,24},{5,1},{9,5},{13... | collective-permute-start | bytes 589832 | tf_op jit(solution)/shard_map/ppermute | solution.py:27
  1297.4 7.0 collective-permute-start.6
  1298.9 7.0 collective-permute-start.7
  1366.0 39.7 %copy-start.1 = (f32[512,512]{1,0:T(8,128)S(1)}, f32[512,512]{1,0:T(8,128)}, u32[]{:S(2)}) copy-start(f32[512,512]{1,0:T(8,128)} %param.11) | copy-start | bytes 3145732
  (18 other events, 139.3 us)
where the time goes:
time: 1420 us; the launch traced here: 1410 us
  local copies, waits for them, and re-layouts  315 us (22%)
  waiting for transfers between devices  308 us (22%)
  other arithmetic  301 us (21%)
  blocking collectives  238 us (17%)
  starting transfers between devices  155 us (11%)
  matrix products  88.1 us (6%)
    all_to_all x2, waiting for transfers between devices, solve_lines(): lax.all_to_all(solved, 'narrow', split_axis=1, concat_axis=2, tiled=True)  146 us
    all_to_all x2, waiting for transfers between devices, line_y(): lax.all_to_all(field, 'narrow', split_axis=2, concat_axis=1, tiled=True)  105 us
    all_to_all x1, blocking collectives, line_y(): lax.all_to_all(field, 'narrow', split_axis=2, concat_axis=1, tiled=True)  99.5 us
    all_to_all x1, blocking collectives, solve_lines(): lax.all_to_all(solved, 'narrow', split_axis=1, concat_axis=2, tiled=True)  98.2 us
    dot_general x9, matrix products, contract(): jnp.einsum(matrix_form + ',' + letters + '->' + result_form, matrix, fiel...  88.1 us
    all_to_all x3, starting transfers between devices, solve_lines(): lax.all_to_all(solved, 'wide', split_axis=0, concat_axis=1, tiled=True)  75.7 us
    slice x8, local copies, waits for them, and re-layouts, along_third(): return jnp.concatenate([values[..., 1:], zero_layer], axis=-1)  65.8 us
    unnamed x54, local copies, waits for them, and re-layouts  63.1 us
  transfers between devices with their start and end apart: 26, of which 10 were waited for; matrix products, arithmetic and copies ran while one was open for 32% of the time, Pallas kernels for 0%

commit v1 on v0

--- a/solution.py
+++ b/solution.py
@@ -1,6 +1,9 @@
+import functools
 import jax
 import jax.numpy as jnp
 from jax import lax
+from jax.experimental import pallas as pl
+from jax.experimental.pallas import tpu as pltpu
 from jax.sharding import PartitionSpec as P
 
 PATCHES = 3072
@@ -121,7 +124,7 @@
     return along_third(field, 1) + along_third(field, -1) - 2.0 * field
 
 
-def on_device(state, volatility, cotangent, solve_first, solve_second, solve_third, patch_index):
+def on_device_plain(state, volatility, cotangent, solve_first, solve_second, solve_third, patch_index):
     coefficient = 0.5 * volatility * volatility
     padded = rimmed(state[None])
     parts = second_parts(padded)
@@ -156,6 +159,741 @@
     return (adjoint, vega * vega_scale)
 
 
+F32 = jnp.float32
+BF16 = jnp.bfloat16
+damping = 0.5 * 0.4 * 0.2
+MIB = 1024 * 1024
+PLANES = 8
+
+
+def params(mib):
+    return pltpu.CompilerParams(vmem_limit_bytes=mib * MIB)
+
+
+def cost(flops, mib):
+    return pl.CostEstimate(flops=int(flops), bytes_accessed=int(mib * MIB), transcendentals=0)
+
+
+def halves(x):
+    high = lax.reduce_precision(x, 8, 7)
+    return high.astype(BF16), (x - high).astype(BF16)
+
+
+def left_form(matrix):
+    high, low = halves(matrix)
+    return jnp.concatenate([high, high, low], axis=1)
+
+
+def right_form(matrix):
+    high, low = halves(matrix)
+    return jnp.concatenate([high, high, low], axis=0)
+
+
+def split(x):
+    high = x.astype(BF16)
+    return high, (x - high.astype(F32)).astype(BF16)
+
+
+def left_product(matrix3, field):
+    high, low = split(field)
+    return jnp.dot(matrix3, jnp.concatenate([high, low, high], axis=0), preferred_element_type=F32)
+
+
+def right_product(field, matrix3):
+    high, low = split(field)
+    return jnp.dot(jnp.concatenate([high, low, high], axis=1), matrix3, preferred_element_type=F32)
+
+
+def y_pair(v, low_row, high_row):
+    n = v.shape[0]
+    row = lax.broadcasted_iota(jnp.int32, v.shape, 0)
+    up = jnp.where(row == n - 1, high_row, pltpu.roll(v, n - 1, 0))
+    down = jnp.where(row == 0, low_row, pltpu.roll(v, 1, 0))
+    return up, down
+
+
+def z_pair(v):
+    n = v.shape[1]
+    lane = lax.broadcasted_iota(jnp.int32, v.shape, 1)
+    up = jnp.where(lane == n - 1, 0.0, pltpu.roll(v, n - 1, 1))
+    down = jnp.where(lane == 0, 0.0, pltpu.roll(v, 1, 1))
+    return up, down
+
+
+def sweep(count, plane, rows, emit, full):
+    v, p, rest, inner = {}, {}, {}, {}
+    for k in range(-1, count + 1):
+        centre = plane(k)
+        y_up, y_down = y_pair(centre, *rows(k))
+        z_up, z_down = z_pair(centre)
+        e = y_up - y_down
+        v[k] = centre
+        p[k] = 0.125 * e + 0.075 * (z_up - z_down)
+        if 0 <= k < count:
+            e_up, e_down = z_pair(e)
+            rest[k] = -0.1 * (e_up - e_down)
+            if full:
+                inner[k] = (y_up + y_down) + (z_up + z_down) - 4.0 * centre
+        if k >= 1:
+            mixed = (p[k] - p[k - 2]) + rest[k - 1]
+            emit(k - 1, v[k - 1], v[k - 2], v[k], mixed, inner.get(k - 1))
+
+
+def chunk_plane(ref, x):
+    value = ref[:, x]
+    return value.reshape(value.shape[0] * value.shape[1], value.shape[2])
+
+
+def plane_specs(step_block, last, shape):
+    tail = shape[1:]
+    return [
+        pl.BlockSpec((PLANES,) + tail, lambda s, i: (step_block(s, i), 0, 0)),
+        pl.BlockSpec((1,) + tail, lambda s, i: (jnp.maximum(step_block(s, i) * PLANES - 1, 0), 0, 0)),
+        pl.BlockSpec((1,) + tail, lambda s, i: (jnp.minimum(step_block(s, i) * PLANES + PLANES, last), 0, 0)),
+    ]
+
+
+def whole(shape):
+    return pl.BlockSpec(shape, lambda s, i: (0,) * len(shape))
+
+
+def pick_plane(k, count, block, main, before, after, low, high, blocks):
+    if k < 0:
+        return jnp.where(block == 0, low[0], before[0])
+    if k >= count:
+        return jnp.where(block == blocks - 1, high[0], after[0])
+    return main[k]
+
+
+def natural(s, i):
+    return s
+
+
+def rotated(per, n):
+    def block(s, i):
+        return lax.rem(i[0] + s // per, n) * per + lax.rem(s, per)
+
+    return block
+
+
+def piece_map(d, per):
+    return lambda s: jnp.clip(s - d * per, 0, per - 1)
+
+
+def forward_kernel(i, state, before, after, low, high, y_low, y_high, volatility, a_out, source_out, *, blocks):
+    block = pl.program_id(0)
+
+    def emit(k, v, prev, nxt, mixed, inner):
+        second_x = prev + nxt - 2.0 * v
+        source = mixed + second_x + inner
+        sigma = volatility[k]
+        a = v + (time_step * 0.5) * sigma * sigma * source - damping * second_x
+        a_out[:, k] = a.reshape(a_out.shape[0], a_out.shape[2], a_out.shape[3])
+        source_out[k] = time_step * sigma * source
+
+    sweep(
+        PLANES,
+        lambda k: pick_plane(k, PLANES, block, state, before, after, low, high, blocks),
+        lambda k: (y_low[pl.ds(block * PLANES + k + 1, 1), :], y_high[pl.ds(block * PLANES + k + 1, 1), :]),
+        emit,
+        True,
+    )
+
+
+def forward(index, state, volatility, low, high, y_low, y_high, wide):
+    bx, by, bz = state.shape
+    blocks = bx // PLANES
+    return pl.pallas_call(
+        functools.partial(forward_kernel, blocks=blocks),
+        grid_spec=pltpu.PrefetchScalarGridSpec(
+            num_scalar_prefetch=1,
+            grid=(blocks,),
+            in_specs=plane_specs(natural, bx - 1, state.shape)
+            + [whole(low.shape), whole(high.shape), whole(y_low.shape), whole(y_high.shape)]
+            + [pl.BlockSpec((PLANES, by, bz), lambda s, i: (s, 0, 0))],
+            out_specs=[
+                pl.BlockSpec((wide, PLANES, by // wide, bz), lambda s, i: (0, s, 0, 0)),
+                pl.BlockSpec((PLANES, by, bz), lambda s, i: (s, 0, 0)),
+            ],
+        ),
+        out_shape=[
+            jax.ShapeDtypeStruct((wide, bx, by // wide, bz), F32),
+            jax.ShapeDtypeStruct(state.shape, F32),
+        ],
+        compiler_params=params(32),
+        cost_estimate=cost(5e9, 17),
+        name="forward",
+    )(index, state, state, state, low, high, y_low, y_high, volatility)
+
+
+def frozen_kernel(i, state, before, after, low, high, q_low, q_high, third3, out, *, blocks):
+    block = pl.program_id(0)
+
+    def plane(k):
+        v = pick_plane(k, PLANES, block, state, before, after, low, high, blocks)
+        up, down = z_pair(v)
+        return v + damping * right_product(up + down - 2.0 * v, third3[...])
+
+    def emit(k, v, prev, nxt, mixed, inner):
+        out[k] = mixed
+
+    sweep(
+        PLANES,
+        plane,
+        lambda k: (q_low[pl.ds(block * PLANES + k + 1, 1), :], q_high[pl.ds(block * PLANES + k + 1, 1), :]),
+        emit,
+        False,
+    )
+
+
+def frozen(index, state, low, high, q_low, q_high, third3):
+    bx, by, bz = state.shape
+    blocks = bx // PLANES
+    return pl.pallas_call(
+        functools.partial(frozen_kernel, blocks=blocks),
+        grid_spec=pltpu.PrefetchScalarGridSpec(
+            num_scalar_prefetch=1,
+            grid=(blocks,),
+            in_specs=plane_specs(natural, bx - 1, state.shape)
+            + [whole(low.shape), whole(high.shape), whole(q_low.shape), whole(q_high.shape), whole(third3.shape)],
+            out_specs=pl.BlockSpec((PLANES, by, bz), lambda s, i: (s, 0, 0)),
+        ),
+        out_shape=jax.ShapeDtypeStruct(state.shape, F32),
+        compiler_params=params(32),
+        cost_estimate=cost(5e9, 9),
+        name="frozen",
+    )(index, state, state, state, low, high, q_low, q_high, third3)
+
+
+def first_kernel(*refs, count, lines, parts, length, halo):
+    pieces, matrix3, out = refs[:count], refs[count], refs[count + 1]
+    depth = pieces[0].shape[0] // lines
+    rows = length + 2 * halo
+
+    def pair(step, carry):
+        y = step * 2
+        field = jnp.concatenate(
+            [
+                jnp.concatenate([piece[pl.ds(y + t, depth, stride=lines), :] for piece in pieces], axis=0)
+                for t in range(2)
+            ],
+            axis=1,
+        )
+        solved = left_product(matrix3[...], field)
+        width = solved.shape[1] // 2
+        for t in range(2):
+            half = solved[:, t * width : (t + 1) * width]
+            for part in range(parts):
+                base = part * rows
+                out[pl.ds((base + halo) * lines + y + t, length, stride=lines), :] = half[part * length : (part + 1) * length]
+                if halo:
+                    zero = jnp.zeros((1, width), F32)
+                    before = half[part * length - 1 : part * length] if part > 0 else zero
+                    after = half[(part + 1) * length : (part + 1) * length + 1] if part < parts - 1 else zero
+                    out[pl.ds(base * lines + y + t, 1), :] = before
+                    out[pl.ds((base + rows - 1) * lines + y + t, 1), :] = after
+        return carry
+
+    lax.fori_loop(0, lines // 2, pair, 0)
+
+
+def first(pieces, matrix3, halo):
+    wide = pieces[0].shape[0]
+    lines, bz = pieces[0].shape[2:]
+    length = sum(piece.shape[1] for piece in pieces)
+    rows = length + 2 * halo
+    flat = [piece.reshape(-1, bz) for piece in pieces]
+    out = pl.pallas_call(
+        functools.partial(first_kernel, count=len(flat), lines=lines, parts=wide, length=length, halo=halo),
+        in_specs=[pl.BlockSpec(memory_space=pltpu.VMEM)] * (len(flat) + 1),
+        out_specs=pl.BlockSpec(memory_space=pltpu.VMEM),
+        out_shape=jax.ShapeDtypeStruct((wide * rows * lines, bz), F32),
+        compiler_params=params(40),
+        cost_estimate=cost(7e9, 10),
+        name="first",
+    )(*flat, matrix3)
+    return out.reshape(wide, rows, lines, bz)
+
+
+def second_kernel(*refs, count, chunked):
+    pieces, second3, third3, outs = refs[:count], refs[count], refs[count + 1], refs[count + 2 :]
+    per, by, bz = pieces[0].shape
+    length = count * by
+    field = jnp.concatenate([piece[x] for x in range(per) for piece in pieces], axis=0)
+    field = right_product(field, third3[...])
+    field = jnp.concatenate([field[x * length : (x + 1) * length] for x in range(per)], axis=1)
+    solved = left_product(second3[...], field)
+    for x in range(per):
+        half = solved[:, x * bz : (x + 1) * bz]
+        if chunked:
+            for d in range(count):
+                out = outs[d]
+                out[:, x] = half[d * by : (d + 1) * by].reshape(out.shape[0], out.shape[2], bz)
+        else:
+            outs[0][x] = half
+
+
+def second(pieces, second3, third3, wide):
+    count = len(pieces)
+    xs, by, bz = pieces[0].shape
+    per = 2
+    if wide:
+        out_specs = [pl.BlockSpec((wide, per, by // wide, bz), lambda s: (0, s, 0, 0))] * count
+        out_shape = [jax.ShapeDtypeStruct((wide, xs, by // wide, bz), F32)] * count
+    else:
+        out_specs = [pl.BlockSpec((per, count * by, bz), lambda s: (s, 0, 0))]
+        out_shape = [jax.ShapeDtypeStruct((xs, count * by, bz), F32)]
+    return pl.pallas_call(
+        functools.partial(second_kernel, count=count, chunked=bool(wide)),
+        grid=(xs // per,),
+        in_specs=[pl.BlockSpec((per, by, bz), lambda s: (s, 0, 0))] * count
+        + [pl.BlockSpec(second3.shape, lambda s: (0, 0)), pl.BlockSpec(third3.shape, lambda s: (0, 0))],
+        out_specs=out_specs,
+        out_shape=out_shape,
+        compiler_params=params(40),
+        cost_estimate=cost(9e9, 10),
+        name="second",
+    )(*pieces, second3, third3)
+
+
+def piece_specs(xs, tail, per, n):
+    return [pl.BlockSpec((PLANES,) + tail, lambda s, i, d=d: (jnp.clip(s - d * per, 0, per - 1), 0, 0)) for d in range(n)]
+
+
+def chunk_piece_specs(wide, lines, bz, per, order):
+    return [
+        pl.BlockSpec((wide, PLANES, lines, bz), lambda s, i, d=d: (0, jnp.clip(s - d * per, 0, per - 1), 0, 0))
+        for d in order
+    ]
+
+
+def store_piece(outs, step, per, k, value):
+    for d, out in enumerate(outs):
+
+        @pl.when(step // per == d)
+        def _(out=out):
+            out[k] = value
+
+
+def select(values, turn):
+    result = values[0]
+    for d in range(1, len(values)):
+        result = jnp.where(turn == d, values[d], result)
+    return result
+
+
+def lifted_kernel(i, solved, state, y_low, y_high, *outs, per, n):
+    step = pl.program_id(0)
+    block = rotated(per, n)(step, i)
+    for k in range(PLANES):
+        v = state[k]
+        up, down = y_pair(v, y_low[pl.ds(block * PLANES + k + 1, 1), :], y_high[pl.ds(block * PLANES + k + 1, 1), :])
+        store_piece(outs, step, per, k, chunk_plane(solved, k) - damping * (up + down - 2.0 * v))
+
+
+def lifted(index, solved, state, y_low, y_high, n):
+    bx, by, bz = state.shape
+    xs = bx // n
+    per = xs // PLANES
+    wide, lines = solved.shape[0], solved.shape[2]
+    block = rotated(per, n)
+    return pl.pallas_call(
+        functools.partial(lifted_kernel, per=per, n=n),
+        grid_spec=pltpu.PrefetchScalarGridSpec(
+            num_scalar_prefetch=1,
+            grid=(n * per,),
+            in_specs=[
+                pl.BlockSpec((wide, PLANES, lines, bz), lambda s, i: (0, block(s, i), 0, 0)),
+                pl.BlockSpec((PLANES, by, bz), lambda s, i: (block(s, i), 0, 0)),
+                whole(y_low.shape),
+                whole(y_high.shape),
+            ],
+            out_specs=piece_specs(xs, (by, bz), per, n),
+        ),
+        out_shape=[jax.ShapeDtypeStruct((xs, by, bz), F32)] * n,
+        compiler_params=params(32),
+        cost_estimate=cost(2e9, 13),
+        name="lifted",
+    )(index, solved, state, y_low, y_high)
+
+
+def reaction_kernel(
+    i, carried, carried_low, carried_high, vol, before, after, low, high, vol_low, vol_high, cotangent, *outs, per, n, blocks
+):
+    step = pl.program_id(0)
+    block = rotated(per, n)(step, i)
+
+    def plane(k):
+        sigma = pick_plane(k, PLANES, block, vol, before, after, low, high, blocks)
+        return (0.5 * correction) * sigma * sigma * chunk_plane(carried, block * PLANES + k + 1)
+
+    def rows(k):
+        at = pl.ds(block * PLANES + k + 1, 1)
+        s_low, s_high = vol_low[at, :], vol_high[at, :]
+        return (
+            (0.5 * correction) * s_low * s_low * carried_low[at, :],
+            (0.5 * correction) * s_high * s_high * carried_high[at, :],
+        )
+
+    def emit(k, v, prev, nxt, mixed, inner):
+        store_piece(outs, step, per, k, cotangent[k] + mixed)
+
+    sweep(PLANES, plane, rows, emit, False)
+
+
+def react(index, carried, carried_low, carried_high, vol, low, high, vol_low, vol_high, cotangent, n):
+    bx, by, bz = vol.shape
+    xs = bx // n
+    per = xs // PLANES
+    block = rotated(per, n)
+    return pl.pallas_call(
+        functools.partial(reaction_kernel, per=per, n=n, blocks=bx // PLANES),
+        grid_spec=pltpu.PrefetchScalarGridSpec(
+            num_scalar_prefetch=1,
+            grid=(n * per,),
+            in_specs=[whole(carried.shape), whole(carried_low.shape), whole(carried_high.shape)]
+            + plane_specs(block, bx - 1, vol.shape)
+            + [whole(low.shape), whole(high.shape), whole(vol_low.shape), whole(vol_high.shape)]
+            + [pl.BlockSpec((PLANES, by, bz), lambda s, i: (block(s, i), 0, 0))],
+            out_specs=piece_specs(xs, (by, bz), per, n),
+        ),
+        out_shape=[jax.ShapeDtypeStruct((xs, by, bz), F32)] * n,
+        compiler_params=params(40),
+        cost_estimate=cost(4e9, 17),
+        name="reaction",
+    )(index, carried, carried_low, carried_high, vol, vol, vol, low, high, vol_low, vol_high, cotangent)
+
+
+def lines_kernel(i, *refs, per, n):
+    totals, uppers = refs[:n], refs[n : 2 * n]
+    cotangent, upper_low, upper_high, third3, out = refs[2 * n :]
+    step = pl.program_id(0)
+    turn = step // per
+    block = rotated(per, n)(step, i)
+    for k in range(PLANES):
+        total = select([ref[k] for ref in totals], turn)
+        upper = select([chunk_plane(ref, k) for ref in uppers], turn)
+        at = pl.ds(block * PLANES + k, 1)
+        up, down = y_pair(upper, upper_low[at, :], upper_high[at, :])
+        third = right_product(total, third3[...])
+        z_up, z_down = z_pair(third)
+        lines = (up + down - 2.0 * upper) + (z_up + z_down - 2.0 * third)
+        out[k] = cotangent[k] - total - damping * lines
+
+
+def gather_lines(index, totals, uppers, cotangent, upper_low, upper_high, third3):
+    n = len(totals)
+    bx, by, bz = cotangent.shape
+    xs = bx // n
+    per = xs // PLANES
+    wide, lines = uppers[0].shape[0], uppers[0].shape[2]
+    block = rotated(per, n)
+    order = [(n - e) % n for e in range(n)]
+    return pl.pallas_call(
+        functools.partial(lines_kernel, per=per, n=n),
+        grid_spec=pltpu.PrefetchScalarGridSpec(
+            num_scalar_prefetch=1,
+            grid=(n * per,),
+            in_specs=piece_specs(xs, (by, bz), per, n)
+            + chunk_piece_specs(wide, lines, bz, per, range(n))
+            + [pl.BlockSpec((PLANES, by, bz), lambda s, i: (block(s, i), 0, 0))]
+            + [whole(upper_low.shape), whole(upper_high.shape), whole(third3.shape)],
+            out_specs=pl.BlockSpec((PLANES, by, bz), lambda s, i: (block(s, i), 0, 0)),
+        ),
+        out_shape=jax.ShapeDtypeStruct(cotangent.shape, F32),
+        compiler_params=params(40),
+        cost_estimate=cost(5e9, 17),
+        name="lines",
+    )(index, *totals, *[uppers[order[d]] for d in range(n)], cotangent, upper_low, upper_high, third3)
+
+
+def mixed_kernel(i, field, low, high, *refs, n):
+    outs, scratch = refs[:n], refs[n]
+    count = field.shape[0]
+    by = outs[0].shape[1]
+
+    def emit(k, v, prev, nxt, mixed, inner):
+        scratch[...] = mixed
+        for d, out in enumerate(outs):
+            start = pl.multiple_of(lax.rem(i[0] + d, n) * by, by)
+            out[k] = scratch[pl.ds(start, by), :]
+
+    zero = jnp.zeros((1, field.shape[2]), F32)
+    sweep(
+        count,
+        lambda k: low[0] if k < 0 else high[0] if k >= count else field[k],
+        lambda k: (zero, zero),
+        emit,
+        False,
+    )
+
+
+def mix(index, field, low, high, n):
+    xs, ny, bz = field.shape
+    by = ny // n
+    return pl.pallas_call(
+        functools.partial(mixed_kernel, n=n),
+        grid_spec=pltpu.PrefetchScalarGridSpec(
+            num_scalar_prefetch=1,
+            grid=(1,),
+            in_specs=[whole(field.shape), whole(low.shape), whole(high.shape)],
+            out_specs=[whole((xs, by, bz))] * n,
+            scratch_shapes=[pltpu.VMEM((ny, bz), F32)],
+        ),
+        out_shape=[jax.ShapeDtypeStruct((xs, by, bz), F32)] * n,
+        compiler_params=params(40),
+        cost_estimate=cost(4e9, 9),
+        name="mixed",
+    )(index, field, low, high)
+
+
+def patch_sums(out, step, planes, patch, patch_t, groups):
+    @pl.when(step == 0)
+    def _():
+        out[...] = jnp.zeros_like(out)
+
+    acc = None
+    for k, value in enumerate(planes):
+        column = jnp.sum(value, axis=1, keepdims=True)
+        number = patch[pl.ds(k, 1), :]
+        coarse = lax.broadcasted_iota(jnp.int32, (groups, number.shape[1]), 0) == lax.shift_right_logical(number, 7)
+        number_t = patch_t[k]
+        lane = lax.broadcasted_iota(jnp.int32, (number_t.shape[0], 128), 1)
+        fine = jnp.where(lane == lax.bitwise_and(number_t, 127), column, 0.0)
+        high, low = split(fine)
+        term = jnp.dot(
+            jnp.where(coarse, 1.0, 0.0).astype(BF16), jnp.concatenate([high, low], axis=1), preferred_element_type=F32
+        )
+        acc = term if acc is None else acc + term
+    out[...] += acc
+
+
+def drift_kernel(i, *refs, per, n, groups):
+    drifts = refs[:n]
+    frozen_part, carried, vol, patch, patch_t, out = refs[n:]
+    step = pl.program_id(0)
+    turn = step // per
+    block = rotated(per, n)(step, i)
+    planes = []
+    for k in range(PLANES):
+        drift = select([ref[k] for ref in drifts], turn) - frozen_part[k]
+        planes.append(correction * vol[k] * chunk_plane(carried, block * PLANES + k + 1) * drift)
+    patch_sums(out, step, planes, patch, patch_t, groups)
+
+
+def drift_sums(index, drifts, frozen_part, carried, vol, patch, patch_t, groups):
+    n = len(drifts)
+    bx, by, bz = vol.shape
+    xs = bx // n
+    per = xs // PLANES
+    block = rotated(per, n)
+    order = [(n - e) % n for e in range(n)]
+    main = pl.BlockSpec((PLANES, by, bz), lambda s, i: (block(s, i), 0, 0))
+    return pl.pallas_call(
+        functools.partial(drift_kernel, per=per, n=n, groups=groups),
+        grid_spec=pltpu.PrefetchScalarGridSpec(
+            num_scalar_prefetch=1,
+            grid=(n * per,),
+            in_specs=piece_specs(xs, (by, bz), per, n)
+            + [main, whole(carried.shape), main]
+            + [pl.BlockSpec((PLANES, by), lambda s, i: (block(s, i), 0))]
+            + [pl.BlockSpec((PLANES, by, 1), lambda s, i: (block(s, i), 0, 0))],
+            out_specs=whole((groups, 256)),
+        ),
+        out_shape=jax.ShapeDtypeStruct((groups, 256), F32),
+        compiler_params=params(40),
+        cost_estimate=cost(4e9, 17),
+        name="drift",
+    )(index, *[drifts[order[d]] for d in range(n)], frozen_part, carried, vol, patch, patch_t)
+
+
+def source_kernel(i, adjoint_start, source, patch, patch_t, given, out, *, groups):
+    step = pl.program_id(0)
+    planes = [source[k] * chunk_plane(adjoint_start, step * PLANES + k + 1) for k in range(PLANES)]
+    patch_sums(out, step, planes, patch, patch_t, groups)
+
+    @pl.when(step == pl.num_programs(0) - 1)
+    def _():
+        out[...] += given[...]
+
+
+def source_sums(index, adjoint_start, source, patch, patch_t, given):
+    bx, by, bz = source.shape
+    groups = given.shape[0]
+    return pl.pallas_call(
+        functools.partial(source_kernel, groups=groups),
+        grid_spec=pltpu.PrefetchScalarGridSpec(
+            num_scalar_prefetch=1,
+            grid=(bx // PLANES,),
+            in_specs=[whole(adjoint_start.shape), pl.BlockSpec((PLANES, by, bz), lambda s, i: (s, 0, 0))]
+            + [pl.BlockSpec((PLANES, by), lambda s, i: (s, 0))]
+            + [pl.BlockSpec((PLANES, by, 1), lambda s, i: (s, 0, 0)), whole(given.shape)],
+            out_specs=whole(given.shape),
+        ),
+        out_shape=jax.ShapeDtypeStruct(given.shape, F32),
+        compiler_params=params(40),
+        cost_estimate=cost(3e9, 9),
+        name="source",
+    )(index, adjoint_start, source, patch, patch_t, given)
+
+
+def adjoint_kernel(
+    i, start, start_low, start_high, vol, before, after, low, high, vol_low, vol_high, tail, out, *, blocks
+):
+    block = pl.program_id(0)
+    raw = {}
+
+    def plane(k):
+        sigma = pick_plane(k, PLANES, block, vol, before, after, low, high, blocks)
+        raw[k] = chunk_plane(start, block * PLANES + k + 1)
+        return (0.5 * time_step) * sigma * sigma * raw[k]
+
+    def rows(k):
+        at = pl.ds(block * PLANES + k + 1, 1)
+        s_low, s_high = vol_low[at, :], vol_high[at, :]
+        return (
+            (0.5 * time_step) * s_low * s_low * start_low[at, :],
+            (0.5 * time_step) * s_high * s_high * start_high[at, :],
+        )
+
+    def emit(k, v, prev, nxt, mixed, inner):
+        spread = mixed + (prev + nxt - 2.0 * v) + inner
+        lines = raw[k - 1] + raw[k + 1] - 2.0 * raw[k]
+        out[k] = raw[k] + spread + tail[k] - damping * lines
+
+    sweep(PLANES, plane, rows, emit, True)
+
+
+def finish(index, start, start_low, start_high, vol, low, high, vol_low, vol_high, tail):
+    bx, by, bz = vol.shape
+    return pl.pallas_call(
+        functools.partial(adjoint_kernel, blocks=bx // PLANES),
+        grid_spec=pltpu.PrefetchScalarGridSpec(
+            num_scalar_prefetch=1,
+            grid=(bx // PLANES,),
+            in_specs=[whole(start.shape), whole(start_low.shape), whole(start_high.shape)]
+            + plane_specs(natural, bx - 1, vol.shape)
+            + [whole(low.shape), whole(high.shape), whole(vol_low.shape), whole(vol_high.shape)]
+            + [pl.BlockSpec((PLANES, by, bz), lambda s, i: (s, 0, 0))],
+            out_specs=pl.BlockSpec((PLANES, by, bz), lambda s, i: (s, 0, 0)),
+        ),
+        out_shape=jax.ShapeDtypeStruct(vol.shape, F32),
+        compiler_params=params(40),
+        cost_estimate=cost(5e9, 17),
+        name="adjoint",
+    )(index, start, start_low, start_high, vol, vol, vol, low, high, vol_low, vol_high, tail)
+
+
+def neighbours(low_edge, high_edge, axis):
+    count = lax.axis_size(axis)
+    up = [(k, k + 1) for k in range(count - 1)]
+    down = [(k + 1, k) for k in range(count - 1)]
+    return lax.ppermute(high_edge, axis, up), lax.ppermute(low_edge, axis, down)
+
+
+def scatter_pieces(pieces, order=(2, 1, 3)):
+    n = len(pieces)
+    result = [pieces[0]] + [None] * (n - 1)
+    for d in sorted(range(1, n), key=lambda d: -min(d, n - d)):
+        result[d] = lax.ppermute(pieces[d], "narrow", [(k, (k + d) % n) for k in range(n)])
+    return result
+
+
+def across(piece):
+    return lax.all_to_all(piece, "wide", split_axis=0, concat_axis=0, tiled=True)
+
+
+def y_edges(chunks):
+    return neighbours(chunks[0, :, 0, :], chunks[-1, :, -1, :], "narrow")
+
+
+def on_device_kernels(state, volatility, cotangent, solve_first, solve_second, solve_third, patch_index):
+    n, wide = lax.axis_size("narrow"), lax.axis_size("wide")
+    here = lax.axis_index("narrow")
+    index = here.astype(jnp.int32).reshape(1)
+    bx, by, bz = state.shape
+    xs = bx // n
+    groups = PATCHES // 128
+
+    ahead = (here + jnp.arange(n)) % n
+    back = (here - jnp.arange(n)) % n
+
+    cot_pieces = [lax.dynamic_slice_in_dim(cotangent, ahead[d] * xs, xs, 0) for d in range(n)]
+    cot_lines = scatter_pieces(cot_pieces)
+
+    both_low, both_high = neighbours(
+        jnp.stack([state[0], volatility[0]]), jnp.stack([state[-1], volatility[-1]]), "wide"
+    )
+    both = jnp.stack([state[:, :: by - 1], volatility[:, :: by - 1]])
+    both = jnp.concatenate([both_low[:, None, :: by - 1], both, both_high[:, None, :: by - 1]], axis=1)
+    y_low, y_high = neighbours(both[:, :, 0], both[:, :, 1], "narrow")
+    state_x = (both_low[0:1], both_high[0:1])
+    vol_x = (both_low[1:2], both_high[1:2])
+    state_y = (y_low[0], y_high[0])
+    vol_y = (y_low[1], y_high[1])
+
+    second_t = solve_second.T.reshape(n, by, n, by)
+    second_t3 = left_form(second_t[ahead][:, :, back].reshape(n * by, n * by))
+    second_n = solve_second.reshape(n * by, n, by)
+    second_n3 = left_form(second_n[:, back].reshape(n * by, n * by))
+    third_t3 = right_form(solve_third)
+    third_n3 = right_form(solve_third.T)
+    first_n3 = left_form(solve_first)
+    first_t = solve_first.T.reshape(wide * bx, wide, n, xs)
+    first_t3 = left_form(first_t[:, :, back].transpose(0, 2, 1, 3).reshape(wide * bx, wide * bx))
+
+    a, source = forward(index, state, volatility, *state_x, *state_y, wide)
+    solved = across(first([across(a)], first_n3, 0))
+
+    back_second = scatter_pieces(second(cot_lines, second_t3, third_t3, wide))
+    carried = across(first([across(piece) for piece in back_second], first_t3, 1))
+
+    level = second(scatter_pieces(lifted(index, solved, state, *state_y, n)), second_n3, third_n3, 0)[0]
+    count = n * wide
+    joint = ("wide", "narrow")
+    level_low = lax.ppermute(level[-1:], joint, [(k, k + 1) for k in range(count - 1)])
+    level_high = lax.ppermute(level[:1], joint, [(k + 1, k) for k in range(count - 1)])
+    drift_pieces = mix(index, level, level_low, level_high, n)
+
+    def frozen_rows(rows):
+        padded = jnp.pad(rows, ((0, 0), (1, 1)))
+        curved = padded[:, 2:] + padded[:, :-2] - 2.0 * rows
+        return rows + damping * jnp.dot(curved, solve_third.T, precision=lax.Precision.HIGHEST)
+
+    frozen_part = frozen(index, state, *state_x, frozen_rows(state_y[0]), frozen_rows(state_y[1]), third_n3)
+
+    carried_y = y_edges(carried)
+    totals = react(index, carried, *carried_y, volatility, *vol_x, *vol_y, cotangent, n)
+    uppers = scatter_pieces(second(scatter_pieces(totals), second_t3, third_t3, wide))
+    start = across(first([across(piece) for piece in uppers], first_t3, 1))
+
+    drifts = scatter_pieces(drift_pieces)
+    order = (here - jnp.arange(n)) % n
+    edge_low = jnp.stack([piece[0, :, 0] for piece in uppers])[order].reshape(bx, bz)
+    edge_high = jnp.stack([piece[-1, :, -1] for piece in uppers])[order].reshape(bx, bz)
+    upper_y = neighbours(edge_low, edge_high, "narrow")
+    tail = gather_lines(index, totals, uppers, cotangent, *upper_y, third_t3)
+
+    patch_t = patch_index[:, :, None]
+    sums = drift_sums(index, drifts, frozen_part, carried, volatility, patch_index, patch_t, groups)
+    sums = source_sums(index, start, source, patch_index, patch_t, sums)
+    sums = (sums[:, :128] + sums[:, 128:]).reshape(count, PATCHES // count)
+    shares = lax.all_to_all(sums, joint, split_axis=0, concat_axis=0, tiled=True)
+    vega = jnp.sum(shares, axis=0)
+
+    start_y = y_edges(start)
+    adjoint = finish(index, start, *start_y, volatility, *vol_x, *vol_y, tail)
+    return (adjoint, vega * vega_scale)
+
+
+def on_device(*args):
+    n, wide = lax.axis_size("narrow"), lax.axis_size("wide")
+    bx, by, bz = args[0].shape
+    aligned = bx % (n * PLANES) == 0 and by % 128 == 0 and by % (wide * 8) == 0 and bz == 128
+    aligned = aligned and PATCHES % (n * wide) == 0 and by // wide % 2 == 0
+    return on_device_kernels(*args) if aligned else on_device_plain(*args)
+
+
 def solution(mesh):
     placed = (
         P("wide", "narrow", None),

time: 1420 us -> 904 us (0.64)
  other arithmetic: 301 us -> 11.6 us
  blocking collectives: 238 us -> 0 us
  local copies, waits for them, and re-layouts: 315 us -> 111 us
  Pallas kernels: 0 us -> 140 us
  starting transfers between devices: 155 us -> 249 us
  matrix products: 88.1 us -> 2.69 us
  waiting for transfers between devices: 308 us -> 382 us
    ppermute x16 -> x30, waiting for transfers between devices: 3.4 us -> 284 us  [the longest x18 246 us: scatter_pieces(): lax.ppermute(pieces[d], 'narrow', [(k, (k + d) % n) for k in range(n)])]
    all_to_all x10 -> x13, waiting for transfers between devices: 305 us -> 97.5 us  [the longest x12 96.5 us: across(): lax.all_to_all(piece, 'wide', split_axis=0, concat_axis=0, tiled=True)]
    all_to_all x2 -> x0, blocking collectives: 198 us -> none  [the longest x1 99.5 us: line_y(): lax.all_to_all(field, 'narrow', split_axis=2, concat_axis=1, tiled=True)]
    pallas_call x0 -> x15, Pallas kernels: none -> 140 us  [the longest x3 31.2 us: second(): pl.pallas_call(functools.partial(second_kernel, count=count, chunked=bool...]
    ppermute x16 -> x30, starting transfers between devices: 44.1 us -> 181 us  [the longest x18 100 us: scatter_pieces(): lax.ppermute(pieces[d], 'narrow', [(k, (k + d) % n) for k in range(n)])]
    all_to_all x22 -> x3, local copies, waits for them, and re-layouts: 112 us -> 5.71 us  [the longest x2 5.03 us: across(): lax.all_to_all(piece, 'wide', split_axis=0, concat_axis=0, tiled=True)]
    dot_general x9 -> x2, matrix products: 88.1 us -> 2.69 us  [frozen_rows(): jnp.dot(curved, solve_third.T, precision=lax.Precision.HIGHEST)]
    sub x3 -> x0, other arithmetic: 74.5 us -> none  [the longest x1 39.7 us: on_device(): adjoint = adjoint_start + spread - reaction - damping * lines]
  transfers between devices with their start and end apart: 26 -> 43, of which waited for: 10 -> 21; matrix products, arithmetic and copies ran while one was open for 32% -> 8% of each run, Pallas kernels for 0% -> 12%
where the time goes in v1:
time: 904 us; the launch traced here: 900 us
  waiting for transfers between devices  382 us (42%)
  starting transfers between devices  249 us (28%)
  Pallas kernels  140 us (15%)
  local copies, waits for them, and re-layouts  111 us (12%)
  other arithmetic  11.6 us (1%)
    ppermute x18, waiting for transfers between devices, scatter_pieces(): lax.ppermute(pieces[d], 'narrow', [(k, (k + d) % n) for k in range(n)])  246 us
    ppermute x18, starting transfers between devices, scatter_pieces(): lax.ppermute(pieces[d], 'narrow', [(k, (k + d) % n) for k in range(n)])  100 us
    all_to_all x12, waiting for transfers between devices, across(): lax.all_to_all(piece, 'wide', split_axis=0, concat_axis=0, tiled=True)  96.5 us
    unnamed x116, local copies, waits for them, and re-layouts  53.6 us
    all_to_all x12, starting transfers between devices, across(): lax.all_to_all(piece, 'wide', split_axis=0, concat_axis=0, tiled=True)  51.3 us
    ppermute x5, starting transfers between devices, neighbours(): lax.ppermute(high_edge, axis, up)  47.9 us
    pallas_call x3, Pallas kernels, second(): pl.pallas_call(functools.partial(second_kernel, count=count, chunked=bool...  31.2 us
    ppermute x1, starting transfers between devices, on_device_kernels(): lax.ppermute(level[-1:], joint, [(k, k + 1) for k in range(count - 1)])  24.9 us
  transfers between devices with their start and end apart: 43, of which 21 were waited for; matrix products, arithmetic and copies ran while one was open for 8% of the time, Pallas kernels for 12%

profile of v1, /device:TPU:0, one launch (start us, length us, event | category | flops | bytes accessed | tf_op | source)
XLA Modules:
  0.0 899.9 jit_solution(3980956073706035347)
XLA Ops:
  24.7 12.7 %collective-permute-done.refs_1_ = f32[16,128,128]{2,1,0:T(8,128)} collective-permute-done((f32[16,128,128]{2,1,0:T(8,128)}, f32[16,128,128]{2,1,0:T(8,128)}, u32[]{:S(2)}, u32[]{:S(2)}) %collective-permute-start) | collective-permute-done | bytes 1048608 | tf_op jit(solution)/shard_map/ppermute | solution.py:798
  37.4 44.1 %collective-permute-done.1.refs_2_ = f32[16,128,128]{2,1,0:T(8,128)} collective-permute-done((f32[16,128,128]{2,1,0:T(8,128)}, f32[16,128,128]{2,1,0:T(8,128)}, u32[]{:S(2)}, u32[]{:S(2)}) %collective-permute-start.1) | collective-permute-done | bytes 1048608 | tf_op jit(solution)/shard_map/ppermute | solution.py:798
  81.5 11.1 %second.3 = (f32[8,16,16,128]{3,2,1,0:T(8,128)S(1)}, f32[8,16,16,128]{3,2,1,0:T(8,128)}, f32[8,16,16,128]{3,2,1,0:T(8,128)S(1)}, f32[8,16,16,128]{3,2,1,0:T(8,128)S(1)}) custom-call(f32[16,128,128]{2,1,0:T(8,128)S(1)} %get-tuple-element.59.refs_0_, f32[16,128,128]{2,1,0:T(8,128)} %collective-permute-done.refs_1_, ...), custom_call_target="tpu_custom_call" | custom-call | flops 8999999488 | bytes 10485760 | tf_op jit(solution)/shard_map/second/pallas_call | solution.py:446
  95.7 22.9 %collective-permute-start.3 = (f32[8,16,16,128]{3,2,1,0:T(8,128)}, f32[8,16,16,128]{3,2,1,0:T(8,128)}, u32[]{:S(2)}, u32[]{:S(2)}) collective-permute-start(f32[8,16,16,128]{3,2,1,0:T(8,128)} %get-tuple-element.25), channel_id=1, source_target_pairs={{0,1},{1,2},{2,3},{3,0},{4,5},{5,6},{6,7},{7,4},{8,9},{9,10},{10,1... | collective-permute-start | bytes 3145736 | tf_op jit(solution)/shard_map/ppermute | solution.py:798
  123.9 13.8 %all-to-all-done = f32[8,16,16,128]{3,2,1,0:T(8,128)S(1)} async-done(((f32[8,16,16,128]{3,2,1,0:T(8,128)}), f32[8,16,16,128]{3,2,1,0:T(8,128)S(1)}, u32[]{:S(2)}, u32[]{:S(2)}) %all-to-all-start) | async-done | bytes 1048608 | tf_op jit(solution)/shard_map/all_to_all | solution.py:803
  160.4 26.9 %collective-permute-done.4 = f32[8,16,16,128]{3,2,1,0:T(8,128)} collective-permute-done((f32[8,16,16,128]{3,2,1,0:T(8,128)}, f32[8,16,16,128]{3,2,1,0:T(8,128)}, u32[]{:S(2)}, u32[]{:S(2)}) %collective-permute-start.4) | collective-permute-done | bytes 1048608 | tf_op jit(solution)/shard_map/ppermute | solution.py:798
  193.5 24.5 %collective-permute-start.10 = (f32[2,66,128]{2,1,0:T(8,128)S(1)}, f32[2,66,128]{2,1,0:T(8,128)S(1)}, u32[]{:S(2)}, u32[]{:S(2)}) collective-permute-start(f32[2,66,128]{2,1,0:T(8,128)S(1)} %get-tuple-element.77), channel_id=1, source_target_pairs={{0,1},{1,2},{2,3},{4,5},{5,6},{6,7},{8,9},{9,10},{10,11},{12,13},{... | collective-permute-start | bytes 202760 | tf_op jit(solution)/shard_map/ppermute | solution.py:791
  248.5 7.6 first.3
  258.2 34.3 %all-to-all-done.10 = f32[8,64,16,128]{3,2,1,0:T(8,128)} async-done(((f32[8,64,16,128]{3,2,1,0:T(8,128)}), f32[8,64,16,128]{3,2,1,0:T(8,128)}, u32[]{:S(2)}, u32[]{:S(2)}) %all-to-all-start.10) | async-done | bytes 4194336 | tf_op jit(solution)/shard_map/all_to_all | solution.py:803
  298.6 8.2 first.5
  308.9 38.8 %all-to-all-done.4.carried.refs_5_ = f32[8,66,16,128]{3,2,1,0:T(8,128)} async-done(((f32[8,66,16,128]{3,2,1,0:T(8,128)}), f32[8,66,16,128]{3,2,1,0:T(8,128)}, u32[]{:S(2)}, u32[]{:S(2)}) %all-to-all-start.4) | async-done | bytes 4325408 | tf_op jit(solution)/shard_map/all_to_all | solution.py:803
  353.3 12.0 %collective-permute-start.6 = (f32[66,128]{1,0:T(8,128)S(1)}, f32[66,128]{1,0:T(8,128)S(1)}, u32[]{:S(2)}, u32[]{:S(2)}) collective-permute-start(f32[66,128]{1,0:T(8,128)S(1)} %bitcast.140), channel_id=1, source_target_pairs={{0,1},{1,2},{2,3},{4,5},{5,6},{6,7},{8,9},{9,10},{10,11},{12,13},{... | collective-permute-start | bytes 101384 | tf_op jit(solution)/shard_map/ppermute | solution.py:791
  375.5 12.5 %reaction.1 = (f32[16,128,128]{2,1,0:T(8,128)S(1)}, f32[16,128,128]{2,1,0:T(8,128)S(1)}, f32[16,128,128]{2,1,0:T(8,128)S(1)}, f32[16,128,128]{2,1,0:T(8,128)S(1)}) custom-call(s32[1]{0:T(128)} %bitcast.i, f32[8,66,16,128]{3,2,1,0:T(8,128)} %all-to-all-done.4.carried.refs_5_, f32[66,128]{1,0:T(8,128)S(1)} %collective-permute-done.6.carried_low, ...), custom_call_target="tpu_custom_call" | custom-call | flops 4000000000 | bytes 17825792 | tf_op jit(solution)/shard_map/reaction/pallas_call | solution.py:549
  397.4 18.7 %collective-permute-done.12.refs_1_ = f32[16,128,128]{2,1,0:T(8,128)S(1)} collective-permute-done((f32[16,128,128]{2,1,0:T(8,128)S(1)}, f32[16,128,128]{2,1,0:T(8,128)S(1)}, u32[]{:S(2)}, u32[]{:S(2)}) %collective-permute-start.12) | collective-permute-done | bytes 1048608 | tf_op jit(solution)/shard_map/ppermute | solution.py:798
  416.1 43.2 %collective-permute-done.13.refs_2_ = f32[16,128,128]{2,1,0:T(8,128)S(1)} collective-permute-done((f32[16,128,128]{2,1,0:T(8,128)S(1)}, f32[16,128,128]{2,1,0:T(8,128)S(1)}, u32[]{:S(2)}, u32[]{:S(2)}) %collective-permute-start.13) | collective-permute-done | bytes 1048608 | tf_op jit(solution)/shard_map/ppermute | solution.py:798
  459.3 9.9 %second.4 = (f32[8,16,16,128]{3,2,1,0:T(8,128)}, f32[8,16,16,128]{3,2,1,0:T(8,128)S(1)}, f32[8,16,16,128]{3,2,1,0:T(8,128)S(1)}, f32[8,16,16,128]{3,2,1,0:T(8,128)S(1)}) custom-call(f32[16,128,128]{2,1,0:T(8,128)S(1)} %get-tuple-element.28.refs_0_, f32[16,128,128]{2,1,0:T(8,128)S(1)} %collective-permute-done.12.refs_1_, ...), custom_call_target="tpu_custom_call" | custom-call | flops 8999999488 | bytes 10485760 | tf_op jit(solution)/shard_map/second/pallas_call | solution.py:446
  471.6 21.9 %collective-permute-start.16 = (f32[8,16,16,128]{3,1,2,0:T(8,128)}, f32[8,16,16,128]{3,1,2,0:T(8,128)}, u32[]{:S(2)}, u32[]{:S(2)}) collective-permute-start(f32[8,16,16,128]{3,1,2,0:T(8,128)} %copy.108), channel_id=1, source_target_pairs={{0,2},{1,3},{2,0},{3,1},{4,6},{5,7},{6,4},{7,5},{8,10},{9,11},{10,... | collective-permute-start | bytes 3145736 | tf_op jit(solution)/shard_map/ppermute | solution.py:798
  503.4 9.5 %all-to-all-done.5 = f32[8,16,16,128]{3,2,1,0:T(8,128)S(1)} async-done(((f32[8,16,16,128]{3,2,1,0:T(8,128)}), f32[8,16,16,128]{3,2,1,0:T(8,128)S(1)}, u32[]{:S(2)}, u32[]{:S(2)}) %all-to-all-start.5) | async-done | bytes 1048608 | tf_op jit(solution)/shard_map/all_to_all | solution.py:803
  512.9 27.5 %collective-permute-done.16 = f32[8,16,16,128]{3,1,2,0:T(8,128)} collective-permute-done((f32[8,16,16,128]{3,1,2,0:T(8,128)}, f32[8,16,16,128]{3,1,2,0:T(8,128)}, u32[]{:S(2)}, u32[]{:S(2)}) %collective-permute-start.16) | collective-permute-done | bytes 1048608 | tf_op jit(solution)/shard_map/ppermute | solution.py:798
  544.6 22.6 %collective-permute-start.15 = (f32[8,16,16,128]{3,2,1,0:T(8,128)}, f32[8,16,16,128]{3,2,1,0:T(8,128)}, u32[]{:S(2)}, u32[]{:S(2)}) collective-permute-start(f32[8,16,16,128]{3,2,1,0:T(8,128)} %copy-done.45), channel_id=1, source_target_pairs={{0,1},{1,2},{2,3},{3,0},{4,5},{5,6},{6,7},{7,4},{8,9},{9,10},{10,1... | collective-permute-start | bytes 3145736 | tf_op jit(solution)/shard_map/ppermute | solution.py:798
  580.2 13.7 %collective-permute-done.15.refs_7_ = f32[8,16,16,128]{3,2,1,0:T(8,128)} collective-permute-done((f32[8,16,16,128]{3,2,1,0:T(8,128)}, f32[8,16,16,128]{3,2,1,0:T(8,128)}, u32[]{:S(2)}, u32[]{:S(2)}) %collective-permute-start.15) | collective-permute-done | bytes 1048608 | tf_op jit(solution)/shard_map/ppermute | solution.py:798
  610.5 8.3 collective-permute-start.22
  651.5 39.1 %collective-permute-done.23.refs_2_ = f32[16,128,128]{2,1,0:T(8,128)} collective-permute-done((f32[16,128,128]{2,1,0:T(8,128)}, f32[16,128,128]{2,1,0:T(8,128)}, u32[]{:S(2)}, u32[]{:S(2)}) %collective-permute-start.23) | collective-permute-done | bytes 1048608 | tf_op jit(solution)/shard_map/ppermute | solution.py:798
  690.6 10.2 %second.5.field = f32[16,512,128]{2,1,0:T(8,128)S(1)} custom-call(f32[16,128,128]{2,1,0:T(8,128)S(1)} %copy-done.48, f32[16,128,128]{2,1,0:T(8,128)} %collective-permute-done.22.refs_1_, f32[16,128,128]{2,1,0:T(8,128)} %collective-permute-done.23.refs_2_, f32[16,128,128]{2,1,0:T(8,128)} %collective-permute-done.24.refs_3_, ...), custom_call_target="tpu_custom_call" | custom-call | flops 8999999488 | bytes 10485760 | tf_op jit(solution)/shard_map/second/pallas_call | solution.py:446
  700.9 24.9 %collective-permute-start.25 = (f32[1,512,128]{2,1,0:T(8,128)S(1)}, f32[1,512,128]{2,1,0:T(8,128)S(1)}, u32[]{:S(2)}, u32[]{:S(2)}) collective-permute-start(f32[1,512,128]{2,1,0:T(8,128)S(1)} %get-tuple-element.51), channel_id=1, source_target_pairs={{0,1},{1,2},{2,3},{3,4},{4,5},{5,6},{6,7},{7,8},{8,9},{9,10},{10,1... | collective-permute-start | bytes 786440 | tf_op jit(solution)/shard_map/ppermute | solution.py:854
  769.0 16.5 %frozen.1.refs_4_ = f32[64,128,128]{2,1,0:T(8,128)S(1)} custom-call(s32[1]{0:T(128)} %bitcast.i, f32[64,128,128]{2,1,0:T(8,128)S(1)} %copy-done.8, f32[64,128,128]{2,1,0:T(8,128)S(1)} %copy-done.8, f32[64,128,128]{2,1,0:T(8,128)S(1)} %copy-done.8, f32[1,128,128]{2,1,0:T(8,128)S(1)} %bitcast.125, f32[1,128,128]{2,1,0:T(8,128)S(1)} %bitcast.127, ...), custom_call_target="tpu_custom_call" | custom-call | flops 5000000000 | bytes 9437184 | tf_op jit(solution)/shard_map/frozen/pallas_call | solution.py:352
  788.8 24.1 %collective-permute-done.20.refs_9_ = f32[64,128]{1,0:T(8,128)S(1)} collective-permute-done((f32[64,128]{1,0:T(8,128)}, f32[64,128]{1,0:T(8,128)S(1)}, u32[]{:S(2)}, u32[]{:S(2)}) %collective-permute-start.20) | collective-permute-done | bytes 32800 | tf_op jit(solution)/shard_map/ppermute | solution.py:791
  812.9 8.3 lines.1.tail
  823.2 13.6 %collective-permute-done.28.refs_2_ = f32[16,128,128]{2,1,0:T(8,128)S(1)} collective-permute-done((f32[16,128,128]{2,1,0:T(8,128)}, f32[16,128,128]{2,1,0:T(8,128)S(1)}, u32[]{:S(2)}, u32[]{:S(2)}) %collective-permute-start.28) | collective-permute-done | bytes 1048608 | tf_op jit(solution)/shard_map/ppermute | solution.py:798
  836.9 9.6 %drift.1.given = f32[24,256]{1,0:T(8,128)S(1)} custom-call(s32[1]{0:T(128)} %bitcast.i, f32[16,128,128]{2,1,0:T(8,128)S(1)} %get-tuple-element.42.refs_0_, f32[16,128,128]{2,1,0:T(8,128)S(1)} %collective-permute-done.27.refs_1_, f32[16,128,128]{2,1,0:T(8,128)S(1)} %collective-permute-done.28.refs_2_, f32[16,128,128]{2,1,0:T(8,128)} %collective-permute-done.29.refs_3_, ...), custom_call_target="tpu_custom_call" | custom-call | flops 4000000000 | bytes 17825792 | tf_op jit(solution)/shard_map/drift/pallas_call | solution.py:692
  858.4 16.8 %all-to-all-start.12 = ((f32[32,1,96]{2,1,0:T(1,128)}), f32[32,1,96]{2,1,0:T(1,128)S(1)}, u32[]{:S(2)}, u32[]{:S(2)}) async-start(f32[32,1,96]{2,1,0:T(1,128)} %bitcast.62), calls=%async_computation.12 | async-start | bytes 32768 | tf_op jit(solution)/shard_map/all_to_all | solution.py:881
  890.2 9.7 %adjoint.1 = f32[64,128,128]{2,1,0:T(8,128)} custom-call(s32[1]{0:T(128)} %bitcast.i, f32[8,66,16,128]{3,2,1,0:T(8,128)} %all-to-all-done.9.start.adjoint_start, f32[66,128]{1,0:T(8,128)S(1)} %collective-permute-done.18.start_low, f32[66,128]{1,0:T(8,128)S(1)} %collective-permute-done.19.start_high, f32[64,128,128]{2,1,0:T(8,128)S(1)} %copy-done.3, ...), custom_call_target="tpu_custom_call" | custom-call | flops 5000000000 | bytes 17825792 | tf_op jit(solution)/shard_map/adjoint/pallas_call | solution.py:769
  (252 shorter events, 278.2 us)
Async XLA Ops:
  7.9 29.5 %collective-permute-start = (f32[16,128,128]{2,1,0:T(8,128)}, f32[16,128,128]{2,1,0:T(8,128)}, u32[]{:S(2)}, u32[]{:S(2)}) collective-permute-start(f32[16,128,128]{2,1,0:T(8,128)} %get-tuple-element.58), channel_id=1, source_target_pairs={{0,1},{1,2},{2,3},{3,0},{4,5},{5,6},{6,7},{7,4},{8,9},{9,10},{10,1... | collective-permute-start | bytes 3145736 | tf_op jit(solution)/shard_map/ppermute | solution.py:798
  10.9 70.6 %collective-permute-start.1 = (f32[16,128,128]{2,1,0:T(8,128)}, f32[16,128,128]{2,1,0:T(8,128)}, u32[]{:S(2)}, u32[]{:S(2)}) collective-permute-start(f32[16,128,128]{2,1,0:T(8,128)} %get-tuple-element.57), channel_id=1, source_target_pairs={{0,2},{1,3},{2,0},{3,1},{4,6},{5,7},{6,4},{7,5},{8,10},{9,11},{10,... | collective-permute-start | bytes 3145736 | tf_op jit(solution)/shard_map/ppermute | solution.py:798
  13.5 68.0 %collective-permute-start.2 = (f32[16,128,128]{2,1,0:T(8,128)}, f32[16,128,128]{2,1,0:T(8,128)}, u32[]{:S(2)}, u32[]{:S(2)}) collective-permute-start(f32[16,128,128]{2,1,0:T(8,128)} %get-tuple-element.56), channel_id=1, source_target_pairs={{0,3},{1,0},{2,1},{3,2},{4,7},{5,4},{6,5},{7,6},{8,11},{9,8},{10,9... | collective-permute-start | bytes 3145736 | tf_op jit(solution)/shard_map/ppermute | solution.py:798
  95.7 48.5 %collective-permute-start.3 = (f32[8,16,16,128]{3,2,1,0:T(8,128)}, f32[8,16,16,128]{3,2,1,0:T(8,128)}, u32[]{:S(2)}, u32[]{:S(2)}) collective-permute-start(f32[8,16,16,128]{3,2,1,0:T(8,128)} %get-tuple-element.25), channel_id=1, source_target_pairs={{0,1},{1,2},{2,3},{3,0},{4,5},{5,6},{6,7},{7,4},{8,9},{9,10},{10,1... | collective-permute-start | bytes 3145736 | tf_op jit(solution)/shard_map/ppermute | solution.py:798
  122.3 65.0 %collective-permute-start.4 = (f32[8,16,16,128]{3,2,1,0:T(8,128)}, f32[8,16,16,128]{3,2,1,0:T(8,128)}, u32[]{:S(2)}, u32[]{:S(2)}) collective-permute-start(f32[8,16,16,128]{3,2,1,0:T(8,128)} %copy-done.46), channel_id=1, source_target_pairs={{0,2},{1,3},{2,0},{3,1},{4,6},{5,7},{6,4},{7,5},{8,10},{9,11},{10,... | collective-permute-start | bytes 3145736 | tf_op jit(solution)/shard_map/ppermute | solution.py:798
  144.1 43.2 %all-to-all-start.1 = ((f32[8,16,16,128]{3,2,1,0:T(8,128)}), f32[8,16,16,128]{3,2,1,0:T(8,128)}, u32[]{:S(2)}, u32[]{:S(2)}) async-start(f32[8,16,16,128]{3,2,1,0:T(8,128)} %collective-permute-done.3), calls=%async_computation.1 | async-start | bytes 2097152 | tf_op jit(solution)/shard_map/all_to_all | solution.py:803
  150.3 41.3 %collective-permute-start.8 = (f32[2,128,128]{2,0,1:T(2,128)S(1)}, f32[2,128,128]{2,0,1:T(2,128)S(1)}, u32[]{:S(2)}, u32[]{:S(2)}) collective-permute-start(f32[2,128,128]{2,0,1:T(2,128)S(1)} %pad_maximum_fusion.5), channel_id=1, source_target_pairs={{0,4},{4,8},{8,12},{12,16},{16,20},{20,24},{24,28},{1,5},{5,9},{9,... | collective-permute-start | bytes 393224 | tf_op jit(solution)/shard_map/ppermute | solution.py:791
  152.6 65.7 %collective-permute-start.5 = (f32[8,16,16,128]{3,2,1,0:T(8,128)}, f32[8,16,16,128]{3,2,1,0:T(8,128)}, u32[]{:S(2)}, u32[]{:S(2)}) collective-permute-start(f32[8,16,16,128]{3,2,1,0:T(8,128)} %copy-done.44), channel_id=1, source_target_pairs={{0,3},{1,0},{2,1},{3,2},{4,7},{5,4},{6,5},{7,6},{8,11},{9,8},{10,9... | collective-permute-start | bytes 3145736 | tf_op jit(solution)/shard_map/ppermute | solution.py:798
  153.4 38.2 %collective-permute-start.9 = (f32[2,128,128]{2,0,1:T(2,128)}, f32[2,128,128]{2,0,1:T(2,128)S(1)}, u32[]{:S(2)}, u32[]{:S(2)}) collective-permute-start(f32[2,128,128]{2,0,1:T(2,128)} %pad_maximum_fusion.6), channel_id=1, source_target_pairs={{4,0},{8,4},{12,8},{16,12},{20,16},{24,20},{28,24},{5,1},{9,5},{13... | collective-permute-start | bytes 393224 | tf_op jit(solution)/shard_map/ppermute | solution.py:791
  187.3 31.0 %all-to-all-start.2 = ((f32[8,16,16,128]{3,2,1,0:T(8,128)}), f32[8,16,16,128]{3,2,1,0:T(8,128)}, u32[]{:S(2)}, u32[]{:S(2)}) async-start(f32[8,16,16,128]{3,2,1,0:T(8,128)} %collective-permute-done.4), calls=%async_computation.2 | async-start | bytes 2097152 | tf_op jit(solution)/shard_map/all_to_all | solution.py:803
  192.3 30.1 %collective-permute-start.11 = (f32[2,66,128]{2,1,0:T(8,128)}, f32[2,66,128]{2,1,0:T(8,128)S(1)}, u32[]{:S(2)}, u32[]{:S(2)}) collective-permute-start(f32[2,66,128]{2,1,0:T(8,128)} %get-tuple-element.76), channel_id=1, source_target_pairs={{1,0},{2,1},{3,2},{5,4},{6,5},{7,6},{9,8},{10,9},{11,10},{13,12},{... | collective-permute-start | bytes 202760 | tf_op jit(solution)/shard_map/ppermute | solution.py:791
  193.5 28.9 %collective-permute-start.10 = (f32[2,66,128]{2,1,0:T(8,128)S(1)}, f32[2,66,128]{2,1,0:T(8,128)S(1)}, u32[]{:S(2)}, u32[]{:S(2)}) collective-permute-start(f32[2,66,128]{2,1,0:T(8,128)S(1)} %get-tuple-element.77), channel_id=1, source_target_pairs={{0,1},{1,2},{2,3},{4,5},{5,6},{6,7},{8,9},{9,10},{10,11},{12,13},{... | collective-permute-start | bytes 202760 | tf_op jit(solution)/shard_map/ppermute | solution.py:791
  238.8 53.7 %all-to-all-start.10 = ((f32[8,64,16,128]{3,2,1,0:T(8,128)}), f32[8,64,16,128]{3,2,1,0:T(8,128)}, u32[]{:S(2)}, u32[]{:S(2)}) async-start(f32[8,64,16,128]{3,2,1,0:T(8,128)} %copy-done.16), calls=%async_computation.10 | async-start | bytes 8388608 | tf_op jit(solution)/shard_map/all_to_all | solution.py:803
  292.5 55.1 %all-to-all-start.4 = ((f32[8,66,16,128]{3,2,1,0:T(8,128)}), f32[8,66,16,128]{3,2,1,0:T(8,128)}, u32[]{:S(2)}, u32[]{:S(2)}) async-start(f32[8,66,16,128]{3,2,1,0:T(8,128)} %bitcast.112), calls=%async_computation.4 | async-start | bytes 8650752 | tf_op jit(solution)/shard_map/all_to_all | solution.py:803
  347.7 145.9 %all-to-all-start.11 = ((f32[8,64,16,128]{3,2,1,0:T(8,128)}), f32[8,64,16,128]{3,2,1,0:T(8,128)}, u32[]{:S(2)}, u32[]{:S(2)}) async-start(f32[8,64,16,128]{3,2,1,0:T(8,128)} %bitcast.113), calls=%async_computation.11 | async-start | bytes 8388608 | tf_op jit(solution)/shard_map/all_to_all | solution.py:803
  388.0 28.1 %collective-permute-start.12 = (f32[16,128,128]{2,1,0:T(8,128)S(1)}, f32[16,128,128]{2,1,0:T(8,128)S(1)}, u32[]{:S(2)}, u32[]{:S(2)}) collective-permute-start(f32[16,128,128]{2,1,0:T(8,128)S(1)} %get-tuple-element.29.refs_1_), channel_id=1, source_target_pairs={{0,1},{1,2},{2,3},{3,0},{4,5},{5,6},{6,7},{7,4},{8,9},{9,10},{10,1... | collective-permute-start | bytes 3145736 | tf_op jit(solution)/shard_map/ppermute | solution.py:798
  391.0 68.3 %collective-permute-start.13 = (f32[16,128,128]{2,1,0:T(8,128)S(1)}, f32[16,128,128]{2,1,0:T(8,128)S(1)}, u32[]{:S(2)}, u32[]{:S(2)}) collective-permute-start(f32[16,128,128]{2,1,0:T(8,128)S(1)} %get-tuple-element.30.refs_2_), channel_id=1, source_target_pairs={{0,2},{1,3},{2,0},{3,1},{4,6},{5,7},{6,4},{7,5},{8,10},{9,11},{10,... | collective-permute-start | bytes 3145736 | tf_op jit(solution)/shard_map/ppermute | solution.py:798
  393.6 65.8 %collective-permute-start.14 = (f32[16,128,128]{2,1,0:T(8,128)S(1)}, f32[16,128,128]{2,1,0:T(8,128)S(1)}, u32[]{:S(2)}, u32[]{:S(2)}) collective-permute-start(f32[16,128,128]{2,1,0:T(8,128)S(1)} %get-tuple-element.31.refs_3_), channel_id=1, source_target_pairs={{0,3},{1,0},{2,1},{3,2},{4,7},{5,4},{6,5},{7,6},{8,11},{9,8},{10,9... | collective-permute-start | bytes 3145736 | tf_op jit(solution)/shard_map/ppermute | solution.py:798
  471.6 68.7 %collective-permute-start.16 = (f32[8,16,16,128]{3,1,2,0:T(8,128)}, f32[8,16,16,128]{3,1,2,0:T(8,128)}, u32[]{:S(2)}, u32[]{:S(2)}) collective-permute-start(f32[8,16,16,128]{3,1,2,0:T(8,128)} %copy.108), channel_id=1, source_target_pairs={{0,2},{1,3},{2,0},{3,1},{4,6},{5,7},{6,4},{7,5},{8,10},{9,11},{10,... | collective-permute-start | bytes 3145736 | tf_op jit(solution)/shard_map/ppermute | solution.py:798
  500.0 67.2 %collective-permute-start.17 = (f32[8,16,16,128]{3,1,2,0:T(8,128)}, f32[8,16,16,128]{3,1,2,0:T(8,128)}, u32[]{:S(2)}, u32[]{:S(2)}) collective-permute-start(f32[8,16,16,128]{3,1,2,0:T(8,128)} %copy.110), channel_id=1, source_target_pairs={{0,3},{1,0},{2,1},{3,2},{4,7},{5,4},{6,5},{7,6},{8,11},{9,8},{10,9... | collective-permute-start | bytes 3145736 | tf_op jit(solution)/shard_map/ppermute | solution.py:798
  544.6 49.4 %collective-permute-start.15 = (f32[8,16,16,128]{3,2,1,0:T(8,128)}, f32[8,16,16,128]{3,2,1,0:T(8,128)}, u32[]{:S(2)}, u32[]{:S(2)}) collective-permute-start(f32[8,16,16,128]{3,2,1,0:T(8,128)} %copy-done.45), channel_id=1, source_target_pairs={{0,1},{1,2},{2,3},{3,0},{4,5},{5,6},{6,7},{7,4},{8,9},{9,10},{10,1... | collective-permute-start | bytes 3145736 | tf_op jit(solution)/shard_map/ppermute | solution.py:798
  594.0 39.8 %all-to-all-start.6 = ((f32[8,16,16,128]{3,2,1,0:T(8,128)}), f32[8,16,16,128]{3,2,1,0:T(8,128)}, u32[]{:S(2)}, u32[]{:S(2)}) async-start(f32[8,16,16,128]{3,2,1,0:T(8,128)} %collective-permute-done.15.refs_7_), calls=%async_computation.6 | async-start | bytes 2097152 | tf_op jit(solution)/shard_map/all_to_all | solution.py:803
  610.5 41.0 %collective-permute-start.22 = (f32[16,128,128]{2,1,0:T(8,128)}, f32[16,128,128]{2,1,0:T(8,128)}, u32[]{:S(2)}, u32[]{:S(2)}) collective-permute-start(f32[16,128,128]{2,1,0:T(8,128)} %get-tuple-element.39), channel_id=1, source_target_pairs={{0,1},{1,2},{2,3},{3,0},{4,5},{5,6},{6,7},{7,4},{8,9},{9,10},{10,1... | collective-permute-start | bytes 3145736 | tf_op jit(solution)/shard_map/ppermute | solution.py:798
  618.8 71.9 %collective-permute-start.23 = (f32[16,128,128]{2,1,0:T(8,128)}, f32[16,128,128]{2,1,0:T(8,128)}, u32[]{:S(2)}, u32[]{:S(2)}) collective-permute-start(f32[16,128,128]{2,1,0:T(8,128)} %get-tuple-element.40), channel_id=1, source_target_pairs={{0,2},{1,3},{2,0},{3,1},{4,6},{5,7},{6,4},{7,5},{8,10},{9,11},{10,... | collective-permute-start | bytes 3145736 | tf_op jit(solution)/shard_map/ppermute | solution.py:798
  622.1 68.5 %collective-permute-start.24 = (f32[16,128,128]{2,1,0:T(8,128)}, f32[16,128,128]{2,1,0:T(8,128)}, u32[]{:S(2)}, u32[]{:S(2)}) collective-permute-start(f32[16,128,128]{2,1,0:T(8,128)} %get-tuple-element.41), channel_id=1, source_target_pairs={{0,3},{1,0},{2,1},{3,2},{4,7},{5,4},{6,5},{7,6},{8,11},{9,8},{10,9... | collective-permute-start | bytes 3145736 | tf_op jit(solution)/shard_map/ppermute | solution.py:798
  646.8 199.7 %all-to-all-start.9 = ((f32[8,66,16,128]{3,2,1,0:T(8,128)}), f32[8,66,16,128]{3,2,1,0:T(8,128)}, u32[]{:S(2)}, u32[]{:S(2)}) async-start(f32[8,66,16,128]{3,2,1,0:T(8,128)} %bitcast.111), calls=%async_computation.9 | async-start | bytes 8650752 | tf_op jit(solution)/shard_map/all_to_all | solution.py:803
  700.9 31.5 %collective-permute-start.25 = (f32[1,512,128]{2,1,0:T(8,128)S(1)}, f32[1,512,128]{2,1,0:T(8,128)S(1)}, u32[]{:S(2)}, u32[]{:S(2)}) collective-permute-start(f32[1,512,128]{2,1,0:T(8,128)S(1)} %get-tuple-element.51), channel_id=1, source_target_pairs={{0,1},{1,2},{2,3},{3,4},{4,5},{5,6},{6,7},{7,8},{8,9},{9,10},{10,1... | collective-permute-start | bytes 786440 | tf_op jit(solution)/shard_map/ppermute | solution.py:854
  744.0 79.2 %collective-permute-start.27 = (f32[16,128,128]{2,1,0:T(8,128)}, f32[16,128,128]{2,1,0:T(8,128)S(1)}, u32[]{:S(2)}, u32[]{:S(2)}) collective-permute-start(f32[16,128,128]{2,1,0:T(8,128)} %get-tuple-element.43), channel_id=1, source_target_pairs={{0,3},{1,0},{2,1},{3,2},{4,7},{5,4},{6,5},{7,6},{8,11},{9,8},{10,9... | collective-permute-start | bytes 3145736 | tf_op jit(solution)/shard_map/ppermute | solution.py:798
  746.1 90.8 %collective-permute-start.28 = (f32[16,128,128]{2,1,0:T(8,128)}, f32[16,128,128]{2,1,0:T(8,128)S(1)}, u32[]{:S(2)}, u32[]{:S(2)}) collective-permute-start(f32[16,128,128]{2,1,0:T(8,128)} %get-tuple-element.44), channel_id=1, source_target_pairs={{0,2},{1,3},{2,0},{3,1},{4,6},{5,7},{6,4},{7,5},{8,10},{9,11},{10,... | collective-permute-start | bytes 3145736 | tf_op jit(solution)/shard_map/ppermute | solution.py:798
  746.1 90.8 %collective-permute-start.29 = (f32[16,128,128]{2,1,0:T(8,128)}, f32[16,128,128]{2,1,0:T(8,128)}, u32[]{:S(2)}, u32[]{:S(2)}) collective-permute-start(f32[16,128,128]{2,1,0:T(8,128)} %get-tuple-element.45), channel_id=1, source_target_pairs={{0,1},{1,2},{2,3},{3,0},{4,5},{5,6},{6,7},{7,4},{8,9},{9,10},{10,1... | collective-permute-start | bytes 3145736 | tf_op jit(solution)/shard_map/ppermute | solution.py:798
  753.4 35.4 %collective-permute-start.21 = (f32[64,128]{1,0:T(8,128)}, f32[64,128]{1,0:T(8,128)}, u32[]{:S(2)}, u32[]{:S(2)}) collective-permute-start(f32[64,128]{1,0:T(8,128)} %bitcast.142), channel_id=1, source_target_pairs={{1,0},{2,1},{3,2},{5,4},{6,5},{7,6},{9,8},{10,9},{11,10},{13,12},{... | collective-permute-start | bytes 98312 | tf_op jit(solution)/shard_map/ppermute | solution.py:791
  758.0 54.8 %collective-permute-start.20 = (f32[64,128]{1,0:T(8,128)}, f32[64,128]{1,0:T(8,128)S(1)}, u32[]{:S(2)}, u32[]{:S(2)}) collective-permute-start(f32[64,128]{1,0:T(8,128)} %bitcast.143), channel_id=1, source_target_pairs={{0,1},{1,2},{2,3},{4,5},{5,6},{6,7},{8,9},{9,10},{10,11},{12,13},{... | collective-permute-start | bytes 98312 | tf_op jit(solution)/shard_map/ppermute | solution.py:791
  (66 other events, 1465.2 us)

commit v2 on v1

--- a/solution.py
+++ b/solution.py
@@ -167,11 +167,11 @@
 
 
 def params(mib):
-    return pltpu.CompilerParams(vmem_limit_bytes=mib * MIB)
+    return pltpu.CompilerParams(vmem_limit_bytes=60 * MIB)
 
 
 def cost(flops, mib):
-    return pl.CostEstimate(flops=int(flops), bytes_accessed=int(mib * MIB), transcendentals=0)
+    return pl.CostEstimate(flops=int(flops / 50), bytes_accessed=int(mib * MIB / 50), transcendentals=0)
 
 
 def halves(x):
@@ -326,45 +326,6 @@
     )(index, state, state, state, low, high, y_low, y_high, volatility)
 
 
-def frozen_kernel(i, state, before, after, low, high, q_low, q_high, third3, out, *, blocks):
-    block = pl.program_id(0)
-
-    def plane(k):
-        v = pick_plane(k, PLANES, block, state, before, after, low, high, blocks)
-        up, down = z_pair(v)
-        return v + damping * right_product(up + down - 2.0 * v, third3[...])
-
-    def emit(k, v, prev, nxt, mixed, inner):
-        out[k] = mixed
-
-    sweep(
-        PLANES,
-        plane,
-        lambda k: (q_low[pl.ds(block * PLANES + k + 1, 1), :], q_high[pl.ds(block * PLANES + k + 1, 1), :]),
-        emit,
-        False,
-    )
-
-
-def frozen(index, state, low, high, q_low, q_high, third3):
-    bx, by, bz = state.shape
-    blocks = bx // PLANES
-    return pl.pallas_call(
-        functools.partial(frozen_kernel, blocks=blocks),
-        grid_spec=pltpu.PrefetchScalarGridSpec(
-            num_scalar_prefetch=1,
-            grid=(blocks,),
-            in_specs=plane_specs(natural, bx - 1, state.shape)
-            + [whole(low.shape), whole(high.shape), whole(q_low.shape), whole(q_high.shape), whole(third3.shape)],
-            out_specs=pl.BlockSpec((PLANES, by, bz), lambda s, i: (s, 0, 0)),
-        ),
-        out_shape=jax.ShapeDtypeStruct(state.shape, F32),
-        compiler_params=params(32),
-        cost_estimate=cost(5e9, 9),
-        name="frozen",
-    )(index, state, state, state, low, high, q_low, q_high, third3)
-
-
 def first_kernel(*refs, count, lines, parts, length, halo):
     pieces, matrix3, out = refs[:count], refs[count], refs[count + 1]
     depth = pieces[0].shape[0] // lines
@@ -456,8 +417,8 @@
     )(*pieces, second3, third3)
 
 
-def piece_specs(xs, tail, per, n):
-    return [pl.BlockSpec((PLANES,) + tail, lambda s, i, d=d: (jnp.clip(s - d * per, 0, per - 1), 0, 0)) for d in range(n)]
+def piece_specs(size, tail, per, n):
+    return [pl.BlockSpec((size,) + tail, lambda s, i, d=d: (jnp.clip(s - d * per, 0, per - 1), 0, 0)) for d in range(n)]
 
 
 def chunk_piece_specs(wide, lines, bz, per, order):
@@ -467,12 +428,12 @@
     ]
 
 
-def store_piece(outs, step, per, k, value):
+def store_piece(outs, turn, kept):
     for d, out in enumerate(outs):
 
-        @pl.when(step // per == d)
+        @pl.when(turn == d)
         def _(out=out):
-            out[k] = value
+            out[...] = kept[...]
 
 
 def select(values, turn):
@@ -482,44 +443,45 @@
     return result
 
 
-def lifted_kernel(i, solved, state, y_low, y_high, *outs, per, n):
+def lifted_kernel(i, solved, state, low, high, y_low, y_high, *refs, per, n, size, xs):
+    outs, kept = refs[:n], refs[n]
     step = pl.program_id(0)
-    block = rotated(per, n)(step, i)
-    for k in range(PLANES):
-        v = state[k]
-        up, down = y_pair(v, y_low[pl.ds(block * PLANES + k + 1, 1), :], y_high[pl.ds(block * PLANES + k + 1, 1), :])
-        store_piece(outs, step, per, k, chunk_plane(solved, k) - damping * (up + down - 2.0 * v))
-
-
-def lifted(index, solved, state, y_low, y_high, n):
+    bx = state.shape[0]
+    base = lax.rem(i[0] + step // per, n) * xs + lax.rem(step, per) * size
+    for k in range(size):
+        row = base + k
+        v = state[jnp.clip(row - 1, 0, bx - 1)]
+        v = jnp.where(row == 0, low[0], jnp.where(row == bx + 1, high[0], v))
+        up, down = y_pair(v, y_low[pl.ds(row, 1), :], y_high[pl.ds(row, 1), :])
+        kept[k] = chunk_plane(solved, row) - damping * (up + down - 2.0 * v)
+    store_piece(outs, step // per, kept)
+
+
+def lifted(index, solved, state, low, high, y_low, y_high, n):
     bx, by, bz = state.shape
     xs = bx // n
-    per = xs // PLANES
-    wide, lines = solved.shape[0], solved.shape[2]
-    block = rotated(per, n)
+    size = next(k for k in range(9, 0, -1) if (xs + 2) % k == 0)
+    per = (xs + 2) // size
     return pl.pallas_call(
-        functools.partial(lifted_kernel, per=per, n=n),
+        functools.partial(lifted_kernel, per=per, n=n, size=size, xs=xs),
         grid_spec=pltpu.PrefetchScalarGridSpec(
             num_scalar_prefetch=1,
             grid=(n * per,),
-            in_specs=[
-                pl.BlockSpec((wide, PLANES, lines, bz), lambda s, i: (0, block(s, i), 0, 0)),
-                pl.BlockSpec((PLANES, by, bz), lambda s, i: (block(s, i), 0, 0)),
-                whole(y_low.shape),
-                whole(y_high.shape),
-            ],
-            out_specs=piece_specs(xs, (by, bz), per, n),
+            in_specs=[whole(v.shape) for v in (solved, state, low, high, y_low, y_high)],
+            out_specs=piece_specs(size, (by, bz), per, n),
+            scratch_shapes=[pltpu.VMEM((size, by, bz), F32)],
         ),
-        out_shape=[jax.ShapeDtypeStruct((xs, by, bz), F32)] * n,
+        out_shape=[jax.ShapeDtypeStruct((xs + 2, by, bz), F32)] * n,
         compiler_params=params(32),
         cost_estimate=cost(2e9, 13),
         name="lifted",
-    )(index, solved, state, y_low, y_high)
+    )(index, solved, state, low, high, y_low, y_high)
 
 
 def reaction_kernel(
-    i, carried, carried_low, carried_high, vol, before, after, low, high, vol_low, vol_high, cotangent, *outs, per, n, blocks
+    i, carried, carried_low, carried_high, vol, before, after, low, high, vol_low, vol_high, cotangent, *refs, per, n, blocks
 ):
+    outs, kept = refs[:n], refs[n]
     step = pl.program_id(0)
     block = rotated(per, n)(step, i)
 
@@ -536,9 +498,10 @@
         )
 
     def emit(k, v, prev, nxt, mixed, inner):
-        store_piece(outs, step, per, k, cotangent[k] + mixed)
+        kept[k] = cotangent[k] + mixed
 
     sweep(PLANES, plane, rows, emit, False)
+    store_piece(outs, step // per, kept)
 
 
 def react(index, carried, carried_low, carried_high, vol, low, high, vol_low, vol_high, cotangent, n):
@@ -555,7 +518,8 @@
             + plane_specs(block, bx - 1, vol.shape)
             + [whole(low.shape), whole(high.shape), whole(vol_low.shape), whole(vol_high.shape)]
             + [pl.BlockSpec((PLANES, by, bz), lambda s, i: (block(s, i), 0, 0))],
-            out_specs=piece_specs(xs, (by, bz), per, n),
+            out_specs=piece_specs(PLANES, (by, bz), per, n),
+            scratch_shapes=[pltpu.VMEM((PLANES, by, bz), F32)],
         ),
         out_shape=[jax.ShapeDtypeStruct((xs, by, bz), F32)] * n,
         compiler_params=params(40),
@@ -594,7 +558,7 @@
         grid_spec=pltpu.PrefetchScalarGridSpec(
             num_scalar_prefetch=1,
             grid=(n * per,),
-            in_specs=piece_specs(xs, (by, bz), per, n)
+            in_specs=piece_specs(PLANES, (by, bz), per, n)
             + chunk_piece_specs(wide, lines, bz, per, range(n))
             + [pl.BlockSpec((PLANES, by, bz), lambda s, i: (block(s, i), 0, 0))]
             + [whole(upper_low.shape), whole(upper_high.shape), whole(third3.shape)],
@@ -607,9 +571,8 @@
     )(index, *totals, *[uppers[order[d]] for d in range(n)], cotangent, upper_low, upper_high, third3)
 
 
-def mixed_kernel(i, field, low, high, *refs, n):
+def mixed_kernel(i, field, *refs, n):
     outs, scratch = refs[:n], refs[n]
-    count = field.shape[0]
     by = outs[0].shape[1]
 
     def emit(k, v, prev, nxt, mixed, inner):
@@ -619,24 +582,18 @@
             out[k] = scratch[pl.ds(start, by), :]
 
     zero = jnp.zeros((1, field.shape[2]), F32)
-    sweep(
-        count,
-        lambda k: low[0] if k < 0 else high[0] if k >= count else field[k],
-        lambda k: (zero, zero),
-        emit,
-        False,
-    )
-
-
-def mix(index, field, low, high, n):
-    xs, ny, bz = field.shape
-    by = ny // n
+    sweep(field.shape[0] - 2, lambda k: field[k + 1], lambda k: (zero, zero), emit, False)
+
+
+def mix(index, field, n):
+    rows, ny, bz = field.shape
+    xs, by = rows - 2, ny // n
     return pl.pallas_call(
         functools.partial(mixed_kernel, n=n),
         grid_spec=pltpu.PrefetchScalarGridSpec(
             num_scalar_prefetch=1,
             grid=(1,),
-            in_specs=[whole(field.shape), whole(low.shape), whole(high.shape)],
+            in_specs=[whole(field.shape)],
             out_specs=[whole((xs, by, bz))] * n,
             scratch_shapes=[pltpu.VMEM((ny, bz), F32)],
         ),
@@ -644,7 +601,7 @@
         compiler_params=params(40),
         cost_estimate=cost(4e9, 9),
         name="mixed",
-    )(index, field, low, high)
+    )(index, field)
 
 
 def patch_sums(out, step, planes, patch, patch_t, groups):
@@ -653,8 +610,12 @@
         out[...] = jnp.zeros_like(out)
 
     acc = None
+    ones = jnp.ones((planes[0].shape[1], 128), BF16)
     for k, value in enumerate(planes):
-        column = jnp.sum(value, axis=1, keepdims=True)
+        value_high, value_low = split(value)
+        column = jnp.dot(value_high, ones, preferred_element_type=F32) + jnp.dot(
+            value_low, ones, preferred_element_type=F32
+        )
         number = patch[pl.ds(k, 1), :]
         coarse = lax.broadcasted_iota(jnp.int32, (groups, number.shape[1]), 0) == lax.shift_right_logical(number, 7)
         number_t = patch_t[k]
@@ -668,73 +629,98 @@
     out[...] += acc
 
 
-def drift_kernel(i, *refs, per, n, groups):
+def frozen_kernel(
+    i, state, before, after, low, high, q_low, q_high, third3, vol, carried, patch, patch_t, weight, out, *, blocks, groups
+):
+    block = pl.program_id(0)
+    planes = []
+
+    def plane(k):
+        v = pick_plane(k, PLANES, block, state, before, after, low, high, blocks)
+        up, down = z_pair(v)
+        return v + damping * right_product(up + down - 2.0 * v, third3[...])
+
+    def emit(k, v, prev, nxt, mixed, inner):
+        w = correction * vol[k] * chunk_plane(carried, block * PLANES + k + 1)
+        weight[k] = w
+        planes.append(-w * mixed)
+
+    sweep(
+        PLANES,
+        plane,
+        lambda k: (q_low[pl.ds(block * PLANES + k + 1, 1), :], q_high[pl.ds(block * PLANES + k + 1, 1), :]),
+        emit,
+        False,
+    )
+    patch_sums(out, block, planes, patch, patch_t, groups)
+
+
+def frozen(index, state, low, high, q_low, q_high, third3, vol, carried, patch, patch_t, groups):
+    bx, by, bz = state.shape
+    blocks = bx // PLANES
+    main = pl.BlockSpec((PLANES, by, bz), lambda s, i: (s, 0, 0))
+    return pl.pallas_call(
+        functools.partial(frozen_kernel, blocks=blocks, groups=groups),
+        grid_spec=pltpu.PrefetchScalarGridSpec(
+            num_scalar_prefetch=1,
+            grid=(blocks,),
+            in_specs=plane_specs(natural, bx - 1, state.shape)
+            + [whole(low.shape), whole(high.shape), whole(q_low.shape), whole(q_high.shape), whole(third3.shape)]
+            + [main, whole(carried.shape)]
+            + [pl.BlockSpec((PLANES, by), lambda s, i: (s, 0))]
+            + [pl.BlockSpec((PLANES, by, 1), lambda s, i: (s, 0, 0))],
+            out_specs=[main, whole((groups, 256))],
+        ),
+        out_shape=[jax.ShapeDtypeStruct(state.shape, F32), jax.ShapeDtypeStruct((groups, 256), F32)],
+        compiler_params=params(32),
+        cost_estimate=cost(5e9, 17),
+        name="frozen",
+    )(index, state, state, state, low, high, q_low, q_high, third3, vol, carried, patch, patch_t)
+
+
+def column_kernel(i, *refs, per, n, groups):
     drifts = refs[:n]
-    frozen_part, carried, vol, patch, patch_t, out = refs[n:]
+    weight, source, start, patch, patch_t, given, out = refs[n:]
     step = pl.program_id(0)
     turn = step // per
     block = rotated(per, n)(step, i)
-    planes = []
-    for k in range(PLANES):
-        drift = select([ref[k] for ref in drifts], turn) - frozen_part[k]
-        planes.append(correction * vol[k] * chunk_plane(carried, block * PLANES + k + 1) * drift)
+    planes = [
+        weight[k] * select([ref[k] for ref in drifts], turn)
+        + source[k] * chunk_plane(start, block * PLANES + k + 1)
+        for k in range(PLANES)
+    ]
     patch_sums(out, step, planes, patch, patch_t, groups)
 
-
-def drift_sums(index, drifts, frozen_part, carried, vol, patch, patch_t, groups):
+    @pl.when(step == pl.num_programs(0) - 1)
+    def _():
+        out[...] += given[...]
+
+
+def column_sums(index, drifts, weight, source, start, patch, patch_t, given):
     n = len(drifts)
-    bx, by, bz = vol.shape
+    bx, by, bz = source.shape
     xs = bx // n
     per = xs // PLANES
+    groups = given.shape[0]
     block = rotated(per, n)
     order = [(n - e) % n for e in range(n)]
     main = pl.BlockSpec((PLANES, by, bz), lambda s, i: (block(s, i), 0, 0))
     return pl.pallas_call(
-        functools.partial(drift_kernel, per=per, n=n, groups=groups),
+        functools.partial(column_kernel, per=per, n=n, groups=groups),
         grid_spec=pltpu.PrefetchScalarGridSpec(
             num_scalar_prefetch=1,
             grid=(n * per,),
-            in_specs=piece_specs(xs, (by, bz), per, n)
-            + [main, whole(carried.shape), main]
+            in_specs=piece_specs(PLANES, (by, bz), per, n)
+            + [main, main, whole(start.shape)]
             + [pl.BlockSpec((PLANES, by), lambda s, i: (block(s, i), 0))]
-            + [pl.BlockSpec((PLANES, by, 1), lambda s, i: (block(s, i), 0, 0))],
-            out_specs=whole((groups, 256)),
-        ),
-        out_shape=jax.ShapeDtypeStruct((groups, 256), F32),
-        compiler_params=params(40),
-        cost_estimate=cost(4e9, 17),
-        name="drift",
-    )(index, *[drifts[order[d]] for d in range(n)], frozen_part, carried, vol, patch, patch_t)
-
-
-def source_kernel(i, adjoint_start, source, patch, patch_t, given, out, *, groups):
-    step = pl.program_id(0)
-    planes = [source[k] * chunk_plane(adjoint_start, step * PLANES + k + 1) for k in range(PLANES)]
-    patch_sums(out, step, planes, patch, patch_t, groups)
-
-    @pl.when(step == pl.num_programs(0) - 1)
-    def _():
-        out[...] += given[...]
-
-
-def source_sums(index, adjoint_start, source, patch, patch_t, given):
-    bx, by, bz = source.shape
-    groups = given.shape[0]
-    return pl.pallas_call(
-        functools.partial(source_kernel, groups=groups),
-        grid_spec=pltpu.PrefetchScalarGridSpec(
-            num_scalar_prefetch=1,
-            grid=(bx // PLANES,),
-            in_specs=[whole(adjoint_start.shape), pl.BlockSpec((PLANES, by, bz), lambda s, i: (s, 0, 0))]
-            + [pl.BlockSpec((PLANES, by), lambda s, i: (s, 0))]
-            + [pl.BlockSpec((PLANES, by, 1), lambda s, i: (s, 0, 0)), whole(given.shape)],
+            + [pl.BlockSpec((PLANES, by, 1), lambda s, i: (block(s, i), 0, 0)), whole(given.shape)],
             out_specs=whole(given.shape),
         ),
         out_shape=jax.ShapeDtypeStruct(given.shape, F32),
         compiler_params=params(40),
-        cost_estimate=cost(3e9, 9),
-        name="source",
-    )(index, adjoint_start, source, patch, patch_t, given)
+        cost_estimate=cost(4e9, 17),
+        name="column",
+    )(index, *[drifts[order[d]] for d in range(n)], weight, source, start, patch, patch_t, given)
 
 
 def adjoint_kernel(
@@ -791,16 +777,52 @@
     return lax.ppermute(high_edge, axis, up), lax.ppermute(low_edge, axis, down)
 
 
-def scatter_pieces(pieces, order=(2, 1, 3)):
+def far_and_near(n):
+    return [n // 2] if n > 1 else [], [d for d in range(1, n) if d != n // 2]
+
+
+def send(pieces, chosen, *earlier):
     n = len(pieces)
-    result = [pieces[0]] + [None] * (n - 1)
-    for d in sorted(range(1, n), key=lambda d: -min(d, n - d)):
-        result[d] = lax.ppermute(pieces[d], "narrow", [(k, (k + d) % n) for k in range(n)])
+    result = list(pieces)
+    for d in chosen:
+        piece = after(pieces[d], *earlier) if earlier else pieces[d]
+        result[d] = lax.ppermute(piece, "narrow", [(k, (k + d) % n) for k in range(n)])
     return result
+
+
+def pick(pieces, chosen):
+    return [pieces[d] for d in chosen]
+
+
+def after(value, *earlier):
+    return lax.optimization_barrier((value, earlier))[0]
 
 
 def across(piece):
     return lax.all_to_all(piece, "wide", split_axis=0, concat_axis=0, tiled=True)
+
+
+def cross_both(pieces, before, between, near, far):
+    lines = list(pieces)
+    met = send(pieces, near)
+    for d in near:
+        lines[d] = met[d]
+    chunks = [across(pieces[0])] + [None] * (len(pieces) - 1)
+    met, chunks[0], waiting = lax.optimization_barrier((pick(lines, near), chunks[0], pick(pieces, far)))
+    for d, value in zip(near, met):
+        lines[d] = value
+    rest = list(pieces)
+    for d, value in zip(far, waiting):
+        rest[d] = value
+    arrived = send(rest, far)
+    last = chunks[0]
+    for d in near:
+        chunks[d] = last = across(after(lines[d], last, *before))
+    gone = pick(arrived, far)
+    for d in far:
+        lines[d] = arrived[d]
+        chunks[d] = across(after(arrived[d], last, *between))
+    return lines, chunks, gone
 
 
 def y_edges(chunks):
@@ -818,13 +840,18 @@
     ahead = (here + jnp.arange(n)) % n
     back = (here - jnp.arange(n)) % n
 
+    far, near = far_and_near(n)
+    every = range(n)
+
     cot_pieces = [lax.dynamic_slice_in_dim(cotangent, ahead[d] * xs, xs, 0) for d in range(n)]
-    cot_lines = scatter_pieces(cot_pieces)
+    early, late = near[:1], near[1:]
+    cot_lines = send(cot_pieces, near)
+    edge_state, edge_volatility = after((state, volatility), cot_pieces)
 
     both_low, both_high = neighbours(
-        jnp.stack([state[0], volatility[0]]), jnp.stack([state[-1], volatility[-1]]), "wide"
+        jnp.stack([edge_state[0], edge_volatility[0]]), jnp.stack([edge_state[-1], edge_volatility[-1]]), "wide"
     )
-    both = jnp.stack([state[:, :: by - 1], volatility[:, :: by - 1]])
+    both = jnp.stack([edge_state[:, :: by - 1], edge_volatility[:, :: by - 1]])
     both = jnp.concatenate([both_low[:, None, :: by - 1], both, both_high[:, None, :: by - 1]], axis=1)
     y_low, y_high = neighbours(both[:, :, 0], both[:, :, 1], "narrow")
     state_x = (both_low[0:1], both_high[0:1])
@@ -842,46 +869,74 @@
     first_t = solve_first.T.reshape(wide * bx, wide, n, xs)
     first_t3 = left_form(first_t[:, :, back].transpose(0, 2, 1, 3).reshape(wide * bx, wide * bx))
 
+    state = after(state, *pick(cot_lines, early))
     a, source = forward(index, state, volatility, *state_x, *state_y, wide)
-    solved = across(first([across(a)], first_n3, 0))
-
-    back_second = scatter_pieces(second(cot_lines, second_t3, third_t3, wide))
-    carried = across(first([across(piece) for piece in back_second], first_t3, 1))
-
-    level = second(scatter_pieces(lifted(index, solved, state, *state_y, n)), second_n3, third_n3, 0)[0]
-    count = n * wide
-    joint = ("wide", "narrow")
-    level_low = lax.ppermute(level[-1:], joint, [(k, k + 1) for k in range(count - 1)])
-    level_high = lax.ppermute(level[:1], joint, [(k + 1, k) for k in range(count - 1)])
-    drift_pieces = mix(index, level, level_low, level_high, n)
+    a = after(a, *pick(cot_lines, late))
+    cot_lines = send(cot_lines, far, *pick(cot_lines, near))
+    back = second(cot_lines, second_t3, third_t3, wide)
+    forward_lines = first([after(across(a), *back)], first_n3, 1)
+    solved = across(forward_lines)
+
+    lifted_pieces = lifted(index, solved, state, *state_x, *state_y, n)
+    back, carried_chunks, gone = cross_both(back, (solved,), lifted_pieces, near, far)
+    carried_lines = first(carried_chunks, first_t3, 1)
+    level_lines = send(lifted_pieces, late, gone)
+    carried = across(after(carried_lines, *pick(level_lines, late)))
+
+    level_lines = send(level_lines, far, *pick(level_lines, late))
+    carried = after(carried, *pick(level_lines, far))
+    carried_y = y_edges(carried)
+    level_lines = send(level_lines, early, *carried_y)
+    totals = react(index, carried, *carried_y, volatility, *vol_x, *vol_y, cotangent, n)
+    total_lines = send(totals, far + near)
+
+    level = second(after(level_lines, totals), second_n3, third_n3, 0)[0]
+    drift_pieces = mix(index, level, n)
 
     def frozen_rows(rows):
         padded = jnp.pad(rows, ((0, 0), (1, 1)))
         curved = padded[:, 2:] + padded[:, :-2] - 2.0 * rows
         return rows + damping * jnp.dot(curved, solve_third.T, precision=lax.Precision.HIGHEST)
 
-    frozen_part = frozen(index, state, *state_x, frozen_rows(state_y[0]), frozen_rows(state_y[1]), third_n3)
-
-    carried_y = y_edges(carried)
-    totals = react(index, carried, *carried_y, volatility, *vol_x, *vol_y, cotangent, n)
-    uppers = scatter_pieces(second(scatter_pieces(totals), second_t3, third_t3, wide))
-    start = across(first([across(piece) for piece in uppers], first_t3, 1))
-
-    drifts = scatter_pieces(drift_pieces)
+    patch_t = patch_index[:, :, None]
+    weight, sums = frozen(
+        index,
+        after(state, *drift_pieces),
+        *state_x,
+        frozen_rows(state_y[0]),
+        frozen_rows(state_y[1]),
+        third_n3,
+        volatility,
+        carried,
+        patch_index,
+        patch_t,
+        groups,
+    )
+
+    total_lines = after(total_lines, drift_pieces, sums)
+    drifts = send(drift_pieces, early, *total_lines)
+    uppers = after(second(total_lines, second_t3, third_t3, wide), *pick(drifts, early))
+    uppers, start_chunks, gone = cross_both(uppers, (), (), near, far)
+    start_lines = first(start_chunks, first_t3, 1)
+    drifts = send(drifts, late, gone)
+    start = across(after(start_lines, *pick(drifts, late)))
+
     order = (here - jnp.arange(n)) % n
     edge_low = jnp.stack([piece[0, :, 0] for piece in uppers])[order].reshape(bx, bz)
     edge_high = jnp.stack([piece[-1, :, -1] for piece in uppers])[order].reshape(bx, bz)
     upper_y = neighbours(edge_low, edge_high, "narrow")
+    drifts = send(drifts, far, *pick(drifts, late), *upper_y)
     tail = gather_lines(index, totals, uppers, cotangent, *upper_y, third_t3)
 
-    patch_t = patch_index[:, :, None]
-    sums = drift_sums(index, drifts, frozen_part, carried, volatility, patch_index, patch_t, groups)
-    sums = source_sums(index, start, source, patch_index, patch_t, sums)
+    start = after(start, tail)
+    start_y = y_edges(start)
+    start = after(start, *start_y)
+    sums = column_sums(index, drifts, weight, source, start, patch_index, patch_t, sums)
+    count, joint = n * wide, ("wide", "narrow")
     sums = (sums[:, :128] + sums[:, 128:]).reshape(count, PATCHES // count)
     shares = lax.all_to_all(sums, joint, split_axis=0, concat_axis=0, tiled=True)
     vega = jnp.sum(shares, axis=0)
 
-    start_y = y_edges(start)
     adjoint = finish(index, start, *start_y, volatility, *vol_x, *vol_y, tail)
     return (adjoint, vega * vega_scale)
 

time: 904 us -> 786 us (0.87)
  starting transfers between devices: 249 us -> 154 us
  local copies, waits for them, and re-layouts: 111 us -> 43.4 us
  Pallas kernels: 140 us -> 176 us
  blocking collectives: 0 us -> 19.6 us
    ppermute x20 -> x18, starting transfers between devices: 126 us -> 71 us  [send(): lax.ppermute(piece, 'narrow', [(k, (k + d) % n) for k in range(n)])]
    unnamed x116 -> x68, local copies, waits for them, and re-layouts: 53.6 us -> 5.56 us
    ppermute x5, waiting for transfers between devices: 7.16 us -> 40.3 us  [neighbours(): lax.ppermute(low_edge, axis, down)]
    ppermute x5, starting transfers between devices: 47.9 us -> 15.1 us  [neighbours(): lax.ppermute(high_edge, axis, up)]
    ppermute x5, waiting for transfers between devices: 24.4 us -> 2.07 us  [neighbours(): lax.ppermute(high_edge, axis, up)]
    all_to_all x0 -> x1, blocking collectives: none -> 19.6 us  [across(): lax.all_to_all(piece, 'wide', split_axis=0, concat_axis=0, tiled=True)]
    all_to_all x12 -> x11, waiting for transfers between devices: 96.5 us -> 81.9 us  [across(): lax.all_to_all(piece, 'wide', split_axis=0, concat_axis=0, tiled=True)]
    all_to_all x1, starting transfers between devices: 16.8 us -> 4.58 us  [on_device_kernels(): lax.all_to_all(sums, joint, split_axis=0, concat_axis=0, tiled=True)]
  transfers between devices with their start and end apart: 43 -> 40, of which waited for: 21 -> 24; matrix products, arithmetic and copies ran while one was open for 8% -> 5% of each run, Pallas kernels for 12% -> 21%
where the time goes in v2:
time: 786 us; the launch traced here: 781 us
  waiting for transfers between devices  373 us (47%)
  Pallas kernels  176 us (22%)
  starting transfers between devices  154 us (20%)
  local copies, waits for them, and re-layouts  43.4 us (6%)
  blocking collectives  19.6 us (2%)
  other arithmetic  8.68 us (1%)
    ppermute x18, waiting for transfers between devices, send(): lax.ppermute(piece, 'narrow', [(k, (k + d) % n) for k in range(n)])  249 us
    all_to_all x11, waiting for transfers between devices, across(): lax.all_to_all(piece, 'wide', split_axis=0, concat_axis=0, tiled=True)  81.9 us
    ppermute x18, starting transfers between devices, send(): lax.ppermute(piece, 'narrow', [(k, (k + d) % n) for k in range(n)])  71 us
    all_to_all x11, starting transfers between devices, across(): lax.all_to_all(piece, 'wide', split_axis=0, concat_axis=0, tiled=True)  57 us
    ppermute x5, waiting for transfers between devices, neighbours(): lax.ppermute(low_edge, axis, down)  40.3 us
    pallas_call x3, Pallas kernels, second(): pl.pallas_call(functools.partial(second_kernel, count=count, chunked=bool...  37.7 us
    pallas_call x3, Pallas kernels, first(): pl.pallas_call(functools.partial(first_kernel, count=len(flat), lines=lin...  32.6 us
    pallas_call x1, Pallas kernels, frozen(): pl.pallas_call(functools.partial(frozen_kernel, blocks=blocks, groups=gro...  25.8 us
  transfers between devices with their start and end apart: 40, of which 24 were waited for; matrix products, arithmetic and copies ran while one was open for 5% of the time, Pallas kernels for 21%

profile of v2, /device:TPU:0, one launch (start us, length us, event | category | flops | bytes accessed | tf_op | source)
XLA Modules:
  0.0 780.7 jit_solution(7337498504144748668)
XLA Ops:
  30.0 29.7 %collective-permute-done.8 = f32[2,66,128]{2,1,0:T(8,128)S(1)} collective-permute-done((f32[2,66,128]{2,1,0:T(8,128)S(1)}, f32[2,66,128]{2,1,0:T(8,128)S(1)}, u32[]{:S(2)}, u32[]{:S(2)}) %collective-permute-start.8) | collective-permute-done | bytes 67616 | tf_op jit(solution)/shard_map/ppermute | solution.py:777
  61.9 11.6 %forward.1 = (f32[8,64,16,128]{3,2,1,0:T(8,128)}, f32[64,128,128]{2,1,0:T(8,128)}) custom-call(s32[1]{0:T(128)} %bitcast.i, f32[64,128,128]{2,1,0:T(8,128)} %after.4, f32[64,128,128]{2,1,0:T(8,128)} %after.4, f32[64,128,128]{2,1,0:T(8,128)} %after.4, f32[1,128,128]{2,1,0:T(8,128)} %bitcast.132, f32[1,128,128]{2,1,0:T(8,128)} %bitcast.129, ...), custom_call_target="tpu_custom_call" | custom-call | flops 100000000 | bytes 356515 | tf_op jit(solution)/shard_map/forward/pallas_call | solution.py:306
  85.3 43.1 %collective-permute-done.2.refs_2_ = f32[16,128,128]{2,1,0:T(8,128)} collective-permute-done((f32[16,128,128]{2,1,0:T(8,128)}, f32[16,128,128]{2,1,0:T(8,128)}, u32[]{:S(2)}, u32[]{:S(2)}) %collective-permute-start.2) | collective-permute-done | bytes 1048608 | tf_op jit(solution)/shard_map/ppermute | solution.py:789
  128.4 12.2 %second.3 = (f32[8,16,16,128]{3,2,1,0:T(8,128)}, f32[8,16,16,128]{3,2,1,0:T(8,128)}, f32[8,16,16,128]{3,2,1,0:T(8,128)}, f32[8,16,16,128]{3,2,1,0:T(8,128)}) custom-call(f32[16,128,128]{2,1,0:T(8,128)} %get-tuple-element.149.refs_0_, f32[16,128,128]{2,1,0:T(8,128)} %copy-done.15, f32[16,128,128]{2,1,0:T(8,128)} %collective-permute-done.2.refs_2_, ...), custom_call_target="tpu_custom_call" | custom-call | flops 180000000 | bytes 209715 | tf_op jit(solution)/shard_map/second/pallas_call | solution.py:407
  140.6 16.0 %all-to-all-start = ((f32[8,16,16,128]{3,2,1,0:T(8,128)}), f32[8,16,16,128]{3,2,1,0:T(8,128)S(1)}, u32[]{:S(2)}, u32[]{:S(2)}) async-start(f32[8,16,16,128]{3,2,1,0:T(8,128)} %get-tuple-element.73), calls=%async_computation | async-start | bytes 2097152 | tf_op jit(solution)/shard_map/all_to_all | solution.py:802
  158.1 10.9 %first.3 = f32[8448,128]{1,0:T(8,128)} custom-call(f32[8192,128]{1,0:T(8,128)} %bitcast.24.refs_0_, bf16[512,1536]{1,0:T(8,128)(2,1)} %pad_maximum_fusion.1.refs_1_), custom_call_target="tpu_custom_call" | custom-call | flops 140000000 | bytes 209715 | tf_op jit(solution)/shard_map/first/pallas_call | solution.py:367
  181.6 24.2 %collective-permute-done.3 = f32[8,16,16,128]{3,2,1,0:T(8,128)S(1)} collective-permute-done((f32[8,16,16,128]{3,2,1,0:T(8,128)}, f32[8,16,16,128]{3,2,1,0:T(8,128)S(1)}, u32[]{:S(2)}, u32[]{:S(2)}) %collective-permute-start.3) | collective-permute-done | bytes 1048608 | tf_op jit(solution)/shard_map/ppermute | solution.py:789
  205.8 20.0 %collective-permute-done.4 = f32[8,16,16,128]{3,2,1,0:T(8,128)S(1)} collective-permute-done((f32[8,16,16,128]{3,2,1,0:T(8,128)}, f32[8,16,16,128]{3,2,1,0:T(8,128)S(1)}, u32[]{:S(2)}, u32[]{:S(2)}) %collective-permute-start.4) | collective-permute-done | bytes 1048608 | tf_op jit(solution)/shard_map/ppermute | solution.py:789
  232.1 15.0 %all-to-all-done.3 = f32[8,16,16,128]{3,2,1,0:T(8,128)S(1)} async-done(((f32[8,16,16,128]{3,2,1,0:T(8,128)}), f32[8,16,16,128]{3,2,1,0:T(8,128)S(1)}, u32[]{:S(2)}, u32[]{:S(2)}) %all-to-all-start.3) | async-done | bytes 1048608 | tf_op jit(solution)/shard_map/all_to_all | solution.py:802
  250.7 9.0 %lifted.1 = (f32[18,128,128]{2,1,0:T(8,128)}, f32[18,128,128]{2,1,0:T(8,128)}, f32[18,128,128]{2,1,0:T(8,128)}, f32[18,128,128]{2,1,0:T(8,128)}) custom-call(s32[1]{0:T(128)} %bitcast.i, f32[8,66,16,128]{3,2,1,0:T(8,128)} %all-to-all-done.2.solved, f32[64,128,128]{2,1,0:T(8,128)} %after.4, f32[1,128,128]{2,1,0:T(8,128)} %bitcast.133, ...), custom_call_target="tpu_custom_call" | custom-call | flops 40000000 | bytes 272629 | tf_op jit(solution)/shard_map/lifted/pallas_call | solution.py:465
  259.7 20.2 %collective-permute-done.9 = f32[8,16,16,128]{3,2,1,0:T(8,128)} collective-permute-done((f32[8,16,16,128]{3,2,1,0:T(8,128)}, f32[8,16,16,128]{3,2,1,0:T(8,128)}, u32[]{:S(2)}, u32[]{:S(2)}) %collective-permute-start.9) | collective-permute-done | bytes 1048608 | tf_op jit(solution)/shard_map/ppermute | solution.py:789
  288.6 13.0 %all-to-all-done.5 = f32[8,16,16,128]{3,2,1,0:T(8,128)S(1)} async-done(((f32[8,16,16,128]{3,2,1,0:T(8,128)}), f32[8,16,16,128]{3,2,1,0:T(8,128)S(1)}, u32[]{:S(2)}, u32[]{:S(2)}) %all-to-all-start.5) | async-done | bytes 1048608 | tf_op jit(solution)/shard_map/all_to_all | solution.py:802
  302.5 10.9 %first.4 = f32[8448,128]{1,0:T(8,128)} custom-call(f32[2048,128]{1,0:T(8,128)} %bitcast.117, f32[2048,128]{1,0:T(8,128)} %bitcast.118, f32[2048,128]{1,0:T(8,128)} %bitcast.122, f32[2048,128]{1,0:T(8,128)} %bitcast.120, bf16[512,1536]{1,0:T(8,128)(2,1)} %pad_maximum_fusion.2.refs_4_), custom_call_target="tpu_custom_call" | custom-call | flops 140000000 | bytes 209715 | tf_op jit(solution)/shard_map/first/pallas_call | solution.py:367
  318.3 53.6 %collective-permute-done.11.refs_2_ = f32[18,128,128]{2,1,0:T(8,128)} collective-permute-done((f32[18,128,128]{2,1,0:T(8,128)S(1)}, f32[18,128,128]{2,1,0:T(8,128)}, u32[]{:S(2)}, u32[]{:S(2)}) %collective-permute-start.11) | collective-permute-done | bytes 1179680 | tf_op jit(solution)/shard_map/ppermute | solution.py:789
  380.9 12.5 %reaction.1 = (f32[16,128,128]{2,1,0:T(8,128)}, f32[16,128,128]{2,1,0:T(8,128)}, f32[16,128,128]{2,1,0:T(8,128)}, f32[16,128,128]{2,1,0:T(8,128)}) custom-call(s32[1]{0:T(128)} %bitcast.i, f32[8,66,16,128]{3,2,1,0:T(8,128)} %all-to-all-done.6.carried, f32[66,128]{1,0:T(8,128)} %copy-done.24, f32[66,128]{1,0:T(8,128)} %copy-done.25, f32[64,128,128]{2,1,0:T(8,128)} %after.5, ...), custom_call_target="tpu_custom_call" | custom-call | flops 80000000 | bytes 356515 | tf_op jit(solution)/shard_map/reaction/pallas_call | solution.py:512
  411.4 13.3 %second.4.field = f32[18,512,128]{2,1,0:T(8,128)} custom-call(f32[18,128,128]{2,1,0:T(8,128)} %get-tuple-element.101.refs_0_, f32[18,128,128]{2,1,0:T(8,128)} %collective-permute-done.17.refs_1_, f32[18,128,128]{2,1,0:T(8,128)} %collective-permute-done.11.refs_2_, f32[18,128,128]{2,1,0:T(8,128)} %collective-permute-done.10.refs_3_, ...), custom_call_target="tpu_custom_call" | custom-call | flops 180000000 | bytes 209715 | tf_op jit(solution)/shard_map/second/pallas_call | solution.py:407
  424.7 10.1 %mixed.1 = (f32[16,128,128]{2,1,0:T(8,128)}, f32[16,128,128]{2,1,0:T(8,128)}, f32[16,128,128]{2,1,0:T(8,128)}, f32[16,128,128]{2,1,0:T(8,128)}) custom-call(s32[1]{0:T(128)} %bitcast.i, f32[18,512,128]{2,1,0:T(8,128)} %second.4.field), custom_call_target="tpu_custom_call" | custom-call | flops 80000000 | bytes 188743 | tf_op jit(solution)/shard_map/mixed/pallas_call | solution.py:591
  434.9 25.8 %frozen.1 = (f32[64,128,128]{2,1,0:T(8,128)}, f32[24,256]{1,0:T(8,128)}) custom-call(s32[1]{0:T(128)} %bitcast.i, f32[64,128,128]{2,1,0:T(8,128)} %after.4, f32[64,128,128]{2,1,0:T(8,128)} %after.4, f32[64,128,128]{2,1,0:T(8,128)} %after.4, f32[1,128,128]{2,1,0:T(8,128)} %bitcast.134, f32[1,128,128]{2,1,0:T(8,128)} %bitcast.131, f32[66,128]{1,0:T(8,128)} %fusion.1.q_low, ...), custom_call_target="tpu_custom_call" | custom-call | flops 100000000 | bytes 356515 | tf_op jit(solution)/shard_map/frozen/pallas_call | solution.py:662
  460.7 15.9 %collective-permute-done.15.refs_2_ = f32[16,128,128]{2,1,0:T(8,128)} collective-permute-done((f32[16,128,128]{2,1,0:T(8,128)}, f32[16,128,128]{2,1,0:T(8,128)}, u32[]{:S(2)}, u32[]{:S(2)}) %collective-permute-start.15) | collective-permute-done | bytes 1048608 | tf_op jit(solution)/shard_map/ppermute | solution.py:789
  476.6 45.4 %collective-permute-start.18 = (f32[16,128,128]{2,1,0:T(8,128)S(1)}, f32[16,128,128]{2,1,0:T(8,128)S(1)}, u32[]{:S(2)}, u32[]{:S(2)}) collective-permute-start(f32[16,128,128]{2,1,0:T(8,128)S(1)} %copy-done.30), channel_id=1, source_target_pairs={{0,1},{1,2},{2,3},{3,0},{4,5},{5,6},{6,7},{7,4},{8,9},{9,10},{10,1... | collective-permute-start | bytes 3145736 | tf_op jit(solution)/shard_map/ppermute | solution.py:789
  522.0 12.2 %second.5 = (f32[8,16,16,128]{3,2,1,0:T(8,128)}, f32[8,16,16,128]{3,2,1,0:T(8,128)}, f32[8,16,16,128]{3,2,1,0:T(8,128)}, f32[8,16,16,128]{3,2,1,0:T(8,128)}) custom-call(f32[16,128,128]{2,1,0:T(8,128)} %get-tuple-element.111.refs_0_, f32[16,128,128]{2,1,0:T(8,128)} %collective-permute-done.14.refs_1_, f32[16,128,128]{2,1,0:T(8,128)} %collective-permute-done.15.refs_2_, ...), custom_call_target="tpu_custom_call" | custom-call | flops 180000000 | bytes 209715 | tf_op jit(solution)/shard_map/second/pallas_call | solution.py:407
  534.2 10.4 %collective-permute-done.18.refs_3_ = f32[16,128,128]{2,1,0:T(8,128)S(1)} collective-permute-done((f32[16,128,128]{2,1,0:T(8,128)S(1)}, f32[16,128,128]{2,1,0:T(8,128)S(1)}, u32[]{:S(2)}, u32[]{:S(2)}) %collective-permute-start.18) | collective-permute-done | bytes 1048608 | tf_op jit(solution)/shard_map/ppermute | solution.py:789
  549.2 19.6 %all_to_all.69 = f32[8,16,16,128]{3,2,1,0:T(8,128)} all-to-all(f32[8,16,16,128]{3,2,1,0:T(8,128)} %get-tuple-element.122.refs_4_), channel_id=1, replica_groups=mesh['wide'=8,'narrow'=4] {'wide'}, dimensions={0} | all-to-all | bytes 2097152 | tf_op jit(solution)/shard_map/all_to_all | solution.py:802
  572.1 23.4 %collective-permute-done.19.refs_7_ = f32[8,16,16,128]{3,2,1,0:T(8,128)} collective-permute-done((f32[8,16,16,128]{3,2,1,0:T(8,128)}, f32[8,16,16,128]{3,2,1,0:T(8,128)}, u32[]{:S(2)}, u32[]{:S(2)}) %collective-permute-start.19) | collective-permute-done | bytes 1048608 | tf_op jit(solution)/shard_map/ppermute | solution.py:789
  600.1 14.6 %all-to-all-done.8 = f32[8,16,16,128]{3,2,1,0:T(8,128)S(1)} async-done(((f32[8,16,16,128]{3,2,1,0:T(8,128)}), f32[8,16,16,128]{3,2,1,0:T(8,128)S(1)}, u32[]{:S(2)}, u32[]{:S(2)}) %all-to-all-start.8) | async-done | bytes 1048608 | tf_op jit(solution)/shard_map/all_to_all | solution.py:802
  618.3 29.5 %collective-permute-done.21 = f32[8,16,16,128]{3,1,2,0:T(8,128)} collective-permute-done((f32[8,16,16,128]{3,1,2,0:T(8,128)S(1)}, f32[8,16,16,128]{3,1,2,0:T(8,128)}, u32[]{:S(2)}, u32[]{:S(2)}) %collective-permute-start.21) | collective-permute-done | bytes 1048608 | tf_op jit(solution)/shard_map/ppermute | solution.py:789
  655.2 14.1 %all-to-all-done.10 = f32[8,16,16,128]{3,1,2,0:T(8,128)S(1)} async-done(((f32[8,16,16,128]{3,1,2,0:T(8,128)}), f32[8,16,16,128]{3,1,2,0:T(8,128)S(1)}, u32[]{:S(2)}, u32[]{:S(2)}) %all-to-all-start.10) | async-done | bytes 1048608 | tf_op jit(solution)/shard_map/all_to_all | solution.py:802
  670.7 10.8 %first.5 = f32[8448,128]{1,0:T(8,128)} custom-call(f32[2048,128]{1,0:T(8,128)} %bitcast.119, f32[2048,128]{1,0:T(8,128)} %bitcast.121, f32[2048,128]{1,0:T(8,128)} %bitcast.124, f32[2048,128]{1,0:T(8,128)} %bitcast.123, bf16[512,1536]{1,0:T(8,128)(2,1)} %pad_maximum_fusion.2.refs_4_), custom_call_target="tpu_custom_call" | custom-call | flops 140000000 | bytes 209715 | tf_op jit(solution)/shard_map/first/pallas_call | solution.py:367
  705.8 11.1 %lines.1.tail = f32[64,128,128]{2,1,0:T(8,128)} custom-call(s32[1]{0:T(128)} %bitcast.i, f32[16,128,128]{2,1,0:T(8,128)} %get-tuple-element.111.refs_0_, f32[16,128,128]{2,1,0:T(8,128)} %get-tuple-element.97.refs_1_, f32[16,128,128]{2,1,0:T(8,128)} %get-tuple-element.98.refs_2_, f32[16,128,128]{2,1,0:T(8,128)} %get-tuple-element.99.refs_3_, ...), custom_call_target="tpu_custom_call" | custom-call | flops 100000000 | bytes 356515 | tf_op jit(solution)/shard_map/lines/pallas_call | solution.py:556
  716.9 19.8 %all-to-all-done.11.start.refs_6_ = f32[8,66,16,128]{3,2,1,0:T(8,128)} async-done(((f32[8,66,16,128]{3,2,1,0:T(8,128)}), f32[8,66,16,128]{3,2,1,0:T(8,128)}, u32[]{:S(2)}, u32[]{:S(2)}) %all-to-all-start.11) | async-done | bytes 4325408 | tf_op jit(solution)/shard_map/all_to_all | solution.py:802
  748.4 13.0 %column.1 = f32[24,256]{1,0:T(8,128)} custom-call(s32[1]{0:T(128)} %bitcast.i, f32[16,128,128]{2,1,0:T(8,128)} %get-tuple-element.105.refs_0_, f32[16,128,128]{2,1,0:T(8,128)} %collective-permute-done.22.refs_1_, f32[16,128,128]{2,1,0:T(8,128)} %copy-done.18, f32[16,128,128]{2,1,0:T(8,128)} %copy-done.17, f32[64,128,128]{2,1,0:T(8,128)} %get-tuple-element.136.refs_4_, ...), custom_call_target="tpu_custom_call" | custom-call | flops 80000000 | bytes 356515 | tf_op jit(solution)/shard_map/column/pallas_call | solution.py:708
  767.5 12.3 %adjoint.1 = f32[64,128,128]{2,1,0:T(8,128)} custom-call(s32[1]{0:T(128)} %bitcast.i, f32[8,66,16,128]{3,2,1,0:T(8,128)} %all-to-all-done.11.start.refs_6_, f32[66,128]{1,0:T(8,128)} %copy-done.22, f32[66,128]{1,0:T(8,128)} %copy-done.23, f32[64,128,128]{2,1,0:T(8,128)} %after.5, f32[64,128,128]{2,1,0:T(8,128)} %after.5, f32[64,128,128]{2,1,0:T(8,128)} %after.5, ...), custom_call_target="tpu_custom_call" | custom-call | flops 100000000 | bytes 356515 | tf_op jit(solution)/shard_map/adjoint/pallas_call | solution.py:755
  (198 shorter events, 173.1 us)
Async XLA Ops:
  7.9 53.0 %collective-permute-start = (f32[16,128,128]{2,1,0:T(8,128)S(1)}, f32[16,128,128]{2,1,0:T(8,128)S(1)}, u32[]{:S(2)}, u32[]{:S(2)}) collective-permute-start(f32[16,128,128]{2,1,0:T(8,128)S(1)} %get-tuple-element.148), channel_id=1, source_target_pairs={{0,1},{1,2},{2,3},{3,0},{4,5},{5,6},{6,7},{7,4},{8,9},{9,10},{10,1... | collective-permute-start | bytes 3145736 | tf_op jit(solution)/shard_map/ppermute | solution.py:789
  10.9 62.6 %collective-permute-start.1 = (f32[16,128,128]{2,1,0:T(8,128)S(1)}, f32[16,128,128]{2,1,0:T(8,128)S(1)}, u32[]{:S(2)}, u32[]{:S(2)}) collective-permute-start(f32[16,128,128]{2,1,0:T(8,128)S(1)} %get-tuple-element.146), channel_id=1, source_target_pairs={{0,3},{1,0},{2,1},{3,2},{4,7},{5,4},{6,5},{7,6},{8,11},{9,8},{10,9... | collective-permute-start | bytes 3145736 | tf_op jit(solution)/shard_map/ppermute | solution.py:789
  22.6 37.0 %collective-permute-start.8 = (f32[2,66,128]{2,1,0:T(8,128)S(1)}, f32[2,66,128]{2,1,0:T(8,128)S(1)}, u32[]{:S(2)}, u32[]{:S(2)}) collective-permute-start(f32[2,66,128]{2,1,0:T(8,128)S(1)} %get-tuple-element.164), channel_id=1, source_target_pairs={{1,0},{2,1},{3,2},{5,4},{6,5},{7,6},{9,8},{10,9},{11,10},{13,12},{... | collective-permute-start | bytes 202760 | tf_op jit(solution)/shard_map/ppermute | solution.py:777
  23.9 36.4 %collective-permute-start.7 = (f32[2,66,128]{2,1,0:T(8,128)S(1)}, f32[2,66,128]{2,1,0:T(8,128)S(1)}, u32[]{:S(2)}, u32[]{:S(2)}) collective-permute-start(f32[2,66,128]{2,1,0:T(8,128)S(1)} %get-tuple-element.165), channel_id=1, source_target_pairs={{0,1},{1,2},{2,3},{4,5},{5,6},{6,7},{8,9},{9,10},{10,11},{12,13},{... | collective-permute-start | bytes 202760 | tf_op jit(solution)/shard_map/ppermute | solution.py:777
  74.5 66.1 %all-to-all-start.1 = ((f32[8,64,16,128]{3,2,1,0:T(8,128)}), f32[8,64,16,128]{3,2,1,0:T(8,128)}, u32[]{:S(2)}, u32[]{:S(2)}) async-start(f32[8,64,16,128]{3,2,1,0:T(8,128)} %get-tuple-element.81), calls=%async_computation.1 | async-start | bytes 8388608 | tf_op jit(solution)/shard_map/all_to_all | solution.py:802
  79.2 49.2 %collective-permute-start.2 = (f32[16,128,128]{2,1,0:T(8,128)}, f32[16,128,128]{2,1,0:T(8,128)}, u32[]{:S(2)}, u32[]{:S(2)}) collective-permute-start(f32[16,128,128]{2,1,0:T(8,128)} %get-tuple-element.70), channel_id=1, source_target_pairs={{0,2},{1,3},{2,0},{3,1},{4,6},{5,7},{6,4},{7,5},{8,10},{9,11},{10,... | collective-permute-start | bytes 3145736 | tf_op jit(solution)/shard_map/ppermute | solution.py:789
  140.6 31.4 %all-to-all-start = ((f32[8,16,16,128]{3,2,1,0:T(8,128)}), f32[8,16,16,128]{3,2,1,0:T(8,128)S(1)}, u32[]{:S(2)}, u32[]{:S(2)}) async-start(f32[8,16,16,128]{3,2,1,0:T(8,128)} %get-tuple-element.73), calls=%async_computation | async-start | bytes 2097152 | tf_op jit(solution)/shard_map/all_to_all | solution.py:802
  173.1 55.1 %all-to-all-start.2 = ((f32[8,66,16,128]{3,2,1,0:T(8,128)}), f32[8,66,16,128]{3,2,1,0:T(8,128)}, u32[]{:S(2)}, u32[]{:S(2)}) async-start(f32[8,66,16,128]{3,2,1,0:T(8,128)} %bitcast.115), calls=%async_computation.2 | async-start | bytes 8650752 | tf_op jit(solution)/shard_map/all_to_all | solution.py:802
  177.7 28.1 %collective-permute-start.3 = (f32[8,16,16,128]{3,2,1,0:T(8,128)}, f32[8,16,16,128]{3,2,1,0:T(8,128)S(1)}, u32[]{:S(2)}, u32[]{:S(2)}) collective-permute-start(f32[8,16,16,128]{3,2,1,0:T(8,128)} %get-tuple-element.71), channel_id=1, source_target_pairs={{0,1},{1,2},{2,3},{3,0},{4,5},{5,6},{6,7},{7,4},{8,9},{9,10},{10,1... | collective-permute-start | bytes 3145736 | tf_op jit(solution)/shard_map/ppermute | solution.py:789
  177.8 48.1 %collective-permute-start.4 = (f32[8,16,16,128]{3,2,1,0:T(8,128)}, f32[8,16,16,128]{3,2,1,0:T(8,128)S(1)}, u32[]{:S(2)}, u32[]{:S(2)}) collective-permute-start(f32[8,16,16,128]{3,2,1,0:T(8,128)} %get-tuple-element.72), channel_id=1, source_target_pairs={{0,3},{1,0},{2,1},{3,2},{4,7},{5,4},{6,5},{7,6},{8,11},{9,8},{10,9... | collective-permute-start | bytes 3145736 | tf_op jit(solution)/shard_map/ppermute | solution.py:789
  228.2 18.9 %all-to-all-start.3 = ((f32[8,16,16,128]{3,2,1,0:T(8,128)}), f32[8,16,16,128]{3,2,1,0:T(8,128)S(1)}, u32[]{:S(2)}, u32[]{:S(2)}) async-start(f32[8,16,16,128]{3,2,1,0:T(8,128)} %copy-done.13), calls=%async_computation.3 | async-start | bytes 2097152 | tf_op jit(solution)/shard_map/all_to_all | solution.py:802
  231.8 48.2 %collective-permute-start.9 = (f32[8,16,16,128]{3,2,1,0:T(8,128)}, f32[8,16,16,128]{3,2,1,0:T(8,128)}, u32[]{:S(2)}, u32[]{:S(2)}) collective-permute-start(f32[8,16,16,128]{3,2,1,0:T(8,128)} %get-tuple-element.84), channel_id=1, source_target_pairs={{0,2},{1,3},{2,0},{3,1},{4,6},{5,7},{6,4},{7,5},{8,10},{9,11},{10,... | collective-permute-start | bytes 3145736 | tf_op jit(solution)/shard_map/ppermute | solution.py:789
  247.1 35.1 %all-to-all-start.4 = ((f32[8,16,16,128]{3,2,1,0:T(8,128)}), f32[8,16,16,128]{3,2,1,0:T(8,128)S(1)}, u32[]{:S(2)}, u32[]{:S(2)}) async-start(f32[8,16,16,128]{3,2,1,0:T(8,128)} %copy-done.11), calls=%async_computation.4 | async-start | bytes 2097152 | tf_op jit(solution)/shard_map/all_to_all | solution.py:802
  280.0 33.5 %collective-permute-start.10 = (f32[18,128,128]{2,1,0:T(8,128)}, f32[18,128,128]{2,1,0:T(8,128)}, u32[]{:S(2)}, u32[]{:S(2)}) collective-permute-start(f32[18,128,128]{2,1,0:T(8,128)} %get-tuple-element.92), channel_id=1, source_target_pairs={{0,3},{1,0},{2,1},{3,2},{4,7},{5,4},{6,5},{7,6},{8,11},{9,8},{10,9... | collective-permute-start | bytes 3538952 | tf_op jit(solution)/shard_map/ppermute | solution.py:789
  282.3 19.3 %all-to-all-start.5 = ((f32[8,16,16,128]{3,2,1,0:T(8,128)}), f32[8,16,16,128]{3,2,1,0:T(8,128)S(1)}, u32[]{:S(2)}, u32[]{:S(2)}) async-start(f32[8,16,16,128]{3,2,1,0:T(8,128)} %collective-permute-done.9), calls=%async_computation.5 | async-start | bytes 2097152 | tf_op jit(solution)/shard_map/all_to_all | solution.py:802
  313.5 58.5 %all-to-all-start.6 = ((f32[8,66,16,128]{3,2,1,0:T(8,128)}), f32[8,66,16,128]{3,2,1,0:T(8,128)}, u32[]{:S(2)}, u32[]{:S(2)}) async-start(f32[8,66,16,128]{3,2,1,0:T(8,128)} %bitcast.116), calls=%async_computation.6 | async-start | bytes 8650752 | tf_op jit(solution)/shard_map/all_to_all | solution.py:802
  318.2 53.7 %collective-permute-start.11 = (f32[18,128,128]{2,1,0:T(8,128)S(1)}, f32[18,128,128]{2,1,0:T(8,128)}, u32[]{:S(2)}, u32[]{:S(2)}) collective-permute-start(f32[18,128,128]{2,1,0:T(8,128)S(1)} %copy-done.28), channel_id=1, source_target_pairs={{0,2},{1,3},{2,0},{3,1},{4,6},{5,7},{6,4},{7,5},{8,10},{9,11},{10,... | collective-permute-start | bytes 3538952 | tf_op jit(solution)/shard_map/ppermute | solution.py:789
  380.2 31.2 %collective-permute-start.17 = (f32[18,128,128]{2,1,0:T(8,128)}, f32[18,128,128]{2,1,0:T(8,128)}, u32[]{:S(2)}, u32[]{:S(2)}) collective-permute-start(f32[18,128,128]{2,1,0:T(8,128)} %get-tuple-element.100), channel_id=1, source_target_pairs={{0,1},{1,2},{2,3},{3,0},{4,5},{5,6},{6,7},{7,4},{8,9},{9,10},{10,1... | collective-permute-start | bytes 3538952 | tf_op jit(solution)/shard_map/ppermute | solution.py:789
  393.4 67.3 %collective-permute-start.14 = (f32[16,128,128]{2,1,0:T(8,128)}, f32[16,128,128]{2,1,0:T(8,128)}, u32[]{:S(2)}, u32[]{:S(2)}) collective-permute-start(f32[16,128,128]{2,1,0:T(8,128)} %get-tuple-element.97.refs_1_), channel_id=1, source_target_pairs={{0,1},{1,2},{2,3},{3,0},{4,5},{5,6},{6,7},{7,4},{8,9},{9,10},{10,1... | collective-permute-start | bytes 3145736 | tf_op jit(solution)/shard_map/ppermute | solution.py:789
  395.4 81.2 %collective-permute-start.15 = (f32[16,128,128]{2,1,0:T(8,128)}, f32[16,128,128]{2,1,0:T(8,128)}, u32[]{:S(2)}, u32[]{:S(2)}) collective-permute-start(f32[16,128,128]{2,1,0:T(8,128)} %get-tuple-element.98.refs_2_), channel_id=1, source_target_pairs={{0,2},{1,3},{2,0},{3,1},{4,6},{5,7},{6,4},{7,5},{8,10},{9,11},{10,... | collective-permute-start | bytes 3145736 | tf_op jit(solution)/shard_map/ppermute | solution.py:789
  397.2 79.4 %collective-permute-start.16 = (f32[16,128,128]{2,1,0:T(8,128)}, f32[16,128,128]{2,1,0:T(8,128)}, u32[]{:S(2)}, u32[]{:S(2)}) collective-permute-start(f32[16,128,128]{2,1,0:T(8,128)} %get-tuple-element.99.refs_3_), channel_id=1, source_target_pairs={{0,3},{1,0},{2,1},{3,2},{4,7},{5,4},{6,5},{7,6},{8,11},{9,8},{10,9... | collective-permute-start | bytes 3145736 | tf_op jit(solution)/shard_map/ppermute | solution.py:789
  476.6 68.0 %collective-permute-start.18 = (f32[16,128,128]{2,1,0:T(8,128)S(1)}, f32[16,128,128]{2,1,0:T(8,128)S(1)}, u32[]{:S(2)}, u32[]{:S(2)}) collective-permute-start(f32[16,128,128]{2,1,0:T(8,128)S(1)} %copy-done.30), channel_id=1, source_target_pairs={{0,1},{1,2},{2,3},{3,0},{4,5},{5,6},{6,7},{7,4},{8,9},{9,10},{10,1... | collective-permute-start | bytes 3145736 | tf_op jit(solution)/shard_map/ppermute | solution.py:789
  546.6 25.5 %collective-permute-start.20 = (f32[8,16,16,128]{3,1,2,0:T(8,128)S(1)}, f32[8,16,16,128]{3,1,2,0:T(8,128)}, u32[]{:S(2)}, u32[]{:S(2)}) collective-permute-start(f32[8,16,16,128]{3,1,2,0:T(8,128)S(1)} %copy.125), channel_id=1, source_target_pairs={{0,3},{1,0},{2,1},{3,2},{4,7},{5,4},{6,5},{7,6},{8,11},{9,8},{10,9... | collective-permute-start | bytes 3145736 | tf_op jit(solution)/shard_map/ppermute | solution.py:789
  547.8 47.6 %collective-permute-start.19 = (f32[8,16,16,128]{3,2,1,0:T(8,128)}, f32[8,16,16,128]{3,2,1,0:T(8,128)}, u32[]{:S(2)}, u32[]{:S(2)}) collective-permute-start(f32[8,16,16,128]{3,2,1,0:T(8,128)} %get-tuple-element.120), channel_id=1, source_target_pairs={{0,1},{1,2},{2,3},{3,0},{4,5},{5,6},{6,7},{7,4},{8,9},{9,10},{10,1... | collective-permute-start | bytes 3145736 | tf_op jit(solution)/shard_map/ppermute | solution.py:789
  595.4 19.3 %all-to-all-start.8 = ((f32[8,16,16,128]{3,2,1,0:T(8,128)}), f32[8,16,16,128]{3,2,1,0:T(8,128)S(1)}, u32[]{:S(2)}, u32[]{:S(2)}) async-start(f32[8,16,16,128]{3,2,1,0:T(8,128)} %collective-permute-done.19.refs_7_), calls=%async_computation.8 | async-start | bytes 2097152 | tf_op jit(solution)/shard_map/all_to_all | solution.py:802
  599.6 48.1 %collective-permute-start.21 = (f32[8,16,16,128]{3,1,2,0:T(8,128)S(1)}, f32[8,16,16,128]{3,1,2,0:T(8,128)}, u32[]{:S(2)}, u32[]{:S(2)}) collective-permute-start(f32[8,16,16,128]{3,1,2,0:T(8,128)S(1)} %copy.126), channel_id=1, source_target_pairs={{0,2},{1,3},{2,0},{3,1},{4,6},{5,7},{6,4},{7,5},{8,10},{9,11},{10,... | collective-permute-start | bytes 3145736 | tf_op jit(solution)/shard_map/ppermute | solution.py:789
  614.7 35.4 %all-to-all-start.9 = ((f32[8,16,16,128]{3,1,2,0:T(8,128)}), f32[8,16,16,128]{3,1,2,0:T(8,128)S(1)}, u32[]{:S(2)}, u32[]{:S(2)}) async-start(f32[8,16,16,128]{3,1,2,0:T(8,128)} %collective-permute-done.20), calls=%async_computation.9 | async-start | bytes 2097152 | tf_op jit(solution)/shard_map/all_to_all | solution.py:802
  647.7 33.8 %collective-permute-start.22 = (f32[16,128,128]{2,1,0:T(8,128)}, f32[16,128,128]{2,1,0:T(8,128)}, u32[]{:S(2)}, u32[]{:S(2)}) collective-permute-start(f32[16,128,128]{2,1,0:T(8,128)} %get-tuple-element.131), channel_id=1, source_target_pairs={{0,3},{1,0},{2,1},{3,2},{4,7},{5,4},{6,5},{7,6},{8,11},{9,8},{10,9... | collective-permute-start | bytes 3145736 | tf_op jit(solution)/shard_map/ppermute | solution.py:789
  650.1 19.3 %all-to-all-start.10 = ((f32[8,16,16,128]{3,1,2,0:T(8,128)}), f32[8,16,16,128]{3,1,2,0:T(8,128)S(1)}, u32[]{:S(2)}, u32[]{:S(2)}) async-start(f32[8,16,16,128]{3,1,2,0:T(8,128)} %collective-permute-done.21), calls=%async_computation.10 | async-start | bytes 2097152 | tf_op jit(solution)/shard_map/all_to_all | solution.py:802
  681.5 55.2 %all-to-all-start.11 = ((f32[8,66,16,128]{3,2,1,0:T(8,128)}), f32[8,66,16,128]{3,2,1,0:T(8,128)}, u32[]{:S(2)}, u32[]{:S(2)}) async-start(f32[8,66,16,128]{3,2,1,0:T(8,128)} %bitcast.114), calls=%async_computation.11 | async-start | bytes 8650752 | tf_op jit(solution)/shard_map/all_to_all | solution.py:802
  699.0 48.4 %collective-permute-start.27 = (f32[16,128,128]{2,1,0:T(8,128)S(1)}, f32[16,128,128]{2,1,0:T(8,128)S(1)}, u32[]{:S(2)}, u32[]{:S(2)}) collective-permute-start(f32[16,128,128]{2,1,0:T(8,128)S(1)} %copy-done.29), channel_id=1, source_target_pairs={{0,2},{1,3},{2,0},{3,1},{4,6},{5,7},{6,4},{7,5},{8,10},{9,11},{10,... | collective-permute-start | bytes 3145736 | tf_op jit(solution)/shard_map/ppermute | solution.py:789
  762.9 16.9 %all-to-all-start.12 = ((f32[32,1,96]{2,1,0:T(1,128)}), f32[32,1,96]{2,1,0:T(1,128)S(1)}, u32[]{:S(2)}, u32[]{:S(2)}) async-start(f32[32,1,96]{2,1,0:T(1,128)} %bitcast.64), calls=%async_computation.12 | async-start | bytes 32768 | tf_op jit(solution)/shard_map/all_to_all | solution.py:937
  (39 other events, 460.8 us)

commit v3 on v2

--- a/solution.py
+++ b/solution.py
@@ -3,6 +3,7 @@
 import jax.numpy as jnp
 from jax import lax
 from jax.experimental import pallas as pl
+from jax.experimental.layout import Layout, with_layout_constraint
 from jax.experimental.pallas import tpu as pltpu
 from jax.sharding import PartitionSpec as P
 
@@ -206,9 +207,10 @@
 
 def y_pair(v, low_row, high_row):
     n = v.shape[0]
-    row = lax.broadcasted_iota(jnp.int32, v.shape, 0)
-    up = jnp.where(row == n - 1, high_row, pltpu.roll(v, n - 1, 0))
-    down = jnp.where(row == 0, low_row, pltpu.roll(v, 1, 0))
+    row = lax.broadcasted_iota(jnp.int32, (8, v.shape[1]), 0)
+    up, down = pltpu.roll(v, n - 1, 0), pltpu.roll(v, 1, 0)
+    up = jnp.concatenate([up[: n - 8], jnp.where(row == 7, high_row, up[n - 8 :])], axis=0)
+    down = jnp.concatenate([jnp.where(row == 0, low_row, down[:8]), down[8:]], axis=0)
     return up, down
 
 
@@ -328,14 +330,15 @@
 
 def first_kernel(*refs, count, lines, parts, length, halo):
     pieces, matrix3, out = refs[:count], refs[count], refs[count + 1]
-    depth = pieces[0].shape[0] // lines
     rows = length + 2 * halo
 
     def pair(step, carry):
         y = step * 2
         field = jnp.concatenate(
             [
-                jnp.concatenate([piece[pl.ds(y + t, depth, stride=lines), :] for piece in pieces], axis=0)
+                jnp.concatenate(
+                    [piece[pl.ds(y + t, piece.shape[0] // lines, stride=lines), :] for piece in pieces], axis=0
+                )
                 for t in range(2)
             ],
             axis=1,
@@ -609,24 +612,18 @@
     def _():
         out[...] = jnp.zeros_like(out)
 
-    acc = None
-    ones = jnp.ones((planes[0].shape[1], 128), BF16)
-    for k, value in enumerate(planes):
-        value_high, value_low = split(value)
-        column = jnp.dot(value_high, ones, preferred_element_type=F32) + jnp.dot(
-            value_low, ones, preferred_element_type=F32
-        )
-        number = patch[pl.ds(k, 1), :]
-        coarse = lax.broadcasted_iota(jnp.int32, (groups, number.shape[1]), 0) == lax.shift_right_logical(number, 7)
-        number_t = patch_t[k]
-        lane = lax.broadcasted_iota(jnp.int32, (number_t.shape[0], 128), 1)
-        fine = jnp.where(lane == lax.bitwise_and(number_t, 127), column, 0.0)
-        high, low = split(fine)
-        term = jnp.dot(
-            jnp.where(coarse, 1.0, 0.0).astype(BF16), jnp.concatenate([high, low], axis=1), preferred_element_type=F32
-        )
-        acc = term if acc is None else acc + term
-    out[...] += acc
+    count, (by, bz) = len(planes), planes[0].shape
+    value_high, value_low = split(jnp.concatenate(planes, axis=0))
+    ones = jnp.ones((2 * bz, 128), BF16)
+    column = jnp.dot(jnp.concatenate([value_high, value_low], axis=1), ones, preferred_element_type=F32)
+    number = jnp.concatenate([patch[pl.ds(k, 1), :] for k in range(count)], axis=1)
+    coarse = lax.broadcasted_iota(jnp.int32, (groups, count * by), 0) == lax.shift_right_logical(number, 7)
+    number_t = patch_t[...].reshape(count * by, 1)
+    lane = lax.broadcasted_iota(jnp.int32, (count * by, 128), 1)
+    high, low = split(jnp.where(lane == lax.bitwise_and(number_t, 127), column, 0.0))
+    out[...] += jnp.dot(
+        jnp.where(coarse, 1.0, 0.0).astype(BF16), jnp.concatenate([high, low], axis=1), preferred_element_type=F32
+    )
 
 
 def frozen_kernel(
@@ -802,27 +799,20 @@
     return lax.all_to_all(piece, "wide", split_axis=0, concat_axis=0, tiled=True)
 
 
+def row_major(value):
+    return with_layout_constraint(value, Layout(major_to_minor=tuple(range(value.ndim))))
+
+
 def cross_both(pieces, before, between, near, far):
-    lines = list(pieces)
-    met = send(pieces, near)
-    for d in near:
-        lines[d] = met[d]
-    chunks = [across(pieces[0])] + [None] * (len(pieces) - 1)
-    met, chunks[0], waiting = lax.optimization_barrier((pick(lines, near), chunks[0], pick(pieces, far)))
-    for d, value in zip(near, met):
-        lines[d] = value
-    rest = list(pieces)
-    for d, value in zip(far, waiting):
-        rest[d] = value
-    arrived = send(rest, far)
-    last = chunks[0]
-    for d in near:
-        chunks[d] = last = across(after(lines[d], last, *before))
-    gone = pick(arrived, far)
+    pieces = [row_major(piece) for piece in pieces]
+    lines = send(pieces, near)
+    lines = send(lines, far, *pick(lines, near))
+    lines = [row_major(line) for line in lines]
+    block = jnp.concatenate(pick(lines, [0] + near), axis=1)
+    chunks = [across(after(block, *before) if before else block)]
     for d in far:
-        lines[d] = arrived[d]
-        chunks[d] = across(after(arrived[d], last, *between))
-    return lines, chunks, gone
+        chunks.append(across(after(lines[d], chunks[-1], *between)))
+    return lines, chunks, pick(lines, far)
 
 
 def y_edges(chunks):
@@ -845,19 +835,17 @@
 
     cot_pieces = [lax.dynamic_slice_in_dim(cotangent, ahead[d] * xs, xs, 0) for d in range(n)]
     early, late = near[:1], near[1:]
-    cot_lines = send(cot_pieces, near)
-    edge_state, edge_volatility = after((state, volatility), cot_pieces)
-
     both_low, both_high = neighbours(
-        jnp.stack([edge_state[0], edge_volatility[0]]), jnp.stack([edge_state[-1], edge_volatility[-1]]), "wide"
+        jnp.stack([state[0], volatility[0]]), jnp.stack([state[-1], volatility[-1]]), "wide"
     )
-    both = jnp.stack([edge_state[:, :: by - 1], edge_volatility[:, :: by - 1]])
+    both = jnp.stack([state[:, :: by - 1], volatility[:, :: by - 1]])
     both = jnp.concatenate([both_low[:, None, :: by - 1], both, both_high[:, None, :: by - 1]], axis=1)
     y_low, y_high = neighbours(both[:, :, 0], both[:, :, 1], "narrow")
     state_x = (both_low[0:1], both_high[0:1])
     vol_x = (both_low[1:2], both_high[1:2])
     state_y = (y_low[0], y_high[0])
     vol_y = (y_low[1], y_high[1])
+    cot_lines = send(cot_pieces, near, y_low, y_high)
 
     second_t = solve_second.T.reshape(n, by, n, by)
     second_t3 = left_form(second_t[ahead][:, :, back].reshape(n * by, n * by))
@@ -867,14 +855,17 @@
     third_n3 = right_form(solve_third.T)
     first_n3 = left_form(solve_first)
     first_t = solve_first.T.reshape(wide * bx, wide, n, xs)
-    first_t3 = left_form(first_t[:, :, back].transpose(0, 2, 1, 3).reshape(wide * bx, wide * bx))
-
-    state = after(state, *pick(cot_lines, early))
+    first_t = first_t[:, :, back]
+    groups_of = [[0] + near] + [[d] for d in far]
+    first_t3 = left_form(
+        jnp.concatenate([first_t[:, :, jnp.array(g)].reshape(wide * bx, -1) for g in groups_of], axis=1)
+    )
+
     a, source = forward(index, state, volatility, *state_x, *state_y, wide)
-    a = after(a, *pick(cot_lines, late))
+    a = after(a, *pick(cot_lines, early))
     cot_lines = send(cot_lines, far, *pick(cot_lines, near))
-    back = second(cot_lines, second_t3, third_t3, wide)
-    forward_lines = first([after(across(a), *back)], first_n3, 1)
+    forward_lines = after(first([across(a)], first_n3, 1), *pick(cot_lines, far), second_t3, third_t3)
+    back = second(after(cot_lines, forward_lines), second_t3, third_t3, wide)
     solved = across(forward_lines)
 
     lifted_pieces = lifted(index, solved, state, *state_x, *state_y, n)

time: 786 us -> 760 us (0.967)
  starting transfers between devices: 154 us -> 124 us
  waiting for transfers between devices: 373 us -> 382 us
    ppermute x18, waiting for transfers between devices: 249 us -> 309 us  [send(): lax.ppermute(piece, 'narrow', [(k, (k + d) % n) for k in range(n)])]
    ppermute x5, waiting for transfers between devices: 40.3 us -> 13.5 us  [neighbours(): lax.ppermute(low_edge, axis, down)]
    all_to_all x11 -> x7, starting transfers between devices: 57 us -> 30.9 us  [across(): lax.all_to_all(piece, 'wide', split_axis=0, concat_axis=0, tiled=True)]
    all_to_all x11 -> x7, waiting for transfers between devices: 81.9 us -> 58.4 us  [across(): lax.all_to_all(piece, 'wide', split_axis=0, concat_axis=0, tiled=True)]
    optimization_barrier x7 -> x0, local copies, waits for them, and re-layouts: 11.5 us -> none  [the longest x4 7.14 us: after(): return lax.optimization_barrier((value, earlier))[0]]
  transfers between devices with their start and end apart: 40 -> 36, of which waited for: 24 -> 22; matrix products, arithmetic and copies ran while one was open for 5% -> 5% of each run, Pallas kernels for 21% -> 21%
where the time goes in v3:
time: 760 us; the launch traced here: 757 us
  waiting for transfers between devices  382 us (50%)
  Pallas kernels  174 us (23%)
  starting transfers between devices  124 us (16%)
  local copies, waits for them, and re-layouts  36.7 us (5%)
  blocking collectives  19.8 us (3%)
  other arithmetic  14.9 us (2%)
    ppermute x18, waiting for transfers between devices, send(): lax.ppermute(piece, 'narrow', [(k, (k + d) % n) for k in range(n)])  309 us
    ppermute x18, starting transfers between devices, send(): lax.ppermute(piece, 'narrow', [(k, (k + d) % n) for k in range(n)])  68.6 us
    all_to_all x7, waiting for transfers between devices, across(): lax.all_to_all(piece, 'wide', split_axis=0, concat_axis=0, tiled=True)  58.4 us
    pallas_call x3, Pallas kernels, second(): pl.pallas_call(functools.partial(second_kernel, count=count, chunked=bool...  37.8 us
    pallas_call x3, Pallas kernels, first(): pl.pallas_call(functools.partial(first_kernel, count=len(flat), lines=lin...  32.5 us
    all_to_all x7, starting transfers between devices, across(): lax.all_to_all(piece, 'wide', split_axis=0, concat_axis=0, tiled=True)  30.9 us
    pallas_call x1, Pallas kernels, frozen(): pl.pallas_call(functools.partial(frozen_kernel, blocks=blocks, groups=gro...  24.8 us
    all_to_all x1, blocking collectives, across(): lax.all_to_all(piece, 'wide', split_axis=0, concat_axis=0, tiled=True)  19.8 us
  transfers between devices with their start and end apart: 36, of which 22 were waited for; matrix products, arithmetic and copies ran while one was open for 5% of the time, Pallas kernels for 21%

profile of v3, /device:TPU:0, one launch (start us, length us, event | category | flops | bytes accessed | tf_op | source)
XLA Modules:
  0.0 756.5 jit_solution(8571925692531795055)
XLA Ops:
  17.2 5.6 collective-permute-start.2
  31.6 11.6 %forward.1 = (f32[8,64,16,128]{3,2,1,0:T(8,128)}, f32[64,128,128]{2,1,0:T(8,128)}) custom-call(s32[1]{0:T(128)} %bitcast.i, f32[64,128,128]{2,1,0:T(8,128)} %after.5, f32[64,128,128]{2,1,0:T(8,128)} %after.5, f32[64,128,128]{2,1,0:T(8,128)} %after.5, f32[1,128,128]{2,1,0:T(8,128)} %bitcast.130, f32[1,128,128]{2,1,0:T(8,128)} %bitcast.127, ...), custom_call_target="tpu_custom_call" | custom-call | flops 100000000 | bytes 356515 | tf_op jit(solution)/shard_map/forward/pallas_call | solution.py:308
  43.2 11.4 %collective-permute-done.4.refs_1_ = f32[16,128,128]{2,1,0:T(8,128)S(1)} collective-permute-done((f32[16,128,128]{2,1,0:T(8,128)S(1)}, f32[16,128,128]{2,1,0:T(8,128)S(1)}, u32[]{:S(2)}, u32[]{:S(2)}) %collective-permute-start.4) | collective-permute-done | bytes 1048608 | tf_op jit(solution)/shard_map/ppermute | solution.py:786
  64.4 21.7 %collective-permute-done.5.refs_3_ = f32[16,128,128]{2,1,0:T(8,128)} collective-permute-done((f32[16,128,128]{2,1,0:T(8,128)}, f32[16,128,128]{2,1,0:T(8,128)}, u32[]{:S(2)}, u32[]{:S(2)}) %collective-permute-start.5) | collective-permute-done | bytes 1048608 | tf_op jit(solution)/shard_map/ppermute | solution.py:786
  89.8 19.6 %all-to-all-done = f32[8,64,16,128]{3,2,1,0:T(8,128)} async-done(((f32[8,64,16,128]{3,2,1,0:T(8,128)}), f32[8,64,16,128]{3,2,1,0:T(8,128)}, u32[]{:S(2)}, u32[]{:S(2)}) %all-to-all-start) | async-done | bytes 4194336 | tf_op jit(solution)/shard_map/all_to_all | solution.py:799
  109.5 10.8 %first.3 = f32[8448,128]{1,0:T(8,128)} custom-call(f32[8192,128]{1,0:T(8,128)} %bitcast.19.refs_0_, bf16[512,1536]{1,0:T(8,128)(2,1)} %pad_maximum_fusion.2.refs_1_), custom_call_target="tpu_custom_call" | custom-call | flops 140000000 | bytes 209715 | tf_op jit(solution)/shard_map/first/pallas_call | solution.py:370
  120.3 13.7 %collective-permute-done.6.refs_2_ = f32[16,128,128]{2,1,0:T(8,128)S(1)} collective-permute-done((f32[16,128,128]{2,1,0:T(8,128)}, f32[16,128,128]{2,1,0:T(8,128)S(1)}, u32[]{:S(2)}, u32[]{:S(2)}) %collective-permute-start.6) | collective-permute-done | bytes 1048608 | tf_op jit(solution)/shard_map/ppermute | solution.py:786
  139.6 12.2 %second.3 = (f32[8,16,16,128]{3,2,1,0:T(8,128)}, f32[8,16,16,128]{3,2,1,0:T(8,128)}, f32[8,16,16,128]{3,2,1,0:T(8,128)}, f32[8,16,16,128]{3,2,1,0:T(8,128)}) custom-call(f32[16,128,128]{2,1,0:T(8,128)} %get-tuple-element.70.refs_0_, f32[16,128,128]{2,1,0:T(8,128)} %copy-done.10, f32[16,128,128]{2,1,0:T(8,128)} %copy-done.11, ...), custom_call_target="tpu_custom_call" | custom-call | flops 180000000 | bytes 209715 | tf_op jit(solution)/shard_map/second/pallas_call | solution.py:410
  155.6 24.2 %collective-permute-done.7 = f32[8,16,16,128]{3,2,1,0:T(8,128)S(1)} collective-permute-done((f32[8,16,16,128]{3,2,1,0:T(8,128)}, f32[8,16,16,128]{3,2,1,0:T(8,128)S(1)}, u32[]{:S(2)}, u32[]{:S(2)}) %collective-permute-start.7) | collective-permute-done | bytes 1048608 | tf_op jit(solution)/shard_map/ppermute | solution.py:786
  179.8 20.1 %collective-permute-done.8 = f32[8,16,16,128]{3,2,1,0:T(8,128)S(1)} collective-permute-done((f32[8,16,16,128]{3,2,1,0:T(8,128)}, f32[8,16,16,128]{3,2,1,0:T(8,128)S(1)}, u32[]{:S(2)}, u32[]{:S(2)}) %collective-permute-start.8) | collective-permute-done | bytes 1048608 | tf_op jit(solution)/shard_map/ppermute | solution.py:786
  210.2 8.9 %lifted.1 = (f32[18,128,128]{2,1,0:T(8,128)}, f32[18,128,128]{2,1,0:T(8,128)}, f32[18,128,128]{2,1,0:T(8,128)}, f32[18,128,128]{2,1,0:T(8,128)}) custom-call(s32[1]{0:T(128)} %bitcast.i, f32[8,66,16,128]{3,2,1,0:T(8,128)} %all-to-all-done.1.solved, f32[64,128,128]{2,1,0:T(8,128)} %after.5, f32[1,128,128]{2,1,0:T(8,128)} %bitcast.131, ...), custom_call_target="tpu_custom_call" | custom-call | flops 40000000 | bytes 272629 | tf_op jit(solution)/shard_map/lifted/pallas_call | solution.py:468
  219.1 37.6 %collective-permute-done.9 = f32[8,16,16,128]{3,2,1,0:T(8,128)} collective-permute-done((f32[8,16,16,128]{3,2,1,0:T(8,128)S(1)}, f32[8,16,16,128]{3,2,1,0:T(8,128)}, u32[]{:S(2)}, u32[]{:S(2)}) %collective-permute-start.9) | collective-permute-done | bytes 1048608 | tf_op jit(solution)/shard_map/ppermute | solution.py:786
  265.7 12.2 %all-to-all-done.3 = f32[8,16,16,128]{3,2,1,0:T(8,128)S(1)} async-done(((f32[8,16,16,128]{3,2,1,0:T(8,128)}), f32[8,16,16,128]{3,2,1,0:T(8,128)S(1)}, u32[]{:S(2)}, u32[]{:S(2)}) %all-to-all-start.3) | async-done | bytes 1048608 | tf_op jit(solution)/shard_map/all_to_all | solution.py:799
  279.0 10.8 %first.4 = f32[8448,128]{1,0:T(8,128)} custom-call(f32[6144,128]{1,0:T(8,128)} %bitcast.25.refs_0_, f32[2048,128]{1,0:T(8,128)} %bitcast.120, bf16[512,1536]{1,0:T(8,128)(2,1)} %pad_maximum_fusion.4.refs_2_), custom_call_target="tpu_custom_call" | custom-call | flops 140000000 | bytes 209715 | tf_op jit(solution)/shard_map/first/pallas_call | solution.py:370
  294.6 53.9 %collective-permute-done.11.refs_2_ = f32[18,128,128]{2,1,0:T(8,128)} collective-permute-done((f32[18,128,128]{2,1,0:T(8,128)S(1)}, f32[18,128,128]{2,1,0:T(8,128)}, u32[]{:S(2)}, u32[]{:S(2)}) %collective-permute-start.11) | collective-permute-done | bytes 1179680 | tf_op jit(solution)/shard_map/ppermute | solution.py:786
  357.4 12.5 %reaction.1 = (f32[16,128,128]{2,1,0:T(8,128)}, f32[16,128,128]{2,1,0:T(8,128)}, f32[16,128,128]{2,1,0:T(8,128)}, f32[16,128,128]{2,1,0:T(8,128)}) custom-call(s32[1]{0:T(128)} %bitcast.i, f32[8,66,16,128]{3,2,1,0:T(8,128)} %all-to-all-done.4.carried, f32[66,128]{1,0:T(8,128)} %copy-done.19, f32[66,128]{1,0:T(8,128)} %copy-done.20, f32[64,128,128]{2,1,0:T(8,128)} %after.6, ...), custom_call_target="tpu_custom_call" | custom-call | flops 80000000 | bytes 356515 | tf_op jit(solution)/shard_map/reaction/pallas_call | solution.py:515
  388.0 13.3 %second.4.field = f32[18,512,128]{2,1,0:T(8,128)} custom-call(f32[18,128,128]{2,1,0:T(8,128)} %get-tuple-element.94.refs_0_, f32[18,128,128]{2,1,0:T(8,128)} %collective-permute-done.17.refs_1_, f32[18,128,128]{2,1,0:T(8,128)} %collective-permute-done.11.refs_2_, f32[18,128,128]{2,1,0:T(8,128)} %collective-permute-done.10.refs_3_, ...), custom_call_target="tpu_custom_call" | custom-call | flops 180000000 | bytes 209715 | tf_op jit(solution)/shard_map/second/pallas_call | solution.py:410
  401.3 10.2 %mixed.1 = (f32[16,128,128]{2,1,0:T(8,128)}, f32[16,128,128]{2,1,0:T(8,128)}, f32[16,128,128]{2,1,0:T(8,128)}, f32[16,128,128]{2,1,0:T(8,128)}) custom-call(s32[1]{0:T(128)} %bitcast.i, f32[18,512,128]{2,1,0:T(8,128)} %second.4.field), custom_call_target="tpu_custom_call" | custom-call | flops 80000000 | bytes 188743 | tf_op jit(solution)/shard_map/mixed/pallas_call | solution.py:594
  411.5 24.8 %frozen.1 = (f32[64,128,128]{2,1,0:T(8,128)}, f32[24,256]{1,0:T(8,128)}) custom-call(s32[1]{0:T(128)} %bitcast.i, f32[64,128,128]{2,1,0:T(8,128)} %after.5, f32[64,128,128]{2,1,0:T(8,128)} %after.5, f32[64,128,128]{2,1,0:T(8,128)} %after.5, f32[1,128,128]{2,1,0:T(8,128)} %bitcast.132, f32[1,128,128]{2,1,0:T(8,128)} %bitcast.129, f32[66,128]{1,0:T(8,128)} %fusion.1.q_low, ...), custom_call_target="tpu_custom_call" | custom-call | flops 100000000 | bytes 356515 | tf_op jit(solution)/shard_map/frozen/pallas_call | solution.py:659
  436.3 16.9 %collective-permute-done.15.refs_2_ = f32[16,128,128]{2,1,0:T(8,128)} collective-permute-done((f32[16,128,128]{2,1,0:T(8,128)}, f32[16,128,128]{2,1,0:T(8,128)}, u32[]{:S(2)}, u32[]{:S(2)}) %collective-permute-start.15) | collective-permute-done | bytes 1048608 | tf_op jit(solution)/shard_map/ppermute | solution.py:786
  453.2 45.4 %collective-permute-start.18 = (f32[16,128,128]{2,1,0:T(8,128)S(1)}, f32[16,128,128]{2,1,0:T(8,128)S(1)}, u32[]{:S(2)}, u32[]{:S(2)}) collective-permute-start(f32[16,128,128]{2,1,0:T(8,128)S(1)} %copy-done.27), channel_id=1, source_target_pairs={{0,1},{1,2},{2,3},{3,0},{4,5},{5,6},{6,7},{7,4},{8,9},{9,10},{10,1... | collective-permute-start | bytes 3145736 | tf_op jit(solution)/shard_map/ppermute | solution.py:786
  498.6 12.2 %second.5 = (f32[8,16,16,128]{3,2,1,0:T(8,128)}, f32[8,16,16,128]{3,2,1,0:T(8,128)}, f32[8,16,16,128]{3,2,1,0:T(8,128)}, f32[8,16,16,128]{3,2,1,0:T(8,128)}) custom-call(f32[16,128,128]{2,1,0:T(8,128)} %get-tuple-element.104.refs_0_, f32[16,128,128]{2,1,0:T(8,128)} %collective-permute-done.14.refs_1_, f32[16,128,128]{2,1,0:T(8,128)} %collective-permute-done.15.refs_2_, ...), custom_call_target="tpu_custom_call" | custom-call | flops 180000000 | bytes 209715 | tf_op jit(solution)/shard_map/second/pallas_call | solution.py:410
  510.8 10.4 %collective-permute-done.18.refs_3_ = f32[16,128,128]{2,1,0:T(8,128)S(1)} collective-permute-done((f32[16,128,128]{2,1,0:T(8,128)S(1)}, f32[16,128,128]{2,1,0:T(8,128)S(1)}, u32[]{:S(2)}, u32[]{:S(2)}) %collective-permute-start.18) | collective-permute-done | bytes 1048608 | tf_op jit(solution)/shard_map/ppermute | solution.py:786
  525.0 24.3 %collective-permute-done.19.refs_7_ = f32[8,16,16,128]{3,2,1,0:T(8,128)S(1)} collective-permute-done((f32[8,16,16,128]{3,2,1,0:T(8,128)}, f32[8,16,16,128]{3,2,1,0:T(8,128)S(1)}, u32[]{:S(2)}, u32[]{:S(2)}) %collective-permute-start.19) | collective-permute-done | bytes 1048608 | tf_op jit(solution)/shard_map/ppermute | solution.py:786
  549.4 20.6 %collective-permute-done.20.refs_5_ = f32[8,16,16,128]{3,2,1,0:T(8,128)S(1)} collective-permute-done((f32[8,16,16,128]{3,2,1,0:T(8,128)}, f32[8,16,16,128]{3,2,1,0:T(8,128)S(1)}, u32[]{:S(2)}, u32[]{:S(2)}) %collective-permute-start.20) | collective-permute-done | bytes 1048608 | tf_op jit(solution)/shard_map/ppermute | solution.py:786
  578.5 48.5 %collective-permute-done.21.refs_6_ = f32[8,16,16,128]{3,2,1,0:T(8,128)S(1)} collective-permute-done((f32[8,16,16,128]{3,2,1,0:T(8,128)}, f32[8,16,16,128]{3,2,1,0:T(8,128)S(1)}, u32[]{:S(2)}, u32[]{:S(2)}) %collective-permute-start.21) | collective-permute-done | bytes 1048608 | tf_op jit(solution)/shard_map/ppermute | solution.py:786
  629.5 19.8 %all_to_all.49 = f32[8,16,16,128]{3,2,1,0:T(8,128)} all-to-all(f32[8,16,16,128]{3,2,1,0:T(8,128)} %copy-done.3), channel_id=1, replica_groups=mesh['wide'=8,'narrow'=4] {'wide'}, dimensions={0} | all-to-all | bytes 2097152 | tf_op jit(solution)/shard_map/all_to_all | solution.py:799
  649.3 10.9 %first.5 = f32[8448,128]{1,0:T(8,128)} custom-call(f32[6144,128]{1,0:T(8,128)} %bitcast.119, f32[2048,128]{1,0:T(8,128)} %bitcast.121, bf16[512,1536]{1,0:T(8,128)(2,1)} %pad_maximum_fusion.4.refs_2_), custom_call_target="tpu_custom_call" | custom-call | flops 140000000 | bytes 209715 | tf_op jit(solution)/shard_map/first/pallas_call | solution.py:370
  677.9 11.0 %lines.1.tail = f32[64,128,128]{2,1,0:T(8,128)} custom-call(s32[1]{0:T(128)} %bitcast.i, f32[16,128,128]{2,1,0:T(8,128)} %get-tuple-element.104.refs_0_, f32[16,128,128]{2,1,0:T(8,128)} %get-tuple-element.90.refs_1_, f32[16,128,128]{2,1,0:T(8,128)} %get-tuple-element.91.refs_2_, f32[16,128,128]{2,1,0:T(8,128)} %get-tuple-element.92.refs_3_, ...), custom_call_target="tpu_custom_call" | custom-call | flops 100000000 | bytes 356515 | tf_op jit(solution)/shard_map/lines/pallas_call | solution.py:559
  688.9 26.5 %all-to-all-done.7.start.refs_6_ = f32[8,66,16,128]{3,2,1,0:T(8,128)} async-done(((f32[8,66,16,128]{3,2,1,0:T(8,128)}), f32[8,66,16,128]{3,2,1,0:T(8,128)}, u32[]{:S(2)}, u32[]{:S(2)}) %all-to-all-start.7) | async-done | bytes 4325408 | tf_op jit(solution)/shard_map/all_to_all | solution.py:799
  726.6 12.6 %column.1 = f32[24,256]{1,0:T(8,128)} custom-call(s32[1]{0:T(128)} %bitcast.i, f32[16,128,128]{2,1,0:T(8,128)} %get-tuple-element.98.refs_0_, f32[16,128,128]{2,1,0:T(8,128)} %collective-permute-done.22.refs_1_, f32[16,128,128]{2,1,0:T(8,128)} %copy-done.13, f32[16,128,128]{2,1,0:T(8,128)} %copy-done.12, f32[64,128,128]{2,1,0:T(8,128)} %get-tuple-element.124.refs_4_, ...), custom_call_target="tpu_custom_call" | custom-call | flops 80000000 | bytes 356515 | tf_op jit(solution)/shard_map/column/pallas_call | solution.py:705
  743.7 12.3 %adjoint.1 = f32[64,128,128]{2,1,0:T(8,128)} custom-call(s32[1]{0:T(128)} %bitcast.i, f32[8,66,16,128]{3,2,1,0:T(8,128)} %all-to-all-done.7.start.refs_6_, f32[66,128]{1,0:T(8,128)} %copy-done.17, f32[66,128]{1,0:T(8,128)} %copy-done.18, f32[64,128,128]{2,1,0:T(8,128)} %after.6, f32[64,128,128]{2,1,0:T(8,128)} %after.6, f32[64,128,128]{2,1,0:T(8,128)} %after.6, ...), custom_call_target="tpu_custom_call" | custom-call | flops 100000000 | bytes 356515 | tf_op jit(solution)/shard_map/adjoint/pallas_call | solution.py:752
  (184 shorter events, 146.0 us)
Async XLA Ops:
  2.5 13.3 %collective-permute-start.1 = (f32[2,128,128]{2,0,1:T(2,128)S(1)}, f32[2,128,128]{2,0,1:T(2,128)S(1)}, u32[]{:S(2)}, u32[]{:S(2)}) collective-permute-start(f32[2,128,128]{2,0,1:T(2,128)S(1)} %pad_maximum_fusion.9), channel_id=1, source_target_pairs={{4,0},{8,4},{12,8},{16,12},{20,16},{24,20},{28,24},{5,1},{9,5},{13... | collective-permute-start | bytes 393224 | tf_op jit(solution)/shard_map/ppermute | solution.py:774
  4.0 11.9 %collective-permute-start = (f32[2,128,128]{2,0,1:T(2,128)S(1)}, f32[2,128,128]{2,0,1:T(2,128)S(1)}, u32[]{:S(2)}, u32[]{:S(2)}) collective-permute-start(f32[2,128,128]{2,0,1:T(2,128)S(1)} %pad_maximum_fusion.8), channel_id=1, source_target_pairs={{0,4},{4,8},{8,12},{12,16},{16,20},{20,24},{24,28},{1,5},{5,9},{9,... | collective-permute-start | bytes 393224 | tf_op jit(solution)/shard_map/ppermute | solution.py:774
  15.9 10.8 %collective-permute-start.3 = (f32[2,66,128]{2,1,0:T(8,128)S(1)}, f32[2,66,128]{2,1,0:T(8,128)S(1)}, u32[]{:S(2)}, u32[]{:S(2)}) collective-permute-start(f32[2,66,128]{2,1,0:T(8,128)S(1)} %get-tuple-element.165), channel_id=1, source_target_pairs={{1,0},{2,1},{3,2},{5,4},{6,5},{7,6},{9,8},{10,9},{11,10},{13,12},{... | collective-permute-start | bytes 202760 | tf_op jit(solution)/shard_map/ppermute | solution.py:774
  17.2 9.5 %collective-permute-start.2 = (f32[2,66,128]{2,1,0:T(8,128)S(1)}, f32[2,66,128]{2,1,0:T(8,128)S(1)}, u32[]{:S(2)}, u32[]{:S(2)}) collective-permute-start(f32[2,66,128]{2,1,0:T(8,128)S(1)} %get-tuple-element.166), channel_id=1, source_target_pairs={{0,1},{1,2},{2,3},{4,5},{5,6},{6,7},{8,9},{9,10},{10,11},{12,13},{... | collective-permute-start | bytes 202760 | tf_op jit(solution)/shard_map/ppermute | solution.py:774
  26.8 27.9 %collective-permute-start.4 = (f32[16,128,128]{2,1,0:T(8,128)S(1)}, f32[16,128,128]{2,1,0:T(8,128)S(1)}, u32[]{:S(2)}, u32[]{:S(2)}) collective-permute-start(f32[16,128,128]{2,1,0:T(8,128)S(1)} %get-tuple-element.64), channel_id=1, source_target_pairs={{0,1},{1,2},{2,3},{3,0},{4,5},{5,6},{6,7},{7,4},{8,9},{9,10},{10,1... | collective-permute-start | bytes 3145736 | tf_op jit(solution)/shard_map/ppermute | solution.py:786
  55.6 53.8 %all-to-all-start = ((f32[8,64,16,128]{3,2,1,0:T(8,128)}), f32[8,64,16,128]{3,2,1,0:T(8,128)}, u32[]{:S(2)}, u32[]{:S(2)}) async-start(f32[8,64,16,128]{3,2,1,0:T(8,128)} %get-tuple-element.68), calls=%async_computation | async-start | bytes 8388608 | tf_op jit(solution)/shard_map/all_to_all | solution.py:799
  60.3 25.8 %collective-permute-start.5 = (f32[16,128,128]{2,1,0:T(8,128)}, f32[16,128,128]{2,1,0:T(8,128)}, u32[]{:S(2)}, u32[]{:S(2)}) collective-permute-start(f32[16,128,128]{2,1,0:T(8,128)} %get-tuple-element.65), channel_id=1, source_target_pairs={{0,3},{1,0},{2,1},{3,2},{4,7},{5,4},{6,5},{7,6},{8,11},{9,8},{10,9... | collective-permute-start | bytes 3145736 | tf_op jit(solution)/shard_map/ppermute | solution.py:786
  86.1 47.9 %collective-permute-start.6 = (f32[16,128,128]{2,1,0:T(8,128)}, f32[16,128,128]{2,1,0:T(8,128)S(1)}, u32[]{:S(2)}, u32[]{:S(2)}) collective-permute-start(f32[16,128,128]{2,1,0:T(8,128)} %get-tuple-element.66), channel_id=1, source_target_pairs={{0,2},{1,3},{2,0},{3,1},{4,6},{5,7},{6,4},{7,5},{8,10},{9,11},{10,... | collective-permute-start | bytes 3145736 | tf_op jit(solution)/shard_map/ppermute | solution.py:786
  135.0 68.2 %all-to-all-start.1 = ((f32[8,66,16,128]{3,2,1,0:T(8,128)}), f32[8,66,16,128]{3,2,1,0:T(8,128)}, u32[]{:S(2)}, u32[]{:S(2)}) async-start(f32[8,66,16,128]{3,2,1,0:T(8,128)} %bitcast.117), calls=%async_computation.1 | async-start | bytes 8650752 | tf_op jit(solution)/shard_map/all_to_all | solution.py:799
  151.8 28.1 %collective-permute-start.7 = (f32[8,16,16,128]{3,2,1,0:T(8,128)}, f32[8,16,16,128]{3,2,1,0:T(8,128)S(1)}, u32[]{:S(2)}, u32[]{:S(2)}) collective-permute-start(f32[8,16,16,128]{3,2,1,0:T(8,128)} %get-tuple-element.75), channel_id=1, source_target_pairs={{0,1},{1,2},{2,3},{3,0},{4,5},{5,6},{6,7},{7,4},{8,9},{9,10},{10,1... | collective-permute-start | bytes 3145736 | tf_op jit(solution)/shard_map/ppermute | solution.py:786
  151.8 48.2 %collective-permute-start.8 = (f32[8,16,16,128]{3,2,1,0:T(8,128)}, f32[8,16,16,128]{3,2,1,0:T(8,128)S(1)}, u32[]{:S(2)}, u32[]{:S(2)}) collective-permute-start(f32[8,16,16,128]{3,2,1,0:T(8,128)} %get-tuple-element.76), channel_id=1, source_target_pairs={{0,3},{1,0},{2,1},{3,2},{4,7},{5,4},{6,5},{7,6},{8,11},{9,8},{10,9... | collective-permute-start | bytes 3145736 | tf_op jit(solution)/shard_map/ppermute | solution.py:786
  203.2 55.5 %all-to-all-start.2 = ((f32[8,48,16,128]{3,2,1,0:T(8,128)}), f32[8,48,16,128]{3,2,1,0:T(8,128)}, u32[]{:S(2)}, u32[]{:S(2)}) async-start(f32[8,48,16,128]{3,2,1,0:T(8,128)} %pad_maximum_fusion), calls=%async_computation.2 | async-start | bytes 6291456 | tf_op jit(solution)/shard_map/all_to_all | solution.py:799
  207.8 48.9 %collective-permute-start.9 = (f32[8,16,16,128]{3,2,1,0:T(8,128)S(1)}, f32[8,16,16,128]{3,2,1,0:T(8,128)}, u32[]{:S(2)}, u32[]{:S(2)}) collective-permute-start(f32[8,16,16,128]{3,2,1,0:T(8,128)S(1)} %copy-done.26), channel_id=1, source_target_pairs={{0,2},{1,3},{2,0},{3,1},{4,6},{5,7},{6,4},{7,5},{8,10},{9,11},{10,... | collective-permute-start | bytes 3145736 | tf_op jit(solution)/shard_map/ppermute | solution.py:786
  256.7 33.1 %collective-permute-start.10 = (f32[18,128,128]{2,1,0:T(8,128)}, f32[18,128,128]{2,1,0:T(8,128)}, u32[]{:S(2)}, u32[]{:S(2)}) collective-permute-start(f32[18,128,128]{2,1,0:T(8,128)} %get-tuple-element.85), channel_id=1, source_target_pairs={{0,3},{1,0},{2,1},{3,2},{4,7},{5,4},{6,5},{7,6},{8,11},{9,8},{10,9... | collective-permute-start | bytes 3538952 | tf_op jit(solution)/shard_map/ppermute | solution.py:786
  258.7 19.3 %all-to-all-start.3 = ((f32[8,16,16,128]{3,2,1,0:T(8,128)}), f32[8,16,16,128]{3,2,1,0:T(8,128)S(1)}, u32[]{:S(2)}, u32[]{:S(2)}) async-start(f32[8,16,16,128]{3,2,1,0:T(8,128)} %collective-permute-done.9), calls=%async_computation.3 | async-start | bytes 2097152 | tf_op jit(solution)/shard_map/all_to_all | solution.py:799
  289.8 58.7 %all-to-all-start.4 = ((f32[8,66,16,128]{3,2,1,0:T(8,128)}), f32[8,66,16,128]{3,2,1,0:T(8,128)}, u32[]{:S(2)}, u32[]{:S(2)}) async-start(f32[8,66,16,128]{3,2,1,0:T(8,128)} %bitcast.118), calls=%async_computation.4 | async-start | bytes 8650752 | tf_op jit(solution)/shard_map/all_to_all | solution.py:799
  294.5 54.0 %collective-permute-start.11 = (f32[18,128,128]{2,1,0:T(8,128)S(1)}, f32[18,128,128]{2,1,0:T(8,128)}, u32[]{:S(2)}, u32[]{:S(2)}) collective-permute-start(f32[18,128,128]{2,1,0:T(8,128)S(1)} %copy-done.24), channel_id=1, source_target_pairs={{0,2},{1,3},{2,0},{3,1},{4,6},{5,7},{6,4},{7,5},{8,10},{9,11},{10,... | collective-permute-start | bytes 3538952 | tf_op jit(solution)/shard_map/ppermute | solution.py:786
  350.9 5.9 collective-permute-start.13
  356.8 31.2 %collective-permute-start.17 = (f32[18,128,128]{2,1,0:T(8,128)}, f32[18,128,128]{2,1,0:T(8,128)}, u32[]{:S(2)}, u32[]{:S(2)}) collective-permute-start(f32[18,128,128]{2,1,0:T(8,128)} %get-tuple-element.93), channel_id=1, source_target_pairs={{0,1},{1,2},{2,3},{3,0},{4,5},{5,6},{6,7},{7,4},{8,9},{9,10},{10,1... | collective-permute-start | bytes 3538952 | tf_op jit(solution)/shard_map/ppermute | solution.py:786
  369.9 66.4 %collective-permute-start.14 = (f32[16,128,128]{2,1,0:T(8,128)}, f32[16,128,128]{2,1,0:T(8,128)}, u32[]{:S(2)}, u32[]{:S(2)}) collective-permute-start(f32[16,128,128]{2,1,0:T(8,128)} %get-tuple-element.90.refs_1_), channel_id=1, source_target_pairs={{0,1},{1,2},{2,3},{3,0},{4,5},{5,6},{6,7},{7,4},{8,9},{9,10},{10,1... | collective-permute-start | bytes 3145736 | tf_op jit(solution)/shard_map/ppermute | solution.py:786
  371.7 81.5 %collective-permute-start.15 = (f32[16,128,128]{2,1,0:T(8,128)}, f32[16,128,128]{2,1,0:T(8,128)}, u32[]{:S(2)}, u32[]{:S(2)}) collective-permute-start(f32[16,128,128]{2,1,0:T(8,128)} %get-tuple-element.91.refs_2_), channel_id=1, source_target_pairs={{0,2},{1,3},{2,0},{3,1},{4,6},{5,7},{6,4},{7,5},{8,10},{9,11},{10,... | collective-permute-start | bytes 3145736 | tf_op jit(solution)/shard_map/ppermute | solution.py:786
  373.7 79.5 %collective-permute-start.16 = (f32[16,128,128]{2,1,0:T(8,128)}, f32[16,128,128]{2,1,0:T(8,128)}, u32[]{:S(2)}, u32[]{:S(2)}) collective-permute-start(f32[16,128,128]{2,1,0:T(8,128)} %get-tuple-element.92.refs_3_), channel_id=1, source_target_pairs={{0,3},{1,0},{2,1},{3,2},{4,7},{5,4},{6,5},{7,6},{8,11},{9,8},{10,9... | collective-permute-start | bytes 3145736 | tf_op jit(solution)/shard_map/ppermute | solution.py:786
  453.2 68.0 %collective-permute-start.18 = (f32[16,128,128]{2,1,0:T(8,128)S(1)}, f32[16,128,128]{2,1,0:T(8,128)S(1)}, u32[]{:S(2)}, u32[]{:S(2)}) collective-permute-start(f32[16,128,128]{2,1,0:T(8,128)S(1)} %copy-done.27), channel_id=1, source_target_pairs={{0,1},{1,2},{2,3},{3,0},{4,5},{5,6},{6,7},{7,4},{8,9},{9,10},{10,1... | collective-permute-start | bytes 3145736 | tf_op jit(solution)/shard_map/ppermute | solution.py:786
  521.2 28.1 %collective-permute-start.19 = (f32[8,16,16,128]{3,2,1,0:T(8,128)}, f32[8,16,16,128]{3,2,1,0:T(8,128)S(1)}, u32[]{:S(2)}, u32[]{:S(2)}) collective-permute-start(f32[8,16,16,128]{3,2,1,0:T(8,128)} %get-tuple-element.114), channel_id=1, source_target_pairs={{0,1},{1,2},{2,3},{3,0},{4,5},{5,6},{6,7},{7,4},{8,9},{9,10},{10,1... | collective-permute-start | bytes 3145736 | tf_op jit(solution)/shard_map/ppermute | solution.py:786
  523.7 46.2 %collective-permute-start.20 = (f32[8,16,16,128]{3,2,1,0:T(8,128)}, f32[8,16,16,128]{3,2,1,0:T(8,128)S(1)}, u32[]{:S(2)}, u32[]{:S(2)}) collective-permute-start(f32[8,16,16,128]{3,2,1,0:T(8,128)} %get-tuple-element.115), channel_id=1, source_target_pairs={{0,3},{1,0},{2,1},{3,2},{4,7},{5,4},{6,5},{7,6},{8,11},{9,8},{10,9... | collective-permute-start | bytes 3145736 | tf_op jit(solution)/shard_map/ppermute | solution.py:786
  574.0 55.5 %all-to-all-start.5 = ((f32[8,48,16,128]{3,2,1,0:T(8,128)}), f32[8,48,16,128]{3,2,1,0:T(8,128)S(1)}, u32[]{:S(2)}, u32[]{:S(2)}) async-start(f32[8,48,16,128]{3,2,1,0:T(8,128)} %pad_maximum_fusion.1), calls=%async_computation.5 | async-start | bytes 6291456 | tf_op jit(solution)/shard_map/all_to_all | solution.py:799
  577.9 49.1 %collective-permute-start.21 = (f32[8,16,16,128]{3,2,1,0:T(8,128)}, f32[8,16,16,128]{3,2,1,0:T(8,128)S(1)}, u32[]{:S(2)}, u32[]{:S(2)}) collective-permute-start(f32[8,16,16,128]{3,2,1,0:T(8,128)} %get-tuple-element.117), channel_id=1, source_target_pairs={{0,2},{1,3},{2,0},{3,1},{4,6},{5,7},{6,4},{7,5},{8,10},{9,11},{10,... | collective-permute-start | bytes 3145736 | tf_op jit(solution)/shard_map/ppermute | solution.py:786
  628.0 32.2 %collective-permute-start.22 = (f32[16,128,128]{2,1,0:T(8,128)}, f32[16,128,128]{2,1,0:T(8,128)}, u32[]{:S(2)}, u32[]{:S(2)}) collective-permute-start(f32[16,128,128]{2,1,0:T(8,128)} %get-tuple-element.119), channel_id=1, source_target_pairs={{0,3},{1,0},{2,1},{3,2},{4,7},{5,4},{6,5},{7,6},{8,11},{9,8},{10,9... | collective-permute-start | bytes 3145736 | tf_op jit(solution)/shard_map/ppermute | solution.py:786
  660.2 55.2 %all-to-all-start.7 = ((f32[8,66,16,128]{3,2,1,0:T(8,128)}), f32[8,66,16,128]{3,2,1,0:T(8,128)}, u32[]{:S(2)}, u32[]{:S(2)}) async-start(f32[8,66,16,128]{3,2,1,0:T(8,128)} %bitcast.116), calls=%async_computation.7 | async-start | bytes 8650752 | tf_op jit(solution)/shard_map/all_to_all | solution.py:799
  677.3 48.3 %collective-permute-start.27 = (f32[16,128,128]{2,1,0:T(8,128)S(1)}, f32[16,128,128]{2,1,0:T(8,128)S(1)}, u32[]{:S(2)}, u32[]{:S(2)}) collective-permute-start(f32[16,128,128]{2,1,0:T(8,128)S(1)} %copy-done.25), channel_id=1, source_target_pairs={{0,2},{1,3},{2,0},{3,1},{4,6},{5,7},{6,4},{7,5},{8,10},{9,11},{10,... | collective-permute-start | bytes 3145736 | tf_op jit(solution)/shard_map/ppermute | solution.py:786
  719.0 6.6 collective-permute-start.26
  740.6 15.3 %all-to-all-start.8 = ((f32[32,1,96]{2,1,0:T(1,128)}), f32[32,1,96]{2,1,0:T(1,128)S(1)}, u32[]{:S(2)}, u32[]{:S(2)}) async-start(f32[32,1,96]{2,1,0:T(1,128)} %bitcast.61), calls=%async_computation.8 | async-start | bytes 32768 | tf_op jit(solution)/shard_map/all_to_all | solution.py:928
  (32 other events, 283.0 us)

commit v4 on v3

--- a/solution.py
+++ b/solution.py
@@ -330,6 +330,8 @@
 
 def first_kernel(*refs, count, lines, parts, length, halo):
     pieces, matrix3, out = refs[:count], refs[count], refs[count + 1]
+    pieces = [piece.reshape(piece.shape[0] * lines, piece.shape[2]) for piece in pieces]
+    out = out.reshape(out.shape[0] * lines, out.shape[2])
     rows = length + 2 * halo
 
     def pair(step, carry):
@@ -366,12 +368,15 @@
     lines, bz = pieces[0].shape[2:]
     length = sum(piece.shape[1] for piece in pieces)
     rows = length + 2 * halo
-    flat = [piece.reshape(-1, bz) for piece in pieces]
+    flat = [piece.reshape(-1, lines, bz) for piece in pieces]
+    block = 8
     out = pl.pallas_call(
-        functools.partial(first_kernel, count=len(flat), lines=lines, parts=wide, length=length, halo=halo),
-        in_specs=[pl.BlockSpec(memory_space=pltpu.VMEM)] * (len(flat) + 1),
-        out_specs=pl.BlockSpec(memory_space=pltpu.VMEM),
-        out_shape=jax.ShapeDtypeStruct((wide * rows * lines, bz), F32),
+        functools.partial(first_kernel, count=len(flat), lines=block, parts=wide, length=length, halo=halo),
+        grid=(lines // block,),
+        in_specs=[pl.BlockSpec((piece.shape[0], block, bz), lambda s: (0, s, 0)) for piece in flat]
+        + [pl.BlockSpec(matrix3.shape, lambda s: (0, 0))],
+        out_specs=pl.BlockSpec((wide * rows, block, bz), lambda s: (0, s, 0)),
+        out_shape=jax.ShapeDtypeStruct((wide * rows, lines, bz), F32),
         compiler_params=params(40),
         cost_estimate=cost(7e9, 10),
         name="first",
@@ -879,7 +884,8 @@
     carried_y = y_edges(carried)
     level_lines = send(level_lines, early, *carried_y)
     totals = react(index, carried, *carried_y, volatility, *vol_x, *vol_y, cotangent, n)
-    total_lines = send(totals, far + near)
+    total_lines = send(totals, near)
+    total_lines = send(total_lines, far, *pick(total_lines, near))
 
     level = second(after(level_lines, totals), second_n3, third_n3, 0)[0]
     drift_pieces = mix(index, level, n)

time: 760 us -> 754 us (level)
  starting transfers between devices: 124 us -> 102 us
  waiting for transfers between devices: 382 us -> 404 us
    ppermute x18, waiting for transfers between devices: 309 us -> 332 us  [send(): lax.ppermute(piece, 'narrow', [(k, (k + d) % n) for k in range(n)])]
    ppermute x18, starting transfers between devices: 68.6 us -> 46.1 us  [send(): lax.ppermute(piece, 'narrow', [(k, (k + d) % n) for k in range(n)])]
  transfers between devices with their start and end apart: 36 -> 36, of which waited for: 22 -> 23; matrix products, arithmetic and copies ran while one was open for 5% -> 5% of each run, Pallas kernels for 21% -> 19%
where the time goes in v4:
time: 754 us; the launch traced here: 751 us
  waiting for transfers between devices  404 us (54%)
  Pallas kernels  167 us (22%)
  starting transfers between devices  102 us (14%)
  local copies, waits for them, and re-layouts  37.3 us (5%)
  blocking collectives  19.8 us (3%)
  other arithmetic  14.9 us (2%)
    ppermute x18, waiting for transfers between devices, send(): lax.ppermute(piece, 'narrow', [(k, (k + d) % n) for k in range(n)])  332 us
    all_to_all x7, waiting for transfers between devices, across(): lax.all_to_all(piece, 'wide', split_axis=0, concat_axis=0, tiled=True)  58.1 us
    ppermute x18, starting transfers between devices, send(): lax.ppermute(piece, 'narrow', [(k, (k + d) % n) for k in range(n)])  46.1 us
    pallas_call x3, Pallas kernels, second(): pl.pallas_call(functools.partial(second_kernel, count=count, chunked=bool...  37.7 us
    all_to_all x7, starting transfers between devices, across(): lax.all_to_all(piece, 'wide', split_axis=0, concat_axis=0, tiled=True)  31 us
    pallas_call x3, Pallas kernels, first(): pl.pallas_call(functools.partial(first_kernel, count=len(flat), lines=blo...  25.6 us
    pallas_call x1, Pallas kernels, frozen(): pl.pallas_call(functools.partial(frozen_kernel, blocks=blocks, groups=gro...  24.8 us
    all_to_all x1, blocking collectives, across(): lax.all_to_all(piece, 'wide', split_axis=0, concat_axis=0, tiled=True)  19.8 us
  transfers between devices with their start and end apart: 36, of which 23 were waited for; matrix products, arithmetic and copies ran while one was open for 5% of the time, Pallas kernels for 19%

profile of v4, /device:TPU:0, one launch (start us, length us, event | category | flops | bytes accessed | tf_op | source)
XLA Modules:
  0.0 751.1 jit_solution(200474155514536487)
XLA Ops:
  31.8 11.6 %forward.1 = (f32[8,64,16,128]{3,2,1,0:T(8,128)}, f32[64,128,128]{2,1,0:T(8,128)}) custom-call(s32[1]{0:T(128)} %bitcast.i, f32[64,128,128]{2,1,0:T(8,128)} %after.5, f32[64,128,128]{2,1,0:T(8,128)} %after.5, f32[64,128,128]{2,1,0:T(8,128)} %after.5, f32[1,128,128]{2,1,0:T(8,128)} %bitcast.130, f32[1,128,128]{2,1,0:T(8,128)} %bitcast.127, ...), custom_call_target="tpu_custom_call" | custom-call | flops 100000000 | bytes 356515 | tf_op jit(solution)/shard_map/forward/pallas_call | solution.py:308
  43.4 11.4 %collective-permute-done.4.refs_1_ = f32[16,128,128]{2,1,0:T(8,128)S(1)} collective-permute-done((f32[16,128,128]{2,1,0:T(8,128)S(1)}, f32[16,128,128]{2,1,0:T(8,128)S(1)}, u32[]{:S(2)}, u32[]{:S(2)}) %collective-permute-start.4) | collective-permute-done | bytes 1048608 | tf_op jit(solution)/shard_map/ppermute | solution.py:791
  64.6 21.6 %collective-permute-done.5.refs_3_ = f32[16,128,128]{2,1,0:T(8,128)} collective-permute-done((f32[16,128,128]{2,1,0:T(8,128)}, f32[16,128,128]{2,1,0:T(8,128)}, u32[]{:S(2)}, u32[]{:S(2)}) %collective-permute-start.5) | collective-permute-done | bytes 1048608 | tf_op jit(solution)/shard_map/ppermute | solution.py:791
  89.9 19.6 %all-to-all-done = f32[8,64,16,128]{3,2,1,0:T(8,128)} async-done(((f32[8,64,16,128]{3,2,1,0:T(8,128)}), f32[8,64,16,128]{3,2,1,0:T(8,128)}, u32[]{:S(2)}, u32[]{:S(2)}) %all-to-all-start) | async-done | bytes 4194336 | tf_op jit(solution)/shard_map/all_to_all | solution.py:804
  109.6 8.5 %first.3 = f32[528,16,128]{2,1,0:T(8,128)} custom-call(f32[512,16,128]{2,1,0:T(8,128)} %bitcast.19.refs_0_, bf16[512,1536]{1,0:T(8,128)(2,1)} %pad_maximum_fusion.2.refs_1_), custom_call_target="tpu_custom_call" | custom-call | flops 140000000 | bytes 209715 | tf_op jit(solution)/shard_map/first/pallas_call | solution.py:373
  118.1 16.1 %collective-permute-done.6.refs_2_ = f32[16,128,128]{2,1,0:T(8,128)S(1)} collective-permute-done((f32[16,128,128]{2,1,0:T(8,128)}, f32[16,128,128]{2,1,0:T(8,128)S(1)}, u32[]{:S(2)}, u32[]{:S(2)}) %collective-permute-start.6) | collective-permute-done | bytes 1048608 | tf_op jit(solution)/shard_map/ppermute | solution.py:791
  139.7 12.2 %second.3 = (f32[8,16,16,128]{3,2,1,0:T(8,128)}, f32[8,16,16,128]{3,2,1,0:T(8,128)}, f32[8,16,16,128]{3,2,1,0:T(8,128)}, f32[8,16,16,128]{3,2,1,0:T(8,128)}) custom-call(f32[16,128,128]{2,1,0:T(8,128)} %get-tuple-element.71.refs_0_, f32[16,128,128]{2,1,0:T(8,128)} %copy-done.10, f32[16,128,128]{2,1,0:T(8,128)} %copy-done.13, ...), custom_call_target="tpu_custom_call" | custom-call | flops 180000000 | bytes 209715 | tf_op jit(solution)/shard_map/second/pallas_call | solution.py:415
  155.8 24.2 %collective-permute-done.7 = f32[8,16,16,128]{3,2,1,0:T(8,128)S(1)} collective-permute-done((f32[8,16,16,128]{3,2,1,0:T(8,128)}, f32[8,16,16,128]{3,2,1,0:T(8,128)S(1)}, u32[]{:S(2)}, u32[]{:S(2)}) %collective-permute-start.7) | collective-permute-done | bytes 1048608 | tf_op jit(solution)/shard_map/ppermute | solution.py:791
  180.0 20.1 %collective-permute-done.8 = f32[8,16,16,128]{3,2,1,0:T(8,128)S(1)} collective-permute-done((f32[8,16,16,128]{3,2,1,0:T(8,128)}, f32[8,16,16,128]{3,2,1,0:T(8,128)S(1)}, u32[]{:S(2)}, u32[]{:S(2)}) %collective-permute-start.8) | collective-permute-done | bytes 1048608 | tf_op jit(solution)/shard_map/ppermute | solution.py:791
  210.3 8.9 %lifted.1 = (f32[18,128,128]{2,1,0:T(8,128)}, f32[18,128,128]{2,1,0:T(8,128)}, f32[18,128,128]{2,1,0:T(8,128)}, f32[18,128,128]{2,1,0:T(8,128)}) custom-call(s32[1]{0:T(128)} %bitcast.i, f32[8,66,16,128]{3,2,1,0:T(8,128)} %all-to-all-done.1.solved, f32[64,128,128]{2,1,0:T(8,128)} %after.5, f32[1,128,128]{2,1,0:T(8,128)} %bitcast.131, ...), custom_call_target="tpu_custom_call" | custom-call | flops 40000000 | bytes 272629 | tf_op jit(solution)/shard_map/lifted/pallas_call | solution.py:473
  219.2 37.6 %collective-permute-done.9 = f32[8,16,16,128]{3,2,1,0:T(8,128)} collective-permute-done((f32[8,16,16,128]{3,2,1,0:T(8,128)S(1)}, f32[8,16,16,128]{3,2,1,0:T(8,128)}, u32[]{:S(2)}, u32[]{:S(2)}) %collective-permute-start.9) | collective-permute-done | bytes 1048608 | tf_op jit(solution)/shard_map/ppermute | solution.py:791
  265.9 12.2 %all-to-all-done.3 = f32[8,16,16,128]{3,2,1,0:T(8,128)S(1)} async-done(((f32[8,16,16,128]{3,2,1,0:T(8,128)}), f32[8,16,16,128]{3,2,1,0:T(8,128)S(1)}, u32[]{:S(2)}, u32[]{:S(2)}) %all-to-all-start.3) | async-done | bytes 1048608 | tf_op jit(solution)/shard_map/all_to_all | solution.py:804
  292.4 53.9 %collective-permute-done.11.refs_2_ = f32[18,128,128]{2,1,0:T(8,128)} collective-permute-done((f32[18,128,128]{2,1,0:T(8,128)S(1)}, f32[18,128,128]{2,1,0:T(8,128)}, u32[]{:S(2)}, u32[]{:S(2)}) %collective-permute-start.11) | collective-permute-done | bytes 1179680 | tf_op jit(solution)/shard_map/ppermute | solution.py:791
  355.2 12.5 %reaction.1 = (f32[16,128,128]{2,1,0:T(8,128)}, f32[16,128,128]{2,1,0:T(8,128)}, f32[16,128,128]{2,1,0:T(8,128)}, f32[16,128,128]{2,1,0:T(8,128)}) custom-call(s32[1]{0:T(128)} %bitcast.i, f32[8,66,16,128]{3,2,1,0:T(8,128)} %all-to-all-done.4.carried, f32[66,128]{1,0:T(8,128)} %copy-done.21, f32[66,128]{1,0:T(8,128)} %copy-done.22, f32[64,128,128]{2,1,0:T(8,128)} %after.6, ...), custom_call_target="tpu_custom_call" | custom-call | flops 80000000 | bytes 356515 | tf_op jit(solution)/shard_map/reaction/pallas_call | solution.py:520
  371.9 23.9 %collective-permute-done.14.refs_1_ = f32[16,128,128]{2,1,0:T(8,128)S(1)} collective-permute-done((f32[16,128,128]{2,1,0:T(8,128)}, f32[16,128,128]{2,1,0:T(8,128)S(1)}, u32[]{:S(2)}, u32[]{:S(2)}) %collective-permute-start.14) | collective-permute-done | bytes 1048608 | tf_op jit(solution)/shard_map/ppermute | solution.py:791
  395.8 19.3 %collective-permute-done.15.refs_3_ = f32[16,128,128]{2,1,0:T(8,128)S(1)} collective-permute-done((f32[16,128,128]{2,1,0:T(8,128)}, f32[16,128,128]{2,1,0:T(8,128)S(1)}, u32[]{:S(2)}, u32[]{:S(2)}) %collective-permute-start.15) | collective-permute-done | bytes 1048608 | tf_op jit(solution)/shard_map/ppermute | solution.py:791
  426.9 16.9 %collective-permute-done.17.refs_1_ = f32[18,128,128]{2,1,0:T(8,128)} collective-permute-done((f32[18,128,128]{2,1,0:T(8,128)}, f32[18,128,128]{2,1,0:T(8,128)}, u32[]{:S(2)}, u32[]{:S(2)}) %collective-permute-start.17) | collective-permute-done | bytes 1179680 | tf_op jit(solution)/shard_map/ppermute | solution.py:791
  443.8 13.3 %second.4.field = f32[18,512,128]{2,1,0:T(8,128)} custom-call(f32[18,128,128]{2,1,0:T(8,128)} %get-tuple-element.96.refs_0_, f32[18,128,128]{2,1,0:T(8,128)} %collective-permute-done.17.refs_1_, f32[18,128,128]{2,1,0:T(8,128)} %collective-permute-done.11.refs_2_, f32[18,128,128]{2,1,0:T(8,128)} %collective-permute-done.10.refs_3_, ...), custom_call_target="tpu_custom_call" | custom-call | flops 180000000 | bytes 209715 | tf_op jit(solution)/shard_map/second/pallas_call | solution.py:415
  457.1 10.2 %mixed.1 = (f32[16,128,128]{2,1,0:T(8,128)}, f32[16,128,128]{2,1,0:T(8,128)}, f32[16,128,128]{2,1,0:T(8,128)}, f32[16,128,128]{2,1,0:T(8,128)}) custom-call(s32[1]{0:T(128)} %bitcast.i, f32[18,512,128]{2,1,0:T(8,128)} %second.4.field), custom_call_target="tpu_custom_call" | custom-call | flops 80000000 | bytes 188743 | tf_op jit(solution)/shard_map/mixed/pallas_call | solution.py:599
  467.3 24.8 %frozen.1 = (f32[64,128,128]{2,1,0:T(8,128)}, f32[24,256]{1,0:T(8,128)}) custom-call(s32[1]{0:T(128)} %bitcast.i, f32[64,128,128]{2,1,0:T(8,128)} %after.5, f32[64,128,128]{2,1,0:T(8,128)} %after.5, f32[64,128,128]{2,1,0:T(8,128)} %after.5, f32[1,128,128]{2,1,0:T(8,128)} %bitcast.132, f32[1,128,128]{2,1,0:T(8,128)} %bitcast.129, f32[66,128]{1,0:T(8,128)} %fusion.1.q_low, ...), custom_call_target="tpu_custom_call" | custom-call | flops 100000000 | bytes 356515 | tf_op jit(solution)/shard_map/frozen/pallas_call | solution.py:664
  492.2 21.1 %collective-permute-start.18 = (f32[16,128,128]{2,1,0:T(8,128)S(1)}, f32[16,128,128]{2,1,0:T(8,128)S(1)}, u32[]{:S(2)}, u32[]{:S(2)}) collective-permute-start(f32[16,128,128]{2,1,0:T(8,128)S(1)} %copy-done.29), channel_id=1, source_target_pairs={{0,1},{1,2},{2,3},{3,0},{4,5},{5,6},{6,7},{7,4},{8,9},{9,10},{10,1... | collective-permute-start | bytes 3145736 | tf_op jit(solution)/shard_map/ppermute | solution.py:791
  513.3 12.2 %second.5 = (f32[8,16,16,128]{3,2,1,0:T(8,128)}, f32[8,16,16,128]{3,2,1,0:T(8,128)}, f32[8,16,16,128]{3,2,1,0:T(8,128)}, f32[8,16,16,128]{3,2,1,0:T(8,128)}) custom-call(f32[16,128,128]{2,1,0:T(8,128)} %get-tuple-element.106.refs_0_, f32[16,128,128]{2,1,0:T(8,128)} %copy-done.11, f32[16,128,128]{2,1,0:T(8,128)} %collective-permute-done.16.refs_2_, ...), custom_call_target="tpu_custom_call" | custom-call | flops 180000000 | bytes 209715 | tf_op jit(solution)/shard_map/second/pallas_call | solution.py:415
  525.5 11.4 %collective-permute-done.18.refs_3_ = f32[16,128,128]{2,1,0:T(8,128)S(1)} collective-permute-done((f32[16,128,128]{2,1,0:T(8,128)S(1)}, f32[16,128,128]{2,1,0:T(8,128)S(1)}, u32[]{:S(2)}, u32[]{:S(2)}) %collective-permute-start.18) | collective-permute-done | bytes 1048608 | tf_op jit(solution)/shard_map/ppermute | solution.py:791
  540.8 14.9 %collective-permute-done.19.refs_7_ = f32[8,16,16,128]{3,2,1,0:T(8,128)S(1)} collective-permute-done((f32[8,16,16,128]{3,2,1,0:T(8,128)}, f32[8,16,16,128]{3,2,1,0:T(8,128)S(1)}, u32[]{:S(2)}, u32[]{:S(2)}) %collective-permute-start.19) | collective-permute-done | bytes 1048608 | tf_op jit(solution)/shard_map/ppermute | solution.py:791
  555.6 11.2 %collective-permute-done.20.refs_5_ = f32[8,16,16,128]{3,2,1,0:T(8,128)S(1)} collective-permute-done((f32[8,16,16,128]{3,2,1,0:T(8,128)}, f32[8,16,16,128]{3,2,1,0:T(8,128)S(1)}, u32[]{:S(2)}, u32[]{:S(2)}) %collective-permute-start.20) | collective-permute-done | bytes 1048608 | tf_op jit(solution)/shard_map/ppermute | solution.py:791
  574.8 49.1 %collective-permute-done.21.refs_6_ = f32[8,16,16,128]{3,2,1,0:T(8,128)S(1)} collective-permute-done((f32[8,16,16,128]{3,2,1,0:T(8,128)}, f32[8,16,16,128]{3,2,1,0:T(8,128)S(1)}, u32[]{:S(2)}, u32[]{:S(2)}) %collective-permute-start.21) | collective-permute-done | bytes 1048608 | tf_op jit(solution)/shard_map/ppermute | solution.py:791
  626.1 19.8 %all_to_all.49 = f32[8,16,16,128]{3,2,1,0:T(8,128)} all-to-all(f32[8,16,16,128]{3,2,1,0:T(8,128)} %copy-done.3), channel_id=1, replica_groups=mesh['wide'=8,'narrow'=4] {'wide'}, dimensions={0} | all-to-all | bytes 2097152 | tf_op jit(solution)/shard_map/all_to_all | solution.py:804
  645.9 8.6 %first.5 = f32[528,16,128]{2,1,0:T(8,128)} custom-call(f32[384,16,128]{2,1,0:T(8,128)} %bitcast.119, f32[128,16,128]{2,1,0:T(8,128)} %bitcast.121, bf16[512,1536]{1,0:T(8,128)(2,1)} %pad_maximum_fusion.4.refs_2_), custom_call_target="tpu_custom_call" | custom-call | flops 140000000 | bytes 209715 | tf_op jit(solution)/shard_map/first/pallas_call | solution.py:373
  672.5 11.0 %lines.1.tail = f32[64,128,128]{2,1,0:T(8,128)} custom-call(s32[1]{0:T(128)} %bitcast.i, f32[16,128,128]{2,1,0:T(8,128)} %get-tuple-element.106.refs_0_, f32[16,128,128]{2,1,0:T(8,128)} %get-tuple-element.91.refs_1_, f32[16,128,128]{2,1,0:T(8,128)} %get-tuple-element.94.refs_2_, f32[16,128,128]{2,1,0:T(8,128)} %get-tuple-element.93.refs_3_, ...), custom_call_target="tpu_custom_call" | custom-call | flops 100000000 | bytes 356515 | tf_op jit(solution)/shard_map/lines/pallas_call | solution.py:564
  683.5 26.2 %all-to-all-done.7.start.refs_6_ = f32[8,66,16,128]{3,2,1,0:T(8,128)} async-done(((f32[8,66,16,128]{3,2,1,0:T(8,128)}), f32[8,66,16,128]{3,2,1,0:T(8,128)}, u32[]{:S(2)}, u32[]{:S(2)}) %all-to-all-start.7) | async-done | bytes 4325408 | tf_op jit(solution)/shard_map/all_to_all | solution.py:804
  721.2 12.6 %column.1 = f32[24,256]{1,0:T(8,128)} custom-call(s32[1]{0:T(128)} %bitcast.i, f32[16,128,128]{2,1,0:T(8,128)} %get-tuple-element.100.refs_0_, f32[16,128,128]{2,1,0:T(8,128)} %collective-permute-done.22.refs_1_, f32[16,128,128]{2,1,0:T(8,128)} %copy-done.15, f32[16,128,128]{2,1,0:T(8,128)} %copy-done.14, f32[64,128,128]{2,1,0:T(8,128)} %get-tuple-element.126.refs_4_, ...), custom_call_target="tpu_custom_call" | custom-call | flops 80000000 | bytes 356515 | tf_op jit(solution)/shard_map/column/pallas_call | solution.py:710
  738.2 12.3 %adjoint.1 = f32[64,128,128]{2,1,0:T(8,128)} custom-call(s32[1]{0:T(128)} %bitcast.i, f32[8,66,16,128]{3,2,1,0:T(8,128)} %all-to-all-done.7.start.refs_6_, f32[66,128]{1,0:T(8,128)} %copy-done.19, f32[66,128]{1,0:T(8,128)} %copy-done.20, f32[64,128,128]{2,1,0:T(8,128)} %after.6, f32[64,128,128]{2,1,0:T(8,128)} %after.6, f32[64,128,128]{2,1,0:T(8,128)} %after.6, ...), custom_call_target="tpu_custom_call" | custom-call | flops 100000000 | bytes 356515 | tf_op jit(solution)/shard_map/adjoint/pallas_call | solution.py:757
  (188 shorter events, 157.7 us)
Async XLA Ops:
  2.5 13.5 %collective-permute-start.1 = (f32[2,128,128]{2,0,1:T(2,128)S(1)}, f32[2,128,128]{2,0,1:T(2,128)S(1)}, u32[]{:S(2)}, u32[]{:S(2)}) collective-permute-start(f32[2,128,128]{2,0,1:T(2,128)S(1)} %pad_maximum_fusion.9), channel_id=1, source_target_pairs={{4,0},{8,4},{12,8},{16,12},{20,16},{24,20},{28,24},{5,1},{9,5},{13... | collective-permute-start | bytes 393224 | tf_op jit(solution)/shard_map/ppermute | solution.py:779
  4.0 12.1 %collective-permute-start = (f32[2,128,128]{2,0,1:T(2,128)S(1)}, f32[2,128,128]{2,0,1:T(2,128)S(1)}, u32[]{:S(2)}, u32[]{:S(2)}) collective-permute-start(f32[2,128,128]{2,0,1:T(2,128)S(1)} %pad_maximum_fusion.8), channel_id=1, source_target_pairs={{0,4},{4,8},{8,12},{12,16},{16,20},{20,24},{24,28},{1,5},{5,9},{9,... | collective-permute-start | bytes 393224 | tf_op jit(solution)/shard_map/ppermute | solution.py:779
  16.1 10.8 %collective-permute-start.3 = (f32[2,66,128]{2,1,0:T(8,128)S(1)}, f32[2,66,128]{2,1,0:T(8,128)S(1)}, u32[]{:S(2)}, u32[]{:S(2)}) collective-permute-start(f32[2,66,128]{2,1,0:T(8,128)S(1)} %get-tuple-element.167), channel_id=1, source_target_pairs={{1,0},{2,1},{3,2},{5,4},{6,5},{7,6},{9,8},{10,9},{11,10},{13,12},{... | collective-permute-start | bytes 202760 | tf_op jit(solution)/shard_map/ppermute | solution.py:779
  17.4 9.5 %collective-permute-start.2 = (f32[2,66,128]{2,1,0:T(8,128)S(1)}, f32[2,66,128]{2,1,0:T(8,128)S(1)}, u32[]{:S(2)}, u32[]{:S(2)}) collective-permute-start(f32[2,66,128]{2,1,0:T(8,128)S(1)} %get-tuple-element.168), channel_id=1, source_target_pairs={{0,1},{1,2},{2,3},{4,5},{5,6},{6,7},{8,9},{9,10},{10,11},{12,13},{... | collective-permute-start | bytes 202760 | tf_op jit(solution)/shard_map/ppermute | solution.py:779
  26.9 27.9 %collective-permute-start.4 = (f32[16,128,128]{2,1,0:T(8,128)S(1)}, f32[16,128,128]{2,1,0:T(8,128)S(1)}, u32[]{:S(2)}, u32[]{:S(2)}) collective-permute-start(f32[16,128,128]{2,1,0:T(8,128)S(1)} %get-tuple-element.65), channel_id=1, source_target_pairs={{0,1},{1,2},{2,3},{3,0},{4,5},{5,6},{6,7},{7,4},{8,9},{9,10},{10,1... | collective-permute-start | bytes 3145736 | tf_op jit(solution)/shard_map/ppermute | solution.py:791
  55.8 53.8 %all-to-all-start = ((f32[8,64,16,128]{3,2,1,0:T(8,128)}), f32[8,64,16,128]{3,2,1,0:T(8,128)}, u32[]{:S(2)}, u32[]{:S(2)}) async-start(f32[8,64,16,128]{3,2,1,0:T(8,128)} %get-tuple-element.69), calls=%async_computation | async-start | bytes 8388608 | tf_op jit(solution)/shard_map/all_to_all | solution.py:804
  60.4 25.8 %collective-permute-start.5 = (f32[16,128,128]{2,1,0:T(8,128)}, f32[16,128,128]{2,1,0:T(8,128)}, u32[]{:S(2)}, u32[]{:S(2)}) collective-permute-start(f32[16,128,128]{2,1,0:T(8,128)} %get-tuple-element.66), channel_id=1, source_target_pairs={{0,3},{1,0},{2,1},{3,2},{4,7},{5,4},{6,5},{7,6},{8,11},{9,8},{10,9... | collective-permute-start | bytes 3145736 | tf_op jit(solution)/shard_map/ppermute | solution.py:791
  86.2 48.0 %collective-permute-start.6 = (f32[16,128,128]{2,1,0:T(8,128)}, f32[16,128,128]{2,1,0:T(8,128)S(1)}, u32[]{:S(2)}, u32[]{:S(2)}) collective-permute-start(f32[16,128,128]{2,1,0:T(8,128)} %get-tuple-element.67), channel_id=1, source_target_pairs={{0,2},{1,3},{2,0},{3,1},{4,6},{5,7},{6,4},{7,5},{8,10},{9,11},{10,... | collective-permute-start | bytes 3145736 | tf_op jit(solution)/shard_map/ppermute | solution.py:791
  135.1 68.2 %all-to-all-start.1 = ((f32[8,66,16,128]{3,2,1,0:T(8,128)}), f32[8,66,16,128]{3,2,1,0:T(8,128)}, u32[]{:S(2)}, u32[]{:S(2)}) async-start(f32[8,66,16,128]{3,2,1,0:T(8,128)} %bitcast.117), calls=%async_computation.1 | async-start | bytes 8650752 | tf_op jit(solution)/shard_map/all_to_all | solution.py:804
  151.9 28.1 %collective-permute-start.7 = (f32[8,16,16,128]{3,2,1,0:T(8,128)}, f32[8,16,16,128]{3,2,1,0:T(8,128)S(1)}, u32[]{:S(2)}, u32[]{:S(2)}) collective-permute-start(f32[8,16,16,128]{3,2,1,0:T(8,128)} %get-tuple-element.76), channel_id=1, source_target_pairs={{0,1},{1,2},{2,3},{3,0},{4,5},{5,6},{6,7},{7,4},{8,9},{9,10},{10,1... | collective-permute-start | bytes 3145736 | tf_op jit(solution)/shard_map/ppermute | solution.py:791
  151.9 48.2 %collective-permute-start.8 = (f32[8,16,16,128]{3,2,1,0:T(8,128)}, f32[8,16,16,128]{3,2,1,0:T(8,128)S(1)}, u32[]{:S(2)}, u32[]{:S(2)}) collective-permute-start(f32[8,16,16,128]{3,2,1,0:T(8,128)} %get-tuple-element.77), channel_id=1, source_target_pairs={{0,3},{1,0},{2,1},{3,2},{4,7},{5,4},{6,5},{7,6},{8,11},{9,8},{10,9... | collective-permute-start | bytes 3145736 | tf_op jit(solution)/shard_map/ppermute | solution.py:791
  203.3 55.5 %all-to-all-start.2 = ((f32[8,48,16,128]{3,2,1,0:T(8,128)}), f32[8,48,16,128]{3,2,1,0:T(8,128)}, u32[]{:S(2)}, u32[]{:S(2)}) async-start(f32[8,48,16,128]{3,2,1,0:T(8,128)} %pad_maximum_fusion), calls=%async_computation.2 | async-start | bytes 6291456 | tf_op jit(solution)/shard_map/all_to_all | solution.py:804
  207.9 48.9 %collective-permute-start.9 = (f32[8,16,16,128]{3,2,1,0:T(8,128)S(1)}, f32[8,16,16,128]{3,2,1,0:T(8,128)}, u32[]{:S(2)}, u32[]{:S(2)}) collective-permute-start(f32[8,16,16,128]{3,2,1,0:T(8,128)S(1)} %copy-done.28), channel_id=1, source_target_pairs={{0,2},{1,3},{2,0},{3,1},{4,6},{5,7},{6,4},{7,5},{8,10},{9,11},{10,... | collective-permute-start | bytes 3145736 | tf_op jit(solution)/shard_map/ppermute | solution.py:791
  256.8 30.8 %collective-permute-start.10 = (f32[18,128,128]{2,1,0:T(8,128)}, f32[18,128,128]{2,1,0:T(8,128)}, u32[]{:S(2)}, u32[]{:S(2)}) collective-permute-start(f32[18,128,128]{2,1,0:T(8,128)} %get-tuple-element.86), channel_id=1, source_target_pairs={{0,3},{1,0},{2,1},{3,2},{4,7},{5,4},{6,5},{7,6},{8,11},{9,8},{10,9... | collective-permute-start | bytes 3538952 | tf_op jit(solution)/shard_map/ppermute | solution.py:791
  258.8 19.3 %all-to-all-start.3 = ((f32[8,16,16,128]{3,2,1,0:T(8,128)}), f32[8,16,16,128]{3,2,1,0:T(8,128)S(1)}, u32[]{:S(2)}, u32[]{:S(2)}) async-start(f32[8,16,16,128]{3,2,1,0:T(8,128)} %collective-permute-done.9), calls=%async_computation.3 | async-start | bytes 2097152 | tf_op jit(solution)/shard_map/all_to_all | solution.py:804
  287.6 58.7 %all-to-all-start.4 = ((f32[8,66,16,128]{3,2,1,0:T(8,128)}), f32[8,66,16,128]{3,2,1,0:T(8,128)}, u32[]{:S(2)}, u32[]{:S(2)}) async-start(f32[8,66,16,128]{3,2,1,0:T(8,128)} %bitcast.118), calls=%async_computation.4 | async-start | bytes 8650752 | tf_op jit(solution)/shard_map/all_to_all | solution.py:804
  292.3 54.0 %collective-permute-start.11 = (f32[18,128,128]{2,1,0:T(8,128)S(1)}, f32[18,128,128]{2,1,0:T(8,128)}, u32[]{:S(2)}, u32[]{:S(2)}) collective-permute-start(f32[18,128,128]{2,1,0:T(8,128)S(1)} %copy-done.26), channel_id=1, source_target_pairs={{0,2},{1,3},{2,0},{3,1},{4,6},{5,7},{6,4},{7,5},{8,10},{9,11},{10,... | collective-permute-start | bytes 3538952 | tf_op jit(solution)/shard_map/ppermute | solution.py:791
  348.7 5.9 collective-permute-start.13
  367.7 28.2 %collective-permute-start.14 = (f32[16,128,128]{2,1,0:T(8,128)}, f32[16,128,128]{2,1,0:T(8,128)S(1)}, u32[]{:S(2)}, u32[]{:S(2)}) collective-permute-start(f32[16,128,128]{2,1,0:T(8,128)} %get-tuple-element.91.refs_1_), channel_id=1, source_target_pairs={{0,1},{1,2},{2,3},{3,0},{4,5},{5,6},{6,7},{7,4},{8,9},{9,10},{10,1... | collective-permute-start | bytes 3145736 | tf_op jit(solution)/shard_map/ppermute | solution.py:791
  368.7 46.4 %collective-permute-start.15 = (f32[16,128,128]{2,1,0:T(8,128)}, f32[16,128,128]{2,1,0:T(8,128)S(1)}, u32[]{:S(2)}, u32[]{:S(2)}) collective-permute-start(f32[16,128,128]{2,1,0:T(8,128)} %get-tuple-element.93.refs_3_), channel_id=1, source_target_pairs={{0,3},{1,0},{2,1},{3,2},{4,7},{5,4},{6,5},{7,6},{8,11},{9,8},{10,9... | collective-permute-start | bytes 3145736 | tf_op jit(solution)/shard_map/ppermute | solution.py:791
  371.7 72.1 %collective-permute-start.17 = (f32[18,128,128]{2,1,0:T(8,128)}, f32[18,128,128]{2,1,0:T(8,128)}, u32[]{:S(2)}, u32[]{:S(2)}) collective-permute-start(f32[18,128,128]{2,1,0:T(8,128)} %get-tuple-element.95), channel_id=1, source_target_pairs={{0,1},{1,2},{2,3},{3,0},{4,5},{5,6},{6,7},{7,4},{8,9},{9,10},{10,1... | collective-permute-start | bytes 3538952 | tf_op jit(solution)/shard_map/ppermute | solution.py:791
  415.2 77.0 %collective-permute-start.16 = (f32[16,128,128]{2,1,0:T(8,128)}, f32[16,128,128]{2,1,0:T(8,128)}, u32[]{:S(2)}, u32[]{:S(2)}) collective-permute-start(f32[16,128,128]{2,1,0:T(8,128)} %get-tuple-element.94.refs_2_), channel_id=1, source_target_pairs={{0,2},{1,3},{2,0},{3,1},{4,6},{5,7},{6,4},{7,5},{8,10},{9,11},{10,... | collective-permute-start | bytes 3145736 | tf_op jit(solution)/shard_map/ppermute | solution.py:791
  492.2 44.8 %collective-permute-start.18 = (f32[16,128,128]{2,1,0:T(8,128)S(1)}, f32[16,128,128]{2,1,0:T(8,128)S(1)}, u32[]{:S(2)}, u32[]{:S(2)}) collective-permute-start(f32[16,128,128]{2,1,0:T(8,128)S(1)} %copy-done.29), channel_id=1, source_target_pairs={{0,1},{1,2},{2,3},{3,0},{4,5},{5,6},{6,7},{7,4},{8,9},{9,10},{10,1... | collective-permute-start | bytes 3145736 | tf_op jit(solution)/shard_map/ppermute | solution.py:791
  536.9 18.7 %collective-permute-start.19 = (f32[8,16,16,128]{3,2,1,0:T(8,128)}, f32[8,16,16,128]{3,2,1,0:T(8,128)S(1)}, u32[]{:S(2)}, u32[]{:S(2)}) collective-permute-start(f32[8,16,16,128]{3,2,1,0:T(8,128)} %get-tuple-element.116), channel_id=1, source_target_pairs={{0,1},{1,2},{2,3},{3,0},{4,5},{5,6},{6,7},{7,4},{8,9},{9,10},{10,1... | collective-permute-start | bytes 3145736 | tf_op jit(solution)/shard_map/ppermute | solution.py:791
  539.4 27.4 %collective-permute-start.20 = (f32[8,16,16,128]{3,2,1,0:T(8,128)}, f32[8,16,16,128]{3,2,1,0:T(8,128)S(1)}, u32[]{:S(2)}, u32[]{:S(2)}) collective-permute-start(f32[8,16,16,128]{3,2,1,0:T(8,128)} %get-tuple-element.117), channel_id=1, source_target_pairs={{0,3},{1,0},{2,1},{3,2},{4,7},{5,4},{6,5},{7,6},{8,11},{9,8},{10,9... | collective-permute-start | bytes 3145736 | tf_op jit(solution)/shard_map/ppermute | solution.py:791
  570.9 55.1 %all-to-all-start.5 = ((f32[8,48,16,128]{3,2,1,0:T(8,128)}), f32[8,48,16,128]{3,2,1,0:T(8,128)S(1)}, u32[]{:S(2)}, u32[]{:S(2)}) async-start(f32[8,48,16,128]{3,2,1,0:T(8,128)} %pad_maximum_fusion.1), calls=%async_computation.5 | async-start | bytes 6291456 | tf_op jit(solution)/shard_map/all_to_all | solution.py:804
  574.8 49.1 %collective-permute-start.21 = (f32[8,16,16,128]{3,2,1,0:T(8,128)}, f32[8,16,16,128]{3,2,1,0:T(8,128)S(1)}, u32[]{:S(2)}, u32[]{:S(2)}) collective-permute-start(f32[8,16,16,128]{3,2,1,0:T(8,128)} %get-tuple-element.119), channel_id=1, source_target_pairs={{0,2},{1,3},{2,0},{3,1},{4,6},{5,7},{6,4},{7,5},{8,10},{9,11},{10,... | collective-permute-start | bytes 3145736 | tf_op jit(solution)/shard_map/ppermute | solution.py:791
  624.9 29.6 %collective-permute-start.22 = (f32[16,128,128]{2,1,0:T(8,128)}, f32[16,128,128]{2,1,0:T(8,128)}, u32[]{:S(2)}, u32[]{:S(2)}) collective-permute-start(f32[16,128,128]{2,1,0:T(8,128)} %get-tuple-element.121), channel_id=1, source_target_pairs={{0,3},{1,0},{2,1},{3,2},{4,7},{5,4},{6,5},{7,6},{8,11},{9,8},{10,9... | collective-permute-start | bytes 3145736 | tf_op jit(solution)/shard_map/ppermute | solution.py:791
  654.5 55.2 %all-to-all-start.7 = ((f32[8,66,16,128]{3,2,1,0:T(8,128)}), f32[8,66,16,128]{3,2,1,0:T(8,128)}, u32[]{:S(2)}, u32[]{:S(2)}) async-start(f32[8,66,16,128]{3,2,1,0:T(8,128)} %bitcast.116), calls=%async_computation.7 | async-start | bytes 8650752 | tf_op jit(solution)/shard_map/all_to_all | solution.py:804
  671.9 48.3 %collective-permute-start.27 = (f32[16,128,128]{2,1,0:T(8,128)S(1)}, f32[16,128,128]{2,1,0:T(8,128)S(1)}, u32[]{:S(2)}, u32[]{:S(2)}) collective-permute-start(f32[16,128,128]{2,1,0:T(8,128)S(1)} %copy-done.27), channel_id=1, source_target_pairs={{0,2},{1,3},{2,0},{3,1},{4,6},{5,7},{6,4},{7,5},{8,10},{9,11},{10,... | collective-permute-start | bytes 3145736 | tf_op jit(solution)/shard_map/ppermute | solution.py:791
  713.6 6.6 collective-permute-start.26
  735.2 15.3 %all-to-all-start.8 = ((f32[32,1,96]{2,1,0:T(1,128)}), f32[32,1,96]{2,1,0:T(1,128)S(1)}, u32[]{:S(2)}, u32[]{:S(2)}) async-start(f32[32,1,96]{2,1,0:T(1,128)} %bitcast.61), calls=%async_computation.8 | async-start | bytes 32768 | tf_op jit(solution)/shard_map/all_to_all | solution.py:934
  (34 other events, 312.8 us)

commit v5 on v4

--- a/solution.py
+++ b/solution.py
@@ -887,7 +887,8 @@
     total_lines = send(totals, near)
     total_lines = send(total_lines, far, *pick(total_lines, near))
 
-    level = second(after(level_lines, totals), second_n3, third_n3, 0)[0]
+    uppers = second(total_lines, second_t3, third_t3, wide)
+    level = second(after(level_lines, uppers), second_n3, third_n3, 0)[0]
     drift_pieces = mix(index, level, n)
 
     def frozen_rows(rows):
@@ -910,13 +911,11 @@
         groups,
     )
 
-    total_lines = after(total_lines, drift_pieces, sums)
-    drifts = send(drift_pieces, early, *total_lines)
-    uppers = after(second(total_lines, second_t3, third_t3, wide), *pick(drifts, early))
     uppers, start_chunks, gone = cross_both(uppers, (), (), near, far)
+    drifts = send(drift_pieces, early, *pick(uppers, near))
     start_lines = first(start_chunks, first_t3, 1)
     drifts = send(drifts, late, gone)
-    start = across(after(start_lines, *pick(drifts, late)))
+    start = across(after(start_lines, *pick(drifts, near)))
 
     order = (here - jnp.arange(n)) % n
     edge_low = jnp.stack([piece[0, :, 0] for piece in uppers])[order].reshape(bx, bz)

time: 754 us -> 778 us (1.032)
  waiting for transfers between devices: 404 us -> 434 us
  starting transfers between devices: 102 us -> 88.3 us
    ppermute x18, waiting for transfers between devices: 332 us -> 374 us  [send(): lax.ppermute(piece, 'narrow', [(k, (k + d) % n) for k in range(n)])]
    ppermute x18, starting transfers between devices: 46.1 us -> 29.9 us  [send(): lax.ppermute(piece, 'narrow', [(k, (k + d) % n) for k in range(n)])]
  transfers between devices with their start and end apart: 36 -> 36, of which waited for: 23 -> 21; matrix products, arithmetic and copies ran while one was open for 5% -> 6% of each run, Pallas kernels for 19% -> 17%
where the time goes in v5:
time: 778 us; the launch traced here: 775 us
  waiting for transfers between devices  434 us (56%)
  Pallas kernels  167 us (21%)
  starting transfers between devices  88.3 us (11%)
  local copies, waits for them, and re-layouts  43.4 us (6%)
  blocking collectives  19.6 us (3%)
  other arithmetic  16.2 us (2%)
    ppermute x18, waiting for transfers between devices, send(): lax.ppermute(piece, 'narrow', [(k, (k + d) % n) for k in range(n)])  374 us
    all_to_all x7, waiting for transfers between devices, across(): lax.all_to_all(piece, 'wide', split_axis=0, concat_axis=0, tiled=True)  52.4 us
    pallas_call x3, Pallas kernels, second(): pl.pallas_call(functools.partial(second_kernel, count=count, chunked=bool...  37.8 us
    all_to_all x7, starting transfers between devices, across(): lax.all_to_all(piece, 'wide', split_axis=0, concat_axis=0, tiled=True)  31 us
    ppermute x18, starting transfers between devices, send(): lax.ppermute(piece, 'narrow', [(k, (k + d) % n) for k in range(n)])  29.9 us
    pallas_call x3, Pallas kernels, first(): pl.pallas_call(functools.partial(first_kernel, count=len(flat), lines=blo...  25.5 us
    pallas_call x1, Pallas kernels, frozen(): pl.pallas_call(functools.partial(frozen_kernel, blocks=blocks, groups=gro...  24.8 us
    all_to_all x1, blocking collectives, across(): lax.all_to_all(piece, 'wide', split_axis=0, concat_axis=0, tiled=True)  19.6 us
  transfers between devices with their start and end apart: 36, of which 21 were waited for; matrix products, arithmetic and copies ran while one was open for 6% of the time, Pallas kernels for 17%

profile of v5, /device:TPU:0, one launch (start us, length us, event | category | flops | bytes accessed | tf_op | source)
XLA Modules:
  0.0 774.7 jit_solution(6266504484926377339)
XLA Ops:
  32.4 11.6 %forward.1 = (f32[8,64,16,128]{3,2,1,0:T(8,128)}, f32[64,128,128]{2,1,0:T(8,128)}) custom-call(s32[1]{0:T(128)} %bitcast.i, f32[64,128,128]{2,1,0:T(8,128)} %after.6, f32[64,128,128]{2,1,0:T(8,128)} %after.6, f32[64,128,128]{2,1,0:T(8,128)} %after.6, f32[1,128,128]{2,1,0:T(8,128)} %bitcast.127, f32[1,128,128]{2,1,0:T(8,128)} %bitcast.130, ...), custom_call_target="tpu_custom_call" | custom-call | flops 100000000 | bytes 356515 | tf_op jit(solution)/shard_map/forward/pallas_call | solution.py:308
  44.0 11.0 %collective-permute-done.4.refs_1_ = f32[16,128,128]{2,1,0:T(8,128)S(1)} collective-permute-done((f32[16,128,128]{2,1,0:T(8,128)S(1)}, f32[16,128,128]{2,1,0:T(8,128)S(1)}, u32[]{:S(2)}, u32[]{:S(2)}) %collective-permute-start.4) | collective-permute-done | bytes 1048608 | tf_op jit(solution)/shard_map/ppermute | solution.py:791
  65.9 20.5 %collective-permute-done.5.refs_3_ = f32[16,128,128]{2,1,0:T(8,128)} collective-permute-done((f32[16,128,128]{2,1,0:T(8,128)}, f32[16,128,128]{2,1,0:T(8,128)}, u32[]{:S(2)}, u32[]{:S(2)}) %collective-permute-start.5) | collective-permute-done | bytes 1048608 | tf_op jit(solution)/shard_map/ppermute | solution.py:791
  90.1 19.7 %all-to-all-done = f32[8,64,16,128]{3,2,1,0:T(8,128)} async-done(((f32[8,64,16,128]{3,2,1,0:T(8,128)}), f32[8,64,16,128]{3,2,1,0:T(8,128)}, u32[]{:S(2)}, u32[]{:S(2)}) %all-to-all-start) | async-done | bytes 4194336 | tf_op jit(solution)/shard_map/all_to_all | solution.py:804
  109.8 8.5 %first.3 = f32[528,16,128]{2,1,0:T(8,128)} custom-call(f32[512,16,128]{2,1,0:T(8,128)} %bitcast.19.refs_0_, bf16[512,1536]{1,0:T(8,128)(2,1)} %pad_maximum_fusion.2.refs_1_), custom_call_target="tpu_custom_call" | custom-call | flops 140000000 | bytes 209715 | tf_op jit(solution)/shard_map/first/pallas_call | solution.py:373
  118.3 16.3 %collective-permute-done.6.refs_2_ = f32[16,128,128]{2,1,0:T(8,128)S(1)} collective-permute-done((f32[16,128,128]{2,1,0:T(8,128)}, f32[16,128,128]{2,1,0:T(8,128)S(1)}, u32[]{:S(2)}, u32[]{:S(2)}) %collective-permute-start.6) | collective-permute-done | bytes 1048608 | tf_op jit(solution)/shard_map/ppermute | solution.py:791
  140.1 12.2 %second.3 = (f32[8,16,16,128]{3,2,1,0:T(8,128)}, f32[8,16,16,128]{3,2,1,0:T(8,128)}, f32[8,16,16,128]{3,2,1,0:T(8,128)}, f32[8,16,16,128]{3,2,1,0:T(8,128)}) custom-call(f32[16,128,128]{2,1,0:T(8,128)} %get-tuple-element.63.refs_0_, f32[16,128,128]{2,1,0:T(8,128)} %copy-done.8, f32[16,128,128]{2,1,0:T(8,128)} %copy-done.9, ...), custom_call_target="tpu_custom_call" | custom-call | flops 180000000 | bytes 209715 | tf_op jit(solution)/shard_map/second/pallas_call | solution.py:415
  156.2 24.2 %collective-permute-done.7 = f32[8,16,16,128]{3,2,1,0:T(8,128)S(1)} collective-permute-done((f32[8,16,16,128]{3,2,1,0:T(8,128)}, f32[8,16,16,128]{3,2,1,0:T(8,128)S(1)}, u32[]{:S(2)}, u32[]{:S(2)}) %collective-permute-start.7) | collective-permute-done | bytes 1048608 | tf_op jit(solution)/shard_map/ppermute | solution.py:791
  180.4 20.1 %collective-permute-done.8 = f32[8,16,16,128]{3,2,1,0:T(8,128)S(1)} collective-permute-done((f32[8,16,16,128]{3,2,1,0:T(8,128)}, f32[8,16,16,128]{3,2,1,0:T(8,128)S(1)}, u32[]{:S(2)}, u32[]{:S(2)}) %collective-permute-start.8) | collective-permute-done | bytes 1048608 | tf_op jit(solution)/shard_map/ppermute | solution.py:791
  210.8 8.9 %lifted.1 = (f32[18,128,128]{2,1,0:T(8,128)}, f32[18,128,128]{2,1,0:T(8,128)}, f32[18,128,128]{2,1,0:T(8,128)}, f32[18,128,128]{2,1,0:T(8,128)}) custom-call(s32[1]{0:T(128)} %bitcast.i, f32[8,66,16,128]{3,2,1,0:T(8,128)} %all-to-all-done.1.solved, f32[64,128,128]{2,1,0:T(8,128)} %after.6, f32[1,128,128]{2,1,0:T(8,128)} %bitcast.128, ...), custom_call_target="tpu_custom_call" | custom-call | flops 40000000 | bytes 272629 | tf_op jit(solution)/shard_map/lifted/pallas_call | solution.py:473
  219.7 37.6 %collective-permute-done.9 = f32[8,16,16,128]{3,2,1,0:T(8,128)} collective-permute-done((f32[8,16,16,128]{3,2,1,0:T(8,128)S(1)}, f32[8,16,16,128]{3,2,1,0:T(8,128)}, u32[]{:S(2)}, u32[]{:S(2)}) %collective-permute-start.9) | collective-permute-done | bytes 1048608 | tf_op jit(solution)/shard_map/ppermute | solution.py:791
  266.4 12.2 %all-to-all-done.3 = f32[8,16,16,128]{3,2,1,0:T(8,128)S(1)} async-done(((f32[8,16,16,128]{3,2,1,0:T(8,128)}), f32[8,16,16,128]{3,2,1,0:T(8,128)S(1)}, u32[]{:S(2)}, u32[]{:S(2)}) %all-to-all-start.3) | async-done | bytes 1048608 | tf_op jit(solution)/shard_map/all_to_all | solution.py:804
  279.6 8.5 %first.4 = f32[528,16,128]{2,1,0:T(8,128)} custom-call(f32[384,16,128]{2,1,0:T(8,128)} %bitcast.25.refs_0_, f32[128,16,128]{2,1,0:T(8,128)} %bitcast.120, bf16[512,1536]{1,0:T(8,128)(2,1)} %pad_maximum_fusion.4.refs_2_), custom_call_target="tpu_custom_call" | custom-call | flops 140000000 | bytes 209715 | tf_op jit(solution)/shard_map/first/pallas_call | solution.py:373
  292.8 53.9 %collective-permute-done.11.refs_2_ = f32[18,128,128]{2,1,0:T(8,128)} collective-permute-done((f32[18,128,128]{2,1,0:T(8,128)S(1)}, f32[18,128,128]{2,1,0:T(8,128)}, u32[]{:S(2)}, u32[]{:S(2)}) %collective-permute-start.11) | collective-permute-done | bytes 1179680 | tf_op jit(solution)/shard_map/ppermute | solution.py:791
  355.6 12.4 %reaction.1 = (f32[16,128,128]{2,1,0:T(8,128)}, f32[16,128,128]{2,1,0:T(8,128)}, f32[16,128,128]{2,1,0:T(8,128)}, f32[16,128,128]{2,1,0:T(8,128)}) custom-call(s32[1]{0:T(128)} %bitcast.i, f32[8,66,16,128]{3,2,1,0:T(8,128)} %all-to-all-done.4.carried, f32[66,128]{1,0:T(8,128)} %copy-done.19, f32[66,128]{1,0:T(8,128)} %copy-done.20, f32[64,128,128]{2,1,0:T(8,128)} %vol.5, ...), custom_call_target="tpu_custom_call" | custom-call | flops 80000000 | bytes 356515 | tf_op jit(solution)/shard_map/reaction/pallas_call | solution.py:520
  371.9 24.3 %collective-permute-done.14.refs_1_ = f32[16,128,128]{2,1,0:T(8,128)S(1)} collective-permute-done((f32[16,128,128]{2,1,0:T(8,128)}, f32[16,128,128]{2,1,0:T(8,128)S(1)}, u32[]{:S(2)}, u32[]{:S(2)}) %collective-permute-start.14) | collective-permute-done | bytes 1048608 | tf_op jit(solution)/shard_map/ppermute | solution.py:791
  396.2 18.9 %collective-permute-done.15.refs_3_ = f32[16,128,128]{2,1,0:T(8,128)S(1)} collective-permute-done((f32[16,128,128]{2,1,0:T(8,128)}, f32[16,128,128]{2,1,0:T(8,128)S(1)}, u32[]{:S(2)}, u32[]{:S(2)}) %collective-permute-start.15) | collective-permute-done | bytes 1048608 | tf_op jit(solution)/shard_map/ppermute | solution.py:791
  417.1 45.0 %collective-permute-done.16.refs_2_ = f32[16,128,128]{2,1,0:T(8,128)S(1)} collective-permute-done((f32[16,128,128]{2,1,0:T(8,128)}, f32[16,128,128]{2,1,0:T(8,128)S(1)}, u32[]{:S(2)}, u32[]{:S(2)}) %collective-permute-start.16) | collective-permute-done | bytes 1048608 | tf_op jit(solution)/shard_map/ppermute | solution.py:791
  463.1 12.2 %second.4 = (f32[8,16,16,128]{3,2,1,0:T(8,128)}, f32[8,16,16,128]{3,2,1,0:T(8,128)}, f32[8,16,16,128]{3,2,1,0:T(8,128)}, f32[8,16,16,128]{3,2,1,0:T(8,128)}) custom-call(f32[16,128,128]{2,1,0:T(8,128)} %get-tuple-element.82.refs_0_, f32[16,128,128]{2,1,0:T(8,128)} %copy-done.10, f32[16,128,128]{2,1,0:T(8,128)} %copy-done.12, f32[16,128,128]{2,1,0:T(8,128)} %copy-done.11, ...), custom_call_target="tpu_custom_call" | custom-call | flops 180000000 | bytes 209715 | tf_op jit(solution)/shard_map/second/pallas_call | solution.py:415
  479.1 24.3 %collective-permute-done.17.refs_7_ = f32[8,16,16,128]{3,2,1,0:T(8,128)S(1)} collective-permute-done((f32[8,16,16,128]{3,2,1,0:T(8,128)}, f32[8,16,16,128]{3,2,1,0:T(8,128)S(1)}, u32[]{:S(2)}, u32[]{:S(2)}) %collective-permute-start.17) | collective-permute-done | bytes 1048608 | tf_op jit(solution)/shard_map/ppermute | solution.py:791
  503.4 19.0 %collective-permute-done.18.refs_5_ = f32[8,16,16,128]{3,2,1,0:T(8,128)S(1)} collective-permute-done((f32[8,16,16,128]{3,2,1,0:T(8,128)}, f32[8,16,16,128]{3,2,1,0:T(8,128)S(1)}, u32[]{:S(2)}, u32[]{:S(2)}) %collective-permute-start.18) | collective-permute-done | bytes 1048608 | tf_op jit(solution)/shard_map/ppermute | solution.py:791
  545.6 15.7 %collective-permute-done.20.refs_1_ = f32[18,128,128]{2,1,0:T(8,128)} collective-permute-done((f32[18,128,128]{2,1,0:T(8,128)}, f32[18,128,128]{2,1,0:T(8,128)}, u32[]{:S(2)}, u32[]{:S(2)}) %collective-permute-start.20) | collective-permute-done | bytes 1179680 | tf_op jit(solution)/shard_map/ppermute | solution.py:791
  561.3 13.3 %second.5.field = f32[18,512,128]{2,1,0:T(8,128)} custom-call(f32[18,128,128]{2,1,0:T(8,128)} %get-tuple-element.94.refs_0_, f32[18,128,128]{2,1,0:T(8,128)} %collective-permute-done.20.refs_1_, f32[18,128,128]{2,1,0:T(8,128)} %collective-permute-done.11.refs_2_, f32[18,128,128]{2,1,0:T(8,128)} %collective-permute-done.10.refs_3_, ...), custom_call_target="tpu_custom_call" | custom-call | flops 180000000 | bytes 209715 | tf_op jit(solution)/shard_map/second/pallas_call | solution.py:415
  574.7 10.2 %mixed.1 = (f32[16,128,128]{2,1,0:T(8,128)}, f32[16,128,128]{2,1,0:T(8,128)}, f32[16,128,128]{2,1,0:T(8,128)}, f32[16,128,128]{2,1,0:T(8,128)}) custom-call(s32[1]{0:T(128)} %bitcast.i, f32[18,512,128]{2,1,0:T(8,128)} %second.5.field), custom_call_target="tpu_custom_call" | custom-call | flops 80000000 | bytes 188743 | tf_op jit(solution)/shard_map/mixed/pallas_call | solution.py:599
  584.8 43.4 %collective-permute-done.19.refs_6_ = f32[8,16,16,128]{3,2,1,0:T(8,128)} collective-permute-done((f32[8,16,16,128]{3,2,1,0:T(8,128)}, f32[8,16,16,128]{3,2,1,0:T(8,128)}, u32[]{:S(2)}, u32[]{:S(2)}) %collective-permute-start.19) | collective-permute-done | bytes 1048608 | tf_op jit(solution)/shard_map/ppermute | solution.py:791
  628.2 19.6 %all_to_all.49 = f32[8,16,16,128]{3,2,1,0:T(8,128)} all-to-all(f32[8,16,16,128]{3,2,1,0:T(8,128)} %collective-permute-done.19.refs_6_), channel_id=1, replica_groups=mesh['wide'=8,'narrow'=4] {'wide'}, dimensions={0} | all-to-all | bytes 2097152 | tf_op jit(solution)/shard_map/all_to_all | solution.py:804
  647.9 8.5 %first.5 = f32[528,16,128]{2,1,0:T(8,128)} custom-call(f32[384,16,128]{2,1,0:T(8,128)} %bitcast.119, f32[128,16,128]{2,1,0:T(8,128)} %bitcast.121, bf16[512,1536]{1,0:T(8,128)(2,1)} %pad_maximum_fusion.4.refs_2_), custom_call_target="tpu_custom_call" | custom-call | flops 140000000 | bytes 209715 | tf_op jit(solution)/shard_map/first/pallas_call | solution.py:373
  680.1 11.1 %lines.1.tail = f32[64,128,128]{2,1,0:T(8,128)} custom-call(s32[1]{0:T(128)} %bitcast.i, f32[16,128,128]{2,1,0:T(8,128)} %get-tuple-element.82.refs_0_, f32[16,128,128]{2,1,0:T(8,128)} %get-tuple-element.83.refs_1_, f32[16,128,128]{2,1,0:T(8,128)} %get-tuple-element.86.refs_2_, f32[16,128,128]{2,1,0:T(8,128)} %get-tuple-element.85.refs_3_, ...), custom_call_target="tpu_custom_call" | custom-call | flops 100000000 | bytes 356515 | tf_op jit(solution)/shard_map/lines/pallas_call | solution.py:564
  691.2 20.5 %all-to-all-done.7.start.refs_6_ = f32[8,66,16,128]{3,2,1,0:T(8,128)} async-done(((f32[8,66,16,128]{3,2,1,0:T(8,128)}), f32[8,66,16,128]{3,2,1,0:T(8,128)}, u32[]{:S(2)}, u32[]{:S(2)}) %all-to-all-start.7) | async-done | bytes 4325408 | tf_op jit(solution)/shard_map/all_to_all | solution.py:804
  718.9 24.8 %frozen.1 = (f32[64,128,128]{2,1,0:T(8,128)}, f32[24,256]{1,0:T(8,128)}) custom-call(s32[1]{0:T(128)} %bitcast.i, f32[64,128,128]{2,1,0:T(8,128)} %after.6, f32[64,128,128]{2,1,0:T(8,128)} %after.6, f32[64,128,128]{2,1,0:T(8,128)} %after.6, f32[1,128,128]{2,1,0:T(8,128)} %bitcast.129, f32[1,128,128]{2,1,0:T(8,128)} %bitcast.132, f32[66,128]{1,0:T(8,128)} %fusion.1.q_low, ...), custom_call_target="tpu_custom_call" | custom-call | flops 100000000 | bytes 356515 | tf_op jit(solution)/shard_map/frozen/pallas_call | solution.py:664
  744.7 12.6 %column.1 = f32[24,256]{1,0:T(8,128)} custom-call(s32[1]{0:T(128)} %bitcast.i, f32[16,128,128]{2,1,0:T(8,128)} %get-tuple-element.105.refs_0_, f32[16,128,128]{2,1,0:T(8,128)} %collective-permute-done.22.refs_1_, f32[16,128,128]{2,1,0:T(8,128)} %copy-done.13, f32[16,128,128]{2,1,0:T(8,128)} %collective-permute-done.21.refs_3_, ...), custom_call_target="tpu_custom_call" | custom-call | flops 80000000 | bytes 356515 | tf_op jit(solution)/shard_map/column/pallas_call | solution.py:710
  761.8 12.3 %adjoint.1 = f32[64,128,128]{2,1,0:T(8,128)} custom-call(s32[1]{0:T(128)} %bitcast.i, f32[8,66,16,128]{3,2,1,0:T(8,128)} %all-to-all-done.7.start.refs_6_, f32[66,128]{1,0:T(8,128)} %copy-done.17, f32[66,128]{1,0:T(8,128)} %copy-done.18, f32[64,128,128]{2,1,0:T(8,128)} %vol.5, f32[64,128,128]{2,1,0:T(8,128)} %vol.5, f32[64,128,128]{2,1,0:T(8,128)} %vol.5, ...), custom_call_target="tpu_custom_call" | custom-call | flops 100000000 | bytes 356515 | tf_op jit(solution)/shard_map/adjoint/pallas_call | solution.py:757
  (182 shorter events, 157.3 us)
Async XLA Ops:
  2.5 13.5 %collective-permute-start.1 = (f32[2,128,128]{2,0,1:T(2,128)S(1)}, f32[2,128,128]{2,0,1:T(2,128)S(1)}, u32[]{:S(2)}, u32[]{:S(2)}) collective-permute-start(f32[2,128,128]{2,0,1:T(2,128)S(1)} %pad_maximum_fusion.9), channel_id=1, source_target_pairs={{4,0},{8,4},{12,8},{16,12},{20,16},{24,20},{28,24},{5,1},{9,5},{13... | collective-permute-start | bytes 393224 | tf_op jit(solution)/shard_map/ppermute | solution.py:779
  4.0 12.1 %collective-permute-start = (f32[2,128,128]{2,0,1:T(2,128)S(1)}, f32[2,128,128]{2,0,1:T(2,128)S(1)}, u32[]{:S(2)}, u32[]{:S(2)}) collective-permute-start(f32[2,128,128]{2,0,1:T(2,128)S(1)} %pad_maximum_fusion.8), channel_id=1, source_target_pairs={{0,4},{4,8},{8,12},{12,16},{16,20},{20,24},{24,28},{1,5},{5,9},{9,... | collective-permute-start | bytes 393224 | tf_op jit(solution)/shard_map/ppermute | solution.py:779
  16.1 10.2 %collective-permute-start.2 = (f32[2,66,128]{2,1,0:T(8,128)S(1)}, f32[2,66,128]{2,1,0:T(8,128)S(1)}, u32[]{:S(2)}, u32[]{:S(2)}) collective-permute-start(f32[2,66,128]{2,1,0:T(8,128)S(1)} %get-tuple-element.152), channel_id=1, source_target_pairs={{0,1},{1,2},{2,3},{4,5},{5,6},{6,7},{8,9},{9,10},{10,11},{12,13},{... | collective-permute-start | bytes 202760 | tf_op jit(solution)/shard_map/ppermute | solution.py:779
  21.1 6.9 collective-permute-start.3
  28.0 27.0 %collective-permute-start.4 = (f32[16,128,128]{2,1,0:T(8,128)S(1)}, f32[16,128,128]{2,1,0:T(8,128)S(1)}, u32[]{:S(2)}, u32[]{:S(2)}) collective-permute-start(f32[16,128,128]{2,1,0:T(8,128)S(1)} %get-tuple-element.57), channel_id=1, source_target_pairs={{0,1},{1,2},{2,3},{3,0},{4,5},{5,6},{6,7},{7,4},{8,9},{9,10},{10,1... | collective-permute-start | bytes 3145736 | tf_op jit(solution)/shard_map/ppermute | solution.py:791
  56.0 53.8 %all-to-all-start = ((f32[8,64,16,128]{3,2,1,0:T(8,128)}), f32[8,64,16,128]{3,2,1,0:T(8,128)}, u32[]{:S(2)}, u32[]{:S(2)}) async-start(f32[8,64,16,128]{3,2,1,0:T(8,128)} %get-tuple-element.61), calls=%async_computation | async-start | bytes 8388608 | tf_op jit(solution)/shard_map/all_to_all | solution.py:804
  60.7 25.8 %collective-permute-start.5 = (f32[16,128,128]{2,1,0:T(8,128)}, f32[16,128,128]{2,1,0:T(8,128)}, u32[]{:S(2)}, u32[]{:S(2)}) collective-permute-start(f32[16,128,128]{2,1,0:T(8,128)} %get-tuple-element.58), channel_id=1, source_target_pairs={{0,3},{1,0},{2,1},{3,2},{4,7},{5,4},{6,5},{7,6},{8,11},{9,8},{10,9... | collective-permute-start | bytes 3145736 | tf_op jit(solution)/shard_map/ppermute | solution.py:791
  86.4 48.2 %collective-permute-start.6 = (f32[16,128,128]{2,1,0:T(8,128)}, f32[16,128,128]{2,1,0:T(8,128)S(1)}, u32[]{:S(2)}, u32[]{:S(2)}) collective-permute-start(f32[16,128,128]{2,1,0:T(8,128)} %get-tuple-element.59), channel_id=1, source_target_pairs={{0,2},{1,3},{2,0},{3,1},{4,6},{5,7},{6,4},{7,5},{8,10},{9,11},{10,... | collective-permute-start | bytes 3145736 | tf_op jit(solution)/shard_map/ppermute | solution.py:791
  135.6 68.2 %all-to-all-start.1 = ((f32[8,66,16,128]{3,2,1,0:T(8,128)}), f32[8,66,16,128]{3,2,1,0:T(8,128)}, u32[]{:S(2)}, u32[]{:S(2)}) async-start(f32[8,66,16,128]{3,2,1,0:T(8,128)} %bitcast.117), calls=%async_computation.1 | async-start | bytes 8650752 | tf_op jit(solution)/shard_map/all_to_all | solution.py:804
  152.4 28.1 %collective-permute-start.7 = (f32[8,16,16,128]{3,2,1,0:T(8,128)}, f32[8,16,16,128]{3,2,1,0:T(8,128)S(1)}, u32[]{:S(2)}, u32[]{:S(2)}) collective-permute-start(f32[8,16,16,128]{3,2,1,0:T(8,128)} %get-tuple-element.68), channel_id=1, source_target_pairs={{0,1},{1,2},{2,3},{3,0},{4,5},{5,6},{6,7},{7,4},{8,9},{9,10},{10,1... | collective-permute-start | bytes 3145736 | tf_op jit(solution)/shard_map/ppermute | solution.py:791
  152.4 48.2 %collective-permute-start.8 = (f32[8,16,16,128]{3,2,1,0:T(8,128)}, f32[8,16,16,128]{3,2,1,0:T(8,128)S(1)}, u32[]{:S(2)}, u32[]{:S(2)}) collective-permute-start(f32[8,16,16,128]{3,2,1,0:T(8,128)} %get-tuple-element.69), channel_id=1, source_target_pairs={{0,3},{1,0},{2,1},{3,2},{4,7},{5,4},{6,5},{7,6},{8,11},{9,8},{10,9... | collective-permute-start | bytes 3145736 | tf_op jit(solution)/shard_map/ppermute | solution.py:791
  203.8 55.5 %all-to-all-start.2 = ((f32[8,48,16,128]{3,2,1,0:T(8,128)}), f32[8,48,16,128]{3,2,1,0:T(8,128)}, u32[]{:S(2)}, u32[]{:S(2)}) async-start(f32[8,48,16,128]{3,2,1,0:T(8,128)} %pad_maximum_fusion), calls=%async_computation.2 | async-start | bytes 6291456 | tf_op jit(solution)/shard_map/all_to_all | solution.py:804
  208.4 48.9 %collective-permute-start.9 = (f32[8,16,16,128]{3,2,1,0:T(8,128)S(1)}, f32[8,16,16,128]{3,2,1,0:T(8,128)}, u32[]{:S(2)}, u32[]{:S(2)}) collective-permute-start(f32[8,16,16,128]{3,2,1,0:T(8,128)S(1)} %copy-done.26), channel_id=1, source_target_pairs={{0,2},{1,3},{2,0},{3,1},{4,6},{5,7},{6,4},{7,5},{8,10},{9,11},{10,... | collective-permute-start | bytes 3145736 | tf_op jit(solution)/shard_map/ppermute | solution.py:791
  257.3 30.8 %collective-permute-start.10 = (f32[18,128,128]{2,1,0:T(8,128)}, f32[18,128,128]{2,1,0:T(8,128)}, u32[]{:S(2)}, u32[]{:S(2)}) collective-permute-start(f32[18,128,128]{2,1,0:T(8,128)} %get-tuple-element.78), channel_id=1, source_target_pairs={{0,3},{1,0},{2,1},{3,2},{4,7},{5,4},{6,5},{7,6},{8,11},{9,8},{10,9... | collective-permute-start | bytes 3538952 | tf_op jit(solution)/shard_map/ppermute | solution.py:791
  259.3 19.3 %all-to-all-start.3 = ((f32[8,16,16,128]{3,2,1,0:T(8,128)}), f32[8,16,16,128]{3,2,1,0:T(8,128)S(1)}, u32[]{:S(2)}, u32[]{:S(2)}) async-start(f32[8,16,16,128]{3,2,1,0:T(8,128)} %collective-permute-done.9), calls=%async_computation.3 | async-start | bytes 2097152 | tf_op jit(solution)/shard_map/all_to_all | solution.py:804
  288.0 58.7 %all-to-all-start.4 = ((f32[8,66,16,128]{3,2,1,0:T(8,128)}), f32[8,66,16,128]{3,2,1,0:T(8,128)}, u32[]{:S(2)}, u32[]{:S(2)}) async-start(f32[8,66,16,128]{3,2,1,0:T(8,128)} %bitcast.118), calls=%async_computation.4 | async-start | bytes 8650752 | tf_op jit(solution)/shard_map/all_to_all | solution.py:804
  292.8 54.0 %collective-permute-start.11 = (f32[18,128,128]{2,1,0:T(8,128)S(1)}, f32[18,128,128]{2,1,0:T(8,128)}, u32[]{:S(2)}, u32[]{:S(2)}) collective-permute-start(f32[18,128,128]{2,1,0:T(8,128)S(1)} %copy-done.24), channel_id=1, source_target_pairs={{0,2},{1,3},{2,0},{3,1},{4,6},{5,7},{6,4},{7,5},{8,10},{9,11},{10,... | collective-permute-start | bytes 3538952 | tf_op jit(solution)/shard_map/ppermute | solution.py:791
  368.0 28.2 %collective-permute-start.14 = (f32[16,128,128]{2,1,0:T(8,128)}, f32[16,128,128]{2,1,0:T(8,128)S(1)}, u32[]{:S(2)}, u32[]{:S(2)}) collective-permute-start(f32[16,128,128]{2,1,0:T(8,128)} %get-tuple-element.83.refs_1_), channel_id=1, source_target_pairs={{0,1},{1,2},{2,3},{3,0},{4,5},{5,6},{6,7},{7,4},{8,9},{9,10},{10,1... | collective-permute-start | bytes 3145736 | tf_op jit(solution)/shard_map/ppermute | solution.py:791
  369.1 45.9 %collective-permute-start.15 = (f32[16,128,128]{2,1,0:T(8,128)}, f32[16,128,128]{2,1,0:T(8,128)S(1)}, u32[]{:S(2)}, u32[]{:S(2)}) collective-permute-start(f32[16,128,128]{2,1,0:T(8,128)} %get-tuple-element.85.refs_3_), channel_id=1, source_target_pairs={{0,3},{1,0},{2,1},{3,2},{4,7},{5,4},{6,5},{7,6},{8,11},{9,8},{10,9... | collective-permute-start | bytes 3145736 | tf_op jit(solution)/shard_map/ppermute | solution.py:791
  415.1 47.1 %collective-permute-start.16 = (f32[16,128,128]{2,1,0:T(8,128)}, f32[16,128,128]{2,1,0:T(8,128)S(1)}, u32[]{:S(2)}, u32[]{:S(2)}) collective-permute-start(f32[16,128,128]{2,1,0:T(8,128)} %get-tuple-element.86.refs_2_), channel_id=1, source_target_pairs={{0,2},{1,3},{2,0},{3,1},{4,6},{5,7},{6,4},{7,5},{8,10},{9,11},{10,... | collective-permute-start | bytes 3145736 | tf_op jit(solution)/shard_map/ppermute | solution.py:791
  475.3 28.1 %collective-permute-start.17 = (f32[8,16,16,128]{3,2,1,0:T(8,128)}, f32[8,16,16,128]{3,2,1,0:T(8,128)S(1)}, u32[]{:S(2)}, u32[]{:S(2)}) collective-permute-start(f32[8,16,16,128]{3,2,1,0:T(8,128)} %get-tuple-element.88), channel_id=1, source_target_pairs={{0,1},{1,2},{2,3},{3,0},{4,5},{5,6},{6,7},{7,4},{8,9},{9,10},{10,1... | collective-permute-start | bytes 3145736 | tf_op jit(solution)/shard_map/ppermute | solution.py:791
  475.3 47.1 %collective-permute-start.18 = (f32[8,16,16,128]{3,2,1,0:T(8,128)}, f32[8,16,16,128]{3,2,1,0:T(8,128)S(1)}, u32[]{:S(2)}, u32[]{:S(2)}) collective-permute-start(f32[8,16,16,128]{3,2,1,0:T(8,128)} %get-tuple-element.89), channel_id=1, source_target_pairs={{0,3},{1,0},{2,1},{3,2},{4,7},{5,4},{6,5},{7,6},{8,11},{9,8},{10,9... | collective-permute-start | bytes 3145736 | tf_op jit(solution)/shard_map/ppermute | solution.py:791
  526.5 101.8 %all-to-all-start.5 = ((f32[8,48,16,128]{3,2,1,0:T(8,128)}), f32[8,48,16,128]{3,2,1,0:T(8,128)S(1)}, u32[]{:S(2)}, u32[]{:S(2)}) async-start(f32[8,48,16,128]{3,2,1,0:T(8,128)} %pad_maximum_fusion.1), calls=%async_computation.5 | async-start | bytes 6291456 | tf_op jit(solution)/shard_map/all_to_all | solution.py:804
  530.3 31.0 %collective-permute-start.20 = (f32[18,128,128]{2,1,0:T(8,128)}, f32[18,128,128]{2,1,0:T(8,128)}, u32[]{:S(2)}, u32[]{:S(2)}) collective-permute-start(f32[18,128,128]{2,1,0:T(8,128)} %get-tuple-element.93), channel_id=1, source_target_pairs={{0,1},{1,2},{2,3},{3,0},{4,5},{5,6},{6,7},{7,4},{8,9},{9,10},{10,1... | collective-permute-start | bytes 3538952 | tf_op jit(solution)/shard_map/ppermute | solution.py:791
  532.1 96.1 %collective-permute-start.19 = (f32[8,16,16,128]{3,2,1,0:T(8,128)}, f32[8,16,16,128]{3,2,1,0:T(8,128)}, u32[]{:S(2)}, u32[]{:S(2)}) collective-permute-start(f32[8,16,16,128]{3,2,1,0:T(8,128)} %get-tuple-element.91), channel_id=1, source_target_pairs={{0,2},{1,3},{2,0},{3,1},{4,6},{5,7},{6,4},{7,5},{8,10},{9,11},{10,... | collective-permute-start | bytes 3145736 | tf_op jit(solution)/shard_map/ppermute | solution.py:791
  584.8 71.6 %collective-permute-start.21 = (f32[16,128,128]{2,1,0:T(8,128)}, f32[16,128,128]{2,1,0:T(8,128)}, u32[]{:S(2)}, u32[]{:S(2)}) collective-permute-start(f32[16,128,128]{2,1,0:T(8,128)} %get-tuple-element.99), channel_id=1, source_target_pairs={{0,1},{1,2},{2,3},{3,0},{4,5},{5,6},{6,7},{7,4},{8,9},{9,10},{10,1... | collective-permute-start | bytes 3145736 | tf_op jit(solution)/shard_map/ppermute | solution.py:791
  628.2 28.2 %collective-permute-start.22 = (f32[16,128,128]{2,1,0:T(8,128)}, f32[16,128,128]{2,1,0:T(8,128)}, u32[]{:S(2)}, u32[]{:S(2)}) collective-permute-start(f32[16,128,128]{2,1,0:T(8,128)} %get-tuple-element.101), channel_id=1, source_target_pairs={{0,3},{1,0},{2,1},{3,2},{4,7},{5,4},{6,5},{7,6},{8,11},{9,8},{10,9... | collective-permute-start | bytes 3145736 | tf_op jit(solution)/shard_map/ppermute | solution.py:791
  656.4 55.2 %all-to-all-start.7 = ((f32[8,66,16,128]{3,2,1,0:T(8,128)}), f32[8,66,16,128]{3,2,1,0:T(8,128)}, u32[]{:S(2)}, u32[]{:S(2)}) async-start(f32[8,66,16,128]{3,2,1,0:T(8,128)} %bitcast.116), calls=%async_computation.7 | async-start | bytes 8650752 | tf_op jit(solution)/shard_map/all_to_all | solution.py:804
  672.8 71.0 %collective-permute-start.27 = (f32[16,128,128]{2,1,0:T(8,128)S(1)}, f32[16,128,128]{2,1,0:T(8,128)S(1)}, u32[]{:S(2)}, u32[]{:S(2)}) collective-permute-start(f32[16,128,128]{2,1,0:T(8,128)S(1)} %copy-done.25), channel_id=1, source_target_pairs={{0,2},{1,3},{2,0},{3,1},{4,6},{5,7},{6,4},{7,5},{8,10},{9,11},{10,... | collective-permute-start | bytes 3145736 | tf_op jit(solution)/shard_map/ppermute | solution.py:791
  712.8 30.9 %collective-permute-start.25 = (f32[66,128]{1,0:T(8,128)S(1)}, f32[66,128]{1,0:T(8,128)S(1)}, u32[]{:S(2)}, u32[]{:S(2)}) collective-permute-start(f32[66,128]{1,0:T(8,128)S(1)} %bitcast.143), channel_id=1, source_target_pairs={{0,1},{1,2},{2,3},{4,5},{5,6},{6,7},{8,9},{9,10},{10,11},{12,13},{... | collective-permute-start | bytes 101384 | tf_op jit(solution)/shard_map/ppermute | solution.py:779
  716.7 27.0 %collective-permute-start.26 = (f32[66,128]{1,0:T(8,128)S(1)}, f32[66,128]{1,0:T(8,128)S(1)}, u32[]{:S(2)}, u32[]{:S(2)}) collective-permute-start(f32[66,128]{1,0:T(8,128)S(1)} %bitcast.144), channel_id=1, source_target_pairs={{1,0},{2,1},{3,2},{5,4},{6,5},{7,6},{9,8},{10,9},{11,10},{13,12},{... | collective-permute-start | bytes 101384 | tf_op jit(solution)/shard_map/ppermute | solution.py:779
  758.8 15.3 %all-to-all-start.8 = ((f32[32,1,96]{2,1,0:T(1,128)}), f32[32,1,96]{2,1,0:T(1,128)S(1)}, u32[]{:S(2)}, u32[]{:S(2)}) async-start(f32[32,1,96]{2,1,0:T(1,128)} %bitcast.61), calls=%async_computation.8 | async-start | bytes 32768 | tf_op jit(solution)/shard_map/all_to_all | solution.py:933
  (31 other events, 366.9 us)

commit v6 on v5

--- a/solution.py
+++ b/solution.py
@@ -887,7 +887,7 @@
     total_lines = send(totals, near)
     total_lines = send(total_lines, far, *pick(total_lines, near))
 
-    uppers = second(total_lines, second_t3, third_t3, wide)
+    uppers = second(after(total_lines, *pick(level_lines, early)), second_t3, third_t3, wide)
     level = second(after(level_lines, uppers), second_n3, third_n3, 0)[0]
     drift_pieces = mix(index, level, n)
 
@@ -911,7 +911,7 @@
         groups,
     )
 
-    uppers, start_chunks, gone = cross_both(uppers, (), (), near, far)
+    uppers, start_chunks, gone = cross_both(uppers, drift_pieces, (sums,), near, far)
     drifts = send(drift_pieces, early, *pick(uppers, near))
     start_lines = first(start_chunks, first_t3, 1)
     drifts = send(drifts, late, gone)

time: 778 us -> 778 us (level)
  transfers between devices with their start and end apart: 36 -> 36, of which waited for: 21 -> 22; matrix products, arithmetic and copies ran while one was open for 6% -> 6% of each run, Pallas kernels for 17% -> 17%
where the time goes in v6:
time: 778 us; the launch traced here: 775 us
  waiting for transfers between devices  440 us (57%)
  Pallas kernels  167 us (21%)
  starting transfers between devices  84.4 us (11%)
  local copies, waits for them, and re-layouts  43 us (6%)
  blocking collectives  19.6 us (3%)
  other arithmetic  14.9 us (2%)
    ppermute x18, waiting for transfers between devices, send(): lax.ppermute(piece, 'narrow', [(k, (k + d) % n) for k in range(n)])  369 us
    all_to_all x7, waiting for transfers between devices, across(): lax.all_to_all(piece, 'wide', split_axis=0, concat_axis=0, tiled=True)  56.9 us
    pallas_call x3, Pallas kernels, second(): pl.pallas_call(functools.partial(second_kernel, count=count, chunked=bool...  37.7 us
    all_to_all x7, starting transfers between devices, across(): lax.all_to_all(piece, 'wide', split_axis=0, concat_axis=0, tiled=True)  31.1 us
    ppermute x18, starting transfers between devices, send(): lax.ppermute(piece, 'narrow', [(k, (k + d) % n) for k in range(n)])  26.1 us
    pallas_call x3, Pallas kernels, first(): pl.pallas_call(functools.partial(first_kernel, count=len(flat), lines=blo...  25.6 us
    pallas_call x1, Pallas kernels, frozen(): pl.pallas_call(functools.partial(frozen_kernel, blocks=blocks, groups=gro...  24.8 us
    all_to_all x1, blocking collectives, across(): lax.all_to_all(piece, 'wide', split_axis=0, concat_axis=0, tiled=True)  19.6 us
  transfers between devices with their start and end apart: 36, of which 22 were waited for; matrix products, arithmetic and copies ran while one was open for 6% of the time, Pallas kernels for 17%

profile of v6, /device:TPU:0, one launch (start us, length us, event | category | flops | bytes accessed | tf_op | source)
XLA Modules:
  0.0 775.2 jit_solution(16527310318132114853)
XLA Ops:
  17.2 5.6 collective-permute-start.2
  31.6 11.6 %forward.1 = (f32[8,64,16,128]{3,2,1,0:T(8,128)}, f32[64,128,128]{2,1,0:T(8,128)}) custom-call(s32[1]{0:T(128)} %bitcast.i, f32[64,128,128]{2,1,0:T(8,128)} %after.5, f32[64,128,128]{2,1,0:T(8,128)} %after.5, f32[64,128,128]{2,1,0:T(8,128)} %after.5, f32[1,128,128]{2,1,0:T(8,128)} %bitcast.130, f32[1,128,128]{2,1,0:T(8,128)} %bitcast.127, ...), custom_call_target="tpu_custom_call" | custom-call | flops 100000000 | bytes 356515 | tf_op jit(solution)/shard_map/forward/pallas_call | solution.py:308
  43.3 11.4 %collective-permute-done.4.refs_1_ = f32[16,128,128]{2,1,0:T(8,128)S(1)} collective-permute-done((f32[16,128,128]{2,1,0:T(8,128)S(1)}, f32[16,128,128]{2,1,0:T(8,128)S(1)}, u32[]{:S(2)}, u32[]{:S(2)}) %collective-permute-start.4) | collective-permute-done | bytes 1048608 | tf_op jit(solution)/shard_map/ppermute | solution.py:791
  64.4 21.7 %collective-permute-done.5.refs_3_ = f32[16,128,128]{2,1,0:T(8,128)} collective-permute-done((f32[16,128,128]{2,1,0:T(8,128)}, f32[16,128,128]{2,1,0:T(8,128)}, u32[]{:S(2)}, u32[]{:S(2)}) %collective-permute-start.5) | collective-permute-done | bytes 1048608 | tf_op jit(solution)/shard_map/ppermute | solution.py:791
  89.8 19.7 %all-to-all-done = f32[8,64,16,128]{3,2,1,0:T(8,128)} async-done(((f32[8,64,16,128]{3,2,1,0:T(8,128)}), f32[8,64,16,128]{3,2,1,0:T(8,128)}, u32[]{:S(2)}, u32[]{:S(2)}) %all-to-all-start) | async-done | bytes 4194336 | tf_op jit(solution)/shard_map/all_to_all | solution.py:804
  109.5 8.5 %first.3 = f32[528,16,128]{2,1,0:T(8,128)} custom-call(f32[512,16,128]{2,1,0:T(8,128)} %bitcast.19.refs_0_, bf16[512,1536]{1,0:T(8,128)(2,1)} %pad_maximum_fusion.2.refs_1_), custom_call_target="tpu_custom_call" | custom-call | flops 140000000 | bytes 209715 | tf_op jit(solution)/shard_map/first/pallas_call | solution.py:373
  118.0 16.0 %collective-permute-done.6.refs_2_ = f32[16,128,128]{2,1,0:T(8,128)S(1)} collective-permute-done((f32[16,128,128]{2,1,0:T(8,128)}, f32[16,128,128]{2,1,0:T(8,128)S(1)}, u32[]{:S(2)}, u32[]{:S(2)}) %collective-permute-start.6) | collective-permute-done | bytes 1048608 | tf_op jit(solution)/shard_map/ppermute | solution.py:791
  139.6 12.2 %second.3 = (f32[8,16,16,128]{3,2,1,0:T(8,128)}, f32[8,16,16,128]{3,2,1,0:T(8,128)}, f32[8,16,16,128]{3,2,1,0:T(8,128)}, f32[8,16,16,128]{3,2,1,0:T(8,128)}) custom-call(f32[16,128,128]{2,1,0:T(8,128)} %get-tuple-element.68.refs_0_, f32[16,128,128]{2,1,0:T(8,128)} %copy-done.9, f32[16,128,128]{2,1,0:T(8,128)} %copy-done.10, ...), custom_call_target="tpu_custom_call" | custom-call | flops 180000000 | bytes 209715 | tf_op jit(solution)/shard_map/second/pallas_call | solution.py:415
  155.7 24.2 %collective-permute-done.7 = f32[8,16,16,128]{3,2,1,0:T(8,128)S(1)} collective-permute-done((f32[8,16,16,128]{3,2,1,0:T(8,128)}, f32[8,16,16,128]{3,2,1,0:T(8,128)S(1)}, u32[]{:S(2)}, u32[]{:S(2)}) %collective-permute-start.7) | collective-permute-done | bytes 1048608 | tf_op jit(solution)/shard_map/ppermute | solution.py:791
  179.9 20.1 %collective-permute-done.8 = f32[8,16,16,128]{3,2,1,0:T(8,128)S(1)} collective-permute-done((f32[8,16,16,128]{3,2,1,0:T(8,128)}, f32[8,16,16,128]{3,2,1,0:T(8,128)S(1)}, u32[]{:S(2)}, u32[]{:S(2)}) %collective-permute-start.8) | collective-permute-done | bytes 1048608 | tf_op jit(solution)/shard_map/ppermute | solution.py:791
  210.2 8.9 %lifted.1 = (f32[18,128,128]{2,1,0:T(8,128)}, f32[18,128,128]{2,1,0:T(8,128)}, f32[18,128,128]{2,1,0:T(8,128)}, f32[18,128,128]{2,1,0:T(8,128)}) custom-call(s32[1]{0:T(128)} %bitcast.i, f32[8,66,16,128]{3,2,1,0:T(8,128)} %all-to-all-done.1.solved, f32[64,128,128]{2,1,0:T(8,128)} %after.5, f32[1,128,128]{2,1,0:T(8,128)} %bitcast.131, ...), custom_call_target="tpu_custom_call" | custom-call | flops 40000000 | bytes 272629 | tf_op jit(solution)/shard_map/lifted/pallas_call | solution.py:473
  219.1 37.6 %collective-permute-done.9 = f32[8,16,16,128]{3,2,1,0:T(8,128)} collective-permute-done((f32[8,16,16,128]{3,2,1,0:T(8,128)S(1)}, f32[8,16,16,128]{3,2,1,0:T(8,128)}, u32[]{:S(2)}, u32[]{:S(2)}) %collective-permute-start.9) | collective-permute-done | bytes 1048608 | tf_op jit(solution)/shard_map/ppermute | solution.py:791
  265.8 12.2 %all-to-all-done.3 = f32[8,16,16,128]{3,2,1,0:T(8,128)S(1)} async-done(((f32[8,16,16,128]{3,2,1,0:T(8,128)}), f32[8,16,16,128]{3,2,1,0:T(8,128)S(1)}, u32[]{:S(2)}, u32[]{:S(2)}) %all-to-all-start.3) | async-done | bytes 1048608 | tf_op jit(solution)/shard_map/all_to_all | solution.py:804
  279.0 8.5 %first.4 = f32[528,16,128]{2,1,0:T(8,128)} custom-call(f32[384,16,128]{2,1,0:T(8,128)} %bitcast.25.refs_0_, f32[128,16,128]{2,1,0:T(8,128)} %bitcast.120, bf16[512,1536]{1,0:T(8,128)(2,1)} %pad_maximum_fusion.4.refs_2_), custom_call_target="tpu_custom_call" | custom-call | flops 140000000 | bytes 209715 | tf_op jit(solution)/shard_map/first/pallas_call | solution.py:373
  292.3 53.9 %collective-permute-done.11.refs_2_ = f32[18,128,128]{2,1,0:T(8,128)} collective-permute-done((f32[18,128,128]{2,1,0:T(8,128)S(1)}, f32[18,128,128]{2,1,0:T(8,128)}, u32[]{:S(2)}, u32[]{:S(2)}) %collective-permute-start.11) | collective-permute-done | bytes 1179680 | tf_op jit(solution)/shard_map/ppermute | solution.py:791
  355.1 12.4 %reaction.1 = (f32[16,128,128]{2,1,0:T(8,128)}, f32[16,128,128]{2,1,0:T(8,128)}, f32[16,128,128]{2,1,0:T(8,128)}, f32[16,128,128]{2,1,0:T(8,128)}) custom-call(s32[1]{0:T(128)} %bitcast.i, f32[8,66,16,128]{3,2,1,0:T(8,128)} %all-to-all-done.4.carried, f32[66,128]{1,0:T(8,128)} %copy-done.20, f32[66,128]{1,0:T(8,128)} %copy-done.21, f32[64,128,128]{2,1,0:T(8,128)} %after.6, ...), custom_call_target="tpu_custom_call" | custom-call | flops 80000000 | bytes 356515 | tf_op jit(solution)/shard_map/reaction/pallas_call | solution.py:520
  371.4 24.3 %collective-permute-done.14.refs_1_ = f32[16,128,128]{2,1,0:T(8,128)S(1)} collective-permute-done((f32[16,128,128]{2,1,0:T(8,128)}, f32[16,128,128]{2,1,0:T(8,128)S(1)}, u32[]{:S(2)}, u32[]{:S(2)}) %collective-permute-start.14) | collective-permute-done | bytes 1048608 | tf_op jit(solution)/shard_map/ppermute | solution.py:791
  395.7 19.3 %collective-permute-done.15.refs_3_ = f32[16,128,128]{2,1,0:T(8,128)S(1)} collective-permute-done((f32[16,128,128]{2,1,0:T(8,128)}, f32[16,128,128]{2,1,0:T(8,128)S(1)}, u32[]{:S(2)}, u32[]{:S(2)}) %collective-permute-start.15) | collective-permute-done | bytes 1048608 | tf_op jit(solution)/shard_map/ppermute | solution.py:791
  418.9 24.7 %collective-permute-done.17.refs_1_ = f32[18,128,128]{2,1,0:T(8,128)} collective-permute-done((f32[18,128,128]{2,1,0:T(8,128)}, f32[18,128,128]{2,1,0:T(8,128)}, u32[]{:S(2)}, u32[]{:S(2)}) %collective-permute-start.17) | collective-permute-done | bytes 1179680 | tf_op jit(solution)/shard_map/ppermute | solution.py:791
  443.6 42.3 %collective-permute-done.16.refs_2_ = f32[16,128,128]{2,1,0:T(8,128)S(1)} collective-permute-done((f32[16,128,128]{2,1,0:T(8,128)}, f32[16,128,128]{2,1,0:T(8,128)S(1)}, u32[]{:S(2)}, u32[]{:S(2)}) %collective-permute-start.16) | collective-permute-done | bytes 1048608 | tf_op jit(solution)/shard_map/ppermute | solution.py:791
  486.9 12.2 %second.4 = (f32[8,16,16,128]{3,2,1,0:T(8,128)}, f32[8,16,16,128]{3,2,1,0:T(8,128)}, f32[8,16,16,128]{3,2,1,0:T(8,128)}, f32[8,16,16,128]{3,2,1,0:T(8,128)}) custom-call(f32[16,128,128]{2,1,0:T(8,128)} %get-tuple-element.93.refs_0_, f32[16,128,128]{2,1,0:T(8,128)} %copy-done.11, f32[16,128,128]{2,1,0:T(8,128)} %copy-done.13, f32[16,128,128]{2,1,0:T(8,128)} %copy-done.12, ...), custom_call_target="tpu_custom_call" | custom-call | flops 180000000 | bytes 209715 | tf_op jit(solution)/shard_map/second/pallas_call | solution.py:415
  514.2 13.3 %second.5.field = f32[18,512,128]{2,1,0:T(8,128)} custom-call(f32[18,128,128]{2,1,0:T(8,128)} %get-tuple-element.101.refs_0_, f32[18,128,128]{2,1,0:T(8,128)} %collective-permute-done.17.refs_1_, f32[18,128,128]{2,1,0:T(8,128)} %collective-permute-done.11.refs_2_, f32[18,128,128]{2,1,0:T(8,128)} %collective-permute-done.10.refs_3_, ...), custom_call_target="tpu_custom_call" | custom-call | flops 180000000 | bytes 209715 | tf_op jit(solution)/shard_map/second/pallas_call | solution.py:415
  527.5 10.2 %mixed.1 = (f32[16,128,128]{2,1,0:T(8,128)}, f32[16,128,128]{2,1,0:T(8,128)}, f32[16,128,128]{2,1,0:T(8,128)}, f32[16,128,128]{2,1,0:T(8,128)}) custom-call(s32[1]{0:T(128)} %bitcast.i, f32[18,512,128]{2,1,0:T(8,128)} %second.5.field), custom_call_target="tpu_custom_call" | custom-call | flops 80000000 | bytes 188743 | tf_op jit(solution)/shard_map/mixed/pallas_call | solution.py:599
  537.7 8.7 %collective-permute-done.19.refs_5_ = f32[8,16,16,128]{3,2,1,0:T(8,128)S(1)} collective-permute-done((f32[8,16,16,128]{3,2,1,0:T(8,128)}, f32[8,16,16,128]{3,2,1,0:T(8,128)S(1)}, u32[]{:S(2)}, u32[]{:S(2)}) %collective-permute-start.19) | collective-permute-done | bytes 1048608 | tf_op jit(solution)/shard_map/ppermute | solution.py:791
  558.6 64.9 %collective-permute-done.20.refs_6_ = f32[8,16,16,128]{3,2,1,0:T(8,128)} collective-permute-done((f32[8,16,16,128]{3,2,1,0:T(8,128)}, f32[8,16,16,128]{3,2,1,0:T(8,128)}, u32[]{:S(2)}, u32[]{:S(2)}) %collective-permute-start.20) | collective-permute-done | bytes 1048608 | tf_op jit(solution)/shard_map/ppermute | solution.py:791
  624.4 24.8 %frozen.1 = (f32[64,128,128]{2,1,0:T(8,128)}, f32[24,256]{1,0:T(8,128)}) custom-call(s32[1]{0:T(128)} %bitcast.i, f32[64,128,128]{2,1,0:T(8,128)} %after.5, f32[64,128,128]{2,1,0:T(8,128)} %after.5, f32[64,128,128]{2,1,0:T(8,128)} %after.5, f32[1,128,128]{2,1,0:T(8,128)} %bitcast.132, f32[1,128,128]{2,1,0:T(8,128)} %bitcast.129, f32[66,128]{1,0:T(8,128)} %fusion.1.q_low, ...), custom_call_target="tpu_custom_call" | custom-call | flops 100000000 | bytes 356515 | tf_op jit(solution)/shard_map/frozen/pallas_call | solution.py:664
  649.2 19.6 %all_to_all.49 = f32[8,16,16,128]{3,2,1,0:T(8,128)} all-to-all(f32[8,16,16,128]{3,2,1,0:T(8,128)} %collective-permute-done.20.refs_6_), channel_id=1, replica_groups=mesh['wide'=8,'narrow'=4] {'wide'}, dimensions={0} | all-to-all | bytes 2097152 | tf_op jit(solution)/shard_map/all_to_all | solution.py:804
  668.8 8.6 %first.5 = f32[528,16,128]{2,1,0:T(8,128)} custom-call(f32[384,16,128]{2,1,0:T(8,128)} %bitcast.119, f32[128,16,128]{2,1,0:T(8,128)} %bitcast.121, bf16[512,1536]{1,0:T(8,128)(2,1)} %pad_maximum_fusion.4.refs_2_), custom_call_target="tpu_custom_call" | custom-call | flops 140000000 | bytes 209715 | tf_op jit(solution)/shard_map/first/pallas_call | solution.py:373
  696.6 11.0 %lines.1.tail = f32[64,128,128]{2,1,0:T(8,128)} custom-call(s32[1]{0:T(128)} %bitcast.i, f32[16,128,128]{2,1,0:T(8,128)} %get-tuple-element.93.refs_0_, f32[16,128,128]{2,1,0:T(8,128)} %get-tuple-element.88.refs_1_, f32[16,128,128]{2,1,0:T(8,128)} %get-tuple-element.91.refs_2_, f32[16,128,128]{2,1,0:T(8,128)} %get-tuple-element.90.refs_3_, ...), custom_call_target="tpu_custom_call" | custom-call | flops 100000000 | bytes 356515 | tf_op jit(solution)/shard_map/lines/pallas_call | solution.py:564
  707.6 25.0 %all-to-all-done.7.start.refs_6_ = f32[8,66,16,128]{3,2,1,0:T(8,128)} async-done(((f32[8,66,16,128]{3,2,1,0:T(8,128)}), f32[8,66,16,128]{3,2,1,0:T(8,128)}, u32[]{:S(2)}, u32[]{:S(2)}) %all-to-all-start.7) | async-done | bytes 4325408 | tf_op jit(solution)/shard_map/all_to_all | solution.py:804
  745.3 12.6 %column.1 = f32[24,256]{1,0:T(8,128)} custom-call(s32[1]{0:T(128)} %bitcast.i, f32[16,128,128]{2,1,0:T(8,128)} %get-tuple-element.105.refs_0_, f32[16,128,128]{2,1,0:T(8,128)} %collective-permute-done.22.refs_1_, f32[16,128,128]{2,1,0:T(8,128)} %copy-done.14, f32[16,128,128]{2,1,0:T(8,128)} %collective-permute-done.21.refs_3_, ...), custom_call_target="tpu_custom_call" | custom-call | flops 80000000 | bytes 356515 | tf_op jit(solution)/shard_map/column/pallas_call | solution.py:710
  762.3 12.3 %adjoint.1 = f32[64,128,128]{2,1,0:T(8,128)} custom-call(s32[1]{0:T(128)} %bitcast.i, f32[8,66,16,128]{3,2,1,0:T(8,128)} %all-to-all-done.7.start.refs_6_, f32[66,128]{1,0:T(8,128)} %copy-done.18, f32[66,128]{1,0:T(8,128)} %copy-done.19, f32[64,128,128]{2,1,0:T(8,128)} %after.6, f32[64,128,128]{2,1,0:T(8,128)} %after.6, f32[64,128,128]{2,1,0:T(8,128)} %after.6, ...), custom_call_target="tpu_custom_call" | custom-call | flops 100000000 | bytes 356515 | tf_op jit(solution)/shard_map/adjoint/pallas_call | solution.py:757
  (184 shorter events, 153.1 us)
Async XLA Ops:
  2.5 13.3 %collective-permute-start.1 = (f32[2,128,128]{2,0,1:T(2,128)S(1)}, f32[2,128,128]{2,0,1:T(2,128)S(1)}, u32[]{:S(2)}, u32[]{:S(2)}) collective-permute-start(f32[2,128,128]{2,0,1:T(2,128)S(1)} %pad_maximum_fusion.9), channel_id=1, source_target_pairs={{4,0},{8,4},{12,8},{16,12},{20,16},{24,20},{28,24},{5,1},{9,5},{13... | collective-permute-start | bytes 393224 | tf_op jit(solution)/shard_map/ppermute | solution.py:779
  4.0 11.9 %collective-permute-start = (f32[2,128,128]{2,0,1:T(2,128)S(1)}, f32[2,128,128]{2,0,1:T(2,128)S(1)}, u32[]{:S(2)}, u32[]{:S(2)}) collective-permute-start(f32[2,128,128]{2,0,1:T(2,128)S(1)} %pad_maximum_fusion.8), channel_id=1, source_target_pairs={{0,4},{4,8},{8,12},{12,16},{16,20},{20,24},{24,28},{1,5},{5,9},{9,... | collective-permute-start | bytes 393224 | tf_op jit(solution)/shard_map/ppermute | solution.py:779
  15.9 10.9 %collective-permute-start.3 = (f32[2,66,128]{2,1,0:T(8,128)S(1)}, f32[2,66,128]{2,1,0:T(8,128)S(1)}, u32[]{:S(2)}, u32[]{:S(2)}) collective-permute-start(f32[2,66,128]{2,1,0:T(8,128)S(1)} %get-tuple-element.161), channel_id=1, source_target_pairs={{1,0},{2,1},{3,2},{5,4},{6,5},{7,6},{9,8},{10,9},{11,10},{13,12},{... | collective-permute-start | bytes 202760 | tf_op jit(solution)/shard_map/ppermute | solution.py:779
  17.2 9.6 %collective-permute-start.2 = (f32[2,66,128]{2,1,0:T(8,128)S(1)}, f32[2,66,128]{2,1,0:T(8,128)S(1)}, u32[]{:S(2)}, u32[]{:S(2)}) collective-permute-start(f32[2,66,128]{2,1,0:T(8,128)S(1)} %get-tuple-element.162), channel_id=1, source_target_pairs={{0,1},{1,2},{2,3},{4,5},{5,6},{6,7},{8,9},{9,10},{10,11},{12,13},{... | collective-permute-start | bytes 202760 | tf_op jit(solution)/shard_map/ppermute | solution.py:779
  26.8 27.9 %collective-permute-start.4 = (f32[16,128,128]{2,1,0:T(8,128)S(1)}, f32[16,128,128]{2,1,0:T(8,128)S(1)}, u32[]{:S(2)}, u32[]{:S(2)}) collective-permute-start(f32[16,128,128]{2,1,0:T(8,128)S(1)} %get-tuple-element.62), channel_id=1, source_target_pairs={{0,1},{1,2},{2,3},{3,0},{4,5},{5,6},{6,7},{7,4},{8,9},{9,10},{10,1... | collective-permute-start | bytes 3145736 | tf_op jit(solution)/shard_map/ppermute | solution.py:791
  55.7 53.8 %all-to-all-start = ((f32[8,64,16,128]{3,2,1,0:T(8,128)}), f32[8,64,16,128]{3,2,1,0:T(8,128)}, u32[]{:S(2)}, u32[]{:S(2)}) async-start(f32[8,64,16,128]{3,2,1,0:T(8,128)} %get-tuple-element.66), calls=%async_computation | async-start | bytes 8388608 | tf_op jit(solution)/shard_map/all_to_all | solution.py:804
  60.4 25.8 %collective-permute-start.5 = (f32[16,128,128]{2,1,0:T(8,128)}, f32[16,128,128]{2,1,0:T(8,128)}, u32[]{:S(2)}, u32[]{:S(2)}) collective-permute-start(f32[16,128,128]{2,1,0:T(8,128)} %get-tuple-element.63), channel_id=1, source_target_pairs={{0,3},{1,0},{2,1},{3,2},{4,7},{5,4},{6,5},{7,6},{8,11},{9,8},{10,9... | collective-permute-start | bytes 3145736 | tf_op jit(solution)/shard_map/ppermute | solution.py:791
  86.1 47.9 %collective-permute-start.6 = (f32[16,128,128]{2,1,0:T(8,128)}, f32[16,128,128]{2,1,0:T(8,128)S(1)}, u32[]{:S(2)}, u32[]{:S(2)}) collective-permute-start(f32[16,128,128]{2,1,0:T(8,128)} %get-tuple-element.64), channel_id=1, source_target_pairs={{0,2},{1,3},{2,0},{3,1},{4,6},{5,7},{6,4},{7,5},{8,10},{9,11},{10,... | collective-permute-start | bytes 3145736 | tf_op jit(solution)/shard_map/ppermute | solution.py:791
  135.0 68.2 %all-to-all-start.1 = ((f32[8,66,16,128]{3,2,1,0:T(8,128)}), f32[8,66,16,128]{3,2,1,0:T(8,128)}, u32[]{:S(2)}, u32[]{:S(2)}) async-start(f32[8,66,16,128]{3,2,1,0:T(8,128)} %bitcast.117), calls=%async_computation.1 | async-start | bytes 8650752 | tf_op jit(solution)/shard_map/all_to_all | solution.py:804
  151.8 28.1 %collective-permute-start.7 = (f32[8,16,16,128]{3,2,1,0:T(8,128)}, f32[8,16,16,128]{3,2,1,0:T(8,128)S(1)}, u32[]{:S(2)}, u32[]{:S(2)}) collective-permute-start(f32[8,16,16,128]{3,2,1,0:T(8,128)} %get-tuple-element.73), channel_id=1, source_target_pairs={{0,1},{1,2},{2,3},{3,0},{4,5},{5,6},{6,7},{7,4},{8,9},{9,10},{10,1... | collective-permute-start | bytes 3145736 | tf_op jit(solution)/shard_map/ppermute | solution.py:791
  151.8 48.2 %collective-permute-start.8 = (f32[8,16,16,128]{3,2,1,0:T(8,128)}, f32[8,16,16,128]{3,2,1,0:T(8,128)S(1)}, u32[]{:S(2)}, u32[]{:S(2)}) collective-permute-start(f32[8,16,16,128]{3,2,1,0:T(8,128)} %get-tuple-element.74), channel_id=1, source_target_pairs={{0,3},{1,0},{2,1},{3,2},{4,7},{5,4},{6,5},{7,6},{8,11},{9,8},{10,9... | collective-permute-start | bytes 3145736 | tf_op jit(solution)/shard_map/ppermute | solution.py:791
  203.2 55.5 %all-to-all-start.2 = ((f32[8,48,16,128]{3,2,1,0:T(8,128)}), f32[8,48,16,128]{3,2,1,0:T(8,128)}, u32[]{:S(2)}, u32[]{:S(2)}) async-start(f32[8,48,16,128]{3,2,1,0:T(8,128)} %pad_maximum_fusion), calls=%async_computation.2 | async-start | bytes 6291456 | tf_op jit(solution)/shard_map/all_to_all | solution.py:804
  207.8 48.9 %collective-permute-start.9 = (f32[8,16,16,128]{3,2,1,0:T(8,128)S(1)}, f32[8,16,16,128]{3,2,1,0:T(8,128)}, u32[]{:S(2)}, u32[]{:S(2)}) collective-permute-start(f32[8,16,16,128]{3,2,1,0:T(8,128)S(1)} %copy-done.27), channel_id=1, source_target_pairs={{0,2},{1,3},{2,0},{3,1},{4,6},{5,7},{6,4},{7,5},{8,10},{9,11},{10,... | collective-permute-start | bytes 3145736 | tf_op jit(solution)/shard_map/ppermute | solution.py:791
  256.7 30.8 %collective-permute-start.10 = (f32[18,128,128]{2,1,0:T(8,128)}, f32[18,128,128]{2,1,0:T(8,128)}, u32[]{:S(2)}, u32[]{:S(2)}) collective-permute-start(f32[18,128,128]{2,1,0:T(8,128)} %get-tuple-element.83), channel_id=1, source_target_pairs={{0,3},{1,0},{2,1},{3,2},{4,7},{5,4},{6,5},{7,6},{8,11},{9,8},{10,9... | collective-permute-start | bytes 3538952 | tf_op jit(solution)/shard_map/ppermute | solution.py:791
  258.7 19.3 %all-to-all-start.3 = ((f32[8,16,16,128]{3,2,1,0:T(8,128)}), f32[8,16,16,128]{3,2,1,0:T(8,128)S(1)}, u32[]{:S(2)}, u32[]{:S(2)}) async-start(f32[8,16,16,128]{3,2,1,0:T(8,128)} %collective-permute-done.9), calls=%async_computation.3 | async-start | bytes 2097152 | tf_op jit(solution)/shard_map/all_to_all | solution.py:804
  287.5 58.7 %all-to-all-start.4 = ((f32[8,66,16,128]{3,2,1,0:T(8,128)}), f32[8,66,16,128]{3,2,1,0:T(8,128)}, u32[]{:S(2)}, u32[]{:S(2)}) async-start(f32[8,66,16,128]{3,2,1,0:T(8,128)} %bitcast.118), calls=%async_computation.4 | async-start | bytes 8650752 | tf_op jit(solution)/shard_map/all_to_all | solution.py:804
  292.2 54.0 %collective-permute-start.11 = (f32[18,128,128]{2,1,0:T(8,128)S(1)}, f32[18,128,128]{2,1,0:T(8,128)}, u32[]{:S(2)}, u32[]{:S(2)}) collective-permute-start(f32[18,128,128]{2,1,0:T(8,128)S(1)} %copy-done.25), channel_id=1, source_target_pairs={{0,2},{1,3},{2,0},{3,1},{4,6},{5,7},{6,4},{7,5},{8,10},{9,11},{10,... | collective-permute-start | bytes 3538952 | tf_op jit(solution)/shard_map/ppermute | solution.py:791
  348.6 5.9 collective-permute-start.13
  367.5 28.2 %collective-permute-start.14 = (f32[16,128,128]{2,1,0:T(8,128)}, f32[16,128,128]{2,1,0:T(8,128)S(1)}, u32[]{:S(2)}, u32[]{:S(2)}) collective-permute-start(f32[16,128,128]{2,1,0:T(8,128)} %get-tuple-element.88.refs_1_), channel_id=1, source_target_pairs={{0,1},{1,2},{2,3},{3,0},{4,5},{5,6},{6,7},{7,4},{8,9},{9,10},{10,1... | collective-permute-start | bytes 3145736 | tf_op jit(solution)/shard_map/ppermute | solution.py:791
  368.6 46.4 %collective-permute-start.15 = (f32[16,128,128]{2,1,0:T(8,128)}, f32[16,128,128]{2,1,0:T(8,128)S(1)}, u32[]{:S(2)}, u32[]{:S(2)}) collective-permute-start(f32[16,128,128]{2,1,0:T(8,128)} %get-tuple-element.90.refs_3_), channel_id=1, source_target_pairs={{0,3},{1,0},{2,1},{3,2},{4,7},{5,4},{6,5},{7,6},{8,11},{9,8},{10,9... | collective-permute-start | bytes 3145736 | tf_op jit(solution)/shard_map/ppermute | solution.py:791
  371.4 72.2 %collective-permute-start.17 = (f32[18,128,128]{2,1,0:T(8,128)}, f32[18,128,128]{2,1,0:T(8,128)}, u32[]{:S(2)}, u32[]{:S(2)}) collective-permute-start(f32[18,128,128]{2,1,0:T(8,128)} %get-tuple-element.92), channel_id=1, source_target_pairs={{0,1},{1,2},{2,3},{3,0},{4,5},{5,6},{6,7},{7,4},{8,9},{9,10},{10,1... | collective-permute-start | bytes 3538952 | tf_op jit(solution)/shard_map/ppermute | solution.py:791
  415.0 70.9 %collective-permute-start.16 = (f32[16,128,128]{2,1,0:T(8,128)}, f32[16,128,128]{2,1,0:T(8,128)S(1)}, u32[]{:S(2)}, u32[]{:S(2)}) collective-permute-start(f32[16,128,128]{2,1,0:T(8,128)} %get-tuple-element.91.refs_2_), channel_id=1, source_target_pairs={{0,2},{1,3},{2,0},{3,1},{4,6},{5,7},{6,4},{7,5},{8,10},{9,11},{10,... | collective-permute-start | bytes 3145736 | tf_op jit(solution)/shard_map/ppermute | solution.py:791
  499.0 38.7 %collective-permute-start.18 = (f32[8,16,16,128]{3,2,1,0:T(8,128)}, f32[8,16,16,128]{3,2,1,0:T(8,128)S(1)}, u32[]{:S(2)}, u32[]{:S(2)}) collective-permute-start(f32[8,16,16,128]{3,2,1,0:T(8,128)} %get-tuple-element.98), channel_id=1, source_target_pairs={{0,1},{1,2},{2,3},{3,0},{4,5},{5,6},{6,7},{7,4},{8,9},{9,10},{10,1... | collective-permute-start | bytes 3145736 | tf_op jit(solution)/shard_map/ppermute | solution.py:791
  499.1 47.4 %collective-permute-start.19 = (f32[8,16,16,128]{3,2,1,0:T(8,128)}, f32[8,16,16,128]{3,2,1,0:T(8,128)S(1)}, u32[]{:S(2)}, u32[]{:S(2)}) collective-permute-start(f32[8,16,16,128]{3,2,1,0:T(8,128)} %get-tuple-element.99), channel_id=1, source_target_pairs={{0,3},{1,0},{2,1},{3,2},{4,7},{5,4},{6,5},{7,6},{8,11},{9,8},{10,9... | collective-permute-start | bytes 3145736 | tf_op jit(solution)/shard_map/ppermute | solution.py:791
  548.4 100.8 %all-to-all-start.5 = ((f32[8,48,16,128]{3,2,1,0:T(8,128)}), f32[8,48,16,128]{3,2,1,0:T(8,128)S(1)}, u32[]{:S(2)}, u32[]{:S(2)}) async-start(f32[8,48,16,128]{3,2,1,0:T(8,128)} %pad_maximum_fusion.1), calls=%async_computation.5 | async-start | bytes 6291456 | tf_op jit(solution)/shard_map/all_to_all | solution.py:804
  552.4 71.1 %collective-permute-start.20 = (f32[8,16,16,128]{3,2,1,0:T(8,128)}, f32[8,16,16,128]{3,2,1,0:T(8,128)}, u32[]{:S(2)}, u32[]{:S(2)}) collective-permute-start(f32[8,16,16,128]{3,2,1,0:T(8,128)} %get-tuple-element.110), channel_id=1, source_target_pairs={{0,2},{1,3},{2,0},{3,1},{4,6},{5,7},{6,4},{7,5},{8,10},{9,11},{10,... | collective-permute-start | bytes 3145736 | tf_op jit(solution)/shard_map/ppermute | solution.py:791
  558.4 119.0 %collective-permute-start.21 = (f32[16,128,128]{2,1,0:T(8,128)}, f32[16,128,128]{2,1,0:T(8,128)}, u32[]{:S(2)}, u32[]{:S(2)}) collective-permute-start(f32[16,128,128]{2,1,0:T(8,128)} %get-tuple-element.114), channel_id=1, source_target_pairs={{0,1},{1,2},{2,3},{3,0},{4,5},{5,6},{6,7},{7,4},{8,9},{9,10},{10,1... | collective-permute-start | bytes 3145736 | tf_op jit(solution)/shard_map/ppermute | solution.py:791
  623.5 53.9 %collective-permute-start.22 = (f32[16,128,128]{2,1,0:T(8,128)}, f32[16,128,128]{2,1,0:T(8,128)}, u32[]{:S(2)}, u32[]{:S(2)}) collective-permute-start(f32[16,128,128]{2,1,0:T(8,128)} %get-tuple-element.115), channel_id=1, source_target_pairs={{0,3},{1,0},{2,1},{3,2},{4,7},{5,4},{6,5},{7,6},{8,11},{9,8},{10,9... | collective-permute-start | bytes 3145736 | tf_op jit(solution)/shard_map/ppermute | solution.py:791
  677.4 55.2 %all-to-all-start.7 = ((f32[8,66,16,128]{3,2,1,0:T(8,128)}), f32[8,66,16,128]{3,2,1,0:T(8,128)}, u32[]{:S(2)}, u32[]{:S(2)}) async-start(f32[8,66,16,128]{3,2,1,0:T(8,128)} %bitcast.116), calls=%async_computation.7 | async-start | bytes 8650752 | tf_op jit(solution)/shard_map/all_to_all | solution.py:804
  696.0 48.3 %collective-permute-start.27 = (f32[16,128,128]{2,1,0:T(8,128)S(1)}, f32[16,128,128]{2,1,0:T(8,128)S(1)}, u32[]{:S(2)}, u32[]{:S(2)}) collective-permute-start(f32[16,128,128]{2,1,0:T(8,128)S(1)} %copy-done.26), channel_id=1, source_target_pairs={{0,2},{1,3},{2,0},{3,1},{4,6},{5,7},{6,4},{7,5},{8,10},{9,11},{10,... | collective-permute-start | bytes 3145736 | tf_op jit(solution)/shard_map/ppermute | solution.py:791
  737.7 6.6 collective-permute-start.26
  759.3 15.3 %all-to-all-start.8 = ((f32[32,1,96]{2,1,0:T(1,128)}), f32[32,1,96]{2,1,0:T(1,128)S(1)}, u32[]{:S(2)}, u32[]{:S(2)}) async-start(f32[32,1,96]{2,1,0:T(1,128)} %bitcast.61), calls=%async_computation.8 | async-start | bytes 32768 | tf_op jit(solution)/shard_map/all_to_all | solution.py:933
  (32 other events, 426.9 us)

commit v7 on v4

--- a/solution.py
+++ b/solution.py
@@ -885,7 +885,6 @@
     level_lines = send(level_lines, early, *carried_y)
     totals = react(index, carried, *carried_y, volatility, *vol_x, *vol_y, cotangent, n)
     total_lines = send(totals, near)
-    total_lines = send(total_lines, far, *pick(total_lines, near))
 
     level = second(after(level_lines, totals), second_n3, third_n3, 0)[0]
     drift_pieces = mix(index, level, n)
@@ -898,7 +897,7 @@
     patch_t = patch_index[:, :, None]
     weight, sums = frozen(
         index,
-        after(state, *drift_pieces),
+        after(state, *totals),
         *state_x,
         frozen_rows(state_y[0]),
         frozen_rows(state_y[1]),
@@ -910,7 +909,8 @@
         groups,
     )
 
-    total_lines = after(total_lines, drift_pieces, sums)
+    total_lines = send(total_lines, far, sums, *pick(total_lines, near))
+    total_lines = after(total_lines, drift_pieces)
     drifts = send(drift_pieces, early, *total_lines)
     uppers = after(second(total_lines, second_t3, third_t3, wide), *pick(drifts, early))
     uppers, start_chunks, gone = cross_both(uppers, (), (), near, far)

time: 754 us -> 746 us (0.989)
  starting transfers between devices: 102 us -> 84.7 us
  waiting for transfers between devices: 404 us -> 413 us
    ppermute x18, starting transfers between devices: 46.1 us -> 31.8 us  [send(): lax.ppermute(piece, 'narrow', [(k, (k + d) % n) for k in range(n)])]
    ppermute x18, waiting for transfers between devices: 332 us -> 339 us  [send(): lax.ppermute(piece, 'narrow', [(k, (k + d) % n) for k in range(n)])]
where the time goes in v7:
time: 746 us; the launch traced here: 743 us
  waiting for transfers between devices  413 us (55%)
  Pallas kernels  167 us (22%)
  starting transfers between devices  84.7 us (11%)
  local copies, waits for them, and re-layouts  37.8 us (5%)
  blocking collectives  19.6 us (3%)
  other arithmetic  14.8 us (2%)
    ppermute x18, waiting for transfers between devices, send(): lax.ppermute(piece, 'narrow', [(k, (k + d) % n) for k in range(n)])  339 us
    all_to_all x7, waiting for transfers between devices, across(): lax.all_to_all(piece, 'wide', split_axis=0, concat_axis=0, tiled=True)  58.9 us
    pallas_call x3, Pallas kernels, second(): pl.pallas_call(functools.partial(second_kernel, count=count, chunked=bool...  37.8 us
    ppermute x18, starting transfers between devices, send(): lax.ppermute(piece, 'narrow', [(k, (k + d) % n) for k in range(n)])  31.8 us
    all_to_all x7, starting transfers between devices, across(): lax.all_to_all(piece, 'wide', split_axis=0, concat_axis=0, tiled=True)  30.9 us
    pallas_call x3, Pallas kernels, first(): pl.pallas_call(functools.partial(first_kernel, count=len(flat), lines=blo...  25.7 us
    pallas_call x1, Pallas kernels, frozen(): pl.pallas_call(functools.partial(frozen_kernel, blocks=blocks, groups=gro...  24.8 us
    all_to_all x1, blocking collectives, across(): lax.all_to_all(piece, 'wide', split_axis=0, concat_axis=0, tiled=True)  19.6 us
  transfers between devices with their start and end apart: 36, of which 23 were waited for; matrix products, arithmetic and copies ran while one was open for 5% of the time, Pallas kernels for 19%

profile of v7, /device:TPU:0, one launch (start us, length us, event | category | flops | bytes accessed | tf_op | source)
XLA Modules:
  0.0 743.0 jit_solution(932570927934883293)
XLA Ops:
  31.9 11.6 %forward.1 = (f32[8,64,16,128]{3,2,1,0:T(8,128)}, f32[64,128,128]{2,1,0:T(8,128)}) custom-call(s32[1]{0:T(128)} %bitcast.i, f32[64,128,128]{2,1,0:T(8,128)} %after.5, f32[64,128,128]{2,1,0:T(8,128)} %after.5, f32[64,128,128]{2,1,0:T(8,128)} %after.5, f32[1,128,128]{2,1,0:T(8,128)} %bitcast.130, f32[1,128,128]{2,1,0:T(8,128)} %bitcast.127, ...), custom_call_target="tpu_custom_call" | custom-call | flops 100000000 | bytes 356515 | tf_op jit(solution)/shard_map/forward/pallas_call | solution.py:308
  43.5 11.4 %collective-permute-done.4.refs_1_ = f32[16,128,128]{2,1,0:T(8,128)S(1)} collective-permute-done((f32[16,128,128]{2,1,0:T(8,128)S(1)}, f32[16,128,128]{2,1,0:T(8,128)S(1)}, u32[]{:S(2)}, u32[]{:S(2)}) %collective-permute-start.4) | collective-permute-done | bytes 1048608 | tf_op jit(solution)/shard_map/ppermute | solution.py:791
  64.7 21.6 %collective-permute-done.5.refs_3_ = f32[16,128,128]{2,1,0:T(8,128)} collective-permute-done((f32[16,128,128]{2,1,0:T(8,128)}, f32[16,128,128]{2,1,0:T(8,128)}, u32[]{:S(2)}, u32[]{:S(2)}) %collective-permute-start.5) | collective-permute-done | bytes 1048608 | tf_op jit(solution)/shard_map/ppermute | solution.py:791
  90.0 19.7 %all-to-all-done = f32[8,64,16,128]{3,2,1,0:T(8,128)} async-done(((f32[8,64,16,128]{3,2,1,0:T(8,128)}), f32[8,64,16,128]{3,2,1,0:T(8,128)}, u32[]{:S(2)}, u32[]{:S(2)}) %all-to-all-start) | async-done | bytes 4194336 | tf_op jit(solution)/shard_map/all_to_all | solution.py:804
  109.7 8.5 %first.3 = f32[528,16,128]{2,1,0:T(8,128)} custom-call(f32[512,16,128]{2,1,0:T(8,128)} %bitcast.19.refs_0_, bf16[512,1536]{1,0:T(8,128)(2,1)} %pad_maximum_fusion.2.refs_1_), custom_call_target="tpu_custom_call" | custom-call | flops 140000000 | bytes 209715 | tf_op jit(solution)/shard_map/first/pallas_call | solution.py:373
  118.2 16.0 %collective-permute-done.6.refs_2_ = f32[16,128,128]{2,1,0:T(8,128)S(1)} collective-permute-done((f32[16,128,128]{2,1,0:T(8,128)}, f32[16,128,128]{2,1,0:T(8,128)S(1)}, u32[]{:S(2)}, u32[]{:S(2)}) %collective-permute-start.6) | collective-permute-done | bytes 1048608 | tf_op jit(solution)/shard_map/ppermute | solution.py:791
  139.8 12.2 %second.3 = (f32[8,16,16,128]{3,2,1,0:T(8,128)}, f32[8,16,16,128]{3,2,1,0:T(8,128)}, f32[8,16,16,128]{3,2,1,0:T(8,128)}, f32[8,16,16,128]{3,2,1,0:T(8,128)}) custom-call(f32[16,128,128]{2,1,0:T(8,128)} %get-tuple-element.71.refs_0_, f32[16,128,128]{2,1,0:T(8,128)} %copy-done.10, f32[16,128,128]{2,1,0:T(8,128)} %copy-done.13, ...), custom_call_target="tpu_custom_call" | custom-call | flops 180000000 | bytes 209715 | tf_op jit(solution)/shard_map/second/pallas_call | solution.py:415
  155.8 24.2 %collective-permute-done.7 = f32[8,16,16,128]{3,2,1,0:T(8,128)S(1)} collective-permute-done((f32[8,16,16,128]{3,2,1,0:T(8,128)}, f32[8,16,16,128]{3,2,1,0:T(8,128)S(1)}, u32[]{:S(2)}, u32[]{:S(2)}) %collective-permute-start.7) | collective-permute-done | bytes 1048608 | tf_op jit(solution)/shard_map/ppermute | solution.py:791
  180.0 20.1 %collective-permute-done.8 = f32[8,16,16,128]{3,2,1,0:T(8,128)S(1)} collective-permute-done((f32[8,16,16,128]{3,2,1,0:T(8,128)}, f32[8,16,16,128]{3,2,1,0:T(8,128)S(1)}, u32[]{:S(2)}, u32[]{:S(2)}) %collective-permute-start.8) | collective-permute-done | bytes 1048608 | tf_op jit(solution)/shard_map/ppermute | solution.py:791
  210.4 9.0 %lifted.1 = (f32[18,128,128]{2,1,0:T(8,128)}, f32[18,128,128]{2,1,0:T(8,128)}, f32[18,128,128]{2,1,0:T(8,128)}, f32[18,128,128]{2,1,0:T(8,128)}) custom-call(s32[1]{0:T(128)} %bitcast.i, f32[8,66,16,128]{3,2,1,0:T(8,128)} %all-to-all-done.1.solved, f32[64,128,128]{2,1,0:T(8,128)} %after.5, f32[1,128,128]{2,1,0:T(8,128)} %bitcast.131, ...), custom_call_target="tpu_custom_call" | custom-call | flops 40000000 | bytes 272629 | tf_op jit(solution)/shard_map/lifted/pallas_call | solution.py:473
  219.4 37.5 %collective-permute-done.9 = f32[8,16,16,128]{3,2,1,0:T(8,128)} collective-permute-done((f32[8,16,16,128]{3,2,1,0:T(8,128)S(1)}, f32[8,16,16,128]{3,2,1,0:T(8,128)}, u32[]{:S(2)}, u32[]{:S(2)}) %collective-permute-start.9) | collective-permute-done | bytes 1048608 | tf_op jit(solution)/shard_map/ppermute | solution.py:791
  266.0 12.2 %all-to-all-done.3 = f32[8,16,16,128]{3,2,1,0:T(8,128)S(1)} async-done(((f32[8,16,16,128]{3,2,1,0:T(8,128)}), f32[8,16,16,128]{3,2,1,0:T(8,128)S(1)}, u32[]{:S(2)}, u32[]{:S(2)}) %all-to-all-start.3) | async-done | bytes 1048608 | tf_op jit(solution)/shard_map/all_to_all | solution.py:804
  279.1 8.6 %first.4 = f32[528,16,128]{2,1,0:T(8,128)} custom-call(f32[384,16,128]{2,1,0:T(8,128)} %bitcast.25.refs_0_, f32[128,16,128]{2,1,0:T(8,128)} %bitcast.120, bf16[512,1536]{1,0:T(8,128)(2,1)} %pad_maximum_fusion.4.refs_2_), custom_call_target="tpu_custom_call" | custom-call | flops 140000000 | bytes 209715 | tf_op jit(solution)/shard_map/first/pallas_call | solution.py:373
  292.5 53.9 %collective-permute-done.11.refs_2_ = f32[18,128,128]{2,1,0:T(8,128)} collective-permute-done((f32[18,128,128]{2,1,0:T(8,128)S(1)}, f32[18,128,128]{2,1,0:T(8,128)}, u32[]{:S(2)}, u32[]{:S(2)}) %collective-permute-start.11) | collective-permute-done | bytes 1179680 | tf_op jit(solution)/shard_map/ppermute | solution.py:791
  355.3 12.4 %reaction.1 = (f32[16,128,128]{2,1,0:T(8,128)}, f32[16,128,128]{2,1,0:T(8,128)}, f32[16,128,128]{2,1,0:T(8,128)}, f32[16,128,128]{2,1,0:T(8,128)}) custom-call(s32[1]{0:T(128)} %bitcast.i, f32[8,66,16,128]{3,2,1,0:T(8,128)} %all-to-all-done.4.carried, f32[66,128]{1,0:T(8,128)} %copy-done.21, f32[66,128]{1,0:T(8,128)} %copy-done.22, f32[64,128,128]{2,1,0:T(8,128)} %after.6, ...), custom_call_target="tpu_custom_call" | custom-call | flops 80000000 | bytes 356515 | tf_op jit(solution)/shard_map/reaction/pallas_call | solution.py:520
  376.9 24.8 %frozen.1 = (f32[64,128,128]{2,1,0:T(8,128)}, f32[24,256]{1,0:T(8,128)}) custom-call(s32[1]{0:T(128)} %bitcast.i, f32[64,128,128]{2,1,0:T(8,128)} %after.5, f32[64,128,128]{2,1,0:T(8,128)} %after.5, f32[64,128,128]{2,1,0:T(8,128)} %after.5, f32[1,128,128]{2,1,0:T(8,128)} %bitcast.132, f32[1,128,128]{2,1,0:T(8,128)} %bitcast.129, f32[66,128]{1,0:T(8,128)} %fusion.1.q_low, ...), custom_call_target="tpu_custom_call" | custom-call | flops 100000000 | bytes 356515 | tf_op jit(solution)/shard_map/frozen/pallas_call | solution.py:664
  401.8 13.4 %collective-permute-done.15.refs_3_ = f32[16,128,128]{2,1,0:T(8,128)S(1)} collective-permute-done((f32[16,128,128]{2,1,0:T(8,128)}, f32[16,128,128]{2,1,0:T(8,128)S(1)}, u32[]{:S(2)}, u32[]{:S(2)}) %collective-permute-start.15) | collective-permute-done | bytes 1048608 | tf_op jit(solution)/shard_map/ppermute | solution.py:791
  422.7 21.1 %collective-permute-done.17.refs_1_ = f32[18,128,128]{2,1,0:T(8,128)} collective-permute-done((f32[18,128,128]{2,1,0:T(8,128)}, f32[18,128,128]{2,1,0:T(8,128)}, u32[]{:S(2)}, u32[]{:S(2)}) %collective-permute-start.17) | collective-permute-done | bytes 1179680 | tf_op jit(solution)/shard_map/ppermute | solution.py:791
  443.9 13.3 %second.4.field = f32[18,512,128]{2,1,0:T(8,128)} custom-call(f32[18,128,128]{2,1,0:T(8,128)} %get-tuple-element.98.refs_0_, f32[18,128,128]{2,1,0:T(8,128)} %collective-permute-done.17.refs_1_, f32[18,128,128]{2,1,0:T(8,128)} %collective-permute-done.11.refs_2_, f32[18,128,128]{2,1,0:T(8,128)} %collective-permute-done.10.refs_3_, ...), custom_call_target="tpu_custom_call" | custom-call | flops 180000000 | bytes 209715 | tf_op jit(solution)/shard_map/second/pallas_call | solution.py:415
  457.2 10.2 %mixed.1 = (f32[16,128,128]{2,1,0:T(8,128)}, f32[16,128,128]{2,1,0:T(8,128)}, f32[16,128,128]{2,1,0:T(8,128)}, f32[16,128,128]{2,1,0:T(8,128)}) custom-call(s32[1]{0:T(128)} %bitcast.i, f32[18,512,128]{2,1,0:T(8,128)} %second.4.field), custom_call_target="tpu_custom_call" | custom-call | flops 80000000 | bytes 188743 | tf_op jit(solution)/shard_map/mixed/pallas_call | solution.py:599
  467.4 18.9 %collective-permute-done.16.refs_2_ = f32[16,128,128]{2,1,0:T(8,128)} collective-permute-done((f32[16,128,128]{2,1,0:T(8,128)}, f32[16,128,128]{2,1,0:T(8,128)}, u32[]{:S(2)}, u32[]{:S(2)}) %collective-permute-start.16) | collective-permute-done | bytes 1048608 | tf_op jit(solution)/shard_map/ppermute | solution.py:791
  488.4 12.2 %second.5 = (f32[8,16,16,128]{3,2,1,0:T(8,128)}, f32[8,16,16,128]{3,2,1,0:T(8,128)}, f32[8,16,16,128]{3,2,1,0:T(8,128)}, f32[8,16,16,128]{3,2,1,0:T(8,128)}) custom-call(f32[16,128,128]{2,1,0:T(8,128)} %get-tuple-element.106.refs_0_, f32[16,128,128]{2,1,0:T(8,128)} %copy-done.11, f32[16,128,128]{2,1,0:T(8,128)} %collective-permute-done.16.refs_2_, ...), custom_call_target="tpu_custom_call" | custom-call | flops 180000000 | bytes 209715 | tf_op jit(solution)/shard_map/second/pallas_call | solution.py:415
  500.6 12.4 %collective-permute-done.18.refs_3_ = f32[16,128,128]{2,1,0:T(8,128)S(1)} collective-permute-done((f32[16,128,128]{2,1,0:T(8,128)}, f32[16,128,128]{2,1,0:T(8,128)S(1)}, u32[]{:S(2)}, u32[]{:S(2)}) %collective-permute-start.18) | collective-permute-done | bytes 1048608 | tf_op jit(solution)/shard_map/ppermute | solution.py:791
  516.9 24.3 %collective-permute-done.19.refs_7_ = f32[8,16,16,128]{3,2,1,0:T(8,128)S(1)} collective-permute-done((f32[8,16,16,128]{3,2,1,0:T(8,128)}, f32[8,16,16,128]{3,2,1,0:T(8,128)S(1)}, u32[]{:S(2)}, u32[]{:S(2)}) %collective-permute-start.19) | collective-permute-done | bytes 1048608 | tf_op jit(solution)/shard_map/ppermute | solution.py:791
  541.1 18.3 %collective-permute-done.20.refs_5_ = f32[8,16,16,128]{3,2,1,0:T(8,128)S(1)} collective-permute-done((f32[8,16,16,128]{3,2,1,0:T(8,128)}, f32[8,16,16,128]{3,2,1,0:T(8,128)S(1)}, u32[]{:S(2)}, u32[]{:S(2)}) %collective-permute-start.20) | collective-permute-done | bytes 1048608 | tf_op jit(solution)/shard_map/ppermute | solution.py:791
  569.8 46.2 %collective-permute-done.21.refs_6_ = f32[8,16,16,128]{3,2,1,0:T(8,128)S(1)} collective-permute-done((f32[8,16,16,128]{3,2,1,0:T(8,128)}, f32[8,16,16,128]{3,2,1,0:T(8,128)S(1)}, u32[]{:S(2)}, u32[]{:S(2)}) %collective-permute-start.21) | collective-permute-done | bytes 1048608 | tf_op jit(solution)/shard_map/ppermute | solution.py:791
  619.6 19.6 %all_to_all.49 = f32[8,16,16,128]{3,2,1,0:T(8,128)} all-to-all(f32[8,16,16,128]{3,2,1,0:T(8,128)} %copy-done.3), channel_id=1, replica_groups=mesh['wide'=8,'narrow'=4] {'wide'}, dimensions={0} | all-to-all | bytes 2097152 | tf_op jit(solution)/shard_map/all_to_all | solution.py:804
  639.2 8.6 %first.5 = f32[528,16,128]{2,1,0:T(8,128)} custom-call(f32[384,16,128]{2,1,0:T(8,128)} %bitcast.119, f32[128,16,128]{2,1,0:T(8,128)} %bitcast.121, bf16[512,1536]{1,0:T(8,128)(2,1)} %pad_maximum_fusion.4.refs_2_), custom_call_target="tpu_custom_call" | custom-call | flops 140000000 | bytes 209715 | tf_op jit(solution)/shard_map/first/pallas_call | solution.py:373
  665.0 11.1 %lines.1.tail = f32[64,128,128]{2,1,0:T(8,128)} custom-call(s32[1]{0:T(128)} %bitcast.i, f32[16,128,128]{2,1,0:T(8,128)} %get-tuple-element.106.refs_0_, f32[16,128,128]{2,1,0:T(8,128)} %get-tuple-element.91.refs_1_, f32[16,128,128]{2,1,0:T(8,128)} %get-tuple-element.96.refs_2_, f32[16,128,128]{2,1,0:T(8,128)} %get-tuple-element.93.refs_3_, ...), custom_call_target="tpu_custom_call" | custom-call | flops 100000000 | bytes 356515 | tf_op jit(solution)/shard_map/lines/pallas_call | solution.py:564
  676.0 27.0 %all-to-all-done.7.start.refs_6_ = f32[8,66,16,128]{3,2,1,0:T(8,128)} async-done(((f32[8,66,16,128]{3,2,1,0:T(8,128)}), f32[8,66,16,128]{3,2,1,0:T(8,128)}, u32[]{:S(2)}, u32[]{:S(2)}) %all-to-all-start.7) | async-done | bytes 4325408 | tf_op jit(solution)/shard_map/all_to_all | solution.py:804
  713.0 12.6 %column.1 = f32[24,256]{1,0:T(8,128)} custom-call(s32[1]{0:T(128)} %bitcast.i, f32[16,128,128]{2,1,0:T(8,128)} %get-tuple-element.102.refs_0_, f32[16,128,128]{2,1,0:T(8,128)} %collective-permute-done.22.refs_1_, f32[16,128,128]{2,1,0:T(8,128)} %copy-done.15, f32[16,128,128]{2,1,0:T(8,128)} %copy-done.14, f32[64,128,128]{2,1,0:T(8,128)} %get-tuple-element.126.refs_4_, ...), custom_call_target="tpu_custom_call" | custom-call | flops 80000000 | bytes 356515 | tf_op jit(solution)/shard_map/column/pallas_call | solution.py:710
  730.1 12.3 %adjoint.1 = f32[64,128,128]{2,1,0:T(8,128)} custom-call(s32[1]{0:T(128)} %bitcast.i, f32[8,66,16,128]{3,2,1,0:T(8,128)} %all-to-all-done.7.start.refs_6_, f32[66,128]{1,0:T(8,128)} %copy-done.19, f32[66,128]{1,0:T(8,128)} %copy-done.20, f32[64,128,128]{2,1,0:T(8,128)} %after.6, f32[64,128,128]{2,1,0:T(8,128)} %after.6, f32[64,128,128]{2,1,0:T(8,128)} %after.6, ...), custom_call_target="tpu_custom_call" | custom-call | flops 100000000 | bytes 356515 | tf_op jit(solution)/shard_map/adjoint/pallas_call | solution.py:757
  (186 shorter events, 153.6 us)
Async XLA Ops:
  2.5 13.5 %collective-permute-start.1 = (f32[2,128,128]{2,0,1:T(2,128)S(1)}, f32[2,128,128]{2,0,1:T(2,128)S(1)}, u32[]{:S(2)}, u32[]{:S(2)}) collective-permute-start(f32[2,128,128]{2,0,1:T(2,128)S(1)} %pad_maximum_fusion.9), channel_id=1, source_target_pairs={{4,0},{8,4},{12,8},{16,12},{20,16},{24,20},{28,24},{5,1},{9,5},{13... | collective-permute-start | bytes 393224 | tf_op jit(solution)/shard_map/ppermute | solution.py:779
  4.0 12.1 %collective-permute-start = (f32[2,128,128]{2,0,1:T(2,128)S(1)}, f32[2,128,128]{2,0,1:T(2,128)S(1)}, u32[]{:S(2)}, u32[]{:S(2)}) collective-permute-start(f32[2,128,128]{2,0,1:T(2,128)S(1)} %pad_maximum_fusion.8), channel_id=1, source_target_pairs={{0,4},{4,8},{8,12},{12,16},{16,20},{20,24},{24,28},{1,5},{5,9},{9,... | collective-permute-start | bytes 393224 | tf_op jit(solution)/shard_map/ppermute | solution.py:779
  16.2 10.8 %collective-permute-start.3 = (f32[2,66,128]{2,1,0:T(8,128)S(1)}, f32[2,66,128]{2,1,0:T(8,128)S(1)}, u32[]{:S(2)}, u32[]{:S(2)}) collective-permute-start(f32[2,66,128]{2,1,0:T(8,128)S(1)} %get-tuple-element.167), channel_id=1, source_target_pairs={{1,0},{2,1},{3,2},{5,4},{6,5},{7,6},{9,8},{10,9},{11,10},{13,12},{... | collective-permute-start | bytes 202760 | tf_op jit(solution)/shard_map/ppermute | solution.py:779
  17.5 9.5 %collective-permute-start.2 = (f32[2,66,128]{2,1,0:T(8,128)S(1)}, f32[2,66,128]{2,1,0:T(8,128)S(1)}, u32[]{:S(2)}, u32[]{:S(2)}) collective-permute-start(f32[2,66,128]{2,1,0:T(8,128)S(1)} %get-tuple-element.168), channel_id=1, source_target_pairs={{0,1},{1,2},{2,3},{4,5},{5,6},{6,7},{8,9},{9,10},{10,11},{12,13},{... | collective-permute-start | bytes 202760 | tf_op jit(solution)/shard_map/ppermute | solution.py:779
  27.0 27.9 %collective-permute-start.4 = (f32[16,128,128]{2,1,0:T(8,128)S(1)}, f32[16,128,128]{2,1,0:T(8,128)S(1)}, u32[]{:S(2)}, u32[]{:S(2)}) collective-permute-start(f32[16,128,128]{2,1,0:T(8,128)S(1)} %get-tuple-element.65), channel_id=1, source_target_pairs={{0,1},{1,2},{2,3},{3,0},{4,5},{5,6},{6,7},{7,4},{8,9},{9,10},{10,1... | collective-permute-start | bytes 3145736 | tf_op jit(solution)/shard_map/ppermute | solution.py:791
  55.9 53.8 %all-to-all-start = ((f32[8,64,16,128]{3,2,1,0:T(8,128)}), f32[8,64,16,128]{3,2,1,0:T(8,128)}, u32[]{:S(2)}, u32[]{:S(2)}) async-start(f32[8,64,16,128]{3,2,1,0:T(8,128)} %get-tuple-element.69), calls=%async_computation | async-start | bytes 8388608 | tf_op jit(solution)/shard_map/all_to_all | solution.py:804
  60.5 25.8 %collective-permute-start.5 = (f32[16,128,128]{2,1,0:T(8,128)}, f32[16,128,128]{2,1,0:T(8,128)}, u32[]{:S(2)}, u32[]{:S(2)}) collective-permute-start(f32[16,128,128]{2,1,0:T(8,128)} %get-tuple-element.66), channel_id=1, source_target_pairs={{0,3},{1,0},{2,1},{3,2},{4,7},{5,4},{6,5},{7,6},{8,11},{9,8},{10,9... | collective-permute-start | bytes 3145736 | tf_op jit(solution)/shard_map/ppermute | solution.py:791
  86.3 48.0 %collective-permute-start.6 = (f32[16,128,128]{2,1,0:T(8,128)}, f32[16,128,128]{2,1,0:T(8,128)S(1)}, u32[]{:S(2)}, u32[]{:S(2)}) collective-permute-start(f32[16,128,128]{2,1,0:T(8,128)} %get-tuple-element.67), channel_id=1, source_target_pairs={{0,2},{1,3},{2,0},{3,1},{4,6},{5,7},{6,4},{7,5},{8,10},{9,11},{10,... | collective-permute-start | bytes 3145736 | tf_op jit(solution)/shard_map/ppermute | solution.py:791
  135.2 68.1 %all-to-all-start.1 = ((f32[8,66,16,128]{3,2,1,0:T(8,128)}), f32[8,66,16,128]{3,2,1,0:T(8,128)}, u32[]{:S(2)}, u32[]{:S(2)}) async-start(f32[8,66,16,128]{3,2,1,0:T(8,128)} %bitcast.117), calls=%async_computation.1 | async-start | bytes 8650752 | tf_op jit(solution)/shard_map/all_to_all | solution.py:804
  152.0 28.1 %collective-permute-start.7 = (f32[8,16,16,128]{3,2,1,0:T(8,128)}, f32[8,16,16,128]{3,2,1,0:T(8,128)S(1)}, u32[]{:S(2)}, u32[]{:S(2)}) collective-permute-start(f32[8,16,16,128]{3,2,1,0:T(8,128)} %get-tuple-element.76), channel_id=1, source_target_pairs={{0,1},{1,2},{2,3},{3,0},{4,5},{5,6},{6,7},{7,4},{8,9},{9,10},{10,1... | collective-permute-start | bytes 3145736 | tf_op jit(solution)/shard_map/ppermute | solution.py:791
  152.0 48.2 %collective-permute-start.8 = (f32[8,16,16,128]{3,2,1,0:T(8,128)}, f32[8,16,16,128]{3,2,1,0:T(8,128)S(1)}, u32[]{:S(2)}, u32[]{:S(2)}) collective-permute-start(f32[8,16,16,128]{3,2,1,0:T(8,128)} %get-tuple-element.77), channel_id=1, source_target_pairs={{0,3},{1,0},{2,1},{3,2},{4,7},{5,4},{6,5},{7,6},{8,11},{9,8},{10,9... | collective-permute-start | bytes 3145736 | tf_op jit(solution)/shard_map/ppermute | solution.py:791
  203.4 55.5 %all-to-all-start.2 = ((f32[8,48,16,128]{3,2,1,0:T(8,128)}), f32[8,48,16,128]{3,2,1,0:T(8,128)}, u32[]{:S(2)}, u32[]{:S(2)}) async-start(f32[8,48,16,128]{3,2,1,0:T(8,128)} %pad_maximum_fusion), calls=%async_computation.2 | async-start | bytes 6291456 | tf_op jit(solution)/shard_map/all_to_all | solution.py:804
  208.0 48.9 %collective-permute-start.9 = (f32[8,16,16,128]{3,2,1,0:T(8,128)S(1)}, f32[8,16,16,128]{3,2,1,0:T(8,128)}, u32[]{:S(2)}, u32[]{:S(2)}) collective-permute-start(f32[8,16,16,128]{3,2,1,0:T(8,128)S(1)} %copy-done.28), channel_id=1, source_target_pairs={{0,2},{1,3},{2,0},{3,1},{4,6},{5,7},{6,4},{7,5},{8,10},{9,11},{10,... | collective-permute-start | bytes 3145736 | tf_op jit(solution)/shard_map/ppermute | solution.py:791
  256.9 30.8 %collective-permute-start.10 = (f32[18,128,128]{2,1,0:T(8,128)}, f32[18,128,128]{2,1,0:T(8,128)}, u32[]{:S(2)}, u32[]{:S(2)}) collective-permute-start(f32[18,128,128]{2,1,0:T(8,128)} %get-tuple-element.86), channel_id=1, source_target_pairs={{0,3},{1,0},{2,1},{3,2},{4,7},{5,4},{6,5},{7,6},{8,11},{9,8},{10,9... | collective-permute-start | bytes 3538952 | tf_op jit(solution)/shard_map/ppermute | solution.py:791
  258.9 19.3 %all-to-all-start.3 = ((f32[8,16,16,128]{3,2,1,0:T(8,128)}), f32[8,16,16,128]{3,2,1,0:T(8,128)S(1)}, u32[]{:S(2)}, u32[]{:S(2)}) async-start(f32[8,16,16,128]{3,2,1,0:T(8,128)} %collective-permute-done.9), calls=%async_computation.3 | async-start | bytes 2097152 | tf_op jit(solution)/shard_map/all_to_all | solution.py:804
  287.7 58.7 %all-to-all-start.4 = ((f32[8,66,16,128]{3,2,1,0:T(8,128)}), f32[8,66,16,128]{3,2,1,0:T(8,128)}, u32[]{:S(2)}, u32[]{:S(2)}) async-start(f32[8,66,16,128]{3,2,1,0:T(8,128)} %bitcast.118), calls=%async_computation.4 | async-start | bytes 8650752 | tf_op jit(solution)/shard_map/all_to_all | solution.py:804
  292.4 54.0 %collective-permute-start.11 = (f32[18,128,128]{2,1,0:T(8,128)S(1)}, f32[18,128,128]{2,1,0:T(8,128)}, u32[]{:S(2)}, u32[]{:S(2)}) collective-permute-start(f32[18,128,128]{2,1,0:T(8,128)S(1)} %copy-done.26), channel_id=1, source_target_pairs={{0,2},{1,3},{2,0},{3,1},{4,6},{5,7},{6,4},{7,5},{8,10},{9,11},{10,... | collective-permute-start | bytes 3538952 | tf_op jit(solution)/shard_map/ppermute | solution.py:791
  348.8 5.9 collective-permute-start.13
  367.7 34.0 %collective-permute-start.14 = (f32[16,128,128]{2,1,0:T(8,128)}, f32[16,128,128]{2,1,0:T(8,128)S(1)}, u32[]{:S(2)}, u32[]{:S(2)}) collective-permute-start(f32[16,128,128]{2,1,0:T(8,128)} %get-tuple-element.91.refs_1_), channel_id=1, source_target_pairs={{0,1},{1,2},{2,3},{3,0},{4,5},{5,6},{6,7},{7,4},{8,9},{9,10},{10,1... | collective-permute-start | bytes 3145736 | tf_op jit(solution)/shard_map/ppermute | solution.py:791
  368.8 46.4 %collective-permute-start.15 = (f32[16,128,128]{2,1,0:T(8,128)}, f32[16,128,128]{2,1,0:T(8,128)S(1)}, u32[]{:S(2)}, u32[]{:S(2)}) collective-permute-start(f32[16,128,128]{2,1,0:T(8,128)} %get-tuple-element.93.refs_3_), channel_id=1, source_target_pairs={{0,3},{1,0},{2,1},{3,2},{4,7},{5,4},{6,5},{7,6},{8,11},{9,8},{10,9... | collective-permute-start | bytes 3145736 | tf_op jit(solution)/shard_map/ppermute | solution.py:791
  376.0 67.9 %collective-permute-start.17 = (f32[18,128,128]{2,1,0:T(8,128)}, f32[18,128,128]{2,1,0:T(8,128)}, u32[]{:S(2)}, u32[]{:S(2)}) collective-permute-start(f32[18,128,128]{2,1,0:T(8,128)} %get-tuple-element.97), channel_id=1, source_target_pairs={{0,1},{1,2},{2,3},{3,0},{4,5},{5,6},{6,7},{7,4},{8,9},{9,10},{10,1... | collective-permute-start | bytes 3538952 | tf_op jit(solution)/shard_map/ppermute | solution.py:791
  416.2 70.1 %collective-permute-start.16 = (f32[16,128,128]{2,1,0:T(8,128)}, f32[16,128,128]{2,1,0:T(8,128)}, u32[]{:S(2)}, u32[]{:S(2)}) collective-permute-start(f32[16,128,128]{2,1,0:T(8,128)} %get-tuple-element.96.refs_2_), channel_id=1, source_target_pairs={{0,2},{1,3},{2,0},{3,1},{4,6},{5,7},{6,4},{7,5},{8,10},{9,11},{10,... | collective-permute-start | bytes 3145736 | tf_op jit(solution)/shard_map/ppermute | solution.py:791
  486.3 26.7 %collective-permute-start.18 = (f32[16,128,128]{2,1,0:T(8,128)}, f32[16,128,128]{2,1,0:T(8,128)S(1)}, u32[]{:S(2)}, u32[]{:S(2)}) collective-permute-start(f32[16,128,128]{2,1,0:T(8,128)} %get-tuple-element.114), channel_id=1, source_target_pairs={{0,1},{1,2},{2,3},{3,0},{4,5},{5,6},{6,7},{7,4},{8,9},{9,10},{10,1... | collective-permute-start | bytes 3145736 | tf_op jit(solution)/shard_map/ppermute | solution.py:791
  513.0 28.1 %collective-permute-start.19 = (f32[8,16,16,128]{3,2,1,0:T(8,128)}, f32[8,16,16,128]{3,2,1,0:T(8,128)S(1)}, u32[]{:S(2)}, u32[]{:S(2)}) collective-permute-start(f32[8,16,16,128]{3,2,1,0:T(8,128)} %get-tuple-element.116), channel_id=1, source_target_pairs={{0,1},{1,2},{2,3},{3,0},{4,5},{5,6},{6,7},{7,4},{8,9},{9,10},{10,1... | collective-permute-start | bytes 3145736 | tf_op jit(solution)/shard_map/ppermute | solution.py:791
  513.0 46.5 %collective-permute-start.20 = (f32[8,16,16,128]{3,2,1,0:T(8,128)}, f32[8,16,16,128]{3,2,1,0:T(8,128)S(1)}, u32[]{:S(2)}, u32[]{:S(2)}) collective-permute-start(f32[8,16,16,128]{3,2,1,0:T(8,128)} %get-tuple-element.117), channel_id=1, source_target_pairs={{0,3},{1,0},{2,1},{3,2},{4,7},{5,4},{6,5},{7,6},{8,11},{9,8},{10,9... | collective-permute-start | bytes 3145736 | tf_op jit(solution)/shard_map/ppermute | solution.py:791
  563.6 56.1 %all-to-all-start.5 = ((f32[8,48,16,128]{3,2,1,0:T(8,128)}), f32[8,48,16,128]{3,2,1,0:T(8,128)S(1)}, u32[]{:S(2)}, u32[]{:S(2)}) async-start(f32[8,48,16,128]{3,2,1,0:T(8,128)} %pad_maximum_fusion.1), calls=%async_computation.5 | async-start | bytes 6291456 | tf_op jit(solution)/shard_map/all_to_all | solution.py:804
  567.4 48.6 %collective-permute-start.21 = (f32[8,16,16,128]{3,2,1,0:T(8,128)}, f32[8,16,16,128]{3,2,1,0:T(8,128)S(1)}, u32[]{:S(2)}, u32[]{:S(2)}) collective-permute-start(f32[8,16,16,128]{3,2,1,0:T(8,128)} %get-tuple-element.119), channel_id=1, source_target_pairs={{0,2},{1,3},{2,0},{3,1},{4,6},{5,7},{6,4},{7,5},{8,10},{9,11},{10,... | collective-permute-start | bytes 3145736 | tf_op jit(solution)/shard_map/ppermute | solution.py:791
  617.0 30.8 %collective-permute-start.22 = (f32[16,128,128]{2,1,0:T(8,128)}, f32[16,128,128]{2,1,0:T(8,128)}, u32[]{:S(2)}, u32[]{:S(2)}) collective-permute-start(f32[16,128,128]{2,1,0:T(8,128)} %get-tuple-element.121), channel_id=1, source_target_pairs={{0,3},{1,0},{2,1},{3,2},{4,7},{5,4},{6,5},{7,6},{8,11},{9,8},{10,9... | collective-permute-start | bytes 3145736 | tf_op jit(solution)/shard_map/ppermute | solution.py:791
  647.8 55.2 %all-to-all-start.7 = ((f32[8,66,16,128]{3,2,1,0:T(8,128)}), f32[8,66,16,128]{3,2,1,0:T(8,128)}, u32[]{:S(2)}, u32[]{:S(2)}) async-start(f32[8,66,16,128]{3,2,1,0:T(8,128)} %bitcast.116), calls=%async_computation.7 | async-start | bytes 8650752 | tf_op jit(solution)/shard_map/all_to_all | solution.py:804
  663.8 48.3 %collective-permute-start.27 = (f32[16,128,128]{2,1,0:T(8,128)S(1)}, f32[16,128,128]{2,1,0:T(8,128)S(1)}, u32[]{:S(2)}, u32[]{:S(2)}) collective-permute-start(f32[16,128,128]{2,1,0:T(8,128)S(1)} %copy-done.27), channel_id=1, source_target_pairs={{0,2},{1,3},{2,0},{3,1},{4,6},{5,7},{6,4},{7,5},{8,10},{9,11},{10,... | collective-permute-start | bytes 3145736 | tf_op jit(solution)/shard_map/ppermute | solution.py:791
  705.4 6.6 collective-permute-start.26
  727.1 15.3 %all-to-all-start.8 = ((f32[32,1,96]{2,1,0:T(1,128)}), f32[32,1,96]{2,1,0:T(1,128)S(1)}, u32[]{:S(2)}, u32[]{:S(2)}) async-start(f32[32,1,96]{2,1,0:T(1,128)} %bitcast.61), calls=%async_computation.8 | async-start | bytes 32768 | tf_op jit(solution)/shard_map/all_to_all | solution.py:934
  (33 other events, 306.0 us)

commit v8 on v7

--- a/solution.py
+++ b/solution.py
@@ -927,7 +927,6 @@
 
     start = after(start, tail)
     start_y = y_edges(start)
-    start = after(start, *start_y)
     sums = column_sums(index, drifts, weight, source, start, patch_index, patch_t, sums)
     count, joint = n * wide, ("wide", "narrow")
     sums = (sums[:, :128] + sums[:, 128:]).reshape(count, PATCHES // count)

time: 746 us -> 756 us (1.013)
    ppermute x18, waiting for transfers between devices: 339 us -> 348 us  [send(): lax.ppermute(piece, 'narrow', [(k, (k + d) % n) for k in range(n)])]
  transfers between devices with their start and end apart: 36 -> 36, of which waited for: 23 -> 24; matrix products, arithmetic and copies ran while one was open for 5% -> 5% of each run, Pallas kernels for 19% -> 17%
where the time goes in v8:
time: 756 us; the launch traced here: 753 us
  waiting for transfers between devices  420 us (56%)
  Pallas kernels  167 us (22%)
  starting transfers between devices  87 us (12%)
  local copies, waits for them, and re-layouts  38.4 us (5%)
  blocking collectives  19.6 us (3%)
  other arithmetic  14.8 us (2%)
    ppermute x18, waiting for transfers between devices, send(): lax.ppermute(piece, 'narrow', [(k, (k + d) % n) for k in range(n)])  348 us
    all_to_all x7, waiting for transfers between devices, across(): lax.all_to_all(piece, 'wide', split_axis=0, concat_axis=0, tiled=True)  58.9 us
    pallas_call x3, Pallas kernels, second(): pl.pallas_call(functools.partial(second_kernel, count=count, chunked=bool...  37.7 us
    ppermute x18, starting transfers between devices, send(): lax.ppermute(piece, 'narrow', [(k, (k + d) % n) for k in range(n)])  31.8 us
    all_to_all x7, starting transfers between devices, across(): lax.all_to_all(piece, 'wide', split_axis=0, concat_axis=0, tiled=True)  30.9 us
    pallas_call x3, Pallas kernels, first(): pl.pallas_call(functools.partial(first_kernel, count=len(flat), lines=blo...  25.7 us
    pallas_call x1, Pallas kernels, frozen(): pl.pallas_call(functools.partial(frozen_kernel, blocks=blocks, groups=gro...  24.8 us
    all_to_all x1, blocking collectives, across(): lax.all_to_all(piece, 'wide', split_axis=0, concat_axis=0, tiled=True)  19.6 us
  transfers between devices with their start and end apart: 36, of which 24 were waited for; matrix products, arithmetic and copies ran while one was open for 5% of the time, Pallas kernels for 17%

profile of v8, /device:TPU:0, one launch (start us, length us, event | category | flops | bytes accessed | tf_op | source)
XLA Modules:
  0.0 752.8 jit_solution(2970475975678483263)
XLA Ops:
  31.9 11.6 %forward.1 = (f32[8,64,16,128]{3,2,1,0:T(8,128)}, f32[64,128,128]{2,1,0:T(8,128)}) custom-call(s32[1]{0:T(128)} %bitcast.i, f32[64,128,128]{2,1,0:T(8,128)} %after.5, f32[64,128,128]{2,1,0:T(8,128)} %after.5, f32[64,128,128]{2,1,0:T(8,128)} %after.5, f32[1,128,128]{2,1,0:T(8,128)} %bitcast.130, f32[1,128,128]{2,1,0:T(8,128)} %bitcast.127, ...), custom_call_target="tpu_custom_call" | custom-call | flops 100000000 | bytes 356515 | tf_op jit(solution)/shard_map/forward/pallas_call | solution.py:308
  43.5 11.4 %collective-permute-done.4.refs_1_ = f32[16,128,128]{2,1,0:T(8,128)S(1)} collective-permute-done((f32[16,128,128]{2,1,0:T(8,128)S(1)}, f32[16,128,128]{2,1,0:T(8,128)S(1)}, u32[]{:S(2)}, u32[]{:S(2)}) %collective-permute-start.4) | collective-permute-done | bytes 1048608 | tf_op jit(solution)/shard_map/ppermute | solution.py:791
  64.7 21.6 %collective-permute-done.5.refs_3_ = f32[16,128,128]{2,1,0:T(8,128)} collective-permute-done((f32[16,128,128]{2,1,0:T(8,128)}, f32[16,128,128]{2,1,0:T(8,128)}, u32[]{:S(2)}, u32[]{:S(2)}) %collective-permute-start.5) | collective-permute-done | bytes 1048608 | tf_op jit(solution)/shard_map/ppermute | solution.py:791
  90.0 19.7 %all-to-all-done = f32[8,64,16,128]{3,2,1,0:T(8,128)} async-done(((f32[8,64,16,128]{3,2,1,0:T(8,128)}), f32[8,64,16,128]{3,2,1,0:T(8,128)}, u32[]{:S(2)}, u32[]{:S(2)}) %all-to-all-start) | async-done | bytes 4194336 | tf_op jit(solution)/shard_map/all_to_all | solution.py:804
  109.7 8.5 %first.3 = f32[528,16,128]{2,1,0:T(8,128)} custom-call(f32[512,16,128]{2,1,0:T(8,128)} %bitcast.19.refs_0_, bf16[512,1536]{1,0:T(8,128)(2,1)} %pad_maximum_fusion.2.refs_1_), custom_call_target="tpu_custom_call" | custom-call | flops 140000000 | bytes 209715 | tf_op jit(solution)/shard_map/first/pallas_call | solution.py:373
  118.2 16.0 %collective-permute-done.6.refs_2_ = f32[16,128,128]{2,1,0:T(8,128)S(1)} collective-permute-done((f32[16,128,128]{2,1,0:T(8,128)}, f32[16,128,128]{2,1,0:T(8,128)S(1)}, u32[]{:S(2)}, u32[]{:S(2)}) %collective-permute-start.6) | collective-permute-done | bytes 1048608 | tf_op jit(solution)/shard_map/ppermute | solution.py:791
  139.8 12.2 %second.3 = (f32[8,16,16,128]{3,2,1,0:T(8,128)}, f32[8,16,16,128]{3,2,1,0:T(8,128)}, f32[8,16,16,128]{3,2,1,0:T(8,128)}, f32[8,16,16,128]{3,2,1,0:T(8,128)}) custom-call(f32[16,128,128]{2,1,0:T(8,128)} %get-tuple-element.70.refs_0_, f32[16,128,128]{2,1,0:T(8,128)} %copy-done.10, f32[16,128,128]{2,1,0:T(8,128)} %copy-done.13, ...), custom_call_target="tpu_custom_call" | custom-call | flops 180000000 | bytes 209715 | tf_op jit(solution)/shard_map/second/pallas_call | solution.py:415
  155.8 24.2 %collective-permute-done.7 = f32[8,16,16,128]{3,2,1,0:T(8,128)S(1)} collective-permute-done((f32[8,16,16,128]{3,2,1,0:T(8,128)}, f32[8,16,16,128]{3,2,1,0:T(8,128)S(1)}, u32[]{:S(2)}, u32[]{:S(2)}) %collective-permute-start.7) | collective-permute-done | bytes 1048608 | tf_op jit(solution)/shard_map/ppermute | solution.py:791
  180.1 20.1 %collective-permute-done.8 = f32[8,16,16,128]{3,2,1,0:T(8,128)S(1)} collective-permute-done((f32[8,16,16,128]{3,2,1,0:T(8,128)}, f32[8,16,16,128]{3,2,1,0:T(8,128)S(1)}, u32[]{:S(2)}, u32[]{:S(2)}) %collective-permute-start.8) | collective-permute-done | bytes 1048608 | tf_op jit(solution)/shard_map/ppermute | solution.py:791
  210.4 9.0 %lifted.1 = (f32[18,128,128]{2,1,0:T(8,128)}, f32[18,128,128]{2,1,0:T(8,128)}, f32[18,128,128]{2,1,0:T(8,128)}, f32[18,128,128]{2,1,0:T(8,128)}) custom-call(s32[1]{0:T(128)} %bitcast.i, f32[8,66,16,128]{3,2,1,0:T(8,128)} %all-to-all-done.1.solved, f32[64,128,128]{2,1,0:T(8,128)} %after.5, f32[1,128,128]{2,1,0:T(8,128)} %bitcast.131, ...), custom_call_target="tpu_custom_call" | custom-call | flops 40000000 | bytes 272629 | tf_op jit(solution)/shard_map/lifted/pallas_call | solution.py:473
  219.4 37.5 %collective-permute-done.9 = f32[8,16,16,128]{3,2,1,0:T(8,128)} collective-permute-done((f32[8,16,16,128]{3,2,1,0:T(8,128)S(1)}, f32[8,16,16,128]{3,2,1,0:T(8,128)}, u32[]{:S(2)}, u32[]{:S(2)}) %collective-permute-start.9) | collective-permute-done | bytes 1048608 | tf_op jit(solution)/shard_map/ppermute | solution.py:791
  266.0 12.2 %all-to-all-done.3 = f32[8,16,16,128]{3,2,1,0:T(8,128)S(1)} async-done(((f32[8,16,16,128]{3,2,1,0:T(8,128)}), f32[8,16,16,128]{3,2,1,0:T(8,128)S(1)}, u32[]{:S(2)}, u32[]{:S(2)}) %all-to-all-start.3) | async-done | bytes 1048608 | tf_op jit(solution)/shard_map/all_to_all | solution.py:804
  279.2 8.6 %first.4 = f32[528,16,128]{2,1,0:T(8,128)} custom-call(f32[384,16,128]{2,1,0:T(8,128)} %bitcast.25.refs_0_, f32[128,16,128]{2,1,0:T(8,128)} %bitcast.120, bf16[512,1536]{1,0:T(8,128)(2,1)} %pad_maximum_fusion.4.refs_2_), custom_call_target="tpu_custom_call" | custom-call | flops 140000000 | bytes 209715 | tf_op jit(solution)/shard_map/first/pallas_call | solution.py:373
  292.5 53.9 %collective-permute-done.11.refs_2_ = f32[18,128,128]{2,1,0:T(8,128)} collective-permute-done((f32[18,128,128]{2,1,0:T(8,128)S(1)}, f32[18,128,128]{2,1,0:T(8,128)}, u32[]{:S(2)}, u32[]{:S(2)}) %collective-permute-start.11) | collective-permute-done | bytes 1179680 | tf_op jit(solution)/shard_map/ppermute | solution.py:791
  355.3 12.4 %reaction.1 = (f32[16,128,128]{2,1,0:T(8,128)}, f32[16,128,128]{2,1,0:T(8,128)}, f32[16,128,128]{2,1,0:T(8,128)}, f32[16,128,128]{2,1,0:T(8,128)}) custom-call(s32[1]{0:T(128)} %bitcast.i, f32[8,66,16,128]{3,2,1,0:T(8,128)} %all-to-all-done.4.carried, f32[66,128]{1,0:T(8,128)} %copy-done.21, f32[66,128]{1,0:T(8,128)} %copy-done.22, f32[64,128,128]{2,1,0:T(8,128)} %after.6, ...), custom_call_target="tpu_custom_call" | custom-call | flops 80000000 | bytes 356515 | tf_op jit(solution)/shard_map/reaction/pallas_call | solution.py:520
  376.9 24.8 %frozen.1 = (f32[64,128,128]{2,1,0:T(8,128)}, f32[24,256]{1,0:T(8,128)}) custom-call(s32[1]{0:T(128)} %bitcast.i, f32[64,128,128]{2,1,0:T(8,128)} %after.5, f32[64,128,128]{2,1,0:T(8,128)} %after.5, f32[64,128,128]{2,1,0:T(8,128)} %after.5, f32[1,128,128]{2,1,0:T(8,128)} %bitcast.132, f32[1,128,128]{2,1,0:T(8,128)} %bitcast.129, f32[66,128]{1,0:T(8,128)} %fusion.1.q_low, ...), custom_call_target="tpu_custom_call" | custom-call | flops 100000000 | bytes 356515 | tf_op jit(solution)/shard_map/frozen/pallas_call | solution.py:664
  401.8 13.4 %collective-permute-done.15.refs_3_ = f32[16,128,128]{2,1,0:T(8,128)S(1)} collective-permute-done((f32[16,128,128]{2,1,0:T(8,128)}, f32[16,128,128]{2,1,0:T(8,128)S(1)}, u32[]{:S(2)}, u32[]{:S(2)}) %collective-permute-start.15) | collective-permute-done | bytes 1048608 | tf_op jit(solution)/shard_map/ppermute | solution.py:791
  422.7 21.1 %collective-permute-done.17.refs_1_ = f32[18,128,128]{2,1,0:T(8,128)} collective-permute-done((f32[18,128,128]{2,1,0:T(8,128)}, f32[18,128,128]{2,1,0:T(8,128)}, u32[]{:S(2)}, u32[]{:S(2)}) %collective-permute-start.17) | collective-permute-done | bytes 1179680 | tf_op jit(solution)/shard_map/ppermute | solution.py:791
  443.9 13.3 %second.4.field = f32[18,512,128]{2,1,0:T(8,128)} custom-call(f32[18,128,128]{2,1,0:T(8,128)} %get-tuple-element.97.refs_0_, f32[18,128,128]{2,1,0:T(8,128)} %collective-permute-done.17.refs_1_, f32[18,128,128]{2,1,0:T(8,128)} %collective-permute-done.11.refs_2_, f32[18,128,128]{2,1,0:T(8,128)} %collective-permute-done.10.refs_3_, ...), custom_call_target="tpu_custom_call" | custom-call | flops 180000000 | bytes 209715 | tf_op jit(solution)/shard_map/second/pallas_call | solution.py:415
  457.2 10.2 %mixed.1 = (f32[16,128,128]{2,1,0:T(8,128)}, f32[16,128,128]{2,1,0:T(8,128)}, f32[16,128,128]{2,1,0:T(8,128)}, f32[16,128,128]{2,1,0:T(8,128)}) custom-call(s32[1]{0:T(128)} %bitcast.i, f32[18,512,128]{2,1,0:T(8,128)} %second.4.field), custom_call_target="tpu_custom_call" | custom-call | flops 80000000 | bytes 188743 | tf_op jit(solution)/shard_map/mixed/pallas_call | solution.py:599
  467.4 18.9 %collective-permute-done.16.refs_2_ = f32[16,128,128]{2,1,0:T(8,128)} collective-permute-done((f32[16,128,128]{2,1,0:T(8,128)}, f32[16,128,128]{2,1,0:T(8,128)}, u32[]{:S(2)}, u32[]{:S(2)}) %collective-permute-start.16) | collective-permute-done | bytes 1048608 | tf_op jit(solution)/shard_map/ppermute | solution.py:791
  488.4 12.2 %second.5 = (f32[8,16,16,128]{3,2,1,0:T(8,128)}, f32[8,16,16,128]{3,2,1,0:T(8,128)}, f32[8,16,16,128]{3,2,1,0:T(8,128)}, f32[8,16,16,128]{3,2,1,0:T(8,128)}) custom-call(f32[16,128,128]{2,1,0:T(8,128)} %get-tuple-element.105.refs_0_, f32[16,128,128]{2,1,0:T(8,128)} %copy-done.11, f32[16,128,128]{2,1,0:T(8,128)} %collective-permute-done.16.refs_2_, ...), custom_call_target="tpu_custom_call" | custom-call | flops 180000000 | bytes 209715 | tf_op jit(solution)/shard_map/second/pallas_call | solution.py:415
  500.7 12.4 %collective-permute-done.18.refs_3_ = f32[16,128,128]{2,1,0:T(8,128)S(1)} collective-permute-done((f32[16,128,128]{2,1,0:T(8,128)}, f32[16,128,128]{2,1,0:T(8,128)S(1)}, u32[]{:S(2)}, u32[]{:S(2)}) %collective-permute-start.18) | collective-permute-done | bytes 1048608 | tf_op jit(solution)/shard_map/ppermute | solution.py:791
  516.9 24.3 %collective-permute-done.19.refs_7_ = f32[8,16,16,128]{3,2,1,0:T(8,128)S(1)} collective-permute-done((f32[8,16,16,128]{3,2,1,0:T(8,128)}, f32[8,16,16,128]{3,2,1,0:T(8,128)S(1)}, u32[]{:S(2)}, u32[]{:S(2)}) %collective-permute-start.19) | collective-permute-done | bytes 1048608 | tf_op jit(solution)/shard_map/ppermute | solution.py:791
  541.2 18.3 %collective-permute-done.20.refs_5_ = f32[8,16,16,128]{3,2,1,0:T(8,128)S(1)} collective-permute-done((f32[8,16,16,128]{3,2,1,0:T(8,128)}, f32[8,16,16,128]{3,2,1,0:T(8,128)S(1)}, u32[]{:S(2)}, u32[]{:S(2)}) %collective-permute-start.20) | collective-permute-done | bytes 1048608 | tf_op jit(solution)/shard_map/ppermute | solution.py:791
  569.8 46.2 %collective-permute-done.21.refs_6_ = f32[8,16,16,128]{3,2,1,0:T(8,128)S(1)} collective-permute-done((f32[8,16,16,128]{3,2,1,0:T(8,128)}, f32[8,16,16,128]{3,2,1,0:T(8,128)S(1)}, u32[]{:S(2)}, u32[]{:S(2)}) %collective-permute-start.21) | collective-permute-done | bytes 1048608 | tf_op jit(solution)/shard_map/ppermute | solution.py:791
  619.6 19.6 %all_to_all.49 = f32[8,16,16,128]{3,2,1,0:T(8,128)} all-to-all(f32[8,16,16,128]{3,2,1,0:T(8,128)} %copy-done.3), channel_id=1, replica_groups=mesh['wide'=8,'narrow'=4] {'wide'}, dimensions={0} | all-to-all | bytes 2097152 | tf_op jit(solution)/shard_map/all_to_all | solution.py:804
  639.2 8.6 %first.5 = f32[528,16,128]{2,1,0:T(8,128)} custom-call(f32[384,16,128]{2,1,0:T(8,128)} %bitcast.119, f32[128,16,128]{2,1,0:T(8,128)} %bitcast.121, bf16[512,1536]{1,0:T(8,128)(2,1)} %pad_maximum_fusion.4.refs_2_), custom_call_target="tpu_custom_call" | custom-call | flops 140000000 | bytes 209715 | tf_op jit(solution)/shard_map/first/pallas_call | solution.py:373
  665.0 11.1 %lines.1.tail = f32[64,128,128]{2,1,0:T(8,128)} custom-call(s32[1]{0:T(128)} %bitcast.i, f32[16,128,128]{2,1,0:T(8,128)} %get-tuple-element.105.refs_0_, f32[16,128,128]{2,1,0:T(8,128)} %get-tuple-element.90.refs_1_, f32[16,128,128]{2,1,0:T(8,128)} %get-tuple-element.95.refs_2_, f32[16,128,128]{2,1,0:T(8,128)} %get-tuple-element.92.refs_3_, ...), custom_call_target="tpu_custom_call" | custom-call | flops 100000000 | bytes 356515 | tf_op jit(solution)/shard_map/lines/pallas_call | solution.py:564
  676.1 26.9 %all-to-all-done.7.start.refs_6_ = f32[8,66,16,128]{3,2,1,0:T(8,128)} async-done(((f32[8,66,16,128]{3,2,1,0:T(8,128)}), f32[8,66,16,128]{3,2,1,0:T(8,128)}, u32[]{:S(2)}, u32[]{:S(2)}) %all-to-all-start.7) | async-done | bytes 4325408 | tf_op jit(solution)/shard_map/all_to_all | solution.py:804
  712.3 12.6 %column.1 = f32[24,256]{1,0:T(8,128)} custom-call(s32[1]{0:T(128)} %bitcast.i, f32[16,128,128]{2,1,0:T(8,128)} %get-tuple-element.101.refs_0_, f32[16,128,128]{2,1,0:T(8,128)} %collective-permute-done.22.refs_1_, f32[16,128,128]{2,1,0:T(8,128)} %copy-done.15, f32[16,128,128]{2,1,0:T(8,128)} %copy-done.14, f32[64,128,128]{2,1,0:T(8,128)} %get-tuple-element.124.refs_4_, ...), custom_call_target="tpu_custom_call" | custom-call | flops 80000000 | bytes 356515 | tf_op jit(solution)/shard_map/column/pallas_call | solution.py:710
  740.5 12.2 %adjoint.1 = f32[64,128,128]{2,1,0:T(8,128)} custom-call(s32[1]{0:T(128)} %bitcast.i, f32[8,66,16,128]{3,2,1,0:T(8,128)} %all-to-all-done.7.start.refs_6_, f32[66,128]{1,0:T(8,128)} %copy-done.19, f32[66,128]{1,0:T(8,128)} %copy-done.20, f32[64,128,128]{2,1,0:T(8,128)} %after.6, f32[64,128,128]{2,1,0:T(8,128)} %after.6, f32[64,128,128]{2,1,0:T(8,128)} %after.6, ...), custom_call_target="tpu_custom_call" | custom-call | flops 100000000 | bytes 356515 | tf_op jit(solution)/shard_map/adjoint/pallas_call | solution.py:757
  (186 shorter events, 163.4 us)
Async XLA Ops:
  2.5 13.6 %collective-permute-start.1 = (f32[2,128,128]{2,0,1:T(2,128)S(1)}, f32[2,128,128]{2,0,1:T(2,128)S(1)}, u32[]{:S(2)}, u32[]{:S(2)}) collective-permute-start(f32[2,128,128]{2,0,1:T(2,128)S(1)} %pad_maximum_fusion.9), channel_id=1, source_target_pairs={{4,0},{8,4},{12,8},{16,12},{20,16},{24,20},{28,24},{5,1},{9,5},{13... | collective-permute-start | bytes 393224 | tf_op jit(solution)/shard_map/ppermute | solution.py:779
  4.0 12.1 %collective-permute-start = (f32[2,128,128]{2,0,1:T(2,128)S(1)}, f32[2,128,128]{2,0,1:T(2,128)S(1)}, u32[]{:S(2)}, u32[]{:S(2)}) collective-permute-start(f32[2,128,128]{2,0,1:T(2,128)S(1)} %pad_maximum_fusion.8), channel_id=1, source_target_pairs={{0,4},{4,8},{8,12},{12,16},{16,20},{20,24},{24,28},{1,5},{5,9},{9,... | collective-permute-start | bytes 393224 | tf_op jit(solution)/shard_map/ppermute | solution.py:779
  16.2 10.8 %collective-permute-start.3 = (f32[2,66,128]{2,1,0:T(8,128)S(1)}, f32[2,66,128]{2,1,0:T(8,128)S(1)}, u32[]{:S(2)}, u32[]{:S(2)}) collective-permute-start(f32[2,66,128]{2,1,0:T(8,128)S(1)} %get-tuple-element.165), channel_id=1, source_target_pairs={{1,0},{2,1},{3,2},{5,4},{6,5},{7,6},{9,8},{10,9},{11,10},{13,12},{... | collective-permute-start | bytes 202760 | tf_op jit(solution)/shard_map/ppermute | solution.py:779
  17.5 9.5 %collective-permute-start.2 = (f32[2,66,128]{2,1,0:T(8,128)S(1)}, f32[2,66,128]{2,1,0:T(8,128)S(1)}, u32[]{:S(2)}, u32[]{:S(2)}) collective-permute-start(f32[2,66,128]{2,1,0:T(8,128)S(1)} %get-tuple-element.166), channel_id=1, source_target_pairs={{0,1},{1,2},{2,3},{4,5},{5,6},{6,7},{8,9},{9,10},{10,11},{12,13},{... | collective-permute-start | bytes 202760 | tf_op jit(solution)/shard_map/ppermute | solution.py:779
  27.0 27.9 %collective-permute-start.4 = (f32[16,128,128]{2,1,0:T(8,128)S(1)}, f32[16,128,128]{2,1,0:T(8,128)S(1)}, u32[]{:S(2)}, u32[]{:S(2)}) collective-permute-start(f32[16,128,128]{2,1,0:T(8,128)S(1)} %get-tuple-element.64), channel_id=1, source_target_pairs={{0,1},{1,2},{2,3},{3,0},{4,5},{5,6},{6,7},{7,4},{8,9},{9,10},{10,1... | collective-permute-start | bytes 3145736 | tf_op jit(solution)/shard_map/ppermute | solution.py:791
  55.9 53.8 %all-to-all-start = ((f32[8,64,16,128]{3,2,1,0:T(8,128)}), f32[8,64,16,128]{3,2,1,0:T(8,128)}, u32[]{:S(2)}, u32[]{:S(2)}) async-start(f32[8,64,16,128]{3,2,1,0:T(8,128)} %get-tuple-element.68), calls=%async_computation | async-start | bytes 8388608 | tf_op jit(solution)/shard_map/all_to_all | solution.py:804
  60.6 25.8 %collective-permute-start.5 = (f32[16,128,128]{2,1,0:T(8,128)}, f32[16,128,128]{2,1,0:T(8,128)}, u32[]{:S(2)}, u32[]{:S(2)}) collective-permute-start(f32[16,128,128]{2,1,0:T(8,128)} %get-tuple-element.65), channel_id=1, source_target_pairs={{0,3},{1,0},{2,1},{3,2},{4,7},{5,4},{6,5},{7,6},{8,11},{9,8},{10,9... | collective-permute-start | bytes 3145736 | tf_op jit(solution)/shard_map/ppermute | solution.py:791
  86.3 48.0 %collective-permute-start.6 = (f32[16,128,128]{2,1,0:T(8,128)}, f32[16,128,128]{2,1,0:T(8,128)S(1)}, u32[]{:S(2)}, u32[]{:S(2)}) collective-permute-start(f32[16,128,128]{2,1,0:T(8,128)} %get-tuple-element.66), channel_id=1, source_target_pairs={{0,2},{1,3},{2,0},{3,1},{4,6},{5,7},{6,4},{7,5},{8,10},{9,11},{10,... | collective-permute-start | bytes 3145736 | tf_op jit(solution)/shard_map/ppermute | solution.py:791
  135.2 68.1 %all-to-all-start.1 = ((f32[8,66,16,128]{3,2,1,0:T(8,128)}), f32[8,66,16,128]{3,2,1,0:T(8,128)}, u32[]{:S(2)}, u32[]{:S(2)}) async-start(f32[8,66,16,128]{3,2,1,0:T(8,128)} %bitcast.117), calls=%async_computation.1 | async-start | bytes 8650752 | tf_op jit(solution)/shard_map/all_to_all | solution.py:804
  152.0 28.1 %collective-permute-start.7 = (f32[8,16,16,128]{3,2,1,0:T(8,128)}, f32[8,16,16,128]{3,2,1,0:T(8,128)S(1)}, u32[]{:S(2)}, u32[]{:S(2)}) collective-permute-start(f32[8,16,16,128]{3,2,1,0:T(8,128)} %get-tuple-element.75), channel_id=1, source_target_pairs={{0,1},{1,2},{2,3},{3,0},{4,5},{5,6},{6,7},{7,4},{8,9},{9,10},{10,1... | collective-permute-start | bytes 3145736 | tf_op jit(solution)/shard_map/ppermute | solution.py:791
  152.0 48.2 %collective-permute-start.8 = (f32[8,16,16,128]{3,2,1,0:T(8,128)}, f32[8,16,16,128]{3,2,1,0:T(8,128)S(1)}, u32[]{:S(2)}, u32[]{:S(2)}) collective-permute-start(f32[8,16,16,128]{3,2,1,0:T(8,128)} %get-tuple-element.76), channel_id=1, source_target_pairs={{0,3},{1,0},{2,1},{3,2},{4,7},{5,4},{6,5},{7,6},{8,11},{9,8},{10,9... | collective-permute-start | bytes 3145736 | tf_op jit(solution)/shard_map/ppermute | solution.py:791
  203.4 55.5 %all-to-all-start.2 = ((f32[8,48,16,128]{3,2,1,0:T(8,128)}), f32[8,48,16,128]{3,2,1,0:T(8,128)}, u32[]{:S(2)}, u32[]{:S(2)}) async-start(f32[8,48,16,128]{3,2,1,0:T(8,128)} %pad_maximum_fusion), calls=%async_computation.2 | async-start | bytes 6291456 | tf_op jit(solution)/shard_map/all_to_all | solution.py:804
  208.0 48.9 %collective-permute-start.9 = (f32[8,16,16,128]{3,2,1,0:T(8,128)S(1)}, f32[8,16,16,128]{3,2,1,0:T(8,128)}, u32[]{:S(2)}, u32[]{:S(2)}) collective-permute-start(f32[8,16,16,128]{3,2,1,0:T(8,128)S(1)} %copy-done.28), channel_id=1, source_target_pairs={{0,2},{1,3},{2,0},{3,1},{4,6},{5,7},{6,4},{7,5},{8,10},{9,11},{10,... | collective-permute-start | bytes 3145736 | tf_op jit(solution)/shard_map/ppermute | solution.py:791
  256.9 30.8 %collective-permute-start.10 = (f32[18,128,128]{2,1,0:T(8,128)}, f32[18,128,128]{2,1,0:T(8,128)}, u32[]{:S(2)}, u32[]{:S(2)}) collective-permute-start(f32[18,128,128]{2,1,0:T(8,128)} %get-tuple-element.85), channel_id=1, source_target_pairs={{0,3},{1,0},{2,1},{3,2},{4,7},{5,4},{6,5},{7,6},{8,11},{9,8},{10,9... | collective-permute-start | bytes 3538952 | tf_op jit(solution)/shard_map/ppermute | solution.py:791
  258.9 19.3 %all-to-all-start.3 = ((f32[8,16,16,128]{3,2,1,0:T(8,128)}), f32[8,16,16,128]{3,2,1,0:T(8,128)S(1)}, u32[]{:S(2)}, u32[]{:S(2)}) async-start(f32[8,16,16,128]{3,2,1,0:T(8,128)} %collective-permute-done.9), calls=%async_computation.3 | async-start | bytes 2097152 | tf_op jit(solution)/shard_map/all_to_all | solution.py:804
  287.7 58.7 %all-to-all-start.4 = ((f32[8,66,16,128]{3,2,1,0:T(8,128)}), f32[8,66,16,128]{3,2,1,0:T(8,128)}, u32[]{:S(2)}, u32[]{:S(2)}) async-start(f32[8,66,16,128]{3,2,1,0:T(8,128)} %bitcast.118), calls=%async_computation.4 | async-start | bytes 8650752 | tf_op jit(solution)/shard_map/all_to_all | solution.py:804
  292.4 54.0 %collective-permute-start.11 = (f32[18,128,128]{2,1,0:T(8,128)S(1)}, f32[18,128,128]{2,1,0:T(8,128)}, u32[]{:S(2)}, u32[]{:S(2)}) collective-permute-start(f32[18,128,128]{2,1,0:T(8,128)S(1)} %copy-done.26), channel_id=1, source_target_pairs={{0,2},{1,3},{2,0},{3,1},{4,6},{5,7},{6,4},{7,5},{8,10},{9,11},{10,... | collective-permute-start | bytes 3538952 | tf_op jit(solution)/shard_map/ppermute | solution.py:791
  348.8 5.9 collective-permute-start.13
  367.8 34.0 %collective-permute-start.14 = (f32[16,128,128]{2,1,0:T(8,128)}, f32[16,128,128]{2,1,0:T(8,128)S(1)}, u32[]{:S(2)}, u32[]{:S(2)}) collective-permute-start(f32[16,128,128]{2,1,0:T(8,128)} %get-tuple-element.90.refs_1_), channel_id=1, source_target_pairs={{0,1},{1,2},{2,3},{3,0},{4,5},{5,6},{6,7},{7,4},{8,9},{9,10},{10,1... | collective-permute-start | bytes 3145736 | tf_op jit(solution)/shard_map/ppermute | solution.py:791
  368.8 46.4 %collective-permute-start.15 = (f32[16,128,128]{2,1,0:T(8,128)}, f32[16,128,128]{2,1,0:T(8,128)S(1)}, u32[]{:S(2)}, u32[]{:S(2)}) collective-permute-start(f32[16,128,128]{2,1,0:T(8,128)} %get-tuple-element.92.refs_3_), channel_id=1, source_target_pairs={{0,3},{1,0},{2,1},{3,2},{4,7},{5,4},{6,5},{7,6},{8,11},{9,8},{10,9... | collective-permute-start | bytes 3145736 | tf_op jit(solution)/shard_map/ppermute | solution.py:791
  376.0 67.9 %collective-permute-start.17 = (f32[18,128,128]{2,1,0:T(8,128)}, f32[18,128,128]{2,1,0:T(8,128)}, u32[]{:S(2)}, u32[]{:S(2)}) collective-permute-start(f32[18,128,128]{2,1,0:T(8,128)} %get-tuple-element.96), channel_id=1, source_target_pairs={{0,1},{1,2},{2,3},{3,0},{4,5},{5,6},{6,7},{7,4},{8,9},{9,10},{10,1... | collective-permute-start | bytes 3538952 | tf_op jit(solution)/shard_map/ppermute | solution.py:791
  416.2 70.1 %collective-permute-start.16 = (f32[16,128,128]{2,1,0:T(8,128)}, f32[16,128,128]{2,1,0:T(8,128)}, u32[]{:S(2)}, u32[]{:S(2)}) collective-permute-start(f32[16,128,128]{2,1,0:T(8,128)} %get-tuple-element.95.refs_2_), channel_id=1, source_target_pairs={{0,2},{1,3},{2,0},{3,1},{4,6},{5,7},{6,4},{7,5},{8,10},{9,11},{10,... | collective-permute-start | bytes 3145736 | tf_op jit(solution)/shard_map/ppermute | solution.py:791
  486.3 26.7 %collective-permute-start.18 = (f32[16,128,128]{2,1,0:T(8,128)}, f32[16,128,128]{2,1,0:T(8,128)S(1)}, u32[]{:S(2)}, u32[]{:S(2)}) collective-permute-start(f32[16,128,128]{2,1,0:T(8,128)} %get-tuple-element.113), channel_id=1, source_target_pairs={{0,1},{1,2},{2,3},{3,0},{4,5},{5,6},{6,7},{7,4},{8,9},{9,10},{10,1... | collective-permute-start | bytes 3145736 | tf_op jit(solution)/shard_map/ppermute | solution.py:791
  513.0 28.1 %collective-permute-start.19 = (f32[8,16,16,128]{3,2,1,0:T(8,128)}, f32[8,16,16,128]{3,2,1,0:T(8,128)S(1)}, u32[]{:S(2)}, u32[]{:S(2)}) collective-permute-start(f32[8,16,16,128]{3,2,1,0:T(8,128)} %get-tuple-element.115), channel_id=1, source_target_pairs={{0,1},{1,2},{2,3},{3,0},{4,5},{5,6},{6,7},{7,4},{8,9},{9,10},{10,1... | collective-permute-start | bytes 3145736 | tf_op jit(solution)/shard_map/ppermute | solution.py:791
  513.0 46.5 %collective-permute-start.20 = (f32[8,16,16,128]{3,2,1,0:T(8,128)}, f32[8,16,16,128]{3,2,1,0:T(8,128)S(1)}, u32[]{:S(2)}, u32[]{:S(2)}) collective-permute-start(f32[8,16,16,128]{3,2,1,0:T(8,128)} %get-tuple-element.116), channel_id=1, source_target_pairs={{0,3},{1,0},{2,1},{3,2},{4,7},{5,4},{6,5},{7,6},{8,11},{9,8},{10,9... | collective-permute-start | bytes 3145736 | tf_op jit(solution)/shard_map/ppermute | solution.py:791
  563.6 56.1 %all-to-all-start.5 = ((f32[8,48,16,128]{3,2,1,0:T(8,128)}), f32[8,48,16,128]{3,2,1,0:T(8,128)S(1)}, u32[]{:S(2)}, u32[]{:S(2)}) async-start(f32[8,48,16,128]{3,2,1,0:T(8,128)} %pad_maximum_fusion.1), calls=%async_computation.5 | async-start | bytes 6291456 | tf_op jit(solution)/shard_map/all_to_all | solution.py:804
  567.4 48.6 %collective-permute-start.21 = (f32[8,16,16,128]{3,2,1,0:T(8,128)}, f32[8,16,16,128]{3,2,1,0:T(8,128)S(1)}, u32[]{:S(2)}, u32[]{:S(2)}) collective-permute-start(f32[8,16,16,128]{3,2,1,0:T(8,128)} %get-tuple-element.118), channel_id=1, source_target_pairs={{0,2},{1,3},{2,0},{3,1},{4,6},{5,7},{6,4},{7,5},{8,10},{9,11},{10,... | collective-permute-start | bytes 3145736 | tf_op jit(solution)/shard_map/ppermute | solution.py:791
  617.0 30.8 %collective-permute-start.22 = (f32[16,128,128]{2,1,0:T(8,128)}, f32[16,128,128]{2,1,0:T(8,128)}, u32[]{:S(2)}, u32[]{:S(2)}) collective-permute-start(f32[16,128,128]{2,1,0:T(8,128)} %get-tuple-element.120), channel_id=1, source_target_pairs={{0,3},{1,0},{2,1},{3,2},{4,7},{5,4},{6,5},{7,6},{8,11},{9,8},{10,9... | collective-permute-start | bytes 3145736 | tf_op jit(solution)/shard_map/ppermute | solution.py:791
  647.8 55.2 %all-to-all-start.7 = ((f32[8,66,16,128]{3,2,1,0:T(8,128)}), f32[8,66,16,128]{3,2,1,0:T(8,128)}, u32[]{:S(2)}, u32[]{:S(2)}) async-start(f32[8,66,16,128]{3,2,1,0:T(8,128)} %bitcast.116), calls=%async_computation.7 | async-start | bytes 8650752 | tf_op jit(solution)/shard_map/all_to_all | solution.py:804
  663.8 47.5 %collective-permute-start.27 = (f32[16,128,128]{2,1,0:T(8,128)S(1)}, f32[16,128,128]{2,1,0:T(8,128)S(1)}, u32[]{:S(2)}, u32[]{:S(2)}) collective-permute-start(f32[16,128,128]{2,1,0:T(8,128)S(1)} %copy-done.27), channel_id=1, source_target_pairs={{0,2},{1,3},{2,0},{3,1},{4,6},{5,7},{6,4},{7,5},{8,10},{9,11},{10,... | collective-permute-start | bytes 3145736 | tf_op jit(solution)/shard_map/ppermute | solution.py:791
  726.3 10.1 %all-to-all-start.8 = ((f32[32,1,96]{2,1,0:T(1,128)}), f32[32,1,96]{2,1,0:T(1,128)S(1)}, u32[]{:S(2)}, u32[]{:S(2)}) async-start(f32[32,1,96]{2,1,0:T(1,128)} %bitcast.61), calls=%async_computation.8 | async-start | bytes 32768 | tf_op jit(solution)/shard_map/all_to_all | solution.py:933
  730.4 6.6 collective-permute-start.25
  (33 other events, 280.3 us)

commit v9 on v7

--- a/solution.py
+++ b/solution.py
@@ -871,7 +871,7 @@
     cot_lines = send(cot_lines, far, *pick(cot_lines, near))
     forward_lines = after(first([across(a)], first_n3, 1), *pick(cot_lines, far), second_t3, third_t3)
     back = second(after(cot_lines, forward_lines), second_t3, third_t3, wide)
-    solved = across(forward_lines)
+    solved = across(after(forward_lines, *back))
 
     lifted_pieces = lifted(index, solved, state, *state_x, *state_y, n)
     back, carried_chunks, gone = cross_both(back, (solved,), lifted_pieces, near, far)

time: 746 us -> 745 us (level)
  transfers between devices with their start and end apart: 36 -> 36, of which waited for: 23 -> 24; matrix products, arithmetic and copies ran while one was open for 5% -> 5% of each run, Pallas kernels for 19% -> 18%
where the time goes in v9:
time: 745 us; the launch traced here: 742 us
  waiting for transfers between devices  413 us (55%)
  Pallas kernels  167 us (22%)
  starting transfers between devices  84.6 us (11%)
  local copies, waits for them, and re-layouts  37.7 us (5%)
  blocking collectives  19.6 us (3%)
  other arithmetic  13.6 us (2%)
    ppermute x18, waiting for transfers between devices, send(): lax.ppermute(piece, 'narrow', [(k, (k + d) % n) for k in range(n)])  340 us
    all_to_all x7, waiting for transfers between devices, across(): lax.all_to_all(piece, 'wide', split_axis=0, concat_axis=0, tiled=True)  59.3 us
    pallas_call x3, Pallas kernels, second(): pl.pallas_call(functools.partial(second_kernel, count=count, chunked=bool...  37.7 us
    ppermute x18, starting transfers between devices, send(): lax.ppermute(piece, 'narrow', [(k, (k + d) % n) for k in range(n)])  31.7 us
    all_to_all x7, starting transfers between devices, across(): lax.all_to_all(piece, 'wide', split_axis=0, concat_axis=0, tiled=True)  31 us
    pallas_call x3, Pallas kernels, first(): pl.pallas_call(functools.partial(first_kernel, count=len(flat), lines=blo...  25.6 us
    pallas_call x1, Pallas kernels, frozen(): pl.pallas_call(functools.partial(frozen_kernel, blocks=blocks, groups=gro...  24.8 us
    all_to_all x1, blocking collectives, across(): lax.all_to_all(piece, 'wide', split_axis=0, concat_axis=0, tiled=True)  19.6 us
  transfers between devices with their start and end apart: 36, of which 24 were waited for; matrix products, arithmetic and copies ran while one was open for 5% of the time, Pallas kernels for 18%

profile of v9, /device:TPU:0, one launch (start us, length us, event | category | flops | bytes accessed | tf_op | source)
XLA Modules:
  0.0 742.0 jit_solution(10707943466140114055)
XLA Ops:
  31.8 11.6 %forward.1 = (f32[8,64,16,128]{3,2,1,0:T(8,128)}, f32[64,128,128]{2,1,0:T(8,128)}) custom-call(s32[1]{0:T(128)} %bitcast.i, f32[64,128,128]{2,1,0:T(8,128)} %after.5, f32[64,128,128]{2,1,0:T(8,128)} %after.5, f32[64,128,128]{2,1,0:T(8,128)} %after.5, f32[1,128,128]{2,1,0:T(8,128)} %bitcast.130, f32[1,128,128]{2,1,0:T(8,128)} %bitcast.127, ...), custom_call_target="tpu_custom_call" | custom-call | flops 100000000 | bytes 356515 | tf_op jit(solution)/shard_map/forward/pallas_call | solution.py:308
  43.4 11.4 %collective-permute-done.4.refs_1_ = f32[16,128,128]{2,1,0:T(8,128)S(1)} collective-permute-done((f32[16,128,128]{2,1,0:T(8,128)S(1)}, f32[16,128,128]{2,1,0:T(8,128)S(1)}, u32[]{:S(2)}, u32[]{:S(2)}) %collective-permute-start.4) | collective-permute-done | bytes 1048608 | tf_op jit(solution)/shard_map/ppermute | solution.py:791
  64.6 21.6 %collective-permute-done.5.refs_3_ = f32[16,128,128]{2,1,0:T(8,128)} collective-permute-done((f32[16,128,128]{2,1,0:T(8,128)}, f32[16,128,128]{2,1,0:T(8,128)}, u32[]{:S(2)}, u32[]{:S(2)}) %collective-permute-start.5) | collective-permute-done | bytes 1048608 | tf_op jit(solution)/shard_map/ppermute | solution.py:791
  89.9 19.7 %all-to-all-done = f32[8,64,16,128]{3,2,1,0:T(8,128)} async-done(((f32[8,64,16,128]{3,2,1,0:T(8,128)}), f32[8,64,16,128]{3,2,1,0:T(8,128)}, u32[]{:S(2)}, u32[]{:S(2)}) %all-to-all-start) | async-done | bytes 4194336 | tf_op jit(solution)/shard_map/all_to_all | solution.py:804
  109.6 8.5 %first.3 = f32[528,16,128]{2,1,0:T(8,128)} custom-call(f32[512,16,128]{2,1,0:T(8,128)} %bitcast.19.refs_0_, bf16[512,1536]{1,0:T(8,128)(2,1)} %pad_maximum_fusion.2.refs_1_), custom_call_target="tpu_custom_call" | custom-call | flops 140000000 | bytes 209715 | tf_op jit(solution)/shard_map/first/pallas_call | solution.py:373
  118.1 16.1 %collective-permute-done.6.refs_2_ = f32[16,128,128]{2,1,0:T(8,128)S(1)} collective-permute-done((f32[16,128,128]{2,1,0:T(8,128)}, f32[16,128,128]{2,1,0:T(8,128)S(1)}, u32[]{:S(2)}, u32[]{:S(2)}) %collective-permute-start.6) | collective-permute-done | bytes 1048608 | tf_op jit(solution)/shard_map/ppermute | solution.py:791
  135.2 12.2 %second.3 = (f32[8,16,16,128]{3,2,1,0:T(8,128)}, f32[8,16,16,128]{3,2,1,0:T(8,128)}, f32[8,16,16,128]{3,2,1,0:T(8,128)}, f32[8,16,16,128]{3,2,1,0:T(8,128)}) custom-call(f32[16,128,128]{2,1,0:T(8,128)} %get-tuple-element.72.refs_0_, f32[16,128,128]{2,1,0:T(8,128)} %copy-done.10, f32[16,128,128]{2,1,0:T(8,128)} %copy-done.13, ...), custom_call_target="tpu_custom_call" | custom-call | flops 180000000 | bytes 209715 | tf_op jit(solution)/shard_map/second/pallas_call | solution.py:415
  155.9 24.2 %collective-permute-done.7 = f32[8,16,16,128]{3,2,1,0:T(8,128)S(1)} collective-permute-done((f32[8,16,16,128]{3,2,1,0:T(8,128)}, f32[8,16,16,128]{3,2,1,0:T(8,128)S(1)}, u32[]{:S(2)}, u32[]{:S(2)}) %collective-permute-start.7) | collective-permute-done | bytes 1048608 | tf_op jit(solution)/shard_map/ppermute | solution.py:791
  180.1 20.0 %collective-permute-done.8 = f32[8,16,16,128]{3,2,1,0:T(8,128)S(1)} collective-permute-done((f32[8,16,16,128]{3,2,1,0:T(8,128)}, f32[8,16,16,128]{3,2,1,0:T(8,128)S(1)}, u32[]{:S(2)}, u32[]{:S(2)}) %collective-permute-start.8) | collective-permute-done | bytes 1048608 | tf_op jit(solution)/shard_map/ppermute | solution.py:791
  209.2 9.0 %lifted.1 = (f32[18,128,128]{2,1,0:T(8,128)}, f32[18,128,128]{2,1,0:T(8,128)}, f32[18,128,128]{2,1,0:T(8,128)}, f32[18,128,128]{2,1,0:T(8,128)}) custom-call(s32[1]{0:T(128)} %bitcast.i, f32[8,66,16,128]{3,2,1,0:T(8,128)} %all-to-all-done.1.solved, f32[64,128,128]{2,1,0:T(8,128)} %after.5, f32[1,128,128]{2,1,0:T(8,128)} %bitcast.131, ...), custom_call_target="tpu_custom_call" | custom-call | flops 40000000 | bytes 272629 | tf_op jit(solution)/shard_map/lifted/pallas_call | solution.py:473
  218.2 37.7 %collective-permute-done.9 = f32[8,16,16,128]{3,2,1,0:T(8,128)} collective-permute-done((f32[8,16,16,128]{3,2,1,0:T(8,128)S(1)}, f32[8,16,16,128]{3,2,1,0:T(8,128)}, u32[]{:S(2)}, u32[]{:S(2)}) %collective-permute-start.9) | collective-permute-done | bytes 1048608 | tf_op jit(solution)/shard_map/ppermute | solution.py:791
  265.1 12.2 %all-to-all-done.3 = f32[8,16,16,128]{3,2,1,0:T(8,128)S(1)} async-done(((f32[8,16,16,128]{3,2,1,0:T(8,128)}), f32[8,16,16,128]{3,2,1,0:T(8,128)S(1)}, u32[]{:S(2)}, u32[]{:S(2)}) %all-to-all-start.3) | async-done | bytes 1048608 | tf_op jit(solution)/shard_map/all_to_all | solution.py:804
  278.3 8.6 %first.4 = f32[528,16,128]{2,1,0:T(8,128)} custom-call(f32[384,16,128]{2,1,0:T(8,128)} %bitcast.25.refs_0_, f32[128,16,128]{2,1,0:T(8,128)} %bitcast.120, bf16[512,1536]{1,0:T(8,128)(2,1)} %pad_maximum_fusion.4.refs_2_), custom_call_target="tpu_custom_call" | custom-call | flops 140000000 | bytes 209715 | tf_op jit(solution)/shard_map/first/pallas_call | solution.py:373
  291.6 53.8 %collective-permute-done.11.refs_2_ = f32[18,128,128]{2,1,0:T(8,128)} collective-permute-done((f32[18,128,128]{2,1,0:T(8,128)S(1)}, f32[18,128,128]{2,1,0:T(8,128)}, u32[]{:S(2)}, u32[]{:S(2)}) %collective-permute-start.11) | collective-permute-done | bytes 1179680 | tf_op jit(solution)/shard_map/ppermute | solution.py:791
  354.4 12.4 %reaction.1 = (f32[16,128,128]{2,1,0:T(8,128)}, f32[16,128,128]{2,1,0:T(8,128)}, f32[16,128,128]{2,1,0:T(8,128)}, f32[16,128,128]{2,1,0:T(8,128)}) custom-call(s32[1]{0:T(128)} %bitcast.i, f32[8,66,16,128]{3,2,1,0:T(8,128)} %all-to-all-done.4.carried, f32[66,128]{1,0:T(8,128)} %copy-done.22, f32[66,128]{1,0:T(8,128)} %copy-done.23, f32[64,128,128]{2,1,0:T(8,128)} %after.6, ...), custom_call_target="tpu_custom_call" | custom-call | flops 80000000 | bytes 356515 | tf_op jit(solution)/shard_map/reaction/pallas_call | solution.py:520
  376.0 24.8 %frozen.1 = (f32[64,128,128]{2,1,0:T(8,128)}, f32[24,256]{1,0:T(8,128)}) custom-call(s32[1]{0:T(128)} %bitcast.i, f32[64,128,128]{2,1,0:T(8,128)} %after.5, f32[64,128,128]{2,1,0:T(8,128)} %after.5, f32[64,128,128]{2,1,0:T(8,128)} %after.5, f32[1,128,128]{2,1,0:T(8,128)} %bitcast.132, f32[1,128,128]{2,1,0:T(8,128)} %bitcast.129, f32[66,128]{1,0:T(8,128)} %fusion.1.q_low, ...), custom_call_target="tpu_custom_call" | custom-call | flops 100000000 | bytes 356515 | tf_op jit(solution)/shard_map/frozen/pallas_call | solution.py:664
  400.9 13.5 %collective-permute-done.15.refs_3_ = f32[16,128,128]{2,1,0:T(8,128)S(1)} collective-permute-done((f32[16,128,128]{2,1,0:T(8,128)}, f32[16,128,128]{2,1,0:T(8,128)S(1)}, u32[]{:S(2)}, u32[]{:S(2)}) %collective-permute-start.15) | collective-permute-done | bytes 1048608 | tf_op jit(solution)/shard_map/ppermute | solution.py:791
  421.9 21.1 %collective-permute-done.17.refs_1_ = f32[18,128,128]{2,1,0:T(8,128)} collective-permute-done((f32[18,128,128]{2,1,0:T(8,128)}, f32[18,128,128]{2,1,0:T(8,128)}, u32[]{:S(2)}, u32[]{:S(2)}) %collective-permute-start.17) | collective-permute-done | bytes 1179680 | tf_op jit(solution)/shard_map/ppermute | solution.py:791
  442.9 13.3 %second.4.field = f32[18,512,128]{2,1,0:T(8,128)} custom-call(f32[18,128,128]{2,1,0:T(8,128)} %get-tuple-element.100.refs_0_, f32[18,128,128]{2,1,0:T(8,128)} %collective-permute-done.17.refs_1_, f32[18,128,128]{2,1,0:T(8,128)} %collective-permute-done.11.refs_2_, f32[18,128,128]{2,1,0:T(8,128)} %collective-permute-done.10.refs_3_, ...), custom_call_target="tpu_custom_call" | custom-call | flops 180000000 | bytes 209715 | tf_op jit(solution)/shard_map/second/pallas_call | solution.py:415
  456.3 10.2 %mixed.1 = (f32[16,128,128]{2,1,0:T(8,128)}, f32[16,128,128]{2,1,0:T(8,128)}, f32[16,128,128]{2,1,0:T(8,128)}, f32[16,128,128]{2,1,0:T(8,128)}) custom-call(s32[1]{0:T(128)} %bitcast.i, f32[18,512,128]{2,1,0:T(8,128)} %second.4.field), custom_call_target="tpu_custom_call" | custom-call | flops 80000000 | bytes 188743 | tf_op jit(solution)/shard_map/mixed/pallas_call | solution.py:599
  466.4 18.9 %collective-permute-done.16.refs_2_ = f32[16,128,128]{2,1,0:T(8,128)} collective-permute-done((f32[16,128,128]{2,1,0:T(8,128)}, f32[16,128,128]{2,1,0:T(8,128)}, u32[]{:S(2)}, u32[]{:S(2)}) %collective-permute-start.16) | collective-permute-done | bytes 1048608 | tf_op jit(solution)/shard_map/ppermute | solution.py:791
  487.5 12.2 %second.5 = (f32[8,16,16,128]{3,2,1,0:T(8,128)}, f32[8,16,16,128]{3,2,1,0:T(8,128)}, f32[8,16,16,128]{3,2,1,0:T(8,128)}, f32[8,16,16,128]{3,2,1,0:T(8,128)}) custom-call(f32[16,128,128]{2,1,0:T(8,128)} %get-tuple-element.108.refs_0_, f32[16,128,128]{2,1,0:T(8,128)} %copy-done.11, f32[16,128,128]{2,1,0:T(8,128)} %collective-permute-done.16.refs_2_, ...), custom_call_target="tpu_custom_call" | custom-call | flops 180000000 | bytes 209715 | tf_op jit(solution)/shard_map/second/pallas_call | solution.py:415
  499.7 12.4 %collective-permute-done.18.refs_3_ = f32[16,128,128]{2,1,0:T(8,128)S(1)} collective-permute-done((f32[16,128,128]{2,1,0:T(8,128)}, f32[16,128,128]{2,1,0:T(8,128)S(1)}, u32[]{:S(2)}, u32[]{:S(2)}) %collective-permute-start.18) | collective-permute-done | bytes 1048608 | tf_op jit(solution)/shard_map/ppermute | solution.py:791
  515.9 24.3 %collective-permute-done.19.refs_7_ = f32[8,16,16,128]{3,2,1,0:T(8,128)S(1)} collective-permute-done((f32[8,16,16,128]{3,2,1,0:T(8,128)}, f32[8,16,16,128]{3,2,1,0:T(8,128)S(1)}, u32[]{:S(2)}, u32[]{:S(2)}) %collective-permute-start.19) | collective-permute-done | bytes 1048608 | tf_op jit(solution)/shard_map/ppermute | solution.py:791
  540.2 18.3 %collective-permute-done.20.refs_5_ = f32[8,16,16,128]{3,2,1,0:T(8,128)S(1)} collective-permute-done((f32[8,16,16,128]{3,2,1,0:T(8,128)}, f32[8,16,16,128]{3,2,1,0:T(8,128)S(1)}, u32[]{:S(2)}, u32[]{:S(2)}) %collective-permute-start.20) | collective-permute-done | bytes 1048608 | tf_op jit(solution)/shard_map/ppermute | solution.py:791
  568.9 46.2 %collective-permute-done.21.refs_6_ = f32[8,16,16,128]{3,2,1,0:T(8,128)S(1)} collective-permute-done((f32[8,16,16,128]{3,2,1,0:T(8,128)}, f32[8,16,16,128]{3,2,1,0:T(8,128)S(1)}, u32[]{:S(2)}, u32[]{:S(2)}) %collective-permute-start.21) | collective-permute-done | bytes 1048608 | tf_op jit(solution)/shard_map/ppermute | solution.py:791
  618.7 19.6 %all_to_all.49 = f32[8,16,16,128]{3,2,1,0:T(8,128)} all-to-all(f32[8,16,16,128]{3,2,1,0:T(8,128)} %copy-done.3), channel_id=1, replica_groups=mesh['wide'=8,'narrow'=4] {'wide'}, dimensions={0} | all-to-all | bytes 2097152 | tf_op jit(solution)/shard_map/all_to_all | solution.py:804
  638.3 8.6 %first.5 = f32[528,16,128]{2,1,0:T(8,128)} custom-call(f32[384,16,128]{2,1,0:T(8,128)} %bitcast.119, f32[128,16,128]{2,1,0:T(8,128)} %bitcast.121, bf16[512,1536]{1,0:T(8,128)(2,1)} %pad_maximum_fusion.4.refs_2_), custom_call_target="tpu_custom_call" | custom-call | flops 140000000 | bytes 209715 | tf_op jit(solution)/shard_map/first/pallas_call | solution.py:373
  664.1 11.1 %lines.1.tail = f32[64,128,128]{2,1,0:T(8,128)} custom-call(s32[1]{0:T(128)} %bitcast.i, f32[16,128,128]{2,1,0:T(8,128)} %get-tuple-element.108.refs_0_, f32[16,128,128]{2,1,0:T(8,128)} %get-tuple-element.93.refs_1_, f32[16,128,128]{2,1,0:T(8,128)} %get-tuple-element.98.refs_2_, f32[16,128,128]{2,1,0:T(8,128)} %get-tuple-element.95.refs_3_, ...), custom_call_target="tpu_custom_call" | custom-call | flops 100000000 | bytes 356515 | tf_op jit(solution)/shard_map/lines/pallas_call | solution.py:564
  675.2 26.9 %all-to-all-done.7.start.refs_6_ = f32[8,66,16,128]{3,2,1,0:T(8,128)} async-done(((f32[8,66,16,128]{3,2,1,0:T(8,128)}), f32[8,66,16,128]{3,2,1,0:T(8,128)}, u32[]{:S(2)}, u32[]{:S(2)}) %all-to-all-start.7) | async-done | bytes 4325408 | tf_op jit(solution)/shard_map/all_to_all | solution.py:804
  712.1 12.6 %column.1 = f32[24,256]{1,0:T(8,128)} custom-call(s32[1]{0:T(128)} %bitcast.i, f32[16,128,128]{2,1,0:T(8,128)} %get-tuple-element.104.refs_0_, f32[16,128,128]{2,1,0:T(8,128)} %collective-permute-done.22.refs_1_, f32[16,128,128]{2,1,0:T(8,128)} %copy-done.16, f32[16,128,128]{2,1,0:T(8,128)} %copy-done.15, f32[64,128,128]{2,1,0:T(8,128)} %get-tuple-element.128.refs_4_, ...), custom_call_target="tpu_custom_call" | custom-call | flops 80000000 | bytes 356515 | tf_op jit(solution)/shard_map/column/pallas_call | solution.py:710
  729.2 12.3 %adjoint.1 = f32[64,128,128]{2,1,0:T(8,128)} custom-call(s32[1]{0:T(128)} %bitcast.i, f32[8,66,16,128]{3,2,1,0:T(8,128)} %all-to-all-done.7.start.refs_6_, f32[66,128]{1,0:T(8,128)} %copy-done.20, f32[66,128]{1,0:T(8,128)} %copy-done.21, f32[64,128,128]{2,1,0:T(8,128)} %after.6, f32[64,128,128]{2,1,0:T(8,128)} %after.6, f32[64,128,128]{2,1,0:T(8,128)} %after.6, ...), custom_call_target="tpu_custom_call" | custom-call | flops 100000000 | bytes 356515 | tf_op jit(solution)/shard_map/adjoint/pallas_call | solution.py:757
  (188 shorter events, 152.7 us)
Async XLA Ops:
  2.5 13.5 %collective-permute-start.1 = (f32[2,128,128]{2,0,1:T(2,128)S(1)}, f32[2,128,128]{2,0,1:T(2,128)S(1)}, u32[]{:S(2)}, u32[]{:S(2)}) collective-permute-start(f32[2,128,128]{2,0,1:T(2,128)S(1)} %pad_maximum_fusion.9), channel_id=1, source_target_pairs={{4,0},{8,4},{12,8},{16,12},{20,16},{24,20},{28,24},{5,1},{9,5},{13... | collective-permute-start | bytes 393224 | tf_op jit(solution)/shard_map/ppermute | solution.py:779
  4.0 12.1 %collective-permute-start = (f32[2,128,128]{2,0,1:T(2,128)S(1)}, f32[2,128,128]{2,0,1:T(2,128)S(1)}, u32[]{:S(2)}, u32[]{:S(2)}) collective-permute-start(f32[2,128,128]{2,0,1:T(2,128)S(1)} %pad_maximum_fusion.8), channel_id=1, source_target_pairs={{0,4},{4,8},{8,12},{12,16},{16,20},{20,24},{24,28},{1,5},{5,9},{9,... | collective-permute-start | bytes 393224 | tf_op jit(solution)/shard_map/ppermute | solution.py:779
  16.1 10.8 %collective-permute-start.3 = (f32[2,66,128]{2,1,0:T(8,128)S(1)}, f32[2,66,128]{2,1,0:T(8,128)S(1)}, u32[]{:S(2)}, u32[]{:S(2)}) collective-permute-start(f32[2,66,128]{2,1,0:T(8,128)S(1)} %get-tuple-element.169), channel_id=1, source_target_pairs={{1,0},{2,1},{3,2},{5,4},{6,5},{7,6},{9,8},{10,9},{11,10},{13,12},{... | collective-permute-start | bytes 202760 | tf_op jit(solution)/shard_map/ppermute | solution.py:779
  17.4 9.5 %collective-permute-start.2 = (f32[2,66,128]{2,1,0:T(8,128)S(1)}, f32[2,66,128]{2,1,0:T(8,128)S(1)}, u32[]{:S(2)}, u32[]{:S(2)}) collective-permute-start(f32[2,66,128]{2,1,0:T(8,128)S(1)} %get-tuple-element.170), channel_id=1, source_target_pairs={{0,1},{1,2},{2,3},{4,5},{5,6},{6,7},{8,9},{9,10},{10,11},{12,13},{... | collective-permute-start | bytes 202760 | tf_op jit(solution)/shard_map/ppermute | solution.py:779
  26.9 27.9 %collective-permute-start.4 = (f32[16,128,128]{2,1,0:T(8,128)S(1)}, f32[16,128,128]{2,1,0:T(8,128)S(1)}, u32[]{:S(2)}, u32[]{:S(2)}) collective-permute-start(f32[16,128,128]{2,1,0:T(8,128)S(1)} %get-tuple-element.66), channel_id=1, source_target_pairs={{0,1},{1,2},{2,3},{3,0},{4,5},{5,6},{6,7},{7,4},{8,9},{9,10},{10,1... | collective-permute-start | bytes 3145736 | tf_op jit(solution)/shard_map/ppermute | solution.py:791
  55.8 53.8 %all-to-all-start = ((f32[8,64,16,128]{3,2,1,0:T(8,128)}), f32[8,64,16,128]{3,2,1,0:T(8,128)}, u32[]{:S(2)}, u32[]{:S(2)}) async-start(f32[8,64,16,128]{3,2,1,0:T(8,128)} %get-tuple-element.70), calls=%async_computation | async-start | bytes 8388608 | tf_op jit(solution)/shard_map/all_to_all | solution.py:804
  60.5 25.8 %collective-permute-start.5 = (f32[16,128,128]{2,1,0:T(8,128)}, f32[16,128,128]{2,1,0:T(8,128)}, u32[]{:S(2)}, u32[]{:S(2)}) collective-permute-start(f32[16,128,128]{2,1,0:T(8,128)} %get-tuple-element.67), channel_id=1, source_target_pairs={{0,3},{1,0},{2,1},{3,2},{4,7},{5,4},{6,5},{7,6},{8,11},{9,8},{10,9... | collective-permute-start | bytes 3145736 | tf_op jit(solution)/shard_map/ppermute | solution.py:791
  86.2 48.0 %collective-permute-start.6 = (f32[16,128,128]{2,1,0:T(8,128)}, f32[16,128,128]{2,1,0:T(8,128)S(1)}, u32[]{:S(2)}, u32[]{:S(2)}) collective-permute-start(f32[16,128,128]{2,1,0:T(8,128)} %get-tuple-element.68), channel_id=1, source_target_pairs={{0,2},{1,3},{2,0},{3,1},{4,6},{5,7},{6,4},{7,5},{8,10},{9,11},{10,... | collective-permute-start | bytes 3145736 | tf_op jit(solution)/shard_map/ppermute | solution.py:791
  147.3 55.3 %all-to-all-start.1 = ((f32[8,66,16,128]{3,2,1,0:T(8,128)}), f32[8,66,16,128]{3,2,1,0:T(8,128)}, u32[]{:S(2)}, u32[]{:S(2)}) async-start(f32[8,66,16,128]{3,2,1,0:T(8,128)} %bitcast.117), calls=%async_computation.1 | async-start | bytes 8650752 | tf_op jit(solution)/shard_map/all_to_all | solution.py:804
  152.0 28.1 %collective-permute-start.7 = (f32[8,16,16,128]{3,2,1,0:T(8,128)}, f32[8,16,16,128]{3,2,1,0:T(8,128)S(1)}, u32[]{:S(2)}, u32[]{:S(2)}) collective-permute-start(f32[8,16,16,128]{3,2,1,0:T(8,128)} %get-tuple-element.77), channel_id=1, source_target_pairs={{0,1},{1,2},{2,3},{3,0},{4,5},{5,6},{6,7},{7,4},{8,9},{9,10},{10,1... | collective-permute-start | bytes 3145736 | tf_op jit(solution)/shard_map/ppermute | solution.py:791
  152.1 48.1 %collective-permute-start.8 = (f32[8,16,16,128]{3,2,1,0:T(8,128)}, f32[8,16,16,128]{3,2,1,0:T(8,128)S(1)}, u32[]{:S(2)}, u32[]{:S(2)}) collective-permute-start(f32[8,16,16,128]{3,2,1,0:T(8,128)} %get-tuple-element.78), channel_id=1, source_target_pairs={{0,3},{1,0},{2,1},{3,2},{4,7},{5,4},{6,5},{7,6},{8,11},{9,8},{10,9... | collective-permute-start | bytes 3145736 | tf_op jit(solution)/shard_map/ppermute | solution.py:791
  202.6 55.4 %all-to-all-start.2 = ((f32[8,48,16,128]{3,2,1,0:T(8,128)}), f32[8,48,16,128]{3,2,1,0:T(8,128)}, u32[]{:S(2)}, u32[]{:S(2)}) async-start(f32[8,48,16,128]{3,2,1,0:T(8,128)} %pad_maximum_fusion), calls=%async_computation.2 | async-start | bytes 6291456 | tf_op jit(solution)/shard_map/all_to_all | solution.py:804
  207.0 48.9 %collective-permute-start.9 = (f32[8,16,16,128]{3,2,1,0:T(8,128)S(1)}, f32[8,16,16,128]{3,2,1,0:T(8,128)}, u32[]{:S(2)}, u32[]{:S(2)}) collective-permute-start(f32[8,16,16,128]{3,2,1,0:T(8,128)S(1)} %copy-done.29), channel_id=1, source_target_pairs={{0,2},{1,3},{2,0},{3,1},{4,6},{5,7},{6,4},{7,5},{8,10},{9,11},{10,... | collective-permute-start | bytes 3145736 | tf_op jit(solution)/shard_map/ppermute | solution.py:791
  255.9 30.9 %collective-permute-start.10 = (f32[18,128,128]{2,1,0:T(8,128)}, f32[18,128,128]{2,1,0:T(8,128)}, u32[]{:S(2)}, u32[]{:S(2)}) collective-permute-start(f32[18,128,128]{2,1,0:T(8,128)} %get-tuple-element.88), channel_id=1, source_target_pairs={{0,3},{1,0},{2,1},{3,2},{4,7},{5,4},{6,5},{7,6},{8,11},{9,8},{10,9... | collective-permute-start | bytes 3538952 | tf_op jit(solution)/shard_map/ppermute | solution.py:791
  258.0 19.3 %all-to-all-start.3 = ((f32[8,16,16,128]{3,2,1,0:T(8,128)}), f32[8,16,16,128]{3,2,1,0:T(8,128)S(1)}, u32[]{:S(2)}, u32[]{:S(2)}) async-start(f32[8,16,16,128]{3,2,1,0:T(8,128)} %collective-permute-done.9), calls=%async_computation.3 | async-start | bytes 2097152 | tf_op jit(solution)/shard_map/all_to_all | solution.py:804
  286.8 58.7 %all-to-all-start.4 = ((f32[8,66,16,128]{3,2,1,0:T(8,128)}), f32[8,66,16,128]{3,2,1,0:T(8,128)}, u32[]{:S(2)}, u32[]{:S(2)}) async-start(f32[8,66,16,128]{3,2,1,0:T(8,128)} %bitcast.118), calls=%async_computation.4 | async-start | bytes 8650752 | tf_op jit(solution)/shard_map/all_to_all | solution.py:804
  291.6 53.9 %collective-permute-start.11 = (f32[18,128,128]{2,1,0:T(8,128)S(1)}, f32[18,128,128]{2,1,0:T(8,128)}, u32[]{:S(2)}, u32[]{:S(2)}) collective-permute-start(f32[18,128,128]{2,1,0:T(8,128)S(1)} %copy-done.27), channel_id=1, source_target_pairs={{0,2},{1,3},{2,0},{3,1},{4,6},{5,7},{6,4},{7,5},{8,10},{9,11},{10,... | collective-permute-start | bytes 3538952 | tf_op jit(solution)/shard_map/ppermute | solution.py:791
  347.9 5.9 collective-permute-start.13
  366.8 34.0 %collective-permute-start.14 = (f32[16,128,128]{2,1,0:T(8,128)}, f32[16,128,128]{2,1,0:T(8,128)S(1)}, u32[]{:S(2)}, u32[]{:S(2)}) collective-permute-start(f32[16,128,128]{2,1,0:T(8,128)} %get-tuple-element.93.refs_1_), channel_id=1, source_target_pairs={{0,1},{1,2},{2,3},{3,0},{4,5},{5,6},{6,7},{7,4},{8,9},{9,10},{10,1... | collective-permute-start | bytes 3145736 | tf_op jit(solution)/shard_map/ppermute | solution.py:791
  367.9 46.4 %collective-permute-start.15 = (f32[16,128,128]{2,1,0:T(8,128)}, f32[16,128,128]{2,1,0:T(8,128)S(1)}, u32[]{:S(2)}, u32[]{:S(2)}) collective-permute-start(f32[16,128,128]{2,1,0:T(8,128)} %get-tuple-element.95.refs_3_), channel_id=1, source_target_pairs={{0,3},{1,0},{2,1},{3,2},{4,7},{5,4},{6,5},{7,6},{8,11},{9,8},{10,9... | collective-permute-start | bytes 3145736 | tf_op jit(solution)/shard_map/ppermute | solution.py:791
  375.1 67.9 %collective-permute-start.17 = (f32[18,128,128]{2,1,0:T(8,128)}, f32[18,128,128]{2,1,0:T(8,128)}, u32[]{:S(2)}, u32[]{:S(2)}) collective-permute-start(f32[18,128,128]{2,1,0:T(8,128)} %get-tuple-element.99), channel_id=1, source_target_pairs={{0,1},{1,2},{2,3},{3,0},{4,5},{5,6},{6,7},{7,4},{8,9},{9,10},{10,1... | collective-permute-start | bytes 3538952 | tf_op jit(solution)/shard_map/ppermute | solution.py:791
  415.3 70.0 %collective-permute-start.16 = (f32[16,128,128]{2,1,0:T(8,128)}, f32[16,128,128]{2,1,0:T(8,128)}, u32[]{:S(2)}, u32[]{:S(2)}) collective-permute-start(f32[16,128,128]{2,1,0:T(8,128)} %get-tuple-element.98.refs_2_), channel_id=1, source_target_pairs={{0,2},{1,3},{2,0},{3,1},{4,6},{5,7},{6,4},{7,5},{8,10},{9,11},{10,... | collective-permute-start | bytes 3145736 | tf_op jit(solution)/shard_map/ppermute | solution.py:791
  485.4 26.7 %collective-permute-start.18 = (f32[16,128,128]{2,1,0:T(8,128)}, f32[16,128,128]{2,1,0:T(8,128)S(1)}, u32[]{:S(2)}, u32[]{:S(2)}) collective-permute-start(f32[16,128,128]{2,1,0:T(8,128)} %get-tuple-element.116), channel_id=1, source_target_pairs={{0,1},{1,2},{2,3},{3,0},{4,5},{5,6},{6,7},{7,4},{8,9},{9,10},{10,1... | collective-permute-start | bytes 3145736 | tf_op jit(solution)/shard_map/ppermute | solution.py:791
  512.1 28.1 %collective-permute-start.19 = (f32[8,16,16,128]{3,2,1,0:T(8,128)}, f32[8,16,16,128]{3,2,1,0:T(8,128)S(1)}, u32[]{:S(2)}, u32[]{:S(2)}) collective-permute-start(f32[8,16,16,128]{3,2,1,0:T(8,128)} %get-tuple-element.118), channel_id=1, source_target_pairs={{0,1},{1,2},{2,3},{3,0},{4,5},{5,6},{6,7},{7,4},{8,9},{9,10},{10,1... | collective-permute-start | bytes 3145736 | tf_op jit(solution)/shard_map/ppermute | solution.py:791
  512.1 46.4 %collective-permute-start.20 = (f32[8,16,16,128]{3,2,1,0:T(8,128)}, f32[8,16,16,128]{3,2,1,0:T(8,128)S(1)}, u32[]{:S(2)}, u32[]{:S(2)}) collective-permute-start(f32[8,16,16,128]{3,2,1,0:T(8,128)} %get-tuple-element.119), channel_id=1, source_target_pairs={{0,3},{1,0},{2,1},{3,2},{4,7},{5,4},{6,5},{7,6},{8,11},{9,8},{10,9... | collective-permute-start | bytes 3145736 | tf_op jit(solution)/shard_map/ppermute | solution.py:791
  562.6 56.1 %all-to-all-start.5 = ((f32[8,48,16,128]{3,2,1,0:T(8,128)}), f32[8,48,16,128]{3,2,1,0:T(8,128)S(1)}, u32[]{:S(2)}, u32[]{:S(2)}) async-start(f32[8,48,16,128]{3,2,1,0:T(8,128)} %pad_maximum_fusion.1), calls=%async_computation.5 | async-start | bytes 6291456 | tf_op jit(solution)/shard_map/all_to_all | solution.py:804
  566.5 48.6 %collective-permute-start.21 = (f32[8,16,16,128]{3,2,1,0:T(8,128)}, f32[8,16,16,128]{3,2,1,0:T(8,128)S(1)}, u32[]{:S(2)}, u32[]{:S(2)}) collective-permute-start(f32[8,16,16,128]{3,2,1,0:T(8,128)} %get-tuple-element.121), channel_id=1, source_target_pairs={{0,2},{1,3},{2,0},{3,1},{4,6},{5,7},{6,4},{7,5},{8,10},{9,11},{10,... | collective-permute-start | bytes 3145736 | tf_op jit(solution)/shard_map/ppermute | solution.py:791
  616.0 30.8 %collective-permute-start.22 = (f32[16,128,128]{2,1,0:T(8,128)}, f32[16,128,128]{2,1,0:T(8,128)}, u32[]{:S(2)}, u32[]{:S(2)}) collective-permute-start(f32[16,128,128]{2,1,0:T(8,128)} %get-tuple-element.123), channel_id=1, source_target_pairs={{0,3},{1,0},{2,1},{3,2},{4,7},{5,4},{6,5},{7,6},{8,11},{9,8},{10,9... | collective-permute-start | bytes 3145736 | tf_op jit(solution)/shard_map/ppermute | solution.py:791
  646.8 55.2 %all-to-all-start.7 = ((f32[8,66,16,128]{3,2,1,0:T(8,128)}), f32[8,66,16,128]{3,2,1,0:T(8,128)}, u32[]{:S(2)}, u32[]{:S(2)}) async-start(f32[8,66,16,128]{3,2,1,0:T(8,128)} %bitcast.116), calls=%async_computation.7 | async-start | bytes 8650752 | tf_op jit(solution)/shard_map/all_to_all | solution.py:804
  662.9 48.3 %collective-permute-start.27 = (f32[16,128,128]{2,1,0:T(8,128)S(1)}, f32[16,128,128]{2,1,0:T(8,128)S(1)}, u32[]{:S(2)}, u32[]{:S(2)}) collective-permute-start(f32[16,128,128]{2,1,0:T(8,128)S(1)} %copy-done.28), channel_id=1, source_target_pairs={{0,2},{1,3},{2,0},{3,1},{4,6},{5,7},{6,4},{7,5},{8,10},{9,11},{10,... | collective-permute-start | bytes 3145736 | tf_op jit(solution)/shard_map/ppermute | solution.py:791
  704.5 6.6 collective-permute-start.26
  726.2 15.3 %all-to-all-start.8 = ((f32[32,1,96]{2,1,0:T(1,128)}), f32[32,1,96]{2,1,0:T(1,128)S(1)}, u32[]{:S(2)}, u32[]{:S(2)}) async-start(f32[32,1,96]{2,1,0:T(1,128)} %bitcast.61), calls=%async_computation.8 | async-start | bytes 32768 | tf_op jit(solution)/shard_map/all_to_all | solution.py:934
  (34 other events, 359.2 us)
